TPU v7x, 32 devices: a whole 2x2x4 slice. The times are simulated.
32 devices in a mesh: dp: 8 (over y, x, core), fsdp: 4 (over z).
Axes of the slice: x: 2, y: 2, z: 4, core: 2. Of those that a mesh axis runs over, the one named last changes fastest.
Arguments:
- tokens: bfloat16 [16384, 1024], P(('dp', 'fsdp')), may hold values from -6 to 6
- cotangent: bfloat16 [16384, 1024], P(('dp', 'fsdp')), may hold values from -6 to 6
- cont_lengths: int32 [8, 8], P('dp'), may hold values from 1 to 256, 1024 in all within a row
- ln1_gain: bfloat16 [1, 1024], P(None, 'fsdp'), may hold values from 0.099609375 to 1.8984375
- ln1_bias: bfloat16 [1, 1024], P(None, 'fsdp'), may hold values from -3 to 3
- w_qkv: bfloat16 [1, 1024, 3072], P(None, 'fsdp'), may hold values from -0.1875 to 0.1875
- q_bias: bfloat16 [1, 1024], P(None, 'fsdp'), may hold values from -3 to 3
- v_bias: bfloat16 [1, 1024], P(None, 'fsdp'), may hold values from -3 to 3
- w_out: bfloat16 [1, 1024, 1024], P(None, 'fsdp'), may hold values from -1 to 1
- out_bias: bfloat16 [1, 1024], P(None, 'fsdp'), may hold values from -2 to 2
- ln2_gain: bfloat16 [1, 1024], P(None, 'fsdp'), may hold values from 0.099609375 to 1.8984375
- ln2_bias: bfloat16 [1, 1024], P(None, 'fsdp'), may hold values from -3 to 3
- w_up: bfloat16 [1, 1024, 4096], P(None, 'fsdp'), may hold values from -0.1875 to 0.1875
- up_bias: bfloat16 [1, 4096], P(None, 'fsdp'), may hold values from -3 to 3
- w_down: bfloat16 [1, 4096, 1024], P(None, 'fsdp'), may hold values from -0.125 to 0.125
- down_bias: bfloat16 [1, 1024], P(None, 'fsdp'), may hold values from -2 to 2
Outputs:
- output: bfloat16 [16384, 1024], P(('dp', 'fsdp'))
- input_grad: bfloat16 [16384, 1024], P(('dp', 'fsdp'))
- grad_ln1_gain: float32 [1, 1024], P(None, 'fsdp')
- grad_ln1_bias: float32 [1, 1024], P(None, 'fsdp')
- grad_w_qkv: float32 [1, 1024, 3072], P(None, 'fsdp')
- grad_q_bias: float32 [1, 1024], P(None, 'fsdp')
- grad_v_bias: float32 [1, 1024], P(None, 'fsdp')
- grad_w_out: float32 [1, 1024, 1024], P(None, 'fsdp')
- grad_out_bias: float32 [1, 1024], P(None, 'fsdp')
- grad_ln2_gain: float32 [1, 1024], P(None, 'fsdp')
- grad_ln2_bias: float32 [1, 1024], P(None, 'fsdp')
- grad_w_up: float32 [1, 1024, 4096], P(None, 'fsdp')
- grad_up_bias: float32 [1, 4096], P(None, 'fsdp')
- grad_w_down: float32 [1, 4096, 1024], P(None, 'fsdp')
- grad_down_bias: float32 [1, 1024], P(None, 'fsdp')
Inputs may be any that keep to these rules, and one draw needn't show every extreme that they name: `cont_lengths`: each group's 8 continuation lengths sum to 1024, and in every group the longest equals 256.
All inputs are finite; a program needn't handle non-finite values.
Results may differ from a plain program's by a relative error of at most 0.025.
Values may be sent and summed in bfloat16 or wider, within the bound.
No kernel may reach another device: no remote copies, remote signals or barrier semaphores. Data moves between devices by JAX's collectives and lax.ppermute only.
A program may use at most 192 MiB of HBM per device.

v0:
```python
import jax
import jax.numpy as jnp
from jax import lax
from jax.sharding import PartitionSpec as P

H = 16
LAYERS = 1


EPSILON = 1e-05
NEG_LARGE = -1e30


def norm_apply(stream, norm_gain, norm_bias):
    row_mean = jnp.mean(stream, -1, keepdims=True)
    centered = stream - row_mean
    variance = jnp.mean(centered * centered, -1, keepdims=True)
    return centered * lax.rsqrt(variance + EPSILON) * norm_gain + norm_bias


def gelu_tanh(values_in):
    return jax.nn.gelu(values_in, approximate=True)


def segment_ids(lengths, group_len):
    prompt_len = group_len // 2
    cont_ends = jnp.cumsum(lengths)
    positions = jnp.arange(prompt_len, dtype=jnp.int32)
    cont_ids = 1 + jnp.sum((positions[:, None] >= cont_ends[None, :]).astype(jnp.int32), 1)
    return jnp.concatenate([jnp.zeros((prompt_len,), jnp.int32), cont_ids])


def fetch_weights(params, layer_index):
    sliced = [weight_array[layer_index] for weight_array in params]
    return (
        lax.all_gather(sliced[0], "fsdp", axis=0, tiled=True),
        lax.all_gather(sliced[1], "fsdp", axis=0, tiled=True),
        lax.all_gather(sliced[2], "fsdp", axis=0, tiled=True),
        lax.all_gather(sliced[3], "fsdp", axis=0, tiled=True),
        lax.all_gather(sliced[4], "fsdp", axis=0, tiled=True),
        lax.all_gather(sliced[5], "fsdp", axis=0, tiled=True),
        lax.all_gather(sliced[6], "fsdp", axis=0, tiled=True),
        lax.all_gather(sliced[7], "fsdp", axis=0, tiled=True),
        lax.all_gather(sliced[8], "fsdp", axis=0, tiled=True),
        lax.all_gather(sliced[9], "fsdp", axis=0, tiled=True),
        lax.all_gather(sliced[10], "fsdp", axis=0, tiled=True),
        lax.all_gather(sliced[11], "fsdp", axis=0, tiled=True),
        lax.all_gather(sliced[12], "fsdp", axis=0, tiled=True),
    )


def fetch_again(params, layer_index):
    sliced = [weight_array[layer_index] for weight_array in params]
    return (
        lax.all_gather(sliced[0], "fsdp", axis=0, tiled=True),
        lax.all_gather(sliced[1], "fsdp", axis=0, tiled=True),
        lax.all_gather(sliced[2], "fsdp", axis=0, tiled=True),
        lax.all_gather(sliced[3], "fsdp", axis=0, tiled=True),
        lax.all_gather(sliced[4], "fsdp", axis=0, tiled=True),
        lax.all_gather(sliced[5], "fsdp", axis=0, tiled=True),
        lax.all_gather(sliced[6], "fsdp", axis=0, tiled=True),
        lax.all_gather(sliced[7], "fsdp", axis=0, tiled=True),
        lax.all_gather(sliced[8], "fsdp", axis=0, tiled=True),
        lax.all_gather(sliced[9], "fsdp", axis=0, tiled=True),
        lax.all_gather(sliced[10], "fsdp", axis=0, tiled=True),
        lax.all_gather(sliced[11], "fsdp", axis=0, tiled=True),
        lax.all_gather(sliced[12], "fsdp", axis=0, tiled=True),
    )


def reduce_sectioned(grads):
    shards = (
        lax.psum_scatter(
            grads[0].astype(jnp.bfloat16), "fsdp", scatter_dimension=0, tiled=True
        ).astype(jnp.float32),
        lax.psum_scatter(
            grads[1].astype(jnp.bfloat16), "fsdp", scatter_dimension=0, tiled=True
        ).astype(jnp.float32),
        lax.psum_scatter(
            grads[2].astype(jnp.bfloat16), "fsdp", scatter_dimension=0, tiled=True
        ).astype(jnp.float32),
        lax.psum_scatter(
            grads[3].astype(jnp.bfloat16), "fsdp", scatter_dimension=0, tiled=True
        ).astype(jnp.float32),
        lax.psum_scatter(
            grads[4].astype(jnp.bfloat16), "fsdp", scatter_dimension=0, tiled=True
        ).astype(jnp.float32),
        lax.psum_scatter(
            grads[5].astype(jnp.bfloat16), "fsdp", scatter_dimension=0, tiled=True
        ).astype(jnp.float32),
        lax.psum_scatter(
            grads[6].astype(jnp.bfloat16), "fsdp", scatter_dimension=0, tiled=True
        ).astype(jnp.float32),
        lax.psum_scatter(
            grads[7].astype(jnp.bfloat16), "fsdp", scatter_dimension=0, tiled=True
        ).astype(jnp.float32),
        lax.psum_scatter(
            grads[8].astype(jnp.bfloat16), "fsdp", scatter_dimension=0, tiled=True
        ).astype(jnp.float32),
        lax.psum_scatter(
            grads[9].astype(jnp.bfloat16), "fsdp", scatter_dimension=0, tiled=True
        ).astype(jnp.float32),
        lax.psum_scatter(
            grads[10].astype(jnp.bfloat16), "fsdp", scatter_dimension=0, tiled=True
        ).astype(jnp.float32),
        lax.psum_scatter(
            grads[11].astype(jnp.bfloat16), "fsdp", scatter_dimension=0, tiled=True
        ).astype(jnp.float32),
        lax.psum_scatter(
            grads[12].astype(jnp.bfloat16), "fsdp", scatter_dimension=0, tiled=True
        ).astype(jnp.float32),
    )
    return (
        lax.psum(shards[0].astype(jnp.bfloat16), "dp").astype(jnp.float32),
        lax.psum(shards[1].astype(jnp.bfloat16), "dp").astype(jnp.float32),
        lax.psum(shards[2].astype(jnp.bfloat16), "dp").astype(jnp.float32),
        lax.psum(shards[3].astype(jnp.bfloat16), "dp").astype(jnp.float32),
        lax.psum(shards[4].astype(jnp.bfloat16), "dp").astype(jnp.float32),
        lax.psum(shards[5].astype(jnp.bfloat16), "dp").astype(jnp.float32),
        lax.psum(shards[6].astype(jnp.bfloat16), "dp").astype(jnp.float32),
        lax.psum(shards[7].astype(jnp.bfloat16), "dp").astype(jnp.float32),
        lax.psum(shards[8].astype(jnp.bfloat16), "dp").astype(jnp.float32),
        lax.psum(shards[9].astype(jnp.bfloat16), "dp").astype(jnp.float32),
        lax.psum(shards[10].astype(jnp.bfloat16), "dp").astype(jnp.float32),
        lax.psum(shards[11].astype(jnp.bfloat16), "dp").astype(jnp.float32),
        lax.psum(shards[12].astype(jnp.bfloat16), "dp").astype(jnp.float32),
    )


def body(
    tokens,
    cotangent,
    cont_lengths,
    ln1_gain,
    ln1_bias,
    w_qkv,
    q_bias,
    v_bias,
    w_out,
    out_bias,
    ln2_gain,
    ln2_bias,
    w_up,
    up_bias,
    w_down,
    down_bias,
):
    params = (
        ln1_gain,
        ln1_bias,
        w_qkv,
        q_bias,
        v_bias,
        w_out,
        out_bias,
        ln2_gain,
        ln2_bias,
        w_up,
        up_bias,
        w_down,
        down_bias,
    )
    row_count = tokens.shape[0]
    model_width = tokens.shape[1]
    fsdp_size = lax.axis_size("fsdp")
    group_len = row_count * fsdp_size
    head_count = H
    head_dim = model_width // head_count
    score_scale = head_dim ** (-0.5)
    block_size = min(512, group_len // 2)
    block_total = group_len // block_size
    seg_all = segment_ids(cont_lengths[0], group_len)
    first_pos = lax.axis_index("fsdp") * row_count
    query_pos = first_pos + jnp.arange(row_count, dtype=jnp.int32)
    query_seg = lax.dynamic_slice_in_dim(seg_all, first_pos, row_count)
    key_range = jnp.arange(block_size, dtype=jnp.int32)

    def block_keys(block_index):
        block_start = block_index * block_size
        key_seg = lax.dynamic_slice_in_dim(seg_all, block_start, block_size)
        key_pos = block_start + key_range
        allowed = (key_pos[None, :] <= query_pos[:, None]) & (
            (key_seg[None, :] == 0) | (key_seg[None, :] == query_seg[:, None])
        )
        needed_flag = (block_start <= first_pos + row_count - 1) & (
            (key_seg[0] == 0) | (key_seg[block_size - 1] >= query_seg[0])
        )
        return (block_start, allowed, needed_flag)

    def key_value_block(keys_all, values_all, block_start):
        key_block = lax.dynamic_slice_in_dim(keys_all, block_start, block_size, 0).reshape(
            block_size, head_count, head_dim
        )
        value_block = lax.dynamic_slice_in_dim(values_all, block_start, block_size, 0).reshape(
            block_size, head_count, head_dim
        )
        return (key_block, value_block)

    stream = tokens.astype(jnp.float32)
    layer_index = 0
    weights = fetch_weights(params, layer_index)
    (
        gain_one,
        bias_one,
        weight_qkv,
        bias_q,
        bias_v,
        weight_out,
        bias_out,
        gain_two,
        bias_two,
        weight_up,
        bias_up,
        weight_down,
        bias_down,
    ) = weights
    hidden_one = norm_apply(
        stream, gain_one.astype(jnp.float32), bias_one.astype(jnp.float32)
    ).astype(jnp.bfloat16)
    combined = jnp.dot(hidden_one, weight_qkv, preferred_element_type=jnp.float32)
    queries = (combined[:, :model_width] + bias_q.astype(jnp.float32)).astype(jnp.bfloat16)
    keys_local = combined[:, model_width : 2 * model_width].astype(jnp.bfloat16)
    values_local = (combined[:, 2 * model_width :] + bias_v.astype(jnp.float32)).astype(
        jnp.bfloat16
    )
    keys_all = lax.all_gather(keys_local, "fsdp", axis=0, tiled=True)
    values_all = lax.all_gather(values_local, "fsdp", axis=0, tiled=True)
    query_heads = queries.reshape(row_count, head_count, head_dim)
    start_state = (
        jnp.full((head_count, row_count), NEG_LARGE, jnp.float32),
        jnp.zeros((head_count, row_count), jnp.float32),
        jnp.zeros((row_count, head_count, head_dim), jnp.float32),
    )

    def visit(block_index, carry):
        block_start, allowed, needed_flag = block_keys(block_index)

        def visit_work(state):
            row_max, row_total, weighted = state
            key_block, value_block = key_value_block(keys_all, values_all, block_start)
            scores = (
                jnp.einsum(
                    "qhd,khd->hqk", query_heads, key_block, preferred_element_type=jnp.float32
                )
                * score_scale
            )
            scores = jnp.where(allowed[None], scores, NEG_LARGE)
            new_max = jnp.maximum(row_max, jnp.max(scores, -1))
            probs = jnp.where(allowed[None], jnp.exp(scores - new_max[:, :, None]), 0.0)
            fade = jnp.exp(row_max - new_max)
            row_total = row_total * fade + jnp.sum(probs, -1)
            weighted = weighted * fade.T[:, :, None] + jnp.einsum(
                "hqk,khd->qhd",
                probs.astype(jnp.bfloat16),
                value_block,
                preferred_element_type=jnp.float32,
            )
            return (new_max, row_total, weighted)

        return lax.cond(needed_flag, visit_work, lambda state: state, carry)

    row_max, row_total, weighted = lax.fori_loop(0, block_total, visit, start_state)
    attended = (weighted / row_total.T[:, :, None]).reshape(row_count, model_width)
    attended, log_total = (attended, row_max + jnp.log(row_total))
    attn_low = attended.astype(jnp.bfloat16)
    middle = stream + (
        jnp.dot(attn_low, weight_out, preferred_element_type=jnp.float32)
        + bias_out.astype(jnp.float32)
    )
    hidden_two = norm_apply(
        middle, gain_two.astype(jnp.float32), bias_two.astype(jnp.float32)
    ).astype(jnp.bfloat16)
    before_act = jnp.dot(
        hidden_two, weight_up, preferred_element_type=jnp.float32
    ) + bias_up.astype(jnp.float32)
    activated = gelu_tanh(before_act).astype(jnp.bfloat16)
    result = middle + (
        jnp.dot(activated, weight_down, preferred_element_type=jnp.float32)
        + bias_down.astype(jnp.float32)
    )
    stream, saved = (
        result,
        (
            stream,
            hidden_one,
            queries,
            keys_all,
            values_all,
            attended,
            log_total,
            attn_low,
            middle,
            hidden_two,
            before_act,
            activated,
        ),
    )
    saved_layers = [saved]
    output = stream.astype(jnp.bfloat16)
    grad_stream = cotangent.astype(jnp.float32)
    reduced = [None] * LAYERS
    for layer_index in reversed(range(LAYERS)):
        weights = fetch_again(params, layer_index)
        (
            layer_gain_one,
            layer_bias_one,
            layer_weight_qkv,
            layer_bias_q,
            layer_bias_v,
            layer_weight_out,
            layer_bias_out,
            layer_gain_two,
            layer_bias_two,
            layer_weight_up,
            layer_bias_up,
            layer_weight_down,
            layer_bias_down,
        ) = weights
        (
            layer_stream,
            layer_hidden_one,
            layer_queries,
            layer_keys_all,
            layer_values_all,
            layer_attended,
            layer_log_total,
            layer_attn_low,
            layer_middle,
            layer_hidden_two,
            layer_before_act,
            layer_activated,
        ) = saved_layers[layer_index]
        grad_branch = grad_stream.astype(jnp.bfloat16)
        grad_bias_down = jnp.sum(grad_branch.astype(jnp.float32), 0)
        grad_weight_down = jnp.einsum(
            "tf,td->fd", layer_activated, grad_branch, preferred_element_type=jnp.float32
        )
        grad_activated = jnp.einsum(
            "td,fd->tf", grad_branch, layer_weight_down, preferred_element_type=jnp.float32
        )
        grad_before = jax.vjp(gelu_tanh, layer_before_act)[1](grad_activated)[0].astype(
            jnp.bfloat16
        )
        grad_bias_up = jnp.sum(grad_before.astype(jnp.float32), 0)
        grad_weight_up = jnp.einsum(
            "td,tf->df", layer_hidden_two, grad_before, preferred_element_type=jnp.float32
        )
        grad_hidden_two = jnp.einsum(
            "tf,df->td", grad_before, layer_weight_up, preferred_element_type=jnp.float32
        )
        norm_pull = jax.vjp(
            norm_apply,
            layer_middle,
            layer_gain_two.astype(jnp.float32),
            layer_bias_two.astype(jnp.float32),
        )[1]
        grad_middle_norm, grad_gain_two, grad_bias_two = norm_pull(grad_hidden_two)
        grad_middle = grad_stream + grad_middle_norm
        grad_attn_branch = grad_middle.astype(jnp.bfloat16)
        grad_bias_out = jnp.sum(grad_attn_branch.astype(jnp.float32), 0)
        grad_weight_out = jnp.einsum(
            "td,te->de", layer_attn_low, grad_attn_branch, preferred_element_type=jnp.float32
        )
        grad_attended = jnp.einsum(
            "te,de->td", grad_attn_branch, layer_weight_out, preferred_element_type=jnp.float32
        ).astype(jnp.bfloat16)
        layer_row_delta = jnp.sum(
            (grad_attended.astype(jnp.float32) * layer_attended).reshape(
                row_count, head_count, head_dim
            ),
            -1,
        ).T
        attend_keys_all = layer_keys_all
        attend_values_all = layer_values_all
        row_delta = layer_row_delta
        attend_log_total = layer_log_total
        attend_query_heads = layer_queries.reshape(row_count, head_count, head_dim)
        grad_heads = grad_attended.reshape(row_count, head_count, head_dim)
        empty_keys = jnp.zeros((group_len, head_count, head_dim), jnp.float32)
        empty_query = jnp.zeros((row_count, head_count, head_dim), jnp.float32)
        attend_start_state = (empty_query, empty_keys, empty_keys)

        def attend_visit(block_index, carry):
            block_start, allowed, needed_flag = block_keys(block_index)

            def attend_work(state):
                key_block, value_block = key_value_block(
                    attend_keys_all, attend_values_all, block_start
                )
                scores = (
                    jnp.einsum(
                        "qhd,khd->hqk",
                        attend_query_heads,
                        key_block,
                        preferred_element_type=jnp.float32,
                    )
                    * score_scale
                )
                probs = jnp.where(
                    allowed[None], jnp.exp(scores - attend_log_total[:, :, None]), 0.0
                )
                grad_probs = jnp.einsum(
                    "qhd,khd->hqk", grad_heads, value_block, preferred_element_type=jnp.float32
                )
                grad_scores = (probs * (grad_probs - row_delta[:, :, None])).astype(jnp.bfloat16)
                grad_query = (
                    state[0]
                    + jnp.einsum(
                        "hqk,khd->qhd", grad_scores, key_block, preferred_element_type=jnp.float32
                    )
                    * score_scale
                )
                key_part = (
                    jnp.einsum(
                        "hqk,qhd->khd",
                        grad_scores,
                        attend_query_heads,
                        preferred_element_type=jnp.float32,
                    )
                    * score_scale
                )
                value_part = jnp.einsum(
                    "hqk,qhd->khd",
                    probs.astype(jnp.bfloat16),
                    grad_heads,
                    preferred_element_type=jnp.float32,
                )
                grad_key = lax.dynamic_update_slice_in_dim(state[1], key_part, block_start, 0)
                grad_value = lax.dynamic_update_slice_in_dim(state[2], value_part, block_start, 0)
                return (grad_query, grad_key, grad_value)

            return lax.cond(needed_flag, attend_work, lambda state: state, carry)

        final_state = lax.fori_loop(0, block_total, attend_visit, attend_start_state)
        layer_grad_query = final_state[0].reshape(row_count, model_width)
        grad_key_all = final_state[1].reshape(group_len, model_width)
        grad_value_all = final_state[2].reshape(group_len, model_width)
        grad_keys = lax.psum_scatter(
            grad_key_all.astype(jnp.bfloat16), "fsdp", scatter_dimension=0, tiled=True
        )
        grad_values = lax.psum_scatter(
            grad_value_all.astype(jnp.bfloat16), "fsdp", scatter_dimension=0, tiled=True
        )
        grad_query_low = layer_grad_query.astype(jnp.bfloat16)
        grad_combined = jnp.concatenate([grad_query_low, grad_keys, grad_values], 1)
        grad_bias_q = jnp.sum(grad_query_low.astype(jnp.float32), 0)
        grad_bias_v = jnp.sum(grad_values.astype(jnp.float32), 0)
        grad_weight_qkv = jnp.einsum(
            "td,te->de", layer_hidden_one, grad_combined, preferred_element_type=jnp.float32
        )
        grad_hidden_one = jnp.einsum(
            "te,de->td", grad_combined, layer_weight_qkv, preferred_element_type=jnp.float32
        )
        norm_pull_one = jax.vjp(
            norm_apply,
            layer_stream,
            layer_gain_one.astype(jnp.float32),
            layer_bias_one.astype(jnp.float32),
        )[1]
        grad_stream_norm, grad_gain_one, grad_bias_one = norm_pull_one(grad_hidden_one)
        grads = (
            grad_gain_one,
            grad_bias_one,
            grad_weight_qkv,
            grad_bias_q,
            grad_bias_v,
            grad_weight_out,
            grad_bias_out,
            grad_gain_two,
            grad_bias_two,
            grad_weight_up,
            grad_bias_up,
            grad_weight_down,
            grad_bias_down,
        )
        grad_stream, grads = (grad_middle + grad_stream_norm, grads)
        reduced[layer_index] = reduce_sectioned(grads)
    stacked = [jnp.stack([reduced[0][slot]]) for slot in range(13)]
    return (
        output,
        grad_stream.astype(jnp.bfloat16),
        stacked[0],
        stacked[1],
        stacked[2],
        stacked[3],
        stacked[4],
        stacked[5],
        stacked[6],
        stacked[7],
        stacked[8],
        stacked[9],
        stacked[10],
        stacked[11],
        stacked[12],
    )


def solution(mesh):
    in_specs = (
        P(("dp", "fsdp"), None),
        P(("dp", "fsdp"), None),
        P("dp", None),
        P(None, "fsdp"),
        P(None, "fsdp"),
        P(None, "fsdp", None),
        P(None, "fsdp"),
        P(None, "fsdp"),
        P(None, "fsdp", None),
        P(None, "fsdp"),
        P(None, "fsdp"),
        P(None, "fsdp"),
        P(None, "fsdp", None),
        P(None, "fsdp"),
        P(None, "fsdp", None),
        P(None, "fsdp"),
    )
    out_specs = (
        P(("dp", "fsdp"), None),
        P(("dp", "fsdp"), None),
        P(None, "fsdp"),
        P(None, "fsdp"),
        P(None, "fsdp", None),
        P(None, "fsdp"),
        P(None, "fsdp"),
        P(None, "fsdp", None),
        P(None, "fsdp"),
        P(None, "fsdp"),
        P(None, "fsdp"),
        P(None, "fsdp", None),
        P(None, "fsdp"),
        P(None, "fsdp", None),
        P(None, "fsdp"),
    )
    return jax.shard_map(body, mesh=mesh, in_specs=in_specs, out_specs=out_specs, check_vma=False)
```

profile of v0, /device:TPU:0, one launch (start us, length us, event | category | flops | bytes accessed | tf_op | source)
XLA Modules:
  0.0 1592.2 jit_solution(2388046085369659554)
XLA Ops:
  8.0 12.8 all-gather
  20.8 8.0 all-gather.1
  28.8 15.7 all-gather.3
  44.5 8.6 all-gather.4
  56.8 71.0 %all-gather.24.cloned.1.call-done = bf16[1,1024,3072]{2,1,0:T(8,128)(2,1)} async-done(((bf16[1,256,3072]{2,1,0:T(8,128)(2,1)}), bf16[1,1024,3072]{2,1,0:T(8,128)(2,1)}) %all-gather.24.cloned.1.call-update) | async-done | bytes 6291472 | tf_op jit(solution)/shard_map/all_gather | solution.py:38
  127.8 6.1 fusion.46
  133.9 2.6 copy-done.12
  138.2 2.7 slice.83
  143.1 7.9 all-gather.6
  151.0 11.9 all-gather.7
  163.0 7.7 all-gather.8
  170.7 13.4 all-gather.10
  184.7 32.8 %all-gather.22.cloned.1.call-done = bf16[2048,1024]{1,0:T(8,128)(2,1)} async-done(((bf16[512,1024]{1,0:T(8,128)(2,1)}), bf16[2048,1024]{1,0:T(8,128)(2,1)}) %all-gather.22.cloned.1.call-update) | async-done | bytes 4194320 | tf_op jit(solution)/shard_map/all_gather | solution.py:227
  217.5 6.4 copy.73
  224.0 75.1 %all-gather.20.cloned.1.call-done = bf16[2048,1024]{1,0:T(8,128)(2,1)} async-done(((bf16[512,1024]{1,0:T(8,128)(2,1)}), bf16[2048,1024]{1,0:T(8,128)(2,1)}) %all-gather.20.cloned.1.call-update) | async-done | bytes 4194320 | tf_op jit(solution)/shard_map/all_gather | solution.py:226
  299.0 6.4 copy.72
  307.1 28.4 %while.40 = (s32[]{:T(128)}, f32[16,512]{1,0:T(8,128)S(1)}, f32[16,512]{1,0:T(8,128)S(1)}, f32[512,16,64]{0,2,1:T(8,128)}, s32[]{:T(128)}, /*index=5*/s32[2048]{...) while((s32[]{:T(128)}, f32[16,512]{1,0:T(8,128)S(1)}, ...), condition=%wide.region_9.10_spmd.clone, body=%wide.region_4.9_spmd.clone.sunk | while | flops 1130391040 | bytes 63464908 | solution.py:262
  310.2 15.6 conditional.6
  312.3 2.7 fusion.8
  315.0 4.0 fusion.10
  319.0 6.8 bitcast_add_fusion
  335.5 3.3 broadcast_divide_fusion
  338.8 3.2 copy.75
  342.0 3.0 all-gather.26.cloned.1.call-done
  345.0 3.6 fusion.91
  350.3 144.5 %all-gather.28.cloned.1.call-done = bf16[1,1024,4096]{2,1,0:T(8,128)(2,1)} async-done(((bf16[1,256,4096]{2,1,0:T(8,128)(2,1)}), bf16[1,1024,4096]{2,1,0:T(8,128)(2,1)}) %all-gather.28.cloned.1.call-update) | async-done | bytes 8388624 | tf_op jit(solution)/shard_map/all_gather | solution.py:45
  494.8 12.3 fusion.42
  507.1 137.0 %all-gather.30.cloned.1.call-done = bf16[1,4096,1024]{2,1,0:T(8,128)(2,1)} async-done(((bf16[1,1024,1024]{2,1,0:T(8,128)(2,1)}), bf16[1,4096,1024]{2,1,0:T(8,128)(2,1)}) %all-gather.30.cloned.1.call-update) | async-done | bytes 8388624 | tf_op jit(solution)/shard_map/all_gather | solution.py:47
  644.1 16.3 %fusion.92 = (bf16[4096]{0:T(1024)(128)(2,1)}, bf16[512,4096]{1,0:T(8,128)(2,1)}) fusion(f32[512,4096]{1,0:T(8,128)} %fusion.42, f32[4096]{0:T(1024)S(1)} %bitcast.155, bf16[512,1024]{1,0:T(8,128)(2,1)S(1)} %copy-done.13, bf16[1,4096,1024]{2,1,0:T(8,128)(2,1)} %all-gather.30.cloned.1.call-done), kind=kOutput, calls=%fused_computation.132 | convolution fusion | flops 4341100544 | bytes 22044672 | tf_op jit(solution)/shard_map/td,fd->tf/dot_general | solution.py:338
  660.4 8.0 multiply_reduce_fusion
  671.7 3.0 convert_multiply_fusion
  676.9 2.3 copy.74
  680.8 2.4 broadcast_in_dim.107.clone
  683.2 2.6 broadcast_in_dim.107
  685.8 52.0 %while.41 = (s32[]{:T(128)}, f32[512,16,64]{0,2,1:T(8,128)}, bf16[2048,16,64]{0,2,1:T(8,128)(2,1)}, bf16[2048,16,64]{0,2,1:T(8,128)(2,1)}, s32[]{:T(128)}, /*ind...) while((s32[]{:T(128)}, f32[512,16,64]{0,2,1:T(8,128)}, ...), condition=%wide.region_18.19_spmd.clone, body=%wide.region_15.18_spmd.clone.sunk | while | flops 2728920576 | bytes 129885760 | solution.py:434
  689.1 39.1 %conditional.7 = ((f32[512,16,64]{0,2,1:T(8,128)}, bf16[2048,16,64]{0,2,1:T(8,128)(2,1)}, bf16[2048,16,64]{0,2,1:T(8,128)(2,1)})) conditional(s32[]{:T(128)} %convert_element_type.325, (f32[512,16,64]{0,2,1:T(8,128)}, bf16[2048,16,64]{0,2,1:T(8,128)(2,1)}, bf16[2048,16,64]{0,2,1:T(8,128)(2,1)}) %tuple.133, (s32[]{:T(128)}, ...), branch_computations={%region_16.16_spmd, %region_17.17_spmd} | conditional | flops 2728920576 | bytes 129879184 | solution.py:432
  691.2 8.1 fusion.93
  699.3 10.3 bitcast_dynamic-update-slice_fusion
  709.6 9.3 fusion.20
  718.9 4.6 bitcast_add_fusion.1
  723.5 2.6 bitcast_dynamic-update-slice_fusion.1
  726.2 2.1 copy-done.3
  739.4 3.8 convolution_convert_fusion.3
  743.5 13.1 convolution_convert_fusion
  758.2 9.2 convolution_convert_fusion.1
  767.5 2.7 fusion.87
  770.2 160.1 %reduce-scatter.9.cloned.1.call-done = bf16[512,1024]{0,1:T(8,128)(2,1)} async-done(((bf16[2048,1024]{0,1:T(8,128)(2,1)}), bf16[512,1024]{0,1:T(8,128)(2,1)}) %reduce-scatter.9.cloned.1.call-update) | async-done | bytes 1048592 | tf_op jit(solution)/shard_map/reduce_scatter | solution.py:441
  930.3 79.7 %reduce-scatter.7.cloned.1.call-done = bf16[512,1024]{0,1:T(8,128)(2,1)} async-done(((bf16[2048,1024]{0,1:T(8,128)(2,1)}), bf16[512,1024]{0,1:T(8,128)(2,1)}) %reduce-scatter.7.cloned.1.call-update) | async-done | bytes 1048592 | tf_op jit(solution)/shard_map/reduce_scatter | solution.py:438
  1010.0 8.2 convolution_convert_fusion.2
  1020.8 10.4 all-gather.12
  1031.2 26.1 %reduce-scatter.13.cloned.1.call-done = bf16[256,1024]{1,0:T(8,128)(2,1)} async-done(((bf16[1024,1024]{1,0:T(8,128)(2,1)}), bf16[256,1024]{1,0:T(8,128)(2,1)}) %reduce-scatter.13.cloned.1.call-update) | async-done | bytes 524304 | tf_op jit(solution)/shard_map/reduce_scatter | solution.py:88
  1057.3 146.1 %reduce-scatter.17.cloned.1.call-done = bf16[1024,1024]{1,0:T(8,128)(2,1)} async-done(((bf16[4096,1024]{1,0:T(8,128)(2,1)}), bf16[1024,1024]{1,0:T(8,128)(2,1)}) %reduce-scatter.17.cloned.1.call-update) | async-done | bytes 2097168 | tf_op jit(solution)/shard_map/reduce_scatter | solution.py:106
  1203.4 147.7 %reduce-scatter.15.cloned.1.call-done = bf16[256,4096]{1,0:T(8,128)(2,1)} async-done(((bf16[1024,4096]{1,0:T(8,128)(2,1)}), bf16[256,4096]{1,0:T(8,128)(2,1)}) %reduce-scatter.15.cloned.1.call-update) | async-done | bytes 2097168 | tf_op jit(solution)/shard_map/reduce_scatter | solution.py:100
  1351.1 113.8 %reduce-scatter.11.cloned.1.call-done = bf16[256,3072]{1,0:T(8,128)(2,1)} async-done(((bf16[1024,3072]{1,0:T(8,128)(2,1)}), bf16[256,3072]{1,0:T(8,128)(2,1)}) %reduce-scatter.11.cloned.1.call-update) | async-done | bytes 1572880 | tf_op jit(solution)/shard_map/reduce_scatter | solution.py:79
  1465.0 12.2 add_convert_fusion.1
  1478.8 7.4 fusion.84
  1488.6 18.1 %all-reduce.12 = (bf16[1024]{0:T(1024)(128)(2,1)S(1)}, bf16[1024]{0:T(1024)(128)(2,1)S(1)}, bf16[1024]{0:T(1024)(128)(2,1)S(1)}, bf16[1024]{0:T(1024)(128)(2,1)S...) all-reduce(bf16[1024]{0:T(1024)(128)(2,1)S(1)} %get-tuple-element.9, ...), channel_id=17, replica_groups=mesh['dp'=8,'fsdp'=4] {'fsdp'}, use_global_device_ids=true, to_apply=%region_24.25.clone | all-reduce | flops 12288 | bytes 49152
  1507.4 22.8 %all-reduce.10 = (bf16[1,256]{1,0:T(2,128)(2,1)S(1)}, bf16[1,256]{1,0:T(2,128)(2,1)S(1)}, bf16[1,256]{1,0:T(2,128)(2,1)S(1)}, bf16[1,256]{1,0:T(2,128)(2,1)S(1)}...) all-reduce(bf16[1,256]{1,0:T(2,128)(2,1)S(1)} %stack.78, ...), channel_id=1, replica_groups=mesh['dp'=8,'fsdp'=4] {'dp'}, use_global_device_ids=true, to_apply=%region_25.26 | all-reduce | flops 3072 | bytes 12288 | tf_op jit(solution)/shard_map/psum | solution.py:114
  1535.3 3.2 add_convert_fusion
  1538.5 36.0 %all-reduce.15.cloned.1.call-done = (bf16[1,256,3072]{2,1,0:T(8,128)(2,1)}, bf16[1,256,1024]{2,1,0:T(8,128)(2,1)}, bf16[1,256,4096]{2,1,0:T(8,128)(2,1)}, bf16[1,1024,1024]{2,1,0:T(8,128)(2,1)}) async-done(((bf16[1,256,3072]{2,1,0:T(8,128)(2,1)}, bf16[1,256,1024]{2,1,0:T(8,128)(2,1)}, bf16[1,256,4096]{2,1,0:T(8,128)(2,1)}, bf16[1,1024,1024]{2,1,0:T(8,128)(2,1)}), (bf16[1,256,3072]{2,1,0:T(8,128)(2,1)}, ...) | async-done | bytes 6291472 | tf_op jit(solution)/shard_map/psum | solution.py:116
  1574.5 2.3 stack.89
  1576.8 3.4 stack.83
  1580.2 2.5 stack.97
  1582.7 2.5 stack.101
  (248 shorter events, 47.1 us)
Async XLA Ops:
  7.2 120.6 %all-gather.24.cloned.1.call-start = ((), (), s32[]{:S(2)}) async-start(), calls=%async_computation.14 | async-start | bytes 7864320 | tf_op jit(solution)/shard_map/all_gather | solution.py:38
  7.9 209.6 %all-gather.22.cloned.1.call-start = ((), (), s32[]{:S(2)}) async-start(), calls=%async_computation.7 | async-start | bytes 5242880 | tf_op jit(solution)/shard_map/all_gather | solution.py:227
  20.8 113.0 %copy-start.19 = (f32[1,1024]{1,0:T(1,128)}, f32[1,1024]{1,0:T(1,128)S(1)}, u32[]{:S(2)}) copy-start(f32[1,1024]{1,0:T(1,128)S(1)} %convert_element_type.233) | copy-start | bytes 12292
  28.8 105.1 %copy-start.41 = (f32[1,1024]{1,0:T(1,128)}, f32[1,1024]{1,0:T(1,128)S(1)}, u32[]{:S(2)}) copy-start(f32[1,1024]{1,0:T(1,128)S(1)} %convert_element_type.234) | copy-start | bytes 12292
  54.5 79.3 %copy-start.21 = (f32[512]{0:T(512)}, f32[512]{0:T(512)S(1)}, u32[]{:S(2)}) copy-start(f32[512]{0:T(512)S(1)} %broadcast_multiply_fusion.1) | copy-start | bytes 6148
  56.8 77.1 %copy-start.27 = (f32[512]{0:T(512)}, f32[512]{0:T(512)S(1)}, u32[]{:S(2)}) copy-start(f32[512]{0:T(512)S(1)} %fusion.77) | copy-start | bytes 6148
  133.9 2.6 copy-start.12
  138.1 4.7 copy-start.52
  138.1 4.9 copy-start.47
  138.1 12.9 copy-start.48
  138.2 24.8 %copy-start.49 = (bf16[1,256]{1,0:T(2,128)(2,1)S(1)}, bf16[1,256]{1,0:T(2,128)(2,1)}, u32[]{:S(2)}) copy-start(bf16[1,256]{1,0:T(2,128)(2,1)} %param.35) | copy-start | bytes 1540
  138.2 32.5 %copy-start.40 = (bf16[1,1024]{1,0:T(2,128)(2,1)S(1)}, bf16[1,1024]{1,0:T(2,128)(2,1)}, u32[]{:S(2)}) copy-start(bf16[1,1024]{1,0:T(2,128)(2,1)} %param.37) | copy-start | bytes 6148
  138.2 160.9 %all-gather.20.cloned.1.call-start = ((), (), s32[]{:S(2)}) async-start(), calls=%async_computation.6 | async-start | bytes 5242880 | tf_op jit(solution)/shard_map/all_gather | solution.py:226
  141.0 204.0 %all-gather.26.cloned.1.call-start = ((), (), s32[]{:S(2)}) async-start(), calls=%async_computation.15 | async-start | bytes 2621440 | tf_op jit(solution)/shard_map/all_gather | solution.py:41
  141.6 353.2 %all-gather.28.cloned.1.call-start = ((), (), s32[]{:S(2)}) async-start(), calls=%async_computation.16 | async-start | bytes 10485760 | tf_op jit(solution)/shard_map/all_gather | solution.py:45
  142.1 501.9 %all-gather.30.cloned.1.call-start = ((), (), s32[]{:S(2)}) async-start(), calls=%async_computation.17 | async-start | bytes 10485760 | tf_op jit(solution)/shard_map/all_gather | solution.py:47
  142.7 787.6 %reduce-scatter.9.cloned.1.call-start = ((), (), s32[]{:S(2)}) async-start(), calls=%async_computation.9 | async-start | bytes 5242880 | tf_op jit(solution)/shard_map/reduce_scatter | solution.py:441
  163.0 505.5 %copy-start.33 = (f32[1,1024]{1,0:T(1,128)}, f32[1,1024]{1,0:T(1,128)S(1)}, u32[]{:S(2)}) copy-start(f32[1,1024]{1,0:T(1,128)S(1)} %convert_element_type.238) | copy-start | bytes 12292
  170.7 324.1 %copy-start.43 = (f32[1,1024]{1,0:T(1,128)}, f32[1,1024]{1,0:T(1,128)S(1)}, u32[]{:S(2)}) copy-start(f32[1,1024]{1,0:T(1,128)S(1)} %convert_element_type.239) | copy-start | bytes 12292
  184.1 460.0 %copy-start.31 = (f32[1,4096]{1,0:T(1,128)}, f32[1,4096]{1,0:T(1,128)S(1)}, u32[]{:S(2)}) copy-start(f32[1,4096]{1,0:T(1,128)S(1)} %convert_element_type.240) | copy-start | bytes 49156
  335.4 9.5 copy-start.4
  348.6 319.9 %copy-start.29 = (f32[512]{0:T(512)}, f32[512]{0:T(512)S(1)}, u32[]{:S(2)}) copy-start(f32[512]{0:T(512)S(1)} %broadcast_multiply_fusion) | copy-start | bytes 6148
  350.2 318.2 %copy-start.37 = (f32[512]{0:T(512)}, f32[512]{0:T(512)S(1)}, u32[]{:S(2)}) copy-start(f32[512]{0:T(512)S(1)} %fusion.78) | copy-start | bytes 6148
  494.8 149.3 %copy-start.13 = (bf16[512,1024]{1,0:T(8,128)(2,1)S(1)}, bf16[512,1024]{1,0:T(8,128)(2,1)}, u32[]{:S(2)}) copy-start(bf16[512,1024]{1,0:T(8,128)(2,1)} %param.25) | copy-start | bytes 3145732
  644.1 16.3 %copy-start.8 = (f32[512,1024]{1,0:T(8,128)S(1)}, f32[512,1024]{1,0:T(8,128)}, u32[]{:S(2)}) copy-start(f32[512,1024]{1,0:T(8,128)} %copy-done.7) | copy-start | bytes 6291460
  644.1 16.3 %copy-start.51 = (bf16[1,1024,4096]{2,1,0:T(8,128)(2,1)S(1)}, bf16[1,1024,4096]{2,1,0:T(8,128)(2,1)}, u32[]{:S(2)}) copy-start(bf16[1,1024,4096]{2,1,0:T(8,128)(2,1)} %all-gather.28.cloned.1.call-done) | copy-start | bytes 25165828
  668.5 1.9 copy-start.11
  668.5 3.2 copy-start.18
  669.2 5.4 copy-start
  669.2 5.4 copy-start.23
  670.4 4.2 copy-start.15
  718.9 4.6 copy-start.2
  726.2 2.1 copy-start.3
  737.8 1.6 copy-start.10
  737.9 272.1 %reduce-scatter.7.cloned.1.call-start = ((), (), s32[]{:S(2)}) async-start(), calls=%async_computation.8 | async-start | bytes 5242880 | tf_op jit(solution)/shard_map/reduce_scatter | solution.py:438
  738.6 4.9 copy-start.14
  738.6 4.9 copy-start.32
  738.6 318.7 %reduce-scatter.13.cloned.1.call-start = ((), (), s32[]{:S(2)}) async-start(), calls=%async_computation.11 | async-start | bytes 2621440 | tf_op jit(solution)/shard_map/reduce_scatter | solution.py:88
  743.2 460.2 %reduce-scatter.17.cloned.1.call-start = ((), (), s32[]{:S(2)}) async-start(), calls=%async_computation.13 | async-start | bytes 10485760 | tf_op jit(solution)/shard_map/reduce_scatter | solution.py:106
  756.6 1.6 copy-start.9
  756.6 1.6 copy-start.30
  756.6 1.6 copy-start.34
  756.6 1.6 copy-start.38
  756.6 1.6 copy-start.44
  756.6 594.5 %reduce-scatter.15.cloned.1.call-start = ((), (), s32[]{:S(2)}) async-start(), calls=%async_computation.12 | async-start | bytes 10485760 | tf_op jit(solution)/shard_map/reduce_scatter | solution.py:100
  767.4 242.6 %copy-start.5 = (bf16[512,1024]{1,0:T(8,128)(2,1)S(1)}, bf16[512,1024]{1,0:T(8,128)(2,1)}, u32[]{:S(2)}) copy-start(bf16[512,1024]{1,0:T(8,128)(2,1)} %param.24) | copy-start | bytes 3145732
  767.4 242.6 %copy-start.20 = (f32[1,1024]{1,0:T(1,128)S(1)}, f32[1,1024]{1,0:T(1,128)}, u32[]{:S(2)}) copy-start(f32[1,1024]{1,0:T(1,128)} %copy-done.19) | copy-start | bytes 12292
  767.4 242.6 %copy-start.22 = (f32[512]{0:T(512)S(1)}, f32[512]{0:T(512)}, u32[]{:S(2)}) copy-start(f32[512]{0:T(512)} %copy-done.21) | copy-start | bytes 6148
  767.4 242.6 %copy-start.28 = (f32[512]{0:T(512)S(1)}, f32[512]{0:T(512)}, u32[]{:S(2)}) copy-start(f32[512]{0:T(512)} %copy-done.27) | copy-start | bytes 6148
  767.4 242.6 %copy-start.42 = (f32[1,1024]{1,0:T(1,128)S(1)}, f32[1,1024]{1,0:T(1,128)}, u32[]{:S(2)}) copy-start(f32[1,1024]{1,0:T(1,128)} %copy-done.41) | copy-start | bytes 12292
  767.4 697.5 %reduce-scatter.11.cloned.1.call-start = ((), (), s32[]{:S(2)}) async-start(), calls=%async_computation.10 | async-start | bytes 7864320 | tf_op jit(solution)/shard_map/reduce_scatter | solution.py:79
  1018.2 2.5 copy-start.50
  1018.3 556.3 %all-reduce.15.cloned.1.call-start = ((), (), s32[]{:S(2)}) async-start(), calls=%async_computation.18 | async-start | bytes 12582912 | tf_op jit(solution)/shard_map/psum | solution.py:116
  1478.7 7.5 copy-start.26
  1478.7 9.9 copy-start.35
  1478.7 9.9 copy-start.36
  1478.7 9.9 copy-start.39
  1478.7 9.9 copy-start.45
  1478.7 9.9 copy-start.46
  1478.8 56.5 %copy-start.24 = (f32[512]{0:T(512)S(1)}, f32[512]{0:T(512)}, u32[]{:S(2)}) copy-start(f32[512]{0:T(512)} %copy-done.23) | copy-start | bytes 6148
  1486.2 1.3 copy-start.6
  1486.2 49.1 %copy-start.1 = (f32[512,1024]{1,0:T(8,128)S(1)}, f32[512,1024]{1,0:T(8,128)}, u32[]{:S(2)}) copy-start(f32[512,1024]{1,0:T(8,128)} %copy-done) | copy-start | bytes 6291460
  1574.5 5.7 copy-start.17
  1580.2 2.5 copy-start.16
  (3 other events, 2.5 us)
Sparse Core Ops, SparseCore 0:
  9.6 118.1 all-gather.23
  138.2 79.2 all-gather.21
  219.7 79.3 all-gather.19
  300.5 44.4 all-gather.25
  346.4 148.3 all-gather.27
  496.2 147.8 all-gather.29
  738.0 192.2 reduce-scatter.8
  932.7 77.2 reduce-scatter.6
  1012.8 44.4 reduce-scatter.12
  1059.6 143.7 reduce-scatter.16
  1205.9 145.1 reduce-scatter.14
  1353.4 111.4 reduce-scatter.10
  1469.0 105.5 all-reduce.14
where the time goes:
time: 1600 us; the launch traced here: 1590 us
  waiting for transfers between devices  1180 us (74%)
  matrix products  148 us (9%)
  blocking collectives  137 us (9%)
  local copies, waits for them, and re-layouts  58.1 us (4%)
  other arithmetic  39.8 us (2%)
  loops' own time  16.4 us (1%)
  between operations  16.3 us (1%)
    reduce_scatter x1, waiting for transfers between devices, body(): lax.psum_scatter(grad_value_all.astype(jnp.bfloat16), 'fsdp', scatter_dim...  160 us
    reduce_scatter x1, waiting for transfers between devices, reduce_sectioned(): lax.psum_scatter(grads[9].astype(jnp.bfloat16), 'fsdp', scatter_dimension...  148 us
    reduce_scatter x1, waiting for transfers between devices, reduce_sectioned(): lax.psum_scatter(grads[11].astype(jnp.bfloat16), 'fsdp', scatter_dimensio...  146 us
    all_gather x1, waiting for transfers between devices, fetch_weights(): lax.all_gather(sliced[9], 'fsdp', axis=0, tiled=True)  145 us
    all_gather x1, waiting for transfers between devices, fetch_weights(): lax.all_gather(sliced[11], 'fsdp', axis=0, tiled=True)  137 us
    reduce_scatter x1, waiting for transfers between devices, reduce_sectioned(): lax.psum_scatter(grads[2].astype(jnp.bfloat16), 'fsdp', scatter_dimension...  114 us
    reduce_scatter x1, waiting for transfers between devices, body(): lax.psum_scatter(grad_key_all.astype(jnp.bfloat16), 'fsdp', scatter_dimen...  79.7 us
    all_gather x1, waiting for transfers between devices, body(): keys_all = lax.all_gather(keys_local, 'fsdp', axis=0, tiled=True)  75.1 us
  transfers between devices with their start and end apart: 13, of which 13 were waited for; matrix products, arithmetic and copies ran while one was open for 8% of the time, Pallas kernels for 0%

commit v1 on v0

--- a/solution.py
+++ b/solution.py
@@ -24,7 +24,8 @@
 
 def segment_ids(lengths, group_len):
     prompt_len = group_len // 2
-    cont_ends = jnp.cumsum(lengths)
+    order = jnp.arange(lengths.shape[0], dtype=jnp.int32)
+    cont_ends = jnp.sum(jnp.where(order[:, None] <= order[None, :], lengths[:, None], 0), 0)
     positions = jnp.arange(prompt_len, dtype=jnp.int32)
     cont_ids = 1 + jnp.sum((positions[:, None] >= cont_ends[None, :]).astype(jnp.int32), 1)
     return jnp.concatenate([jnp.zeros((prompt_len,), jnp.int32), cont_ids])

time: 1600 us -> 1600 us (level)
  no operation moved by 1% of the time
where the time goes in v1:
time: 1600 us; the launch traced here: 1590 us
  waiting for transfers between devices  1180 us (74%)
  matrix products  148 us (9%)
  blocking collectives  135 us (8%)
  local copies, waits for them, and re-layouts  58.1 us (4%)
  other arithmetic  39.7 us (2%)
  loops' own time  16.4 us (1%)
  between operations  16.3 us (1%)
    reduce_scatter x1, waiting for transfers between devices, body(): lax.psum_scatter(grad_value_all.astype(jnp.bfloat16), 'fsdp', scatter_dim...  160 us
    reduce_scatter x1, waiting for transfers between devices, reduce_sectioned(): lax.psum_scatter(grads[9].astype(jnp.bfloat16), 'fsdp', scatter_dimension...  148 us
    reduce_scatter x1, waiting for transfers between devices, reduce_sectioned(): lax.psum_scatter(grads[11].astype(jnp.bfloat16), 'fsdp', scatter_dimensio...  146 us
    all_gather x1, waiting for transfers between devices, fetch_weights(): lax.all_gather(sliced[9], 'fsdp', axis=0, tiled=True)  145 us
    all_gather x1, waiting for transfers between devices, fetch_weights(): lax.all_gather(sliced[11], 'fsdp', axis=0, tiled=True)  137 us
    reduce_scatter x1, waiting for transfers between devices, reduce_sectioned(): lax.psum_scatter(grads[2].astype(jnp.bfloat16), 'fsdp', scatter_dimension...  114 us
    reduce_scatter x1, waiting for transfers between devices, body(): lax.psum_scatter(grad_key_all.astype(jnp.bfloat16), 'fsdp', scatter_dimen...  79.7 us
    all_gather x1, waiting for transfers between devices, body(): keys_all = lax.all_gather(keys_local, 'fsdp', axis=0, tiled=True)  75.1 us
  transfers between devices with their start and end apart: 13, of which 13 were waited for; matrix products, arithmetic and copies ran while one was open for 8% of the time, Pallas kernels for 0%

profile of v1, /device:TPU:0, one launch (start us, length us, event | category | flops | bytes accessed | tf_op | source)
XLA Modules:
  0.0 1592.2 jit_solution(1188810776521431435)
XLA Ops:
  8.0 12.8 all-gather
  20.8 8.0 all-gather.1
  28.8 15.7 all-gather.3
  44.5 8.6 all-gather.4
  56.8 71.0 %all-gather.24.cloned.1.call-done = bf16[1,1024,3072]{2,1,0:T(8,128)(2,1)} async-done(((bf16[1,256,3072]{2,1,0:T(8,128)(2,1)}), bf16[1,1024,3072]{2,1,0:T(8,128)(2,1)}) %all-gather.24.cloned.1.call-update) | async-done | bytes 6291472 | tf_op jit(solution)/shard_map/all_gather | solution.py:39
  127.8 6.1 fusion.46
  133.9 2.6 copy-done.12
  138.2 2.7 slice.83
  143.0 7.9 all-gather.6
  150.9 9.4 all-gather.7
  160.4 8.4 all-gather.8
  168.8 13.3 all-gather.10
  182.8 34.8 %all-gather.22.cloned.1.call-done = bf16[2048,1024]{1,0:T(8,128)(2,1)} async-done(((bf16[512,1024]{1,0:T(8,128)(2,1)}), bf16[2048,1024]{1,0:T(8,128)(2,1)}) %all-gather.22.cloned.1.call-update) | async-done | bytes 4194320 | tf_op jit(solution)/shard_map/all_gather | solution.py:228
  217.6 6.4 copy.73
  224.0 75.1 %all-gather.20.cloned.1.call-done = bf16[2048,1024]{1,0:T(8,128)(2,1)} async-done(((bf16[512,1024]{1,0:T(8,128)(2,1)}), bf16[2048,1024]{1,0:T(8,128)(2,1)}) %all-gather.20.cloned.1.call-update) | async-done | bytes 4194320 | tf_op jit(solution)/shard_map/all_gather | solution.py:227
  299.1 6.4 copy.72
  307.1 28.4 %while.40 = (s32[]{:T(128)}, f32[16,512]{1,0:T(8,128)S(1)}, f32[16,512]{1,0:T(8,128)S(1)}, f32[512,16,64]{0,2,1:T(8,128)}, s32[]{:T(128)}, /*index=5*/s32[2048]{...) while((s32[]{:T(128)}, f32[16,512]{1,0:T(8,128)S(1)}, ...), condition=%wide.region_9.10_spmd.clone, body=%wide.region_4.9_spmd.clone.sunk | while | flops 1130391040 | bytes 63464908 | solution.py:263
  310.2 15.6 conditional.6
  312.3 2.7 fusion.8
  315.1 4.0 fusion.10
  319.0 6.8 bitcast_add_fusion
  335.5 3.3 broadcast_divide_fusion
  338.8 3.2 copy.75
  342.0 3.0 all-gather.26.cloned.1.call-done
  345.0 3.6 fusion.91
  350.3 144.5 %all-gather.28.cloned.1.call-done = bf16[1,1024,4096]{2,1,0:T(8,128)(2,1)} async-done(((bf16[1,256,4096]{2,1,0:T(8,128)(2,1)}), bf16[1,1024,4096]{2,1,0:T(8,128)(2,1)}) %all-gather.28.cloned.1.call-update) | async-done | bytes 8388624 | tf_op jit(solution)/shard_map/all_gather | solution.py:46
  494.8 12.3 fusion.42
  507.1 137.0 %all-gather.30.cloned.1.call-done = bf16[1,4096,1024]{2,1,0:T(8,128)(2,1)} async-done(((bf16[1,1024,1024]{2,1,0:T(8,128)(2,1)}), bf16[1,4096,1024]{2,1,0:T(8,128)(2,1)}) %all-gather.30.cloned.1.call-update) | async-done | bytes 8388624 | tf_op jit(solution)/shard_map/all_gather | solution.py:48
  644.1 16.2 %fusion.92 = (bf16[4096]{0:T(1024)(128)(2,1)}, bf16[512,4096]{1,0:T(8,128)(2,1)}) fusion(f32[512,4096]{1,0:T(8,128)} %fusion.42, f32[4096]{0:T(1024)S(1)} %bitcast.154, bf16[512,1024]{1,0:T(8,128)(2,1)S(1)} %copy-done.13, bf16[1,4096,1024]{2,1,0:T(8,128)(2,1)} %all-gather.30.cloned.1.call-done), kind=kOutput, calls=%fused_computation.134 | convolution fusion | flops 4341100544 | bytes 22044672 | tf_op jit(solution)/shard_map/td,fd->tf/dot_general | solution.py:339
  660.4 8.1 multiply_reduce_fusion
  671.7 3.0 convert_multiply_fusion
  676.9 2.3 copy.74
  680.8 2.4 broadcast_in_dim.126.clone
  683.2 2.6 broadcast_in_dim.126
  685.8 52.0 %while.41 = (s32[]{:T(128)}, f32[512,16,64]{0,2,1:T(8,128)}, bf16[2048,16,64]{0,2,1:T(8,128)(2,1)}, bf16[2048,16,64]{0,2,1:T(8,128)(2,1)}, s32[]{:T(128)}, /*ind...) while((s32[]{:T(128)}, f32[512,16,64]{0,2,1:T(8,128)}, ...), condition=%wide.region_18.19_spmd.clone, body=%wide.region_15.0_spmd.clone.sunk | while | flops 2728920576 | bytes 129885760 | solution.py:435
  689.1 39.1 %conditional.7 = ((f32[512,16,64]{0,2,1:T(8,128)}, bf16[2048,16,64]{0,2,1:T(8,128)(2,1)}, bf16[2048,16,64]{0,2,1:T(8,128)(2,1)})) conditional(s32[]{:T(128)} %convert_element_type.325, (f32[512,16,64]{0,2,1:T(8,128)}, bf16[2048,16,64]{0,2,1:T(8,128)(2,1)}, bf16[2048,16,64]{0,2,1:T(8,128)(2,1)}) %tuple.133, (s32[]{:T(128)}, ...), branch_computations={%region_16.16_spmd, %region_17.17_spmd} | conditional | flops 2728920576 | bytes 129879184 | solution.py:433
  691.2 8.1 fusion.93
  699.3 10.3 bitcast_dynamic-update-slice_fusion
  709.6 9.3 fusion.20
  718.9 4.6 bitcast_add_fusion.1
  723.5 2.6 bitcast_dynamic-update-slice_fusion.1
  726.2 2.1 copy-done.3
  739.4 3.8 convolution_convert_fusion.3
  743.5 13.1 convolution_convert_fusion
  758.2 9.2 convolution_convert_fusion.1
  767.5 2.7 fusion.87
  770.2 160.1 %reduce-scatter.9.cloned.1.call-done = bf16[512,1024]{0,1:T(8,128)(2,1)} async-done(((bf16[2048,1024]{0,1:T(8,128)(2,1)}), bf16[512,1024]{0,1:T(8,128)(2,1)}) %reduce-scatter.9.cloned.1.call-update) | async-done | bytes 1048592 | tf_op jit(solution)/shard_map/reduce_scatter | solution.py:442
  930.3 79.7 %reduce-scatter.7.cloned.1.call-done = bf16[512,1024]{0,1:T(8,128)(2,1)} async-done(((bf16[2048,1024]{0,1:T(8,128)(2,1)}), bf16[512,1024]{0,1:T(8,128)(2,1)}) %reduce-scatter.7.cloned.1.call-update) | async-done | bytes 1048592 | tf_op jit(solution)/shard_map/reduce_scatter | solution.py:439
  1010.0 8.2 convolution_convert_fusion.2
  1020.8 10.5 all-gather.12
  1031.3 26.1 %reduce-scatter.13.cloned.1.call-done = bf16[256,1024]{1,0:T(8,128)(2,1)} async-done(((bf16[1024,1024]{1,0:T(8,128)(2,1)}), bf16[256,1024]{1,0:T(8,128)(2,1)}) %reduce-scatter.13.cloned.1.call-update) | async-done | bytes 524304 | tf_op jit(solution)/shard_map/reduce_scatter | solution.py:89
  1057.3 146.2 %reduce-scatter.17.cloned.1.call-done = bf16[1024,1024]{1,0:T(8,128)(2,1)} async-done(((bf16[4096,1024]{1,0:T(8,128)(2,1)}), bf16[1024,1024]{1,0:T(8,128)(2,1)}) %reduce-scatter.17.cloned.1.call-update) | async-done | bytes 2097168 | tf_op jit(solution)/shard_map/reduce_scatter | solution.py:107
  1203.5 147.7 %reduce-scatter.15.cloned.1.call-done = bf16[256,4096]{1,0:T(8,128)(2,1)} async-done(((bf16[1024,4096]{1,0:T(8,128)(2,1)}), bf16[256,4096]{1,0:T(8,128)(2,1)}) %reduce-scatter.15.cloned.1.call-update) | async-done | bytes 2097168 | tf_op jit(solution)/shard_map/reduce_scatter | solution.py:101
  1351.2 113.8 %reduce-scatter.11.cloned.1.call-done = bf16[256,3072]{1,0:T(8,128)(2,1)} async-done(((bf16[1024,3072]{1,0:T(8,128)(2,1)}), bf16[256,3072]{1,0:T(8,128)(2,1)}) %reduce-scatter.11.cloned.1.call-update) | async-done | bytes 1572880 | tf_op jit(solution)/shard_map/reduce_scatter | solution.py:80
  1465.0 12.2 add_convert_fusion.1
  1478.8 7.4 fusion.84
  1488.6 18.1 %all-reduce.12 = (bf16[1024]{0:T(1024)(128)(2,1)S(1)}, bf16[1024]{0:T(1024)(128)(2,1)S(1)}, bf16[1024]{0:T(1024)(128)(2,1)S(1)}, bf16[1024]{0:T(1024)(128)(2,1)S...) all-reduce(bf16[1024]{0:T(1024)(128)(2,1)S(1)} %get-tuple-element.9, ...), channel_id=17, replica_groups=mesh['dp'=8,'fsdp'=4] {'fsdp'}, use_global_device_ids=true, to_apply=%region_24.25.clone | all-reduce | flops 12288 | bytes 49152
  1507.5 22.8 %all-reduce.10 = (bf16[1,256]{1,0:T(2,128)(2,1)S(1)}, bf16[1,256]{1,0:T(2,128)(2,1)S(1)}, bf16[1,256]{1,0:T(2,128)(2,1)S(1)}, bf16[1,256]{1,0:T(2,128)(2,1)S(1)}...) all-reduce(bf16[1,256]{1,0:T(2,128)(2,1)S(1)} %stack.78, ...), channel_id=1, replica_groups=mesh['dp'=8,'fsdp'=4] {'dp'}, use_global_device_ids=true, to_apply=%region_25.26 | all-reduce | flops 3072 | bytes 12288 | tf_op jit(solution)/shard_map/psum | solution.py:115
  1535.3 3.2 add_convert_fusion
  1538.6 36.0 %all-reduce.15.cloned.1.call-done = (bf16[1,256,3072]{2,1,0:T(8,128)(2,1)}, bf16[1,256,1024]{2,1,0:T(8,128)(2,1)}, bf16[1,256,4096]{2,1,0:T(8,128)(2,1)}, bf16[1,1024,1024]{2,1,0:T(8,128)(2,1)}) async-done(((bf16[1,256,3072]{2,1,0:T(8,128)(2,1)}, bf16[1,256,1024]{2,1,0:T(8,128)(2,1)}, bf16[1,256,4096]{2,1,0:T(8,128)(2,1)}, bf16[1,1024,1024]{2,1,0:T(8,128)(2,1)}), (bf16[1,256,3072]{2,1,0:T(8,128)(2,1)}, ...) | async-done | bytes 6291472 | tf_op jit(solution)/shard_map/psum | solution.py:117
  1574.5 2.3 stack.89
  1576.8 3.4 stack.83
  1580.2 2.5 stack.97
  1582.8 2.5 stack.101
  (248 shorter events, 47.0 us)
Async XLA Ops:
  7.2 120.6 %all-gather.24.cloned.1.call-start = ((), (), s32[]{:S(2)}) async-start(), calls=%async_computation.14 | async-start | bytes 7864320 | tf_op jit(solution)/shard_map/all_gather | solution.py:39
  7.9 209.7 %all-gather.22.cloned.1.call-start = ((), (), s32[]{:S(2)}) async-start(), calls=%async_computation.7 | async-start | bytes 5242880 | tf_op jit(solution)/shard_map/all_gather | solution.py:228
  20.8 113.0 %copy-start.19 = (f32[1,1024]{1,0:T(1,128)}, f32[1,1024]{1,0:T(1,128)S(1)}, u32[]{:S(2)}) copy-start(f32[1,1024]{1,0:T(1,128)S(1)} %convert_element_type.233) | copy-start | bytes 12292
  28.8 105.1 %copy-start.41 = (f32[1,1024]{1,0:T(1,128)}, f32[1,1024]{1,0:T(1,128)S(1)}, u32[]{:S(2)}) copy-start(f32[1,1024]{1,0:T(1,128)S(1)} %convert_element_type.234) | copy-start | bytes 12292
  54.5 79.3 %copy-start.21 = (f32[512]{0:T(512)}, f32[512]{0:T(512)S(1)}, u32[]{:S(2)}) copy-start(f32[512]{0:T(512)S(1)} %broadcast_multiply_fusion.1) | copy-start | bytes 6148
  56.8 77.1 %copy-start.27 = (f32[512]{0:T(512)}, f32[512]{0:T(512)S(1)}, u32[]{:S(2)}) copy-start(f32[512]{0:T(512)S(1)} %fusion.77) | copy-start | bytes 6148
  133.9 2.6 copy-start.12
  138.1 4.7 copy-start.52
  138.1 4.8 copy-start.47
  138.1 12.8 copy-start.48
  138.2 22.2 %copy-start.49 = (bf16[1,256]{1,0:T(2,128)(2,1)S(1)}, bf16[1,256]{1,0:T(2,128)(2,1)}, u32[]{:S(2)}) copy-start(bf16[1,256]{1,0:T(2,128)(2,1)} %param.35) | copy-start | bytes 1540
  138.2 30.6 %copy-start.40 = (bf16[1,1024]{1,0:T(2,128)(2,1)S(1)}, bf16[1,1024]{1,0:T(2,128)(2,1)}, u32[]{:S(2)}) copy-start(bf16[1,1024]{1,0:T(2,128)(2,1)} %param.37) | copy-start | bytes 6148
  138.2 160.9 %all-gather.20.cloned.1.call-start = ((), (), s32[]{:S(2)}) async-start(), calls=%async_computation.6 | async-start | bytes 5242880 | tf_op jit(solution)/shard_map/all_gather | solution.py:227
  141.0 204.0 %all-gather.26.cloned.1.call-start = ((), (), s32[]{:S(2)}) async-start(), calls=%async_computation.15 | async-start | bytes 2621440 | tf_op jit(solution)/shard_map/all_gather | solution.py:42
  141.6 353.2 %all-gather.28.cloned.1.call-start = ((), (), s32[]{:S(2)}) async-start(), calls=%async_computation.16 | async-start | bytes 10485760 | tf_op jit(solution)/shard_map/all_gather | solution.py:46
  142.1 502.0 %all-gather.30.cloned.1.call-start = ((), (), s32[]{:S(2)}) async-start(), calls=%async_computation.17 | async-start | bytes 10485760 | tf_op jit(solution)/shard_map/all_gather | solution.py:48
  142.7 787.6 %reduce-scatter.9.cloned.1.call-start = ((), (), s32[]{:S(2)}) async-start(), calls=%async_computation.9 | async-start | bytes 5242880 | tf_op jit(solution)/shard_map/reduce_scatter | solution.py:442
  160.3 508.1 %copy-start.33 = (f32[1,1024]{1,0:T(1,128)}, f32[1,1024]{1,0:T(1,128)S(1)}, u32[]{:S(2)}) copy-start(f32[1,1024]{1,0:T(1,128)S(1)} %convert_element_type.238) | copy-start | bytes 12292
  168.8 326.0 %copy-start.43 = (f32[1,1024]{1,0:T(1,128)}, f32[1,1024]{1,0:T(1,128)S(1)}, u32[]{:S(2)}) copy-start(f32[1,1024]{1,0:T(1,128)S(1)} %convert_element_type.239) | copy-start | bytes 12292
  182.1 462.0 %copy-start.31 = (f32[1,4096]{1,0:T(1,128)}, f32[1,4096]{1,0:T(1,128)S(1)}, u32[]{:S(2)}) copy-start(f32[1,4096]{1,0:T(1,128)S(1)} %convert_element_type.240) | copy-start | bytes 49156
  335.5 9.5 copy-start.4
  348.6 319.8 %copy-start.29 = (f32[512]{0:T(512)}, f32[512]{0:T(512)S(1)}, u32[]{:S(2)}) copy-start(f32[512]{0:T(512)S(1)} %broadcast_multiply_fusion) | copy-start | bytes 6148
  350.3 318.2 %copy-start.37 = (f32[512]{0:T(512)}, f32[512]{0:T(512)S(1)}, u32[]{:S(2)}) copy-start(f32[512]{0:T(512)S(1)} %fusion.78) | copy-start | bytes 6148
  494.8 149.3 %copy-start.13 = (bf16[512,1024]{1,0:T(8,128)(2,1)S(1)}, bf16[512,1024]{1,0:T(8,128)(2,1)}, u32[]{:S(2)}) copy-start(bf16[512,1024]{1,0:T(8,128)(2,1)} %param.25) | copy-start | bytes 3145732
  644.1 16.2 %copy-start.8 = (f32[512,1024]{1,0:T(8,128)S(1)}, f32[512,1024]{1,0:T(8,128)}, u32[]{:S(2)}) copy-start(f32[512,1024]{1,0:T(8,128)} %copy-done.7) | copy-start | bytes 6291460
  644.1 16.2 %copy-start.51 = (bf16[1,1024,4096]{2,1,0:T(8,128)(2,1)S(1)}, bf16[1,1024,4096]{2,1,0:T(8,128)(2,1)}, u32[]{:S(2)}) copy-start(bf16[1,1024,4096]{2,1,0:T(8,128)(2,1)} %all-gather.28.cloned.1.call-done) | copy-start | bytes 25165828
  668.5 1.9 copy-start.11
  668.5 3.2 copy-start.18
  669.2 5.4 copy-start
  669.2 5.4 copy-start.23
  670.4 4.2 copy-start.15
  718.9 4.6 copy-start.2
  726.2 2.1 copy-start.3
  737.8 1.6 copy-start.10
  737.9 272.1 %reduce-scatter.7.cloned.1.call-start = ((), (), s32[]{:S(2)}) async-start(), calls=%async_computation.8 | async-start | bytes 5242880 | tf_op jit(solution)/shard_map/reduce_scatter | solution.py:439
  738.6 4.9 copy-start.14
  738.6 4.9 copy-start.32
  738.6 318.7 %reduce-scatter.13.cloned.1.call-start = ((), (), s32[]{:S(2)}) async-start(), calls=%async_computation.11 | async-start | bytes 2621440 | tf_op jit(solution)/shard_map/reduce_scatter | solution.py:89
  743.2 460.3 %reduce-scatter.17.cloned.1.call-start = ((), (), s32[]{:S(2)}) async-start(), calls=%async_computation.13 | async-start | bytes 10485760 | tf_op jit(solution)/shard_map/reduce_scatter | solution.py:107
  756.6 1.6 copy-start.9
  756.6 1.6 copy-start.30
  756.6 1.6 copy-start.34
  756.6 1.6 copy-start.38
  756.6 1.6 copy-start.44
  756.6 594.6 %reduce-scatter.15.cloned.1.call-start = ((), (), s32[]{:S(2)}) async-start(), calls=%async_computation.12 | async-start | bytes 10485760 | tf_op jit(solution)/shard_map/reduce_scatter | solution.py:101
  767.4 242.6 %copy-start.5 = (bf16[512,1024]{1,0:T(8,128)(2,1)S(1)}, bf16[512,1024]{1,0:T(8,128)(2,1)}, u32[]{:S(2)}) copy-start(bf16[512,1024]{1,0:T(8,128)(2,1)} %param.24) | copy-start | bytes 3145732
  767.4 242.6 %copy-start.20 = (f32[1,1024]{1,0:T(1,128)S(1)}, f32[1,1024]{1,0:T(1,128)}, u32[]{:S(2)}) copy-start(f32[1,1024]{1,0:T(1,128)} %copy-done.19) | copy-start | bytes 12292
  767.4 242.6 %copy-start.22 = (f32[512]{0:T(512)S(1)}, f32[512]{0:T(512)}, u32[]{:S(2)}) copy-start(f32[512]{0:T(512)} %copy-done.21) | copy-start | bytes 6148
  767.4 242.6 %copy-start.28 = (f32[512]{0:T(512)S(1)}, f32[512]{0:T(512)}, u32[]{:S(2)}) copy-start(f32[512]{0:T(512)} %copy-done.27) | copy-start | bytes 6148
  767.4 242.6 %copy-start.42 = (f32[1,1024]{1,0:T(1,128)S(1)}, f32[1,1024]{1,0:T(1,128)}, u32[]{:S(2)}) copy-start(f32[1,1024]{1,0:T(1,128)} %copy-done.41) | copy-start | bytes 12292
  767.4 697.5 %reduce-scatter.11.cloned.1.call-start = ((), (), s32[]{:S(2)}) async-start(), calls=%async_computation.10 | async-start | bytes 7864320 | tf_op jit(solution)/shard_map/reduce_scatter | solution.py:80
  1018.3 2.5 copy-start.50
  1018.3 556.2 %all-reduce.15.cloned.1.call-start = ((), (), s32[]{:S(2)}) async-start(), calls=%async_computation.18 | async-start | bytes 12582912 | tf_op jit(solution)/shard_map/psum | solution.py:117
  1478.7 7.6 copy-start.26
  1478.7 9.9 copy-start.35
  1478.8 9.9 copy-start.36
  1478.8 9.9 copy-start.39
  1478.8 9.9 copy-start.45
  1478.8 9.9 copy-start.46
  1478.8 56.5 %copy-start.24 = (f32[512]{0:T(512)S(1)}, f32[512]{0:T(512)}, u32[]{:S(2)}) copy-start(f32[512]{0:T(512)} %copy-done.23) | copy-start | bytes 6148
  1486.3 1.3 copy-start.6
  1486.3 49.1 %copy-start.1 = (f32[512,1024]{1,0:T(8,128)S(1)}, f32[512,1024]{1,0:T(8,128)}, u32[]{:S(2)}) copy-start(f32[512,1024]{1,0:T(8,128)} %copy-done) | copy-start | bytes 6291460
  1574.5 5.7 copy-start.17
  1580.2 2.5 copy-start.16
  (3 other events, 2.5 us)
Sparse Core Ops, SparseCore 0:
  9.6 118.1 all-gather.23
  138.2 79.2 all-gather.21
  219.7 79.2 all-gather.19
  300.5 44.4 all-gather.25
  346.4 148.3 all-gather.27
  496.2 147.8 all-gather.29
  738.0 192.2 reduce-scatter.8
  932.7 77.2 reduce-scatter.6
  1012.9 44.4 reduce-scatter.12
  1059.7 143.7 reduce-scatter.16
  1206.0 145.1 reduce-scatter.14
  1353.5 111.4 reduce-scatter.10
  1469.0 105.4 all-reduce.14

commit v2 on v0

v2 whole, which is shorter than its diff:
```python
import functools

import jax
import jax.numpy as jnp
from jax import lax
from jax.experimental import pallas as pl
from jax.experimental.pallas import tpu as pltpu
from jax.sharding import PartitionSpec as P

H = 16
EPSILON = 1e-05
NEG_LARGE = -1e30
F32 = jnp.float32
BF = jnp.bfloat16
MIB = 2**20


def rnd(v):
    return v.astype(BF)


def dot_last(left, right):
    return lax.dot_general(left, right, (((1,), (1,)), ((), ())), preferred_element_type=F32)


def dot_mm(left, right):
    return jnp.dot(left, right, preferred_element_type=F32)


def key_ranges(start, group_len):
    prompt = group_len // 2
    if start < prompt:
        return start, start
    return prompt, max(prompt, start - group_len // 8)


def allowed_mask(shape, key_start, query_start, low_row):
    key_pos = lax.broadcasted_iota(jnp.int32, shape, 0) + key_start
    query_pos = lax.broadcasted_iota(jnp.int32, shape, 1) + query_start
    return (key_pos <= query_pos) & (key_pos >= low_row)


def attend_kernel(group_len, head_dim, q_ref, k_ref, v_ref, low_ref, o_ref, lse_ref):
    size = min(512, group_len // 4)
    scale = jnp.asarray(head_dim**-0.5, BF)
    values_t = v_ref[...].astype(F32).T.astype(BF)
    for start in range(0, group_len, size):
        stop = start + size
        full, near = key_ranges(start, group_len)
        results = []
        for head in range(128 // head_dim):
            lanes = slice(head * head_dim, (head + 1) * head_dim)
            queries = q_ref[start:stop, lanes] * scale
            part = dot_last(k_ref[near:stop, lanes], queries)
            ok = allowed_mask(part.shape, near, start, low_ref[0:1, start:stop])
            part = jnp.where(ok, part, NEG_LARGE)
            top = jnp.max(part, 0, keepdims=True)
            if full:
                rest = dot_last(k_ref[0:full, lanes], queries)
                top = jnp.maximum(top, jnp.max(rest, 0, keepdims=True))
            part = jnp.exp(part - top)
            total = jnp.sum(part, 0, keepdims=True)
            mixed = dot_mm(values_t[lanes, near:stop], part.astype(BF))
            if full:
                rest = jnp.exp(rest - top)
                total += jnp.sum(rest, 0, keepdims=True)
                mixed += dot_mm(values_t[lanes, 0:full], rest.astype(BF))
            results.append(mixed * (1.0 / total))
            lse_ref[0, head : head + 1, start:stop] = top + jnp.log(total)
        o_ref[start:stop, :] = jnp.concatenate(results, 0).T.astype(BF)


def attend_grad_kernel(
    group_len, head_dim, q_ref, k_ref, v_ref, low_ref, o_ref, lse_ref, do_ref, dq_ref, dk_ref, dv_ref, dk_sum, dv_sum
):
    size = min(256, group_len // 8)
    scale = jnp.asarray(head_dim**-0.5, BF)
    keys_t = k_ref[...].astype(F32).T.astype(BF)
    dk_sum[...] = jnp.zeros_like(dk_sum)
    dv_sum[...] = jnp.zeros_like(dv_sum)
    for start in range(0, group_len, size):
        stop = start + size
        full, near = key_ranges(start, group_len)
        product_t = (do_ref[start:stop, :].astype(F32) * o_ref[start:stop, :].astype(F32)).T
        results = []
        for head in range(128 // head_dim):
            lanes = slice(head * head_dim, (head + 1) * head_dim)
            queries = q_ref[start:stop, lanes] * scale
            grads = do_ref[start:stop, lanes]
            delta = jnp.sum(product_t[lanes, :], 0, keepdims=True)
            lse = lse_ref[0, head : head + 1, start:stop]
            dq_t = jnp.zeros((head_dim, size), F32)
            for first, last, masked in ((near, stop, True), (0, full, False)):
                if first == last:
                    continue
                probs = jnp.exp(dot_last(k_ref[first:last, lanes], queries) - lse)
                if masked:
                    ok = allowed_mask(probs.shape, first, start, low_ref[0:1, start:stop])
                    probs = jnp.where(ok, probs, 0.0)
                grad_probs = dot_last(v_ref[first:last, lanes], grads)
                ds = (probs * (grad_probs - delta)).astype(BF)
                dv_sum[head, first:last, :] += dot_mm(probs.astype(BF), grads)
                dk_sum[head, first:last, :] += dot_mm(ds, queries)
                dq_t += dot_mm(keys_t[lanes, first:last], ds)
            results.append(dq_t * head_dim**-0.5)
        dq_ref[start:stop, :] = jnp.concatenate(results, 0).T.astype(BF)
    heads = range(128 // head_dim)
    dk_ref[...] = jnp.concatenate([dk_sum[head] for head in heads], 1).astype(BF)
    dv_ref[...] = jnp.concatenate([dv_sum[head] for head in heads], 1).astype(BF)


def attend(combined, low, head_dim):
    group_len, width = combined.shape[0], combined.shape[1] // 3
    steps = width // 128
    heads = 128 // head_dim
    block = lambda offset: pl.BlockSpec((group_len, 128), lambda i: (0, offset + i))
    return pl.pallas_call(
        functools.partial(attend_kernel, group_len, head_dim),
        grid=(steps,),
        in_specs=[block(0), block(steps), block(2 * steps), pl.BlockSpec((1, group_len), lambda i: (0, 0))],
        out_specs=[block(0), pl.BlockSpec((1, heads, group_len), lambda i: (i, 0, 0))],
        out_shape=[
            jax.ShapeDtypeStruct((group_len, width), BF),
            jax.ShapeDtypeStruct((steps, heads, group_len), F32),
        ],
        compiler_params=pltpu.CompilerParams(vmem_limit_bytes=56 * MIB),
        cost_estimate=pl.CostEstimate(flops=15 * 10**9, bytes_accessed=4 * MIB, transcendentals=0),
    )(combined, combined, combined, low)


def attend_grad(combined, low, mixed, lse, grad_mixed, head_dim):
    group_len, width = mixed.shape
    steps = width // 128
    heads = 128 // head_dim
    block = lambda offset: pl.BlockSpec((group_len, 128), lambda i: (0, offset + i))
    return pl.pallas_call(
        functools.partial(attend_grad_kernel, group_len, head_dim),
        grid=(steps,),
        in_specs=[
            block(0),
            block(steps),
            block(2 * steps),
            pl.BlockSpec((1, group_len), lambda i: (0, 0)),
            block(0),
            pl.BlockSpec((1, heads, group_len), lambda i: (i, 0, 0)),
            block(0),
        ],
        out_specs=[block(0)] * 3,
        out_shape=[jax.ShapeDtypeStruct((group_len, width), BF)] * 3,
        scratch_shapes=[pltpu.VMEM((heads, group_len, head_dim), F32)] * 2,
        compiler_params=pltpu.CompilerParams(vmem_limit_bytes=56 * MIB),
        cost_estimate=pl.CostEstimate(flops=25 * 10**9, bytes_accessed=8 * MIB, transcendentals=0),
    )(combined, combined, combined, low, mixed, lse, grad_mixed)


class Cut:
    def __init__(self, rows, columns, column_parts, replicas, shards):
        self.rows, self.columns, self.shards, self.replicas = rows, columns, shards, replicas
        self.nc, self.nr = column_parts, replicas // column_parts
        self.r, self.c = rows // self.nr, columns // self.nc

    def place(self, piece):
        row = lax.rem(piece, self.nr) * self.r
        column = lax.div(piece, self.nr) * self.c
        return pl.multiple_of(row, 8 if self.r % 16 else 16), pl.multiple_of(column, 128)

    def spot(self, piece, base=0):
        row, column = self.place(piece)
        return pl.ds(base + row, self.r), pl.ds(column, self.c)

    def of(self, shard, piece):
        return lax.dynamic_slice(shard, self.place(piece), (self.r, self.c))

    @property
    def copies(self):
        return 1 + (self.shards - 1) * self.replicas


def fetch(cut, me, z, slots, shard, whole, sems):
    base = pl.multiple_of(z * cut.rows, 16)
    copies = [pltpu.make_async_copy(shard, whole.at[pl.ds(base, cut.rows), :], sems.at[0])]
    for d in range(1, cut.shards):
        base = pl.multiple_of(lax.rem(z + cut.shards - d, cut.shards) * cut.rows, 16)
        for j in range(cut.replicas):
            copies.append(
                pltpu.make_async_copy(
                    slots[j].at[d - 1],
                    whole.at[cut.spot(jnp.bitwise_xor(me, j), base)],
                    sems.at[len(copies)],
                )
            )
    return copies


def start(copies):
    for copy in copies:
        copy.start()


def finish(copies):
    for copy in copies:
        copy.wait()


SMEM_SPEC = pl.BlockSpec(memory_space=pltpu.SMEM)
ANY_SPEC = pl.BlockSpec(memory_space=pl.ANY)
VMEM_SPEC = pl.BlockSpec(memory_space=pltpu.VMEM)


def cost(flops, size):
    return pl.CostEstimate(flops=int(flops), bytes_accessed=int(size), transcendentals=0)


def moments(stream):
    mean = jnp.mean(stream, -1, keepdims=True)
    centered = stream - mean
    scale = lax.rsqrt(jnp.mean(centered * centered, -1, keepdims=True) + EPSILON)
    return centered * scale, scale


def norm_grad(grad_hidden, gain, normal, scale):
    t = grad_hidden * gain
    return scale * (
        t - jnp.mean(t, -1, keepdims=True) - normal * jnp.mean(t * normal, -1, keepdims=True)
    )


def project_kernel(place, block, gain, bias, weight, bias_qkv, h_in, c_in, h_out, c_out):
    normal, _ = moments(block[...].astype(F32))
    hidden = rnd(normal * gain[...] + bias[...])
    h_out[...] = hidden
    c_out[...] = rnd(dot_mm(hidden, weight[...]) + bias_qkv[...])


def project(place, block, gain, bias, weight, bias_qkv, h_all, c_all, distance, shards):
    rows, width = block.shape
    whole = lambda a: pl.BlockSpec(a.shape, lambda i, s: (0,) * a.ndim)
    at = lambda i, s: (lax.rem(s[1] + shards - distance, shards), 0)
    return pl.pallas_call(
        project_kernel,
        grid_spec=pltpu.PrefetchScalarGridSpec(
            num_scalar_prefetch=1,
            grid=(1,),
            in_specs=[whole(a) for a in (block, gain, bias, weight, bias_qkv)] + [ANY_SPEC] * 2,
            out_specs=[pl.BlockSpec((rows, width), at), pl.BlockSpec((rows, c_all.shape[1]), at)],
        ),
        out_shape=[jax.ShapeDtypeStruct(a.shape, BF) for a in (h_all, c_all)],
        input_output_aliases={6: 0, 7: 1},
        compiler_params=pltpu.CompilerParams(vmem_limit_bytes=40 * MIB),
        cost_estimate=cost(2 * rows * width * c_all.shape[1], 6 * MIB),
    )(place, block, gain, bias, weight, bias_qkv, h_all, c_all)


GELU_A = 0.7978845608028654
GELU_B = 0.044715


def gelu_both(u):
    square = u * u
    t = jnp.tanh(GELU_A * u * (1.0 + GELU_B * square))
    value = 0.5 * u * (1.0 + t)
    slope = 0.5 * (1.0 + t) + 0.5 * u * (1.0 - t * t) * (GELU_A * (1.0 + 3.0 * GELU_B * square))
    return value, slope


def forward_kernel(cuts, step, place, mixed, tokens, vectors, bias_up, *refs):
    count = cuts[0].replicas
    lists, refs = refs[: 3 * (count + 1)], refs[3 * (count + 1) :]
    out, hidden, middle, acted, slope, w_out, w_up, w_down, *sems = refs
    me, z = place[0], place[1]
    loads = []
    for n, (cut, whole) in enumerate(zip(cuts, (w_out, w_up, w_down))):
        own = lists[n * (count + 1) : (n + 1) * (count + 1)]
        loads.append(fetch(cut, me, z, own[:count], own[count], whole, sems[n]))
        start(loads[-1])
    finish(loads[0])
    stream = tokens[...].astype(F32) + (dot_mm(mixed[...], w_out[...]) + vectors[0:1, :])
    middle[...] = stream
    normal, _ = moments(stream)
    hidden[...] = rnd(normal * vectors[1:2, :] + vectors[2:3, :])
    finish(loads[1])
    finish(loads[2])
    total = vectors[3:4, :] + stream
    for block in range(0, w_up.shape[1], step):
        columns = slice(block, block + step)
        u = dot_mm(hidden[...], w_up[:, columns]) + bias_up[:, columns]
        value, grad = gelu_both(u)
        value = rnd(value)
        acted[:, columns] = value
        slope[:, columns] = rnd(grad)
        total += dot_mm(value, w_down[columns, :])
    out[...] = rnd(total)


def feed_forward(place, mixed, tokens, vectors, bias_up, cuts, lists):
    rows, width = tokens.shape
    hidden = bias_up.shape[1]
    flat = [a for own in lists for a in own]
    return pl.pallas_call(
        functools.partial(forward_kernel, cuts, min(1024, hidden)),
        in_specs=[SMEM_SPEC] + [VMEM_SPEC] * 4 + [ANY_SPEC] * len(flat),
        out_specs=[VMEM_SPEC] * 5,
        out_shape=[
            jax.ShapeDtypeStruct((rows, width), BF),
            jax.ShapeDtypeStruct((rows, width), BF),
            jax.ShapeDtypeStruct((rows, width), F32),
            jax.ShapeDtypeStruct((rows, hidden), BF),
            jax.ShapeDtypeStruct((rows, hidden), BF),
        ],
        scratch_shapes=[
            pltpu.VMEM((width, width), BF),
            pltpu.VMEM((width, hidden), BF),
            pltpu.VMEM((hidden, width), BF),
        ]
        + [pltpu.SemaphoreType.DMA((cut.copies,)) for cut in cuts],
        compiler_params=pltpu.CompilerParams(vmem_limit_bytes=60 * MIB),
        cost_estimate=cost(2 * rows * width * (width + 2 * hidden), 34 * MIB),
    )(place, mixed, tokens, vectors, bias_up, *flat)


def backward_kernel(cuts, step, place, dm, slope, middle, vectors, *refs):
    count = cuts[0].replicas
    lists, refs = refs[: 3 * (count + 1)], refs[3 * (count + 1) :]
    du, dx2, da, do, grad_up, sums, w_out, w_up, w_down, *sems = refs
    me, z = place[0], place[1]
    loads = []
    for n, whole in ((2, w_down), (1, w_up), (0, w_out)):
        own = lists[n * (count + 1) : (n + 1) * (count + 1)]
        loads.append(fetch(cuts[n], me, z, own[:count], own[count], whole, sems[n]))
        start(loads[-1])
    finish(loads[0])
    finish(loads[1])
    dh2 = jnp.zeros(middle.shape, F32)
    for block in range(0, w_up.shape[1], step):
        columns = slice(block, block + step)
        part = rnd(dot_last(dm[...], w_down[columns, :]) * slope[:, columns].astype(F32))
        du[:, columns] = part
        grad_up[:, columns] = jnp.sum(part.astype(F32), 0, keepdims=True)
        dh2 += dot_last(part, w_up[:, columns])
    normal, scale = moments(middle[...])
    incoming = dm[...].astype(F32)
    stream = incoming + norm_grad(dh2, vectors[1:2, :], normal, scale)
    dx2[...] = stream
    low = rnd(stream)
    da[...] = low
    finish(loads[2])
    do[...] = rnd(dot_last(low, w_out[...]))
    sums[0:1, :] = jnp.sum(incoming, 0, keepdims=True)
    sums[1:2, :] = jnp.sum(dh2 * normal, 0, keepdims=True)
    sums[2:3, :] = jnp.sum(dh2, 0, keepdims=True)
    sums[3:4, :] = jnp.sum(low.astype(F32), 0, keepdims=True)
    sums[4:8, :] = jnp.zeros((4, sums.shape[1]), F32)


def feed_backward(place, dm, slope, middle, vectors, cuts, lists):
    rows, width = dm.shape
    hidden = slope.shape[1]
    flat = [a for own in lists for a in own]
    return pl.pallas_call(
        functools.partial(backward_kernel, cuts, min(1024, hidden)),
        in_specs=[SMEM_SPEC] + [VMEM_SPEC] * 4 + [ANY_SPEC] * len(flat),
        out_specs=[VMEM_SPEC] * 6,
        out_shape=[
            jax.ShapeDtypeStruct((rows, hidden), BF),
            jax.ShapeDtypeStruct((rows, width), F32),
            jax.ShapeDtypeStruct((rows, width), BF),
            jax.ShapeDtypeStruct((rows, width), BF),
            jax.ShapeDtypeStruct((1, hidden), F32),
            jax.ShapeDtypeStruct((8, width), F32),
        ],
        scratch_shapes=[
            pltpu.VMEM((width, width), BF),
            pltpu.VMEM((width, hidden), BF),
            pltpu.VMEM((hidden, width), BF),
        ]
        + [pltpu.SemaphoreType.DMA((cut.copies,)) for cut in cuts],
        compiler_params=pltpu.CompilerParams(vmem_limit_bytes=60 * MIB),
        cost_estimate=cost(2 * rows * width * (width + 2 * hidden), 34 * MIB),
    )(place, dm, slope, middle, vectors, *flat)


def weight_grad_kernel(cut, place, left, right, keep, send, whole):
    whole[...] = lax.dot_general(
        left[...], right[...], (((0,), (0,)), ((), ())), preferred_element_type=F32
    )
    for j in range(cut.replicas):
        value = whole[cut.spot(jnp.bitwise_xor(place[0], j))]
        (keep, send)[j & 1][j >> 1, 0] = rnd(value)


def weight_grad(cut, place, left, right):
    tokens, shards = left.shape[0], cut.shards
    shape = (cut.replicas // 2, shards, cut.r, cut.c)
    piece = pl.BlockSpec((cut.replicas // 2, 1, cut.r, cut.c), lambda d, s: (0, d, 0, 0))
    return pl.pallas_call(
        functools.partial(weight_grad_kernel, cut),
        grid_spec=pltpu.PrefetchScalarGridSpec(
            num_scalar_prefetch=1,
            grid=(shards,),
            in_specs=[
                pl.BlockSpec((tokens, cut.rows), lambda d, s: (0, lax.rem(s[1] + shards - d, shards))),
                pl.BlockSpec(right.shape, lambda d, s: (0, 0)),
            ],
            out_specs=[piece] * 2,
            scratch_shapes=[pltpu.VMEM((cut.rows, cut.columns), F32)],
        ),
        out_shape=[jax.ShapeDtypeStruct(shape, BF)] * 2,
        compiler_params=pltpu.CompilerParams(vmem_limit_bytes=56 * MIB),
        cost_estimate=cost(
            2 * tokens * shards * cut.rows * cut.columns, 2 * shards * cut.rows * cut.columns
        ),
    )(place, left, right)


def widen_kernel(cut, place, *refs):
    out = refs[-1]
    for j in range(cut.replicas):
        out[cut.spot(jnp.bitwise_xor(place[0], j))] = refs[j][...].astype(F32)


def widen(cut, place, slots):
    return pl.pallas_call(
        functools.partial(widen_kernel, cut),
        in_specs=[SMEM_SPEC] + [VMEM_SPEC] * cut.replicas,
        out_specs=VMEM_SPEC,
        out_shape=jax.ShapeDtypeStruct((cut.rows, cut.columns), F32),
        compiler_params=pltpu.CompilerParams(vmem_limit_bytes=48 * MIB),
        cost_estimate=cost(0, 6 * cut.rows * cut.columns),
    )(place, *slots)


def hidden_grad_kernel(place, block, dq, dk, dv, weight, out, sums):
    local = dq.shape[1]
    grad = dot_last(dq[...], weight[:, 0:local])
    grad += dot_last(dk[...], weight[:, local : 2 * local])
    grad += dot_last(dv[...], weight[:, 2 * local :])
    out[...] = rnd(grad)
    normal, _ = moments(block[...].astype(F32))
    sums[0:1, :] = jnp.sum(grad * normal, 0, keepdims=True)
    sums[1:2, :] = jnp.sum(grad, 0, keepdims=True)
    sums[2:8, :] = jnp.zeros((6, sums.shape[1]), F32)


def hidden_grad(place, block, dq, dk, dv, weight, distance, shards):
    rows, width = block.shape
    local = dq.shape[1]
    at = lambda i, s: (lax.rem(s[1] + shards - distance, shards), 0)
    here = lambda i, s: (0, 0)
    return pl.pallas_call(
        hidden_grad_kernel,
        grid_spec=pltpu.PrefetchScalarGridSpec(
            num_scalar_prefetch=1,
            grid=(1,),
            in_specs=[pl.BlockSpec((rows, width), here)]
            + [pl.BlockSpec((rows, local), at)] * 3
            + [pl.BlockSpec(weight.shape, here)],
            out_specs=[pl.BlockSpec((rows, width), here), pl.BlockSpec((8, width), here)],
        ),
        out_shape=[jax.ShapeDtypeStruct((rows, width), BF), jax.ShapeDtypeStruct((8, width), F32)],
        compiler_params=pltpu.CompilerParams(vmem_limit_bytes=40 * MIB),
        cost_estimate=cost(6 * rows * width * local, 5 * MIB),
    )(place, block, dq, dk, dv, weight)


def last_kernel(tokens, travel, own, dx2, gain, out):
    normal, scale = moments(tokens[...].astype(F32))
    grad = travel[...].astype(F32) + own[...].astype(F32)
    out[...] = rnd(dx2[...] + norm_grad(grad, gain[...], normal, scale))


def last(tokens, travel, own, dx2, gain):
    return pl.pallas_call(
        last_kernel,
        in_specs=[VMEM_SPEC] * 5,
        out_specs=VMEM_SPEC,
        out_shape=jax.ShapeDtypeStruct(tokens.shape, BF),
        compiler_params=pltpu.CompilerParams(vmem_limit_bytes=40 * MIB),
        cost_estimate=cost(0, 6 * MIB),
    )(tokens, travel, own, dx2, gain)


def swap(value, bit, replicas):
    return lax.ppermute(value, "dp", [(i, i ^ bit) for i in range(replicas)])


def turn(value, shards, step=1):
    return lax.ppermute(value, "fsdp", [(i, (i + step) % shards) for i in range(shards)])


def chip_bits(replicas, reverse):
    bits = [1 << n for n in range(1, replicas.bit_length() - 1)]
    return bits[::-1] if reverse else bits


def share(piece, replicas, reverse=False):
    parts = {0: piece}
    for bit in chip_bits(replicas, reverse):
        parts |= {m | bit: swap(part, bit, replicas) for m, part in list(parts.items())}
    parts |= {m | 1: swap(part, 1, replicas) for m, part in list(parts.items())}
    return [parts[j] for j in range(replicas)]


def add_low(left, right):
    return rnd(left.astype(F32) + right.astype(F32))


def plane_scatter(keep, send, replicas, reverse=False):
    got = swap(send, 1, replicas)
    parts = {2 * m: add_low(keep[m], got[m]) for m in range(replicas // 2)}
    for bit in chip_bits(replicas, reverse):
        there = [m for m in parts if m & bit]
        moved = swap(jnp.stack([parts[m] for m in there]), bit, replicas)
        parts = {m ^ bit: add_low(parts[m ^ bit], moved[n]) for n, m in enumerate(there)}
    return parts[0]


def ring_sum(parts, shards):
    total = parts[1]
    for d in range(2, shards + 1):
        total = add_low(turn(total, shards), parts[d % shards])
    return total


def gather_weight(cut, place, shard, reverse=False):
    piece = cut.of(shard, place[0])
    slots = jnp.stack([turn(piece, cut.shards, d) for d in range(1, cut.shards)])
    return share(slots, cut.replicas, reverse) + [shard]


def reduce_weight(cut, place, keep, send, reverse=False):
    total = ring_sum(plane_scatter(keep, send, cut.replicas, reverse), cut.shards)
    return widen(cut, place, share(total, cut.replicas, reverse))


def flip_by(value, axis, me, replicas):
    shape = value.shape
    bits = replicas.bit_length() - 1
    value = value.reshape(shape[:axis] + (2,) * bits + shape[axis + 1 :])
    for n in range(bits):
        where = axis + bits - 1 - n
        value = jnp.where((me >> n) & 1 == 1, jnp.flip(value, where), value)
    return value.reshape(shape)


def window_low(lengths, group_len):
    prompt = group_len // 2
    order = jnp.arange(lengths.shape[0], dtype=jnp.int32)
    ends = jnp.sum(jnp.where(order[:, None] <= order[None, :], lengths[:, None], 0), 0)
    pos = jnp.arange(prompt, dtype=jnp.int32)
    starts = jnp.max(jnp.where(ends[:, None] <= pos[None, :], ends[:, None], 0), 0)
    return jnp.concatenate([jnp.zeros((prompt,), jnp.int32), prompt + starts])[None]


def body(
    tokens,
    cotangent,
    cont_lengths,
    ln1_gain,
    ln1_bias,
    w_qkv,
    q_bias,
    v_bias,
    w_out,
    out_bias,
    ln2_gain,
    ln2_bias,
    w_up,
    up_bias,
    w_down,
    down_bias,
):
    rows, width = tokens.shape
    shards, replicas = lax.axis_size("fsdp"), lax.axis_size("dp")
    z, me = lax.axis_index("fsdp"), lax.axis_index("dp")
    place = jnp.stack([me, z]).astype(jnp.int32)
    group_len = rows * shards
    head_dim = width // H
    local = width // shards
    hidden = w_up.shape[2]
    w_qkv, w_out, w_up, w_down = w_qkv[0], w_out[0], w_up[0], w_down[0]
    out_parts = 1
    while w_out.shape[0] * out_parts // replicas < 16:
        out_parts *= 2
    cut_out = Cut(w_out.shape[0], width, out_parts, replicas, shards)
    cut_up = Cut(w_up.shape[0], hidden, hidden // width, replicas, shards)
    cut_down = Cut(w_down.shape[0], width, 1, replicas, shards)
    cuts = (cut_out, cut_up, cut_down)

    blocks = {0: tokens}
    for d in range(1, shards // 2 + 1):
        blocks[d] = turn(blocks[d - 1], shards)
        if shards - d not in blocks:
            blocks[shards - d] = turn(blocks[(shards - d + 1) % shards], shards, shards - 1)

    vectors = (ln1_gain, ln1_bias, q_bias, v_bias, out_bias, ln2_gain, ln2_bias, down_bias, up_bias)
    packed = jnp.concatenate(vectors, 1)
    turned = [packed] + [turn(packed, shards, step) for step in range(shards - 1, 0, -1)]
    turned = jnp.concatenate(turned + turned, 0)
    packed_all = lax.dynamic_slice_in_dim(turned, lax.rem(shards - z, shards), shards)
    full = []
    offset = 0
    for vector in vectors:
        size = vector.shape[1]
        full.append(packed_all[:, offset : offset + size].reshape(1, shards * size).astype(F32))
        offset += size
    gain_one, bias_one, _, _, bias_out, gain_two, bias_two, bias_down, bias_up = full
    middle_vectors = jnp.concatenate([bias_out, gain_two, bias_two, bias_down] * 2, 0)
    start_at = z * local
    bias_q = lax.dynamic_slice_in_dim(full[2], start_at, local, 1)
    bias_v = lax.dynamic_slice_in_dim(full[3], start_at, local, 1)
    bias_qkv = jnp.concatenate([bias_q, jnp.zeros_like(bias_q), bias_v], 1)

    slim = w_qkv.shape[0] // replicas
    mine = lax.dynamic_slice_in_dim(w_qkv, me * slim, slim, 0)
    mine = mine.reshape(slim, 3, shards, local).transpose(2, 0, 1, 3).reshape(shards, slim, 3 * local)
    mine = lax.all_to_all(mine, "fsdp", 0, 0, tiled=True)
    weight_qkv = flip_by(jnp.stack(share(mine, replicas)), 0, me, replicas)
    weight_qkv = weight_qkv.transpose(1, 0, 2, 3).reshape(width, 3 * local)

    h_all = jnp.zeros((group_len, width), BF)
    combined = jnp.zeros((group_len, 3 * local), BF)
    for d in [0] + sorted(range(1, shards), key=lambda d: min(d, shards - d)):
        h_all, combined = project(
            place, blocks[d], gain_one, bias_one, weight_qkv, bias_qkv, h_all, combined, d, shards
        )

    lists = [
        gather_weight(cut_out, place, w_out),
        gather_weight(cut_up, place, w_up),
        gather_weight(cut_down, place, w_down, True),
    ]

    low = window_low(cont_lengths[0], group_len)
    mixed, lse = attend(combined, low, head_dim)
    attended = lax.all_to_all(mixed, "fsdp", 0, 1, tiled=True)
    output, hidden_two, middle, acted, slope = feed_forward(
        place, attended, tokens, middle_vectors, bias_up, cuts, lists
    )

    dm = cotangent
    du, dx2, da, do, grad_bias_up, sums = feed_backward(
        place, dm, slope, middle, middle_vectors, cuts, lists
    )
    grad_mixed = lax.all_to_all(do, "fsdp", 1, 0, tiled=True)
    out_w_down = reduce_weight(cut_down, place, *weight_grad(cut_down, place, acted, dm))
    out_w_up = reduce_weight(cut_up, place, *weight_grad(cut_up, place, hidden_two, du), True)
    out_w_out = reduce_weight(cut_out, place, *weight_grad(cut_out, place, attended, da))

    dq, dk, dv = attend_grad(combined, low, mixed, lse, grad_mixed, head_dim)
    first_sums = jnp.zeros((8, width), F32)
    parts = {}
    for d in [*range(1, shards), 0]:
        parts[d], part_sums = hidden_grad(place, blocks[d], dq, dk, dv, weight_qkv, d, shards)
        first_sums += part_sums
    travel = parts[1]
    for d in range(2, shards):
        travel = add_low(turn(travel, shards), parts[d])
    input_grad = last(tokens, turn(travel, shards), parts[0], dx2, gain_one)

    dc = jnp.concatenate([dq, dk, dv], 1)
    grad_bias_qkv = jnp.sum(dc.astype(F32), 0)
    grad_w_qkv = rnd(jnp.einsum("td,te->de", h_all, dc, preferred_element_type=F32))
    rel = grad_w_qkv.reshape(shards, replicas, slim, 3 * local).transpose(1, 0, 2, 3)
    rel = flip_by(rel, 0, me, replicas)
    rel = rel.reshape(replicas // 2, 2, shards, slim, 3 * local)
    piece = plane_scatter(rel[:, 0], rel[:, 1], replicas)
    piece = lax.all_to_all(piece, "fsdp", 0, 0, tiled=True)
    piece = piece.reshape(shards, slim, 3, local).transpose(1, 2, 0, 3).reshape(slim, 3 * width)
    out_w_qkv = flip_by(jnp.stack(share(piece, replicas)), 0, me, replicas)
    out_w_qkv = out_w_qkv.reshape(w_qkv.shape).astype(F32)

    spread = jnp.zeros((width,), F32)
    grad_bias_q = lax.dynamic_update_slice(spread, grad_bias_qkv[:local], (start_at,))
    grad_bias_v = lax.dynamic_update_slice(spread, grad_bias_qkv[2 * local :], (start_at,))
    small = (
        first_sums[0],
        first_sums[1],
        grad_bias_q,
        grad_bias_v,
        sums[3],
        sums[1],
        sums[2],
        sums[0],
        grad_bias_up,
    )
    total = jnp.concatenate([g.reshape(shards, -1) for g in small], 1)
    bit = 1
    while bit < replicas:
        total = total + swap(total, bit, replicas)
        bit *= 2
    bit = 1
    while bit < shards:
        total = total + lax.ppermute(total, "fsdp", [(i, i ^ bit) for i in range(shards)])
        bit *= 2
    total = lax.dynamic_slice_in_dim(total, z, 1)
    outs = []
    offset = 0
    for vector in vectors:
        outs.append(total[:, offset : offset + vector.shape[1]])
        offset += vector.shape[1]
    return (
        output,
        input_grad,
        outs[0],
        outs[1],
        out_w_qkv[None],
        outs[2],
        outs[3],
        out_w_out[None],
        outs[4],
        outs[5],
        outs[6],
        out_w_up[None],
        outs[8],
        out_w_down[None],
        outs[7],
    )


def solution(mesh):
    vec = P(None, "fsdp")
    mat = P(None, "fsdp", None)
    tok = P(("dp", "fsdp"), None)
    in_specs = (tok, tok, P("dp", None), vec, vec, mat, vec, vec, mat, vec, vec, vec, mat, vec, mat, vec)
    out_specs = (tok, tok, vec, vec, mat, vec, vec, mat, vec, vec, vec, mat, vec, mat, vec)
    return jax.shard_map(body, mesh=mesh, in_specs=in_specs, out_specs=out_specs, check_vma=False)
```

time: 1600 us -> 622 us (0.39)
  waiting for transfers between devices: 1180 us -> 291 us
  Pallas kernels: 0 us -> 152 us
  matrix products: 148 us -> 6.68 us
  blocking collectives: 137 us -> 0 us
  starting transfers between devices: 0.73 us -> 87.9 us
  local copies, waits for them, and re-layouts: 58.1 us -> 37.7 us
  loops' own time: 16.4 us -> 0 us
    reduce_scatter x6 -> x0, waiting for transfers between devices: 673 us -> none  [the longest x1 160 us: body(): lax.psum_scatter(grad_value_all.astype(jnp.bfloat16), 'fsdp', scatter_dim...]
    all_gather x6 -> x0, waiting for transfers between devices: 463 us -> none  [the longest x1 145 us: fetch_weights(): lax.all_gather(sliced[9], 'fsdp', axis=0, tiled=True)]
    ppermute x0 -> x100, waiting for transfers between devices: none -> 291 us  [the longest x71 151 us: swap(): return lax.ppermute(value, 'dp', [(i, i ^ bit) for i in range(replicas)])]
    pallas_call x0 -> x19, Pallas kernels: none -> 152 us  [the longest x1 28.8 us: attend_grad(): pl.pallas_call(functools.partial(attend_grad_kernel, group_len, head_dim)...]
    dot_general x19 -> x1, matrix products: 148 us -> 6.68 us  [body(): jnp.einsum('td,te->de', h_all, dc, preferred_element_type=F32)]
    all_gather x9 -> x0, blocking collectives: 96.4 us -> none  [the longest x1 15.7 us: fetch_weights(): lax.all_gather(sliced[3], 'fsdp', axis=0, tiled=True)]
    ppermute x0 -> x100, starting transfers between devices: none -> 71.5 us  [the longest x71 40.7 us: swap(): return lax.ppermute(value, 'dp', [(i, i ^ bit) for i in range(replicas)])]
    psum x1 -> x0, waiting for transfers between devices: 36 us -> none  [reduce_sectioned(): lax.psum(shards[2].astype(jnp.bfloat16), 'dp').astype(jnp.float32)]
  transfers between devices with their start and end apart: 13 -> 104, of which waited for: 13 -> 44; matrix products, arithmetic and copies ran while one was open for 8% -> 9% of each run, Pallas kernels for 0% -> 16%
where the time goes in v2:
time: 622 us; the launch traced here: 612 us
  waiting for transfers between devices  291 us (47%)
  Pallas kernels  152 us (24%)
  starting transfers between devices  87.9 us (14%)
  local copies, waits for them, and re-layouts  37.7 us (6%)
  other arithmetic  34.6 us (6%)
  matrix products  6.68 us (1%)
    ppermute x71, waiting for transfers between devices, swap(): return lax.ppermute(value, 'dp', [(i, i ^ bit) for i in range(replicas)])  151 us
    ppermute x27, waiting for transfers between devices, turn(): lax.ppermute(value, 'fsdp', [(i, (i + step) % shards) for i in range(shar...  135 us
    ppermute x71, starting transfers between devices, swap(): return lax.ppermute(value, 'dp', [(i, i ^ bit) for i in range(replicas)])  40.7 us
    pallas_call x1, Pallas kernels, attend_grad(): pl.pallas_call(functools.partial(attend_grad_kernel, group_len, head_dim)...  28.8 us
    ppermute x27, starting transfers between devices, turn(): lax.ppermute(value, 'fsdp', [(i, (i + step) % shards) for i in range(shar...  27.3 us
    pallas_call x3, Pallas kernels, weight_grad(): pl.pallas_call(functools.partial(weight_grad_kernel, cut), grid_spec=pltp...  26.4 us
    pallas_call x1, Pallas kernels, feed_forward(): pl.pallas_call(functools.partial(forward_kernel, cuts, min(1024, hidden))...  24.7 us
    unnamed x115, local copies, waits for them, and re-layouts  24 us
  transfers between devices with their start and end apart: 104, of which 44 were waited for; matrix products, arithmetic and copies ran while one was open for 9% of the time, Pallas kernels for 16%

profile of v2, /device:TPU:0, one launch (start us, length us, event | category | flops | bytes accessed | tf_op | source)
XLA Modules:
  0.0 611.9 jit_solution(16387699837492113193)
XLA Ops:
  7.0 5.0 collective-permute-start.2
  14.3 4.1 all-to-all-start
  19.2 3.8 collective-permute-start.15
  28.1 2.9 collective-permute-start.24
  31.3 20.8 %collective-permute-done.14 = bf16[32,1024]{1,0:T(8,128)(2,1)S(1)} collective-permute-done((bf16[32,1024]{1,0:T(8,128)(2,1)S(1)}, bf16[32,1024]{1,0:T(8,128)(2,1)S(1)}, u32[]{:S(2)}, u32[]{:S(2)}) %collective-permute-start.14) | collective-permute-done | bytes 65568 | tf_op jit(solution)/shard_map/ppermute | solution.py:487
  54.9 22.4 %collective-permute-done.24 = bf16[128,1024]{1,0:T(8,128)(2,1)S(1)} collective-permute-done((bf16[128,1024]{1,0:T(8,128)(2,1)S(1)}, bf16[128,1024]{1,0:T(8,128)(2,1)S(1)}, u32[]{:S(2)}, u32[]{:S(2)}) %collective-permute-start.24) | collective-permute-done | bytes 262176 | tf_op jit(solution)/shard_map/ppermute | solution.py:487
  77.4 3.8 collective-permute-start.12
  81.4 18.4 %collective-permute-done.34 = bf16[128,1024]{1,0:T(8,128)(2,1)S(1)} collective-permute-done((bf16[128,1024]{1,0:T(8,128)(2,1)S(1)}, bf16[128,1024]{1,0:T(8,128)(2,1)S(1)}, u32[]{:S(2)}, u32[]{:S(2)}) %collective-permute-start.34) | collective-permute-done | bytes 262176 | tf_op jit(solution)/shard_map/ppermute | solution.py:487
  103.9 4.2 collective-permute-done.6
  113.7 2.1 collective-permute-done.10
  115.8 3.8 collective-permute-done.17.refs_2_
  126.4 3.3 shard_map.272
  129.7 3.3 shard_map.273
  133.0 14.8 %collective-permute-done.1.block = bf16[512,1024]{1,0:T(8,128)(2,1)S(1)} collective-permute-done((bf16[512,1024]{1,0:T(8,128)(2,1)}, bf16[512,1024]{1,0:T(8,128)(2,1)S(1)}, u32[]{:S(2)}, u32[]{:S(2)}) %collective-permute-start.1) | collective-permute-done | bytes 1048608 | tf_op jit(solution)/shard_map/ppermute | solution.py:487
  157.0 17.8 %shard_map.275 = (bf16[2048,256]{1,0:T(8,128)(2,1)}, f32[2,2,2048]{2,1,0:T(2,128)}) custom-call(bf16[2048,768]{1,0:T(8,128)(2,1)} %copy-done.3, bf16[2048,768]{1,0:T(8,128)(2,1)} %copy-done.3, bf16[2048,768]{1,0:T(8,128)(2,1)} %copy-done.3, s32[1,2048]{1,0:T(1,128)} %bitcast.266), custom_call_target="tpu_custom_call" | custom-call | flops 15000000512 | bytes 4194304 | tf_op jit(solution)/shard_map/pallas_call | solution.py:117
  174.9 3.9 all-to-all-start.1
  181.6 10.6 %collective-permute-done.39.refs_22_ = bf16[3,128,1024]{2,1,0:T(8,128)(2,1)} collective-permute-done((bf16[3,128,1024]{2,1,0:T(8,128)(2,1)}, bf16[3,128,1024]{2,1,0:T(8,128)(2,1)}, u32[]{:S(2)}, u32[]{:S(2)}) %collective-permute-start.39) | collective-permute-done | bytes 786464 | tf_op jit(solution)/shard_map/ppermute | solution.py:483
  193.0 7.0 %collective-permute-done.37.refs_20_ = bf16[3,128,1024]{2,1,0:T(8,128)(2,1)} collective-permute-done((bf16[3,128,1024]{2,1,0:T(8,128)(2,1)}, bf16[3,128,1024]{2,1,0:T(8,128)(2,1)}, u32[]{:S(2)}, u32[]{:S(2)}) %collective-permute-start.37) | collective-permute-done | bytes 786464 | tf_op jit(solution)/shard_map/ppermute | solution.py:483
  200.4 7.9 %collective-permute-done.31.refs_15_ = bf16[3,128,1024]{2,1,0:T(8,128)(2,1)} collective-permute-done((bf16[3,128,1024]{2,1,0:T(8,128)(2,1)}, bf16[3,128,1024]{2,1,0:T(8,128)(2,1)}, u32[]{:S(2)}, u32[]{:S(2)}) %collective-permute-start.31) | collective-permute-done | bytes 786464 | tf_op jit(solution)/shard_map/ppermute | solution.py:483
  208.3 7.7 %collective-permute-done.41.refs_24_ = bf16[3,128,1024]{2,1,0:T(8,128)(2,1)} collective-permute-done((bf16[3,128,1024]{2,1,0:T(8,128)(2,1)}, bf16[3,128,1024]{2,1,0:T(8,128)(2,1)}, u32[]{:S(2)}, u32[]{:S(2)}) %collective-permute-start.41) | collective-permute-done | bytes 786464 | tf_op jit(solution)/shard_map/ppermute | solution.py:483
  218.6 24.7 %shard_map.276 = (bf16[512,1024]{1,0:T(8,128)(2,1)}, bf16[512,1024]{1,0:T(8,128)(2,1)}, f32[512,1024]{1,0:T(8,128)}, bf16[512,4096]{1,0:T(8,128)(2,1)}, bf16[512,4096]{1,0:T(8,128)(2,1)}) custom-call(s32[2]{0:T(128)} %copy-done.19, bf16[512,1024]{1,0:T(8,128)(2,1)} %bitcast.238, bf16[512,1024]{1,0:T(8,128)(2,1)} %tokens.3, f32[8,1024]{1,0:T(8,128)} %concatenate.28.vectors, ...), custom_call_target="tpu_custom_call" | custom-call | flops 9663676416 | bytes 35651584 | tf_op jit(solution)/shard_map/pallas_call | solution.py:299
  243.3 23.6 %shard_map.277 = (bf16[512,4096]{1,0:T(8,128)(2,1)}, f32[512,1024]{1,0:T(8,128)}, bf16[512,1024]{1,0:T(8,128)(2,1)}, bf16[512,1024]{1,0:T(8,128)(2,1)}, f32[1,4096]{1,0:T(1,128)}, /*index=5*/f32[8,1024]{1,0:T(8,128)}) custom-call(s32[2]{0:T(128)} %copy-done.19, bf16[512,1024]{1,0:T(8,128)(2,1)} %right.1, bf16[512,4096]{1,0:T(8,128)(2,1)} %get-tuple-element.63.slope, ...), custom_call_target="tpu_custom_call" | custom-call | flops 9663676416 | bytes 35651584 | tf_op jit(solution)/shard_map/pallas_call | solution.py:359
  266.9 2.3 copy.94
  269.2 5.1 all-to-all-start.2
  274.3 5.7 shard_map.284
  281.6 10.4 %shard_map.286 = (bf16[4,4,128,1024]{3,2,1,0:T(8,128)(2,1)}, bf16[4,4,128,1024]{3,2,1,0:T(8,128)(2,1)}) custom-call(s32[2]{0:T(128)} %copy-done.19, bf16[512,1024]{1,0:T(8,128)(2,1)} %get-tuple-element.84.left, bf16[512,4096]{1,0:T(8,128)(2,1)} %get-tuple-element.85.right), custom_call_target="tpu_custom_call" | custom-call | flops 4294967296 | bytes 8388608 | tf_op jit(solution)/shard_map/pallas_call | solution.py:395
  292.2 10.3 %shard_map.288 = (bf16[4,4,128,1024]{3,2,1,0:T(8,128)(2,1)}, bf16[4,4,128,1024]{3,2,1,0:T(8,128)(2,1)}) custom-call(s32[2]{0:T(128)} %copy-done.19, bf16[512,4096]{1,0:T(8,128)(2,1)} %get-tuple-element.88.left, bf16[512,1024]{1,0:T(8,128)(2,1)} %right.1), custom_call_target="tpu_custom_call" | custom-call | flops 4294967296 | bytes 8388608 | tf_op jit(solution)/shard_map/pallas_call | solution.py:395
  304.7 28.8 %shard_map.278 = (bf16[2048,256]{1,0:T(8,128)(2,1)}, bf16[2048,256]{1,0:T(8,128)(2,1)}, bf16[2048,256]{1,0:T(8,128)(2,1)}) custom-call(bf16[2048,768]{1,0:T(8,128)(2,1)} %copy-done.3, bf16[2048,768]{1,0:T(8,128)(2,1)} %copy-done.3, bf16[2048,768]{1,0:T(8,128)(2,1)} %copy-done.3, s32[1,2048]{1,0:T(1,128)} %bitcast.267, ...), custom_call_target="tpu_custom_call" | custom-call | flops 24999999488 | bytes 8388608 | tf_op jit(solution)/shard_map/pallas_call | solution.py:136
  333.5 2.4 constant_dynamic-update-slice_fusion.11
  340.1 3.1 shard_map.281
  347.1 3.1 shard_map.279
  351.3 2.3 constant_dynamic-update-slice_fusion.10
  354.6 2.4 convert_reduce_fusion
  357.4 6.7 %convolution_convert_fusion = bf16[1024,768]{1,0:T(8,128)(2,1)S(1)} fusion(bf16[2048,1024]{1,0:T(8,128)(2,1)} %copy-done.2, bf16[2048,768]{1,0:T(8,128)(2,1)} %constant_dynamic-update-slice_fusion.9), kind=kOutput, calls=%fused_computation.28 | convolution fusion | flops 3222011904 | bytes 8912896 | tf_op jit(solution)/shard_map/td,te->de/dot_general | solution.py:662
  368.1 6.6 %collective-permute-done.63 = bf16[1,4,32,1024]{3,2,1,0:T(8,128)(2,1)S(1)} collective-permute-done((bf16[1,4,32,1024]{3,2,1,0:T(8,128)(2,1)S(1)}, bf16[1,4,32,1024]{3,2,1,0:T(8,128)(2,1)S(1)}, u32[]{:S(2)}, u32[]{:S(2)}) %collective-permute-start.63) | collective-permute-done | bytes 262176 | tf_op jit(solution)/shard_map/ppermute | solution.py:483
  376.9 4.1 collective-permute-done.64
  382.4 2.8 collective-permute-done.47
  391.0 3.1 collective-permute-done.49
  406.0 4.1 collective-permute-done.52
  415.3 3.5 collective-permute-done.53
  420.6 3.4 all-to-all-start.3
  423.9 3.7 collective-permute-done.43
  427.6 2.6 add_convert_fusion.15
  433.6 5.9 collective-permute-done.55
  441.0 3.2 add_convert_fusion.12
  446.4 2.6 add_convert_fusion.7
  451.3 41.6 %collective-permute-done.75 = bf16[2,4,128,1024]{3,2,1,0:T(8,128)(2,1)S(1)} collective-permute-done((bf16[2,4,128,1024]{3,2,1,0:T(8,128)(2,1)S(1)}, bf16[2,4,128,1024]{3,2,1,0:T(8,128)(2,1)S(1)}, u32[]{:S(2)}, u32[]{:S(2)}) %collective-permute-start.75) | collective-permute-done | bytes 2097184 | tf_op jit(solution)/shard_map/ppermute | solution.py:483
  500.2 19.5 %collective-permute-done.76 = bf16[1,4,128,1024]{3,2,1,0:T(8,128)(2,1)S(1)} collective-permute-done((bf16[1,4,128,1024]{3,2,1,0:T(8,128)(2,1)S(1)}, bf16[1,4,128,1024]{3,2,1,0:T(8,128)(2,1)S(1)}, u32[]{:S(2)}, u32[]{:S(2)}) %collective-permute-start.76) | collective-permute-done | bytes 1048608 | tf_op jit(solution)/shard_map/ppermute | solution.py:483
  519.8 2.1 add_convert_fusion.1
  522.0 2.2 collective-permute-done.89
  524.3 2.1 add_convert_fusion
  526.5 5.8 collective-permute-done.77
  532.5 5.5 collective-permute-done.90
  539.8 3.8 collective-permute-done.78
  543.7 5.5 collective-permute-done.91
  549.6 27.7 %collective-permute-done.79 = bf16[128,1024]{1,0:T(8,128)(2,1)S(1)} collective-permute-done((bf16[128,1024]{1,0:T(8,128)(2,1)S(1)}, bf16[128,1024]{1,0:T(8,128)(2,1)S(1)}, u32[]{:S(2)}, u32[]{:S(2)}) %collective-permute-start.79) | collective-permute-done | bytes 262176 | tf_op jit(solution)/shard_map/ppermute | solution.py:487
  579.4 2.2 collective-permute-done.92
  584.0 4.1 collective-permute-done.83.refs_4_
  588.9 3.3 collective-permute-done.94.refs_2_
  593.8 3.6 collective-permute-done.85.refs_6_
  597.4 2.3 collective-permute-done.98.refs_6_
  603.3 2.5 shard_map.283
  605.8 2.8 shard_map.287
  608.6 2.8 shard_map.289
  (385 shorter events, 126.3 us)
Async XLA Ops:
  7.0 19.4 %collective-permute-start.2 = (bf16[1,3072]{1,0:T(2,128)(2,1)S(1)}, bf16[1,3072]{1,0:T(2,128)(2,1)S(1)}, u32[]{:S(2)}, u32[]{:S(2)}) collective-permute-start(bf16[1,3072]{1,0:T(2,128)(2,1)S(1)} %constant_dynamic-update-slice_fusion), channel_id=1, source_target_pairs={{0,3},{1,0},{2,1},{3,2},{4,7},{5,4},{6,5},{7,6},{8,11},{9,8},{10,9... | collective-permute-start | bytes 18440 | tf_op jit(solution)/shard_map/ppermute | solution.py:487
  12.1 14.5 %collective-permute-start.3 = (bf16[1,3072]{1,0:T(2,128)(2,1)S(1)}, bf16[1,3072]{1,0:T(2,128)(2,1)S(1)}, u32[]{:S(2)}, u32[]{:S(2)}) collective-permute-start(bf16[1,3072]{1,0:T(2,128)(2,1)S(1)} %constant_dynamic-update-slice_fusion), channel_id=1, source_target_pairs={{0,2},{1,3},{2,0},{3,1},{4,6},{5,7},{6,4},{7,5},{8,10},{9,11},{10,... | collective-permute-start | bytes 18440 | tf_op jit(solution)/shard_map/ppermute | solution.py:487
  12.1 16.0 %collective-permute-start.4 = (bf16[1,3072]{1,0:T(2,128)(2,1)S(1)}, bf16[1,3072]{1,0:T(2,128)(2,1)S(1)}, u32[]{:S(2)}, u32[]{:S(2)}) collective-permute-start(bf16[1,3072]{1,0:T(2,128)(2,1)S(1)} %constant_dynamic-update-slice_fusion), channel_id=1, source_target_pairs={{0,1},{1,2},{2,3},{3,0},{4,5},{5,6},{6,7},{7,4},{8,9},{9,10},{10,1... | collective-permute-start | bytes 18440 | tf_op jit(solution)/shard_map/ppermute | solution.py:487
  14.3 86.6 %all-to-all-start = ((bf16[4,32,768]{2,1,0:T(8,128)(2,1)}), bf16[4,32,768]{2,1,0:T(8,128)(2,1)S(1)}, u32[]{:S(2)}, u32[]{:S(2)}) async-start(bf16[4,32,768]{2,1,0:T(8,128)(2,1)} %reshape.330), calls=%async_computation | async-start | bytes 393216 | tf_op jit(solution)/shard_map/all_to_all | solution.py:616
  19.2 12.0 %collective-permute-start.15 = (bf16[32,1024]{1,0:T(8,128)(2,1)S(1)}, bf16[32,1024]{1,0:T(8,128)(2,1)S(1)}, u32[]{:S(2)}, u32[]{:S(2)}) collective-permute-start(bf16[32,1024]{1,0:T(8,128)(2,1)S(1)} %dynamic-slice_bitcast_fusion.2), channel_id=1, source_target_pairs={{0,3},{1,0},{2,1},{3,2},{4,7},{5,4},{6,5},{7,6},{8,11},{9,8},{10,9... | collective-permute-start | bytes 196616 | tf_op jit(solution)/shard_map/ppermute | solution.py:487
  24.0 28.2 %collective-permute-start.25 = (bf16[128,1024]{1,0:T(8,128)(2,1)S(1)}, bf16[128,1024]{1,0:T(8,128)(2,1)S(1)}, u32[]{:S(2)}, u32[]{:S(2)}) collective-permute-start(bf16[128,1024]{1,0:T(8,128)(2,1)S(1)} %dynamic-slice_bitcast_fusion.1), channel_id=1, source_target_pairs={{0,3},{1,0},{2,1},{3,2},{4,7},{5,4},{6,5},{7,6},{8,11},{9,8},{10,9... | collective-permute-start | bytes 786440 | tf_op jit(solution)/shard_map/ppermute | solution.py:487
  26.5 25.7 %collective-permute-start.14 = (bf16[32,1024]{1,0:T(8,128)(2,1)S(1)}, bf16[32,1024]{1,0:T(8,128)(2,1)S(1)}, u32[]{:S(2)}, u32[]{:S(2)}) collective-permute-start(bf16[32,1024]{1,0:T(8,128)(2,1)S(1)} %dynamic-slice_bitcast_fusion.2), channel_id=1, source_target_pairs={{0,2},{1,3},{2,0},{3,1},{4,6},{5,7},{6,4},{7,5},{8,10},{9,11},{10,... | collective-permute-start | bytes 196616 | tf_op jit(solution)/shard_map/ppermute | solution.py:487
  26.5 25.6 %collective-permute-start.13 = (bf16[32,1024]{1,0:T(8,128)(2,1)S(1)}, bf16[32,1024]{1,0:T(8,128)(2,1)S(1)}, u32[]{:S(2)}, u32[]{:S(2)}) collective-permute-start(bf16[32,1024]{1,0:T(8,128)(2,1)S(1)} %dynamic-slice_bitcast_fusion.2), channel_id=1, source_target_pairs={{0,1},{1,2},{2,3},{3,0},{4,5},{5,6},{6,7},{7,4},{8,9},{9,10},{10,1... | collective-permute-start | bytes 196616 | tf_op jit(solution)/shard_map/ppermute | solution.py:487
  28.1 49.3 %collective-permute-start.24 = (bf16[128,1024]{1,0:T(8,128)(2,1)S(1)}, bf16[128,1024]{1,0:T(8,128)(2,1)S(1)}, u32[]{:S(2)}, u32[]{:S(2)}) collective-permute-start(bf16[128,1024]{1,0:T(8,128)(2,1)S(1)} %dynamic-slice_bitcast_fusion.1), channel_id=1, source_target_pairs={{0,2},{1,3},{2,0},{3,1},{4,6},{5,7},{6,4},{7,5},{8,10},{9,11},{10,... | collective-permute-start | bytes 786440 | tf_op jit(solution)/shard_map/ppermute | solution.py:487
  31.2 46.2 %collective-permute-start.23 = (bf16[128,1024]{1,0:T(8,128)(2,1)S(1)}, bf16[128,1024]{1,0:T(8,128)(2,1)S(1)}, u32[]{:S(2)}, u32[]{:S(2)}) collective-permute-start(bf16[128,1024]{1,0:T(8,128)(2,1)S(1)} %dynamic-slice_bitcast_fusion.1), channel_id=1, source_target_pairs={{0,1},{1,2},{2,3},{3,0},{4,5},{5,6},{6,7},{7,4},{8,9},{9,10},{10,1... | collective-permute-start | bytes 786440 | tf_op jit(solution)/shard_map/ppermute | solution.py:487
  52.1 29.2 %collective-permute-start.35 = (bf16[128,1024]{1,0:T(8,128)(2,1)S(1)}, bf16[128,1024]{1,0:T(8,128)(2,1)S(1)}, u32[]{:S(2)}, u32[]{:S(2)}) collective-permute-start(bf16[128,1024]{1,0:T(8,128)(2,1)S(1)} %dynamic-slice_bitcast_fusion), channel_id=1, source_target_pairs={{0,3},{1,0},{2,1},{3,2},{4,7},{5,4},{6,5},{7,6},{8,11},{9,8},{10,9... | collective-permute-start | bytes 786440 | tf_op jit(solution)/shard_map/ppermute | solution.py:487
  52.1 47.7 %collective-permute-start.34 = (bf16[128,1024]{1,0:T(8,128)(2,1)S(1)}, bf16[128,1024]{1,0:T(8,128)(2,1)S(1)}, u32[]{:S(2)}, u32[]{:S(2)}) collective-permute-start(bf16[128,1024]{1,0:T(8,128)(2,1)S(1)} %dynamic-slice_bitcast_fusion), channel_id=1, source_target_pairs={{0,2},{1,3},{2,0},{3,1},{4,6},{5,7},{6,4},{7,5},{8,10},{9,11},{10,... | collective-permute-start | bytes 786440 | tf_op jit(solution)/shard_map/ppermute | solution.py:487
  52.2 47.7 %collective-permute-start.33 = (bf16[128,1024]{1,0:T(8,128)(2,1)S(1)}, bf16[128,1024]{1,0:T(8,128)(2,1)S(1)}, u32[]{:S(2)}, u32[]{:S(2)}) collective-permute-start(bf16[128,1024]{1,0:T(8,128)(2,1)S(1)} %dynamic-slice_bitcast_fusion), channel_id=1, source_target_pairs={{0,1},{1,2},{2,3},{3,0},{4,5},{5,6},{6,7},{7,4},{8,9},{9,10},{10,1... | collective-permute-start | bytes 786440 | tf_op jit(solution)/shard_map/ppermute | solution.py:487
  77.4 42.7 %collective-permute-start = (bf16[512,1024]{1,0:T(8,128)(2,1)S(1)}, bf16[512,1024]{1,0:T(8,128)(2,1)}, u32[]{:S(2)}, u32[]{:S(2)}) collective-permute-start(bf16[512,1024]{1,0:T(8,128)(2,1)S(1)} %copy-done.7), channel_id=1, source_target_pairs={{0,1},{1,2},{2,3},{3,0},{4,5},{5,6},{6,7},{7,4},{8,9},{9,10},{10,1... | collective-permute-start | bytes 3145736 | tf_op jit(solution)/shard_map/ppermute | solution.py:487
  77.4 49.0 %collective-permute-start.12 = (bf16[512,1024]{1,0:T(8,128)(2,1)S(1)}, bf16[512,1024]{1,0:T(8,128)(2,1)}, u32[]{:S(2)}, u32[]{:S(2)}) collective-permute-start(bf16[512,1024]{1,0:T(8,128)(2,1)S(1)} %copy-done.7), channel_id=1, source_target_pairs={{0,3},{1,0},{2,1},{3,2},{4,7},{5,4},{6,5},{7,6},{8,11},{9,8},{10,9... | collective-permute-start | bytes 3145736 | tf_op jit(solution)/shard_map/ppermute | solution.py:487
  81.3 72.2 %collective-permute-start.16 = (bf16[3,32,1024]{2,1,0:T(8,128)(2,1)}, bf16[3,32,1024]{2,1,0:T(8,128)(2,1)}, u32[]{:S(2)}, u32[]{:S(2)}) collective-permute-start(bf16[3,32,1024]{2,1,0:T(8,128)(2,1)} %pad_maximum_fusion.6.refs_0_), channel_id=1, source_target_pairs={{0,4},{4,0},{8,12},{12,8},{16,20},{20,16},{24,28},{28,24},{1,5},{5... | collective-permute-start | bytes 589832 | tf_op jit(solution)/shard_map/ppermute | solution.py:483
  120.1 34.7 %collective-permute-start.18 = (bf16[3,32,1024]{2,1,0:T(8,128)(2,1)S(1)}, bf16[3,32,1024]{2,1,0:T(8,128)(2,1)S(1)}, u32[]{:S(2)}, u32[]{:S(2)}) collective-permute-start(bf16[3,32,1024]{2,1,0:T(8,128)(2,1)S(1)} %collective-permute-done.17.refs_2_), channel_id=1, source_target_pairs={{0,4},{4,0},{8,12},{12,8},{16,20},{20,16},{24,28},{28,24},{1,5},{5... | collective-permute-start | bytes 589832 | tf_op jit(solution)/shard_map/ppermute | solution.py:483
  120.1 27.6 %collective-permute-start.1 = (bf16[512,1024]{1,0:T(8,128)(2,1)}, bf16[512,1024]{1,0:T(8,128)(2,1)S(1)}, u32[]{:S(2)}, u32[]{:S(2)}) collective-permute-start(bf16[512,1024]{1,0:T(8,128)(2,1)} %collective-permute-done.block), channel_id=1, source_target_pairs={{0,1},{1,2},{2,3},{3,0},{4,5},{5,6},{6,7},{7,4},{8,9},{9,10},{10,1... | collective-permute-start | bytes 3145736 | tf_op jit(solution)/shard_map/ppermute | solution.py:487
  125.9 31.0 %collective-permute-start.21 = (bf16[3,32,1024]{2,1,0:T(8,128)(2,1)S(1)}, bf16[3,32,1024]{2,1,0:T(8,128)(2,1)}, u32[]{:S(2)}, u32[]{:S(2)}) collective-permute-start(bf16[3,32,1024]{2,1,0:T(8,128)(2,1)S(1)} %collective-permute-done.17.refs_2_), channel_id=1, source_target_pairs={{0,16},{4,20},{8,24},{12,28},{16,0},{20,4},{24,8},{28,12},{1,17},{... | collective-permute-start | bytes 589832 | tf_op jit(solution)/shard_map/ppermute | solution.py:483
  126.4 30.0 %collective-permute-start.20 = (bf16[3,32,1024]{2,1,0:T(8,128)(2,1)S(1)}, bf16[3,32,1024]{2,1,0:T(8,128)(2,1)S(1)}, u32[]{:S(2)}, u32[]{:S(2)}) collective-permute-start(bf16[3,32,1024]{2,1,0:T(8,128)(2,1)S(1)} %collective-permute-done.19.refs_4_), channel_id=1, source_target_pairs={{0,4},{4,0},{8,12},{12,8},{16,20},{20,16},{24,28},{28,24},{1,5},{5... | collective-permute-start | bytes 589832 | tf_op jit(solution)/shard_map/ppermute | solution.py:483
  147.7 31.5 %collective-permute-start.26 = (bf16[3,128,1024]{2,1,0:T(8,128)(2,1)S(1)}, bf16[3,128,1024]{2,1,0:T(8,128)(2,1)}, u32[]{:S(2)}, u32[]{:S(2)}) collective-permute-start(bf16[3,128,1024]{2,1,0:T(8,128)(2,1)S(1)} %pad_maximum_fusion.2.refs_9_), channel_id=1, source_target_pairs={{0,4},{4,0},{8,12},{12,8},{16,20},{20,16},{24,28},{28,24},{1,5},{5... | collective-permute-start | bytes 2359304 | tf_op jit(solution)/shard_map/ppermute | solution.py:483
  153.5 26.5 %collective-permute-start.27 = (bf16[3,128,1024]{2,1,0:T(8,128)(2,1)S(1)}, bf16[3,128,1024]{2,1,0:T(8,128)(2,1)}, u32[]{:S(2)}, u32[]{:S(2)}) collective-permute-start(bf16[3,128,1024]{2,1,0:T(8,128)(2,1)S(1)} %pad_maximum_fusion.2.refs_9_), channel_id=1, source_target_pairs={{0,8},{4,12},{8,0},{12,4},{16,24},{20,28},{24,16},{28,20},{1,9},{5... | collective-permute-start | bytes 2359304 | tf_op jit(solution)/shard_map/ppermute | solution.py:483
  154.8 25.2 %collective-permute-start.29 = (bf16[3,128,1024]{2,1,0:T(8,128)(2,1)S(1)}, bf16[3,128,1024]{2,1,0:T(8,128)(2,1)}, u32[]{:S(2)}, u32[]{:S(2)}) collective-permute-start(bf16[3,128,1024]{2,1,0:T(8,128)(2,1)S(1)} %pad_maximum_fusion.2.refs_9_), channel_id=1, source_target_pairs={{0,16},{4,20},{8,24},{12,28},{16,0},{20,4},{24,8},{28,12},{1,17},{... | collective-permute-start | bytes 2359304 | tf_op jit(solution)/shard_map/ppermute | solution.py:483
  156.4 35.8 %collective-permute-start.39 = (bf16[3,128,1024]{2,1,0:T(8,128)(2,1)}, bf16[3,128,1024]{2,1,0:T(8,128)(2,1)}, u32[]{:S(2)}, u32[]{:S(2)}) collective-permute-start(bf16[3,128,1024]{2,1,0:T(8,128)(2,1)} %pad_maximum_fusion.3.refs_18_), channel_id=1, source_target_pairs={{0,16},{4,20},{8,24},{12,28},{16,0},{20,4},{24,8},{28,12},{1,17},{... | collective-permute-start | bytes 2359304 | tf_op jit(solution)/shard_map/ppermute | solution.py:483
  156.9 21.9 %collective-permute-start.22 = (bf16[3,32,1024]{2,1,0:T(8,128)(2,1)}, bf16[3,32,1024]{2,1,0:T(8,128)(2,1)}, u32[]{:S(2)}, u32[]{:S(2)}) collective-permute-start(bf16[3,32,1024]{2,1,0:T(8,128)(2,1)} %collective-permute-done.21.refs_6_), channel_id=1, source_target_pairs={{0,4},{4,0},{8,12},{12,8},{16,20},{20,16},{24,28},{28,24},{1,5},{5... | collective-permute-start | bytes 589832 | tf_op jit(solution)/shard_map/ppermute | solution.py:483
  174.9 42.6 %all-to-all-start.1 = ((bf16[4,512,256]{2,1,0:T(8,128)(2,1)}), bf16[4,512,256]{2,1,0:T(8,128)(2,1)S(1)}, u32[]{:S(2)}, u32[]{:S(2)}) async-start(bf16[4,512,256]{2,1,0:T(8,128)(2,1)} %bitcast.237), calls=%async_computation.1 | async-start | bytes 2097152 | tf_op jit(solution)/shard_map/all_to_all | solution.py:635
  178.8 14.1 %collective-permute-start.36 = (bf16[3,128,1024]{2,1,0:T(8,128)(2,1)}, bf16[3,128,1024]{2,1,0:T(8,128)(2,1)}, u32[]{:S(2)}, u32[]{:S(2)}) collective-permute-start(bf16[3,128,1024]{2,1,0:T(8,128)(2,1)} %pad_maximum_fusion.3.refs_18_), channel_id=1, source_target_pairs={{0,4},{4,0},{8,12},{12,8},{16,20},{20,16},{24,28},{28,24},{1,5},{5... | collective-permute-start | bytes 2359304 | tf_op jit(solution)/shard_map/ppermute | solution.py:483
  179.2 20.7 %collective-permute-start.37 = (bf16[3,128,1024]{2,1,0:T(8,128)(2,1)}, bf16[3,128,1024]{2,1,0:T(8,128)(2,1)}, u32[]{:S(2)}, u32[]{:S(2)}) collective-permute-start(bf16[3,128,1024]{2,1,0:T(8,128)(2,1)} %pad_maximum_fusion.3.refs_18_), channel_id=1, source_target_pairs={{0,8},{4,12},{8,0},{12,4},{16,24},{20,28},{24,16},{28,20},{1,9},{5... | collective-permute-start | bytes 2359304 | tf_op jit(solution)/shard_map/ppermute | solution.py:483
  180.0 19.9 %collective-permute-start.28 = (bf16[3,128,1024]{2,1,0:T(8,128)(2,1)}, bf16[3,128,1024]{2,1,0:T(8,128)(2,1)}, u32[]{:S(2)}, u32[]{:S(2)}) collective-permute-start(bf16[3,128,1024]{2,1,0:T(8,128)(2,1)} %collective-permute-done.27.refs_11_), channel_id=1, source_target_pairs={{0,4},{4,0},{8,12},{12,8},{16,20},{20,16},{24,28},{28,24},{1,5},{5... | collective-permute-start | bytes 2359304 | tf_op jit(solution)/shard_map/ppermute | solution.py:483
  180.0 28.3 %collective-permute-start.31 = (bf16[3,128,1024]{2,1,0:T(8,128)(2,1)}, bf16[3,128,1024]{2,1,0:T(8,128)(2,1)}, u32[]{:S(2)}, u32[]{:S(2)}) collective-permute-start(bf16[3,128,1024]{2,1,0:T(8,128)(2,1)} %collective-permute-done.27.refs_11_), channel_id=1, source_target_pairs={{0,16},{4,20},{8,24},{12,28},{16,0},{20,4},{24,8},{28,12},{1,17},{... | collective-permute-start | bytes 2359304 | tf_op jit(solution)/shard_map/ppermute | solution.py:483
  192.2 23.8 %collective-permute-start.41 = (bf16[3,128,1024]{2,1,0:T(8,128)(2,1)}, bf16[3,128,1024]{2,1,0:T(8,128)(2,1)}, u32[]{:S(2)}, u32[]{:S(2)}) collective-permute-start(bf16[3,128,1024]{2,1,0:T(8,128)(2,1)} %collective-permute-done.39.refs_22_), channel_id=1, source_target_pairs={{0,8},{4,12},{8,0},{12,4},{16,24},{20,28},{24,16},{28,20},{1,9},{5... | collective-permute-start | bytes 2359304 | tf_op jit(solution)/shard_map/ppermute | solution.py:483
  192.9 25.6 %collective-permute-start.40 = (bf16[3,128,1024]{2,1,0:T(8,128)(2,1)}, bf16[3,128,1024]{2,1,0:T(8,128)(2,1)}, u32[]{:S(2)}, u32[]{:S(2)}) collective-permute-start(bf16[3,128,1024]{2,1,0:T(8,128)(2,1)} %collective-permute-done.39.refs_22_), channel_id=1, source_target_pairs={{0,4},{4,0},{8,12},{12,8},{16,20},{20,16},{24,28},{28,24},{1,5},{5... | collective-permute-start | bytes 2359304 | tf_op jit(solution)/shard_map/ppermute | solution.py:483
  199.9 18.6 %collective-permute-start.30 = (bf16[3,128,1024]{2,1,0:T(8,128)(2,1)}, bf16[3,128,1024]{2,1,0:T(8,128)(2,1)}, u32[]{:S(2)}, u32[]{:S(2)}) collective-permute-start(bf16[3,128,1024]{2,1,0:T(8,128)(2,1)} %collective-permute-done.29.refs_13_), channel_id=1, source_target_pairs={{0,4},{4,0},{8,12},{12,8},{16,20},{20,16},{24,28},{28,24},{1,5},{5... | collective-permute-start | bytes 2359304 | tf_op jit(solution)/shard_map/ppermute | solution.py:483
  199.9 18.6 %collective-permute-start.38 = (bf16[3,128,1024]{2,1,0:T(8,128)(2,1)}, bf16[3,128,1024]{2,1,0:T(8,128)(2,1)}, u32[]{:S(2)}, u32[]{:S(2)}) collective-permute-start(bf16[3,128,1024]{2,1,0:T(8,128)(2,1)} %collective-permute-done.37.refs_20_), channel_id=1, source_target_pairs={{0,4},{4,0},{8,12},{12,8},{16,20},{20,16},{24,28},{28,24},{1,5},{5... | collective-permute-start | bytes 2359304 | tf_op jit(solution)/shard_map/ppermute | solution.py:483
  269.2 35.5 %all-to-all-start.2 = ((bf16[512,4,256]{2,0,1:T(8,128)(2,1)}), bf16[512,4,256]{2,0,1:T(8,128)(2,1)}, u32[]{:S(2)}, u32[]{:S(2)}) async-start(bf16[512,4,256]{2,0,1:T(8,128)(2,1)} %bitcast.206), calls=%async_computation.2 | async-start | bytes 2097152 | tf_op jit(solution)/shard_map/all_to_all | solution.py:644
  280.0 22.7 %collective-permute-start.61 = (bf16[4,4,32,1024]{3,2,1,0:T(8,128)(2,1)}, bf16[4,4,32,1024]{3,2,1,0:T(8,128)(2,1)S(1)}, u32[]{:S(2)}, u32[]{:S(2)}) collective-permute-start(bf16[4,4,32,1024]{3,2,1,0:T(8,128)(2,1)} %get-tuple-element.83), channel_id=1, source_target_pairs={{0,4},{4,0},{8,12},{12,8},{16,20},{20,16},{24,28},{28,24},{1,5},{5... | collective-permute-start | bytes 3145736 | tf_op jit(solution)/shard_map/ppermute | solution.py:483
  291.9 149.0 %collective-permute-start.74 = (bf16[4,4,128,1024]{3,2,1,0:T(8,128)(2,1)}, bf16[4,4,128,1024]{3,2,1,0:T(8,128)(2,1)}, u32[]{:S(2)}, u32[]{:S(2)}) collective-permute-start(bf16[4,4,128,1024]{3,2,1,0:T(8,128)(2,1)} %get-tuple-element.87), channel_id=1, source_target_pairs={{0,4},{4,0},{8,12},{12,8},{16,20},{20,16},{24,28},{28,24},{1,5},{5... | collective-permute-start | bytes 12582920 | tf_op jit(solution)/shard_map/ppermute | solution.py:483
  302.5 142.6 %collective-permute-start.87 = (bf16[4,4,128,1024]{3,2,1,0:T(8,128)(2,1)}, bf16[4,4,128,1024]{3,2,1,0:T(8,128)(2,1)}, u32[]{:S(2)}, u32[]{:S(2)}) collective-permute-start(bf16[4,4,128,1024]{3,2,1,0:T(8,128)(2,1)} %get-tuple-element.90), channel_id=1, source_target_pairs={{0,4},{4,0},{8,12},{12,8},{16,20},{20,16},{24,28},{28,24},{1,5},{5... | collective-permute-start | bytes 12582920 | tf_op jit(solution)/shard_map/ppermute | solution.py:483
  303.9 60.7 %collective-permute-start.62 = (bf16[2,4,32,1024]{3,2,1,0:T(8,128)(2,1)}, bf16[2,4,32,1024]{3,2,1,0:T(8,128)(2,1)S(1)}, u32[]{:S(2)}, u32[]{:S(2)}) collective-permute-start(bf16[2,4,32,1024]{3,2,1,0:T(8,128)(2,1)} %pad_maximum_fusion.4), channel_id=1, source_target_pairs={{0,8},{4,12},{8,0},{12,4},{16,24},{20,28},{24,16},{28,20},{1,9},{5... | collective-permute-start | bytes 1572872 | tf_op jit(solution)/shard_map/ppermute | solution.py:483
  357.3 23.7 %collective-permute-start.46 = (f32[4,3072]{1,0:T(4,128)S(1)}, f32[4,3072]{1,0:T(4,128)S(1)}, u32[]{:S(2)}, u32[]{:S(2)}) collective-permute-start(f32[4,3072]{1,0:T(4,128)S(1)} %constant_dynamic-update-slice_fusion.12), channel_id=1, source_target_pairs={{0,4},{4,0},{8,12},{12,8},{16,20},{20,16},{24,28},{28,24},{1,5},{5... | collective-permute-start | bytes 147464 | tf_op jit(solution)/shard_map/ppermute | solution.py:483
  376.8 19.4 %collective-permute-start.51 = (bf16[4,4,32,768]{3,2,1,0:T(8,128)(2,1)S(1)}, bf16[4,4,32,768]{3,2,1,0:T(8,128)(2,1)S(1)}, u32[]{:S(2)}, u32[]{:S(2)}) collective-permute-start(bf16[4,4,32,768]{3,2,1,0:T(8,128)(2,1)S(1)} %slice_bitcast_fusion), channel_id=1, source_target_pairs={{0,4},{4,0},{8,12},{12,8},{16,20},{20,16},{24,28},{28,24},{1,5},{5... | collective-permute-start | bytes 2359304 | tf_op jit(solution)/shard_map/ppermute | solution.py:483
  401.9 25.7 %collective-permute-start.43 = (bf16[512,1024]{1,0:T(8,128)(2,1)}, bf16[512,1024]{1,0:T(8,128)(2,1)}, u32[]{:S(2)}, u32[]{:S(2)}) collective-permute-start(bf16[512,1024]{1,0:T(8,128)(2,1)} %copy-done.21), channel_id=1, source_target_pairs={{0,1},{1,2},{2,3},{3,0},{4,5},{5,6},{6,7},{7,4},{8,9},{9,10},{10,1... | collective-permute-start | bytes 3145736 | tf_op jit(solution)/shard_map/ppermute | solution.py:487
  420.6 11.0 %all-to-all-start.3 = ((bf16[4,32,768]{2,1,0:T(8,128)(2,1)}), bf16[4,32,768]{2,1,0:T(8,128)(2,1)S(1)}, u32[]{:S(2)}, u32[]{:S(2)}) async-start(bf16[4,32,768]{2,1,0:T(8,128)(2,1)} %fusion.6), calls=%async_computation.3 | async-start | bytes 393216 | tf_op jit(solution)/shard_map/all_to_all | solution.py:667
  430.2 107.9 %collective-permute-start.44 = (bf16[512,1024]{1,0:T(8,128)(2,1)}, bf16[512,1024]{1,0:T(8,128)(2,1)}, u32[]{:S(2)}, u32[]{:S(2)}) collective-permute-start(bf16[512,1024]{1,0:T(8,128)(2,1)} %add_convert_fusion.15), channel_id=1, source_target_pairs={{0,1},{1,2},{2,3},{3,0},{4,5},{5,6},{6,7},{7,4},{8,9},{9,10},{10,1... | collective-permute-start | bytes 3145736 | tf_op jit(solution)/shard_map/ppermute | solution.py:487
  432.1 12.3 %collective-permute-start.54 = (bf16[32,3072]{1,0:T(8,128)(2,1)S(1)}, bf16[32,3072]{1,0:T(8,128)(2,1)S(1)}, u32[]{:S(2)}, u32[]{:S(2)}) collective-permute-start(bf16[32,3072]{1,0:T(8,128)(2,1)S(1)} %reshape.340), channel_id=1, source_target_pairs={{0,4},{4,0},{8,12},{12,8},{16,20},{20,16},{24,28},{28,24},{1,5},{5... | collective-permute-start | bytes 589832 | tf_op jit(solution)/shard_map/ppermute | solution.py:483
  439.5 11.2 %collective-permute-start.57 = (bf16[32,3072]{1,0:T(8,128)(2,1)S(1)}, bf16[32,3072]{1,0:T(8,128)(2,1)S(1)}, u32[]{:S(2)}, u32[]{:S(2)}) collective-permute-start(bf16[32,3072]{1,0:T(8,128)(2,1)S(1)} %reshape.340), channel_id=1, source_target_pairs={{0,16},{4,20},{8,24},{12,28},{16,0},{20,4},{24,8},{28,12},{1,17},{... | collective-permute-start | bytes 589832 | tf_op jit(solution)/shard_map/ppermute | solution.py:483
  444.4 48.5 %collective-permute-start.75 = (bf16[2,4,128,1024]{3,2,1,0:T(8,128)(2,1)S(1)}, bf16[2,4,128,1024]{3,2,1,0:T(8,128)(2,1)S(1)}, u32[]{:S(2)}, u32[]{:S(2)}) collective-permute-start(bf16[2,4,128,1024]{3,2,1,0:T(8,128)(2,1)S(1)} %pad_maximum_fusion), channel_id=1, source_target_pairs={{0,16},{4,20},{8,24},{12,28},{16,0},{20,4},{24,8},{28,12},{1,17},{... | collective-permute-start | bytes 6291464 | tf_op jit(solution)/shard_map/ppermute | solution.py:483
  449.2 48.5 %collective-permute-start.88 = (bf16[2,4,128,1024]{3,2,1,0:T(8,128)(2,1)S(1)}, bf16[2,4,128,1024]{3,2,1,0:T(8,128)(2,1)S(1)}, u32[]{:S(2)}, u32[]{:S(2)}) collective-permute-start(bf16[2,4,128,1024]{3,2,1,0:T(8,128)(2,1)S(1)} %pad_maximum_fusion.1), channel_id=1, source_target_pairs={{0,8},{4,12},{8,0},{12,4},{16,24},{20,28},{24,16},{28,20},{1,9},{5... | collective-permute-start | bytes 6291464 | tf_op jit(solution)/shard_map/ppermute | solution.py:483
  450.8 46.0 %collective-permute-start.59 = (bf16[32,3072]{1,0:T(8,128)(2,1)S(1)}, bf16[32,3072]{1,0:T(8,128)(2,1)S(1)}, u32[]{:S(2)}, u32[]{:S(2)}) collective-permute-start(bf16[32,3072]{1,0:T(8,128)(2,1)S(1)} %collective-permute-done.55), channel_id=1, source_target_pairs={{0,16},{4,20},{8,24},{12,28},{16,0},{20,4},{24,8},{28,12},{1,17},{... | collective-permute-start | bytes 589832 | tf_op jit(solution)/shard_map/ppermute | solution.py:483
  451.3 49.0 %collective-permute-start.58 = (bf16[32,3072]{1,0:T(8,128)(2,1)S(1)}, bf16[32,3072]{1,0:T(8,128)(2,1)S(1)}, u32[]{:S(2)}, u32[]{:S(2)}) collective-permute-start(bf16[32,3072]{1,0:T(8,128)(2,1)S(1)} %collective-permute-done.57), channel_id=1, source_target_pairs={{0,4},{4,0},{8,12},{12,8},{16,20},{20,16},{24,28},{28,24},{1,5},{5... | collective-permute-start | bytes 589832 | tf_op jit(solution)/shard_map/ppermute | solution.py:483
  494.8 25.0 %collective-permute-start.76 = (bf16[1,4,128,1024]{3,2,1,0:T(8,128)(2,1)S(1)}, bf16[1,4,128,1024]{3,2,1,0:T(8,128)(2,1)S(1)}, u32[]{:S(2)}, u32[]{:S(2)}) collective-permute-start(bf16[1,4,128,1024]{3,2,1,0:T(8,128)(2,1)S(1)} %add_convert_fusion.9), channel_id=1, source_target_pairs={{0,8},{4,12},{8,0},{12,4},{16,24},{20,28},{24,16},{28,20},{1,9},{5... | collective-permute-start | bytes 3145736 | tf_op jit(solution)/shard_map/ppermute | solution.py:483
  496.7 52.8 %collective-permute-start.60 = (bf16[32,3072]{1,0:T(8,128)(2,1)S(1)}, bf16[32,3072]{1,0:T(8,128)(2,1)S(1)}, u32[]{:S(2)}, u32[]{:S(2)}) collective-permute-start(bf16[32,3072]{1,0:T(8,128)(2,1)S(1)} %collective-permute-done.59), channel_id=1, source_target_pairs={{0,4},{4,0},{8,12},{12,8},{16,20},{20,16},{24,28},{28,24},{1,5},{5... | collective-permute-start | bytes 589832 | tf_op jit(solution)/shard_map/ppermute | solution.py:483
  499.6 24.7 %collective-permute-start.89 = (bf16[1,4,128,1024]{3,2,1,0:T(8,128)(2,1)S(1)}, bf16[1,4,128,1024]{3,2,1,0:T(8,128)(2,1)S(1)}, u32[]{:S(2)}, u32[]{:S(2)}) collective-permute-start(bf16[1,4,128,1024]{3,2,1,0:T(8,128)(2,1)S(1)} %add_convert_fusion.4), channel_id=1, source_target_pairs={{0,16},{4,20},{8,24},{12,28},{16,0},{20,4},{24,8},{28,12},{1,17},{... | collective-permute-start | bytes 3145736 | tf_op jit(solution)/shard_map/ppermute | solution.py:483
  526.4 11.5 %collective-permute-start.90 = (bf16[128,1024]{1,0:T(8,128)(2,1)S(1)}, bf16[128,1024]{1,0:T(8,128)(2,1)S(1)}, u32[]{:S(2)}, u32[]{:S(2)}) collective-permute-start(bf16[128,1024]{1,0:T(8,128)(2,1)S(1)} %slice_bitcast_fusion.4), channel_id=1, source_target_pairs={{0,1},{1,2},{2,3},{3,0},{4,5},{5,6},{6,7},{7,4},{8,9},{9,10},{10,1... | collective-permute-start | bytes 786440 | tf_op jit(solution)/shard_map/ppermute | solution.py:487
  532.4 11.2 %collective-permute-start.78 = (bf16[128,1024]{1,0:T(8,128)(2,1)S(1)}, bf16[128,1024]{1,0:T(8,128)(2,1)S(1)}, u32[]{:S(2)}, u32[]{:S(2)}) collective-permute-start(bf16[128,1024]{1,0:T(8,128)(2,1)S(1)} %fusion.5), channel_id=1, source_target_pairs={{0,1},{1,2},{2,3},{3,0},{4,5},{5,6},{6,7},{7,4},{8,9},{9,10},{10,1... | collective-permute-start | bytes 786440 | tf_op jit(solution)/shard_map/ppermute | solution.py:487
  538.0 11.2 %collective-permute-start.91 = (bf16[128,1024]{1,0:T(8,128)(2,1)S(1)}, bf16[128,1024]{1,0:T(8,128)(2,1)S(1)}, u32[]{:S(2)}, u32[]{:S(2)}) collective-permute-start(bf16[128,1024]{1,0:T(8,128)(2,1)S(1)} %fusion.2), channel_id=1, source_target_pairs={{0,1},{1,2},{2,3},{3,0},{4,5},{5,6},{6,7},{7,4},{8,9},{9,10},{10,1... | collective-permute-start | bytes 786440 | tf_op jit(solution)/shard_map/ppermute | solution.py:487
  539.7 43.8 %collective-permute-start.45 = (bf16[512,1024]{1,0:T(8,128)(2,1)S(1)}, bf16[512,1024]{1,0:T(8,128)(2,1)S(1)}, u32[]{:S(2)}, u32[]{:S(2)}) collective-permute-start(bf16[512,1024]{1,0:T(8,128)(2,1)S(1)} %add_convert_fusion.14), channel_id=1, source_target_pairs={{0,1},{1,2},{2,3},{3,0},{4,5},{5,6},{6,7},{7,4},{8,9},{9,10},{10,1... | collective-permute-start | bytes 3145736 | tf_op jit(solution)/shard_map/ppermute | solution.py:487
  543.6 33.6 %collective-permute-start.79 = (bf16[128,1024]{1,0:T(8,128)(2,1)S(1)}, bf16[128,1024]{1,0:T(8,128)(2,1)S(1)}, u32[]{:S(2)}, u32[]{:S(2)}) collective-permute-start(bf16[128,1024]{1,0:T(8,128)(2,1)S(1)} %fusion.4), channel_id=1, source_target_pairs={{0,1},{1,2},{2,3},{3,0},{4,5},{5,6},{6,7},{7,4},{8,9},{9,10},{10,1... | collective-permute-start | bytes 786440 | tf_op jit(solution)/shard_map/ppermute | solution.py:487
  549.2 32.3 %collective-permute-start.92 = (bf16[128,1024]{1,0:T(8,128)(2,1)S(1)}, bf16[128,1024]{1,0:T(8,128)(2,1)S(1)}, u32[]{:S(2)}, u32[]{:S(2)}) collective-permute-start(bf16[128,1024]{1,0:T(8,128)(2,1)S(1)} %fusion.1), channel_id=1, source_target_pairs={{0,1},{1,2},{2,3},{3,0},{4,5},{5,6},{6,7},{7,4},{8,9},{9,10},{10,1... | collective-permute-start | bytes 786440 | tf_op jit(solution)/shard_map/ppermute | solution.py:487
  577.3 10.8 %collective-permute-start.80 = (bf16[128,1024]{1,0:T(8,128)(2,1)S(1)}, bf16[128,1024]{1,0:T(8,128)(2,1)S(1)}, u32[]{:S(2)}, u32[]{:S(2)}) collective-permute-start(bf16[128,1024]{1,0:T(8,128)(2,1)S(1)} %fusion.3.refs_0_), channel_id=1, source_target_pairs={{0,4},{4,0},{8,12},{12,8},{16,20},{20,16},{24,28},{28,24},{1,5},{5... | collective-permute-start | bytes 786440 | tf_op jit(solution)/shard_map/ppermute | solution.py:483
  577.4 11.3 %collective-permute-start.81 = (bf16[128,1024]{1,0:T(8,128)(2,1)S(1)}, bf16[128,1024]{1,0:T(8,128)(2,1)S(1)}, u32[]{:S(2)}, u32[]{:S(2)}) collective-permute-start(bf16[128,1024]{1,0:T(8,128)(2,1)S(1)} %fusion.3.refs_0_), channel_id=1, source_target_pairs={{0,8},{4,12},{8,0},{12,4},{16,24},{20,28},{24,16},{28,20},{1,9},{5... | collective-permute-start | bytes 786440 | tf_op jit(solution)/shard_map/ppermute | solution.py:483
  593.1 15.5 %collective-permute-start.93 = (bf16[128,1024]{1,0:T(8,128)(2,1)S(1)}, bf16[128,1024]{1,0:T(8,128)(2,1)S(1)}, u32[]{:S(2)}, u32[]{:S(2)}) collective-permute-start(bf16[128,1024]{1,0:T(8,128)(2,1)S(1)} %fusion.refs_0_), channel_id=1, source_target_pairs={{0,4},{4,0},{8,12},{12,8},{16,20},{20,16},{24,28},{28,24},{1,5},{5... | collective-permute-start | bytes 786440 | tf_op jit(solution)/shard_map/ppermute | solution.py:483
  593.2 15.4 %collective-permute-start.95 = (bf16[128,1024]{1,0:T(8,128)(2,1)S(1)}, bf16[128,1024]{1,0:T(8,128)(2,1)S(1)}, u32[]{:S(2)}, u32[]{:S(2)}) collective-permute-start(bf16[128,1024]{1,0:T(8,128)(2,1)S(1)} %collective-permute-done.94.refs_2_), channel_id=1, source_target_pairs={{0,4},{4,0},{8,12},{12,8},{16,20},{20,16},{24,28},{28,24},{1,5},{5... | collective-permute-start | bytes 786440 | tf_op jit(solution)/shard_map/ppermute | solution.py:483
  593.7 14.9 %collective-permute-start.97 = (bf16[128,1024]{1,0:T(8,128)(2,1)S(1)}, bf16[128,1024]{1,0:T(8,128)(2,1)S(1)}, u32[]{:S(2)}, u32[]{:S(2)}) collective-permute-start(bf16[128,1024]{1,0:T(8,128)(2,1)S(1)} %collective-permute-done.96.refs_4_), channel_id=1, source_target_pairs={{0,4},{4,0},{8,12},{12,8},{16,20},{20,16},{24,28},{28,24},{1,5},{5... | collective-permute-start | bytes 786440 | tf_op jit(solution)/shard_map/ppermute | solution.py:483
  (77 other events, 783.9 us)

commit v3 on v2

--- a/solution.py
+++ b/solution.py
@@ -13,10 +13,15 @@
 F32 = jnp.float32
 BF = jnp.bfloat16
 MIB = 2**20
+COST_UNIT = 10**8
 
 
 def rnd(v):
     return v.astype(BF)
+
+
+def cost(time):
+    return pl.CostEstimate(flops=int(time * COST_UNIT), bytes_accessed=1, transcendentals=0)
 
 
 def dot_last(left, right):
@@ -71,8 +76,10 @@
 
 
 def attend_grad_kernel(
-    group_len, head_dim, q_ref, k_ref, v_ref, low_ref, o_ref, lse_ref, do_ref, dq_ref, dk_ref, dv_ref, dk_sum, dv_sum
+    group_len, head_dim, q_ref, k_ref, v_ref, low_ref, o_ref, lse_ref, do_ref, *refs
 ):
+    dq_ref, dk_ref, dv_ref, bias_ref, dk_sum, dv_sum = refs[-6:]
+    bias = jnp.zeros((1, 128), F32)
     size = min(256, group_len // 8)
     scale = jnp.asarray(head_dim**-0.5, BF)
     keys_t = k_ref[...].astype(F32).T.astype(BF)
@@ -103,10 +110,15 @@
                 dk_sum[head, first:last, :] += dot_mm(ds, queries)
                 dq_t += dot_mm(keys_t[lanes, first:last], ds)
             results.append(dq_t * head_dim**-0.5)
-        dq_ref[start:stop, :] = jnp.concatenate(results, 0).T.astype(BF)
+        dq = jnp.concatenate(results, 0).T.astype(BF)
+        dq_ref[start:stop, :] = dq
+        bias += jnp.sum(dq.astype(F32), 0, keepdims=True)
     heads = range(128 // head_dim)
     dk_ref[...] = jnp.concatenate([dk_sum[head] for head in heads], 1).astype(BF)
-    dv_ref[...] = jnp.concatenate([dv_sum[head] for head in heads], 1).astype(BF)
+    dv = jnp.concatenate([dv_sum[head] for head in heads], 1).astype(BF)
+    dv_ref[...] = dv
+    bias_ref[0, 0:1, :] = bias
+    bias_ref[0, 1:2, :] = jnp.sum(dv.astype(F32), 0, keepdims=True)
 
 
 def attend(combined, low, head_dim):
@@ -124,11 +136,11 @@
             jax.ShapeDtypeStruct((steps, heads, group_len), F32),
         ],
         compiler_params=pltpu.CompilerParams(vmem_limit_bytes=56 * MIB),
-        cost_estimate=pl.CostEstimate(flops=15 * 10**9, bytes_accessed=4 * MIB, transcendentals=0),
+        cost_estimate=cost(18),
     )(combined, combined, combined, low)
 
 
-def attend_grad(combined, low, mixed, lse, grad_mixed, head_dim):
+def attend_grad(combined, low, mixed, lse, grad_mixed, head_dim, after=()):
     group_len, width = mixed.shape
     steps = width // 128
     heads = 128 // head_dim
@@ -144,13 +156,15 @@
             block(0),
             pl.BlockSpec((1, heads, group_len), lambda i: (i, 0, 0)),
             block(0),
-        ],
-        out_specs=[block(0)] * 3,
-        out_shape=[jax.ShapeDtypeStruct((group_len, width), BF)] * 3,
+        ]
+        + [pl.BlockSpec(memory_space=pl.ANY)] * len(after),
+        out_specs=[block(0)] * 3 + [pl.BlockSpec((1, 2, 128), lambda i: (i, 0, 0))],
+        out_shape=[jax.ShapeDtypeStruct((group_len, width), BF)] * 3
+        + [jax.ShapeDtypeStruct((steps, 2, 128), F32)],
         scratch_shapes=[pltpu.VMEM((heads, group_len, head_dim), F32)] * 2,
         compiler_params=pltpu.CompilerParams(vmem_limit_bytes=56 * MIB),
-        cost_estimate=pl.CostEstimate(flops=25 * 10**9, bytes_accessed=8 * MIB, transcendentals=0),
-    )(combined, combined, combined, low, mixed, lse, grad_mixed)
+        cost_estimate=cost(28),
+    )(combined, combined, combined, low, mixed, lse, grad_mixed, *after)
 
 
 class Cut:
@@ -160,7 +174,8 @@
         self.r, self.c = rows // self.nr, columns // self.nc
 
     def place(self, piece):
-        row = lax.rem(piece, self.nr) * self.r
+        half = self.nr // 2
+        row = (lax.rem(piece, 2) * half + lax.rem(lax.div(piece, 2), half)) * self.r
         column = lax.div(piece, self.nr) * self.c
         return pl.multiple_of(row, 8 if self.r % 16 else 16), pl.multiple_of(column, 128)
 
@@ -176,7 +191,7 @@
         return 1 + (self.shards - 1) * self.replicas
 
 
-def fetch(cut, me, z, slots, shard, whole, sems):
+def fetch(cut, me, z, slots, first_row, shard, whole, sems):
     base = pl.multiple_of(z * cut.rows, 16)
     copies = [pltpu.make_async_copy(shard, whole.at[pl.ds(base, cut.rows), :], sems.at[0])]
     for d in range(1, cut.shards):
@@ -184,7 +199,7 @@
         for j in range(cut.replicas):
             copies.append(
                 pltpu.make_async_copy(
-                    slots[j].at[d - 1],
+                    slots[j].at[d - 1, pl.ds(first_row, cut.r), :],
                     whole.at[cut.spot(jnp.bitwise_xor(me, j), base)],
                     sems.at[len(copies)],
                 )
@@ -192,6 +207,16 @@
     return copies
 
 
+def loads_of(cuts, place, lists, wholes, sems):
+    count = cuts[0].replicas
+    both, down, shards = lists[:count], lists[count : 2 * count], lists[2 * count :]
+    sources = ((both, 0), (both, cuts[0].r), (down, 0))
+    return [
+        fetch(cut, place[0], place[1], slots, row, shard, whole, sem)
+        for cut, (slots, row), shard, whole, sem in zip(cuts, sources, shards, wholes, sems)
+    ]
+
+
 def start(copies):
     for copy in copies:
         copy.start()
@@ -202,13 +227,10 @@
         copy.wait()
 
 
+MARK = jax.ShapeDtypeStruct((8, 128), F32)
 SMEM_SPEC = pl.BlockSpec(memory_space=pltpu.SMEM)
 ANY_SPEC = pl.BlockSpec(memory_space=pl.ANY)
 VMEM_SPEC = pl.BlockSpec(memory_space=pltpu.VMEM)
-
-
-def cost(flops, size):
-    return pl.CostEstimate(flops=int(flops), bytes_accessed=int(size), transcendentals=0)
 
 
 def moments(stream):
@@ -225,14 +247,15 @@
     )
 
 
-def project_kernel(place, block, gain, bias, weight, bias_qkv, h_in, c_in, h_out, c_out):
+def project_kernel(place, block, gain, bias, weight, bias_qkv, c_in, h_out, c_out, mark):
+    mark[...] = jnp.zeros_like(mark)
     normal, _ = moments(block[...].astype(F32))
     hidden = rnd(normal * gain[...] + bias[...])
     h_out[...] = hidden
     c_out[...] = rnd(dot_mm(hidden, weight[...]) + bias_qkv[...])
 
 
-def project(place, block, gain, bias, weight, bias_qkv, h_all, c_all, distance, shards):
+def project(place, block, gain, bias, weight, bias_qkv, c_all, distance, shards):
     rows, width = block.shape
     whole = lambda a: pl.BlockSpec(a.shape, lambda i, s: (0,) * a.ndim)
     at = lambda i, s: (lax.rem(s[1] + shards - distance, shards), 0)
@@ -241,14 +264,18 @@
         grid_spec=pltpu.PrefetchScalarGridSpec(
             num_scalar_prefetch=1,
             grid=(1,),
-            in_specs=[whole(a) for a in (block, gain, bias, weight, bias_qkv)] + [ANY_SPEC] * 2,
-            out_specs=[pl.BlockSpec((rows, width), at), pl.BlockSpec((rows, c_all.shape[1]), at)],
+            in_specs=[whole(a) for a in (block, gain, bias, weight, bias_qkv)] + [ANY_SPEC],
+            out_specs=[
+                pl.BlockSpec((rows, width), lambda i, s: (0, 0)),
+                pl.BlockSpec((rows, c_all.shape[1]), at),
+                pl.BlockSpec((8, 128), lambda i, s: (0, 0)),
+            ],
         ),
-        out_shape=[jax.ShapeDtypeStruct(a.shape, BF) for a in (h_all, c_all)],
-        input_output_aliases={6: 0, 7: 1},
+        out_shape=[jax.ShapeDtypeStruct(a.shape, BF) for a in (block, c_all)] + [MARK],
+        input_output_aliases={6: 1},
         compiler_params=pltpu.CompilerParams(vmem_limit_bytes=40 * MIB),
-        cost_estimate=cost(2 * rows * width * c_all.shape[1], 6 * MIB),
-    )(place, block, gain, bias, weight, bias_qkv, h_all, c_all)
+        cost_estimate=cost(2.5),
+    )(place, block, gain, bias, weight, bias_qkv, c_all)
 
 
 GELU_A = 0.7978845608028654
@@ -263,18 +290,21 @@
     return value, slope
 
 
-def forward_kernel(cuts, step, place, mixed, tokens, vectors, bias_up, *refs):
-    count = cuts[0].replicas
-    lists, refs = refs[: 3 * (count + 1)], refs[3 * (count + 1) :]
+def forward_kernel(cuts, step, place, tokens, vectors, bias_up, *refs):
+    shards = cuts[0].shards
+    mixed, refs = refs[:shards], refs[shards:]
+    count = 2 * cuts[0].replicas + 3
+    lists, refs = refs[:count], refs[count:]
     out, hidden, middle, acted, slope, w_out, w_up, w_down, *sems = refs
-    me, z = place[0], place[1]
-    loads = []
-    for n, (cut, whole) in enumerate(zip(cuts, (w_out, w_up, w_down))):
-        own = lists[n * (count + 1) : (n + 1) * (count + 1)]
-        loads.append(fetch(cut, me, z, own[:count], own[count], whole, sems[n]))
-        start(loads[-1])
+    loads = loads_of(cuts, place, lists, (w_out, w_up, w_down), sems)
+    for copies in loads:
+        start(copies)
     finish(loads[0])
-    stream = tokens[...].astype(F32) + (dot_mm(mixed[...], w_out[...]) + vectors[0:1, :])
+    stream = tokens[...].astype(F32) + vectors[0:1, :]
+    local = mixed[0].shape[1]
+    for d in range(shards):
+        at = pl.multiple_of(lax.rem(place[1] + shards - d, shards) * local, 16)
+        stream += dot_mm(mixed[d][...], w_out[pl.ds(at, local), :])
     middle[...] = stream
     normal, _ = moments(stream)
     hidden[...] = rnd(normal * vectors[1:2, :] + vectors[2:3, :])
@@ -295,10 +325,9 @@
 def feed_forward(place, mixed, tokens, vectors, bias_up, cuts, lists):
     rows, width = tokens.shape
     hidden = bias_up.shape[1]
-    flat = [a for own in lists for a in own]
     return pl.pallas_call(
         functools.partial(forward_kernel, cuts, min(1024, hidden)),
-        in_specs=[SMEM_SPEC] + [VMEM_SPEC] * 4 + [ANY_SPEC] * len(flat),
+        in_specs=[SMEM_SPEC] + [VMEM_SPEC] * (3 + len(mixed)) + [ANY_SPEC] * len(lists),
         out_specs=[VMEM_SPEC] * 5,
         out_shape=[
             jax.ShapeDtypeStruct((rows, width), BF),
@@ -314,20 +343,17 @@
         ]
         + [pltpu.SemaphoreType.DMA((cut.copies,)) for cut in cuts],
         compiler_params=pltpu.CompilerParams(vmem_limit_bytes=60 * MIB),
-        cost_estimate=cost(2 * rows * width * (width + 2 * hidden), 34 * MIB),
-    )(place, mixed, tokens, vectors, bias_up, *flat)
+        cost_estimate=cost(24),
+    )(place, tokens, vectors, bias_up, *mixed, *lists)
 
 
 def backward_kernel(cuts, step, place, dm, slope, middle, vectors, *refs):
-    count = cuts[0].replicas
-    lists, refs = refs[: 3 * (count + 1)], refs[3 * (count + 1) :]
+    count = 2 * cuts[0].replicas + 3
+    lists, refs = refs[:count], refs[count:]
     du, dx2, da, do, grad_up, sums, w_out, w_up, w_down, *sems = refs
-    me, z = place[0], place[1]
-    loads = []
-    for n, whole in ((2, w_down), (1, w_up), (0, w_out)):
-        own = lists[n * (count + 1) : (n + 1) * (count + 1)]
-        loads.append(fetch(cuts[n], me, z, own[:count], own[count], whole, sems[n]))
-        start(loads[-1])
+    loads = loads_of(cuts, place, lists, (w_out, w_up, w_down), sems)[::-1]
+    for copies in loads:
+        start(copies)
     finish(loads[0])
     finish(loads[1])
     dh2 = jnp.zeros(middle.shape, F32)
@@ -355,10 +381,9 @@
 def feed_backward(place, dm, slope, middle, vectors, cuts, lists):
     rows, width = dm.shape
     hidden = slope.shape[1]
-    flat = [a for own in lists for a in own]
     return pl.pallas_call(
         functools.partial(backward_kernel, cuts, min(1024, hidden)),
-        in_specs=[SMEM_SPEC] + [VMEM_SPEC] * 4 + [ANY_SPEC] * len(flat),
+        in_specs=[SMEM_SPEC] + [VMEM_SPEC] * 4 + [ANY_SPEC] * len(lists),
         out_specs=[VMEM_SPEC] * 6,
         out_shape=[
             jax.ShapeDtypeStruct((rows, hidden), BF),
@@ -375,11 +400,13 @@
         ]
         + [pltpu.SemaphoreType.DMA((cut.copies,)) for cut in cuts],
         compiler_params=pltpu.CompilerParams(vmem_limit_bytes=60 * MIB),
-        cost_estimate=cost(2 * rows * width * (width + 2 * hidden), 34 * MIB),
-    )(place, dm, slope, middle, vectors, *flat)
-
-
-def weight_grad_kernel(cut, place, left, right, keep, send, whole):
+        cost_estimate=cost(24),
+    )(place, dm, slope, middle, vectors, *lists)
+
+
+def weight_grad_kernel(cut, place, left, right, *refs):
+    keep, send, mark, whole = refs[-4:]
+    mark[...] = jnp.zeros_like(mark)
     whole[...] = lax.dot_general(
         left[...], right[...], (((0,), (0,)), ((), ())), preferred_element_type=F32
     )
@@ -388,7 +415,7 @@
         (keep, send)[j & 1][j >> 1, 0] = rnd(value)
 
 
-def weight_grad(cut, place, left, right):
+def weight_grad(cut, place, left, right, after=()):
     tokens, shards = left.shape[0], cut.shards
     shape = (cut.replicas // 2, shards, cut.r, cut.c)
     piece = pl.BlockSpec((cut.replicas // 2, 1, cut.r, cut.c), lambda d, s: (0, d, 0, 0))
@@ -400,36 +427,268 @@
             in_specs=[
                 pl.BlockSpec((tokens, cut.rows), lambda d, s: (0, lax.rem(s[1] + shards - d, shards))),
                 pl.BlockSpec(right.shape, lambda d, s: (0, 0)),
-            ],
-            out_specs=[piece] * 2,
+            ]
+            + [ANY_SPEC] * len(after),
+            out_specs=[piece] * 2 + [pl.BlockSpec((8, 128), lambda d, s: (0, 0))],
             scratch_shapes=[pltpu.VMEM((cut.rows, cut.columns), F32)],
         ),
-        out_shape=[jax.ShapeDtypeStruct(shape, BF)] * 2,
+        out_shape=[jax.ShapeDtypeStruct(shape, BF)] * 2 + [MARK],
         compiler_params=pltpu.CompilerParams(vmem_limit_bytes=56 * MIB),
-        cost_estimate=cost(
-            2 * tokens * shards * cut.rows * cut.columns, 2 * shards * cut.rows * cut.columns
+        cost_estimate=cost(10),
+    )(place, left, right, *after)
+
+
+def gather_rows(cut, place, other, lefts, rows):
+    size = cut.rows // 2
+    half = lax.rem(place[0] + other, 2) * size
+    for d in range(cut.shards):
+        if len(lefts) > 1:
+            part = lefts[d][:, pl.ds(pl.multiple_of(half, 128), size)]
+        else:
+            column = lax.rem(place[1] + cut.shards - d, cut.shards) * cut.rows + half
+            part = lefts[0][:, pl.ds(pl.multiple_of(column, 128), size)]
+        rows[:, d * size : (d + 1) * size] = part
+
+
+def wide_kernel(cut, other, reverse, count, place, right, *refs):
+    lefts, refs = refs[:count], refs[count:]
+    rows, turned, whole = refs[-3:]
+    refs = refs[:-1]
+    refs[-3][...] = jnp.zeros_like(refs[-3])
+    step = pl.program_id(0)
+
+    @pl.when(step == 0)
+    def _():
+        gather_rows(cut, place, other, lefts, rows)
+        turned[...] = rows[...].astype(F32).T.astype(BF)
+
+    whole[...] = dot_mm(turned[...], right[...])
+    half, size = cut.nr // 2, cut.rows // 2
+    chip = lax.rem(lax.div(place[0], 2), half)
+
+    def part(n, d):
+        row = jnp.bitwise_xor(chip, n) * cut.r + d * size
+        return whole[pl.ds(pl.multiple_of(row, 16), cut.r), :]
+
+    for d in range(cut.shards):
+        for n in range(half):
+            if other:
+                refs[-4][n, d] = rnd(part(n, d))
+                continue
+            got, (stay, go) = refs[0], refs[-5:-3]
+            value = rnd(part(n, d) + got[n, d].astype(F32))
+            if cut.nc == 1:
+                leaves, m = (n >= half // 2, n % (half // 2)) if reverse else (n % 2 == 1, n // 2)
+                (go if leaves else stay)[m, d] = value
+            else:
+
+                @pl.when(step < cut.nc // 2)
+                def _():
+                    stay[n, d] = value
+
+                @pl.when(step >= cut.nc // 2)
+                def _():
+                    go[n, d] = value
+
+
+def wide_grad(cut, place, left, right, other, got, reverse, after):
+    lefts = left if isinstance(left, list) else [left]
+    tokens, half, count = right.shape[0], cut.nr // 2, cut.nc // 2
+    block = (half, cut.shards, cut.r, cut.c)
+    here = lambda i, s: (i, 0, 0, 0)
+    if other:
+        specs, sizes = [pl.BlockSpec(block, here)], [cut.replicas // 2]
+    elif cut.nc == 1:
+        specs, sizes = [pl.BlockSpec((half // 2,) + block[1:], here)] * 2, [cut.replicas // 4] * 2
+    else:
+        specs = [
+            pl.BlockSpec(block, lambda i, s: (jnp.minimum(i, count - 1), 0, 0, 0)),
+            pl.BlockSpec(block, lambda i, s: (jnp.maximum(i - count, 0), 0, 0, 0)),
+        ]
+        sizes = [cut.replicas // 4] * 2
+    return pl.pallas_call(
+        functools.partial(wide_kernel, cut, other, reverse, len(lefts)),
+        grid_spec=pltpu.PrefetchScalarGridSpec(
+            num_scalar_prefetch=1,
+            grid=(cut.nc,),
+            in_specs=[
+                pl.BlockSpec(
+                    (tokens, cut.c), lambda i, s: (0, jnp.bitwise_xor(lax.div(s[0], 2 * half), i))
+                ),
+            ]
+            + [pl.BlockSpec(a.shape, lambda i, s: (0, 0)) for a in lefts]
+            + [pl.BlockSpec(block, here)] * len(got)
+            + [ANY_SPEC] * len(after),
+            out_specs=specs + [pl.BlockSpec((8, 128), lambda i, s: (0, 0))],
+            scratch_shapes=[
+                pltpu.VMEM((tokens, cut.shards * cut.rows // 2), BF),
+                pltpu.VMEM((cut.shards * cut.rows // 2, tokens), BF),
+                pltpu.VMEM((cut.shards * cut.rows // 2, cut.c), F32),
+            ],
         ),
-    )(place, left, right)
-
-
-def widen_kernel(cut, place, *refs):
-    out = refs[-1]
-    for j in range(cut.replicas):
-        out[cut.spot(jnp.bitwise_xor(place[0], j))] = refs[j][...].astype(F32)
-
-
-def widen(cut, place, slots):
-    return pl.pallas_call(
-        functools.partial(widen_kernel, cut),
-        in_specs=[SMEM_SPEC] + [VMEM_SPEC] * cut.replicas,
-        out_specs=VMEM_SPEC,
-        out_shape=jax.ShapeDtypeStruct((cut.rows, cut.columns), F32),
+        out_shape=[jax.ShapeDtypeStruct((n, cut.shards, cut.r, cut.c), BF) for n in sizes] + [MARK],
+        compiler_params=pltpu.CompilerParams(vmem_limit_bytes=56 * MIB),
+        cost_estimate=cost(6),
+    )(place, right, *lefts, *got, *after)
+
+
+def half_spots(cut, me):
+    half = cut.nr // 2
+    for m in range(cut.replicas // 2):
+        chip = jnp.bitwise_xor(lax.div(me, 2), m)
+        row = pl.multiple_of(lax.rem(chip, half) * cut.r, 8 if cut.r % 16 else 16)
+        column = pl.multiple_of(lax.div(chip, half) * cut.c, 128)
+        yield m, (pl.ds(row, cut.r), pl.ds(column, cut.c))
+
+
+def send_grad_kernel(cut, place, left, right, *refs):
+    send, mark, whole = refs[-3:]
+    mark[...] = jnp.zeros_like(mark)
+    whole[...] = lax.dot_general(
+        left[...], right[...], (((0,), (0,)), ((), ())), preferred_element_type=F32
+    )
+    for m, spot in half_spots(cut, place[0]):
+        send[m, 0] = rnd(whole[spot])
+
+
+def keep_grad_kernel(cut, reverse, place, left, right, got, *refs):
+    stay, go, mark, whole = refs[-4:]
+    mark[...] = jnp.zeros_like(mark)
+    whole[...] = lax.dot_general(
+        left[...], right[...], (((0,), (0,)), ((), ())), preferred_element_type=F32
+    )
+    count = cut.replicas // 4
+    for m, spot in half_spots(cut, place[0]):
+        leaves, n = (m >= count, m % count) if reverse else (m % 2 == 1, m // 2)
+        (go if leaves else stay)[n, 0] = rnd(whole[spot] + got[m, 0].astype(F32))
+
+
+def half_grad(kernel, cut, place, left, right, other, slots, results, after):
+    tokens, shards = left.shape[0], cut.shards
+    pick = lambda d, s: (
+        0,
+        lax.rem(s[1] + shards - d, shards) * 2 + lax.rem(s[0] + other, 2),
+    )
+    piece = lambda count: pl.BlockSpec((count, 1, cut.r, cut.c), lambda d, s: (0, d, 0, 0))
+    return pl.pallas_call(
+        kernel,
+        grid_spec=pltpu.PrefetchScalarGridSpec(
+            num_scalar_prefetch=1,
+            grid=(shards,),
+            in_specs=[
+                pl.BlockSpec((tokens, cut.rows // 2), pick),
+                pl.BlockSpec(right.shape, lambda d, s: (0, 0)),
+            ]
+            + [piece(a.shape[0]) for a in slots]
+            + [ANY_SPEC] * len(after),
+            out_specs=[piece(n) for n in results] + [pl.BlockSpec((8, 128), lambda d, s: (0, 0))],
+            scratch_shapes=[pltpu.VMEM((cut.rows // 2, cut.columns), F32)],
+        ),
+        out_shape=[jax.ShapeDtypeStruct((n, shards, cut.r, cut.c), BF) for n in results] + [MARK],
+        compiler_params=pltpu.CompilerParams(vmem_limit_bytes=56 * MIB),
+        cost_estimate=cost(7.5),
+    )(place, left, right, *slots, *after)
+
+
+def send_grad(cut, place, left, right, after=()):
+    if cut.rows <= 256:
+        return wide_grad(cut, place, left, right, 1, (), False, after)
+    kernel = functools.partial(send_grad_kernel, cut)
+    return half_grad(kernel, cut, place, left, right, 1, (), (cut.replicas // 2,), after)
+
+
+def keep_grad(cut, place, left, right, got, reverse, after=()):
+    if cut.rows <= 256:
+        return wide_grad(cut, place, left, right, 0, (got,), reverse, after)
+    kernel = functools.partial(keep_grad_kernel, cut, reverse)
+    return half_grad(kernel, cut, place, left, right, 0, (got,), (cut.replicas // 4,) * 2, after)
+
+
+def qkv_grad_kernel(slim, replicas, shards, place, dq, dk, dv, small, *refs):
+    keep, send, mark, whole = refs[-4:]
+    blocks = refs[:shards]
+    rows = blocks[0].shape[0]
+    mark[...] = jnp.zeros_like(mark)
+    local = dq.shape[1]
+    for n, right in enumerate((dq, dk, dv)):
+        total = jnp.zeros((whole.shape[0], local), F32)
+        for d in range(shards):
+            at = pl.ds(pl.multiple_of(lax.rem(place[1] + shards - d, shards) * rows, 16), rows)
+            total += lax.dot_general(
+                blocks[d][...], right[at, :], (((0,), (0,)), ((), ())), preferred_element_type=F32
+            )
+        whole[:, n * local : (n + 1) * local] = total
+    first = lax.broadcasted_iota(jnp.int32, (16, 3 * local), 0) == 0
+    for j in range(replicas):
+        piece = jnp.bitwise_xor(place[0], j)
+        out = (keep, send)[j & 1]
+        out[j >> 1, 0, 0:slim] = rnd(whole[pl.ds(pl.multiple_of(piece * slim, 8), slim), :])
+        out[j >> 1, 0, slim:] = rnd(jnp.where(first, small[0, pl.ds(piece, 1), :], 0.0))
+
+
+def qkv_grad(place, hiddens, dq, dk, dv, small, slim, shards, after):
+    replicas, (tokens, local) = small.shape[1], dq.shape
+    rows, width = slim * replicas, 3 * local
+    here = pl.BlockSpec((tokens, local), lambda f, s: (0, 0))
+    piece = pl.BlockSpec((replicas // 2, 1, slim + 16, width), lambda f, s: (0, f, 0, 0))
+    return pl.pallas_call(
+        functools.partial(qkv_grad_kernel, slim, replicas, shards),
+        grid_spec=pltpu.PrefetchScalarGridSpec(
+            num_scalar_prefetch=1,
+            grid=(shards,),
+            in_specs=[here, here, here]
+            + [pl.BlockSpec((1, replicas, width), lambda f, s: (f, 0, 0))]
+            + [pl.BlockSpec((tokens // shards, rows), lambda f, s: (0, f))] * shards
+            + [ANY_SPEC] * len(after),
+            out_specs=[piece] * 2 + [pl.BlockSpec((8, 128), lambda f, s: (0, 0))],
+            scratch_shapes=[pltpu.VMEM((rows, width), F32)],
+        ),
+        out_shape=[jax.ShapeDtypeStruct((replicas // 2, shards, slim + 16, width), BF)] * 2 + [MARK],
         compiler_params=pltpu.CompilerParams(vmem_limit_bytes=48 * MIB),
-        cost_estimate=cost(0, 6 * cut.rows * cut.columns),
-    )(place, *slots)
-
-
-def hidden_grad_kernel(place, block, dq, dk, dv, weight, out, sums):
+        cost_estimate=cost(6.5),
+    )(place, dq, dk, dv, small, *hiddens, *after)
+
+
+def widen_kernel(cuts, qkv_rows, place, own_a, other_a, own_b, other_b, w_out, w_up, w_down, w_qkv, small):
+    cut_out, cut_up, cut_down = cuts
+    width = own_a.shape[2]
+    for j in range(cut_out.replicas):
+        piece = jnp.bitwise_xor(place[0], j)
+        left, right, m = (own_a, own_b, j >> 1) if j % 2 == 0 else (other_a, other_b, j >> 1)
+        row = cut_out.r
+        w_out[cut_out.spot(piece)] = left[m, 0:row].astype(F32)
+        w_up[cut_up.spot(piece)] = left[m, row : row + cut_up.r].astype(F32)
+        row += cut_up.r
+        spot = pl.ds(pl.multiple_of(piece * 8, 8), 8)
+        small[spot, :] = left[m, row : row + 8].astype(F32)
+        row = cut_down.r
+        w_down[cut_down.spot(piece)] = right[m, 0:row].astype(F32)
+        spot = pl.ds(pl.multiple_of(piece * qkv_rows, 8), qkv_rows)
+        shards, local = cut_out.shards, width // cut_out.shards
+        for k in range(3):
+            for d in range(shards):
+                column = k * width + lax.rem(place[1] + shards - d, shards) * local
+                part = right[m, row : row + qkv_rows, d * local : (d + 1) * local].astype(F32)
+                w_qkv[spot, pl.ds(pl.multiple_of(column, 128), local)] = part
+            row += qkv_rows
+
+
+def widen(cuts, qkv_rows, place, own_a, other_a, own_b, other_b):
+    width = own_a.shape[2]
+    shapes = [(cut.rows, cut.columns) for cut in cuts]
+    shapes += [(qkv_rows * cuts[0].replicas, 3 * width), (8 * cuts[0].replicas, width)]
+    return pl.pallas_call(
+        functools.partial(widen_kernel, cuts, qkv_rows),
+        in_specs=[SMEM_SPEC] + [VMEM_SPEC] * 4,
+        out_specs=[VMEM_SPEC] * 5,
+        out_shape=[jax.ShapeDtypeStruct(shape, F32) for shape in shapes],
+        compiler_params=pltpu.CompilerParams(vmem_limit_bytes=48 * MIB),
+        cost_estimate=cost(7),
+    )(place, own_a, other_a, own_b, other_b)
+
+
+def hidden_grad_kernel(place, block, dq, dk, dv, weight, *refs):
+    out, sums = refs[-2:]
     local = dq.shape[1]
     grad = dot_last(dq[...], weight[:, 0:local])
     grad += dot_last(dk[...], weight[:, local : 2 * local])
@@ -441,7 +700,7 @@
     sums[2:8, :] = jnp.zeros((6, sums.shape[1]), F32)
 
 
-def hidden_grad(place, block, dq, dk, dv, weight, distance, shards):
+def hidden_grad(place, block, dq, dk, dv, weight, distance, shards, after=()):
     rows, width = block.shape
     local = dq.shape[1]
     at = lambda i, s: (lax.rem(s[1] + shards - distance, shards), 0)
@@ -453,16 +712,18 @@
             grid=(1,),
             in_specs=[pl.BlockSpec((rows, width), here)]
             + [pl.BlockSpec((rows, local), at)] * 3
-            + [pl.BlockSpec(weight.shape, here)],
+            + [pl.BlockSpec(weight.shape, here)]
+            + [ANY_SPEC] * len(after),
             out_specs=[pl.BlockSpec((rows, width), here), pl.BlockSpec((8, width), here)],
         ),
         out_shape=[jax.ShapeDtypeStruct((rows, width), BF), jax.ShapeDtypeStruct((8, width), F32)],
         compiler_params=pltpu.CompilerParams(vmem_limit_bytes=40 * MIB),
-        cost_estimate=cost(6 * rows * width * local, 5 * MIB),
-    )(place, block, dq, dk, dv, weight)
-
-
-def last_kernel(tokens, travel, own, dx2, gain, out):
+        cost_estimate=cost(3),
+    )(place, block, dq, dk, dv, weight, *after)
+
+
+def last_kernel(tokens, travel, own, dx2, gain, out, mark):
+    mark[...] = jnp.zeros_like(mark)
     normal, scale = moments(tokens[...].astype(F32))
     grad = travel[...].astype(F32) + own[...].astype(F32)
     out[...] = rnd(dx2[...] + norm_grad(grad, gain[...], normal, scale))
@@ -472,15 +733,24 @@
     return pl.pallas_call(
         last_kernel,
         in_specs=[VMEM_SPEC] * 5,
-        out_specs=VMEM_SPEC,
-        out_shape=jax.ShapeDtypeStruct(tokens.shape, BF),
+        out_specs=[VMEM_SPEC] * 2,
+        out_shape=[jax.ShapeDtypeStruct(tokens.shape, BF), MARK],
         compiler_params=pltpu.CompilerParams(vmem_limit_bytes=40 * MIB),
-        cost_estimate=cost(0, 6 * MIB),
+        cost_estimate=cost(2.5),
     )(tokens, travel, own, dx2, gain)
 
 
 def swap(value, bit, replicas):
     return lax.ppermute(value, "dp", [(i, i ^ bit) for i in range(replicas)])
+
+
+def around(value, shards):
+    blocks = {0: value}
+    for d in range(1, shards // 2 + 1):
+        blocks[d] = turn(blocks[d - 1], shards)
+        if shards - d not in blocks:
+            blocks[shards - d] = turn(blocks[(shards - d + 1) % shards], shards, shards - 1)
+    return blocks
 
 
 def turn(value, shards, step=1):
@@ -492,44 +762,216 @@
     return bits[::-1] if reverse else bits
 
 
-def share(piece, replicas, reverse=False):
+def share_chips(piece, replicas, reverse=False, pause=lambda part: part):
     parts = {0: piece}
-    for bit in chip_bits(replicas, reverse):
-        parts |= {m | bit: swap(part, bit, replicas) for m, part in list(parts.items())}
-    parts |= {m | 1: swap(part, 1, replicas) for m, part in list(parts.items())}
-    return [parts[j] for j in range(replicas)]
+    for n, bit in enumerate(chip_bits(replicas, reverse)):
+        more = {m | bit: swap(part, bit, replicas) for m, part in parts.items()}
+        parts |= {m: part if n else pause(part) for m, part in more.items()}
+    return [parts[2 * m] for m in range(replicas // 2)]
+
+
+def share(piece, replicas, reverse=False, pause=lambda part: part):
+    slots = []
+    for part in share_chips(piece, replicas, reverse, pause):
+        slots += [part, swap(part, 1, replicas)]
+    return slots
+
+
+def idle_kernel(*refs):
+    pass
+
+
+def gate(value, *after):
+    return pl.pallas_call(
+        idle_kernel,
+        in_specs=[ANY_SPEC] * (1 + len(after)),
+        out_specs=ANY_SPEC,
+        out_shape=jax.ShapeDtypeStruct(value.shape, value.dtype),
+        input_output_aliases={0: 0},
+        cost_estimate=cost(0),
+    )(value, *after)
 
 
 def add_low(left, right):
     return rnd(left.astype(F32) + right.astype(F32))
 
 
-def plane_scatter(keep, send, replicas, reverse=False):
-    got = swap(send, 1, replicas)
-    parts = {2 * m: add_low(keep[m], got[m]) for m in range(replicas // 2)}
-    for bit in chip_bits(replicas, reverse):
-        there = [m for m in parts if m & bit]
-        moved = swap(jnp.stack([parts[m] for m in there]), bit, replicas)
-        parts = {m ^ bit: add_low(parts[m ^ bit], moved[n]) for n, m in enumerate(there)}
-    return parts[0]
-
-
-def ring_sum(parts, shards):
-    total = parts[1]
-    for d in range(2, shards + 1):
-        total = add_low(turn(total, shards), parts[d % shards])
-    return total
-
-
-def gather_weight(cut, place, shard, reverse=False):
-    piece = cut.of(shard, place[0])
-    slots = jnp.stack([turn(piece, cut.shards, d) for d in range(1, cut.shards)])
-    return share(slots, cut.replicas, reverse) + [shard]
-
-
-def reduce_weight(cut, place, keep, send, reverse=False):
-    total = ring_sum(plane_scatter(keep, send, cut.replicas, reverse), cut.shards)
-    return widen(cut, place, share(total, cut.replicas, reverse))
+def fold_kernel(left_stay, right_stay, left_go, right_go, *refs):
+    stay, go, mark = refs[-3:]
+    stay[...] = add_low(left_stay[...], right_stay[...])
+    go[...] = add_low(left_go[...], right_go[...])
+    mark[...] = jnp.zeros_like(mark)
+
+
+def fold(left, right, reverse, after=()):
+    n, shards, r, c = left.shape
+    deep = shards if r * c < 2**16 else 1
+    stay = lambda i, d: (i if reverse else 2 * i, d, 0, 0)
+    go = lambda i, d: (i + n // 2 if reverse else 2 * i + 1, d, 0, 0)
+    block = (1, deep, r, c)
+    return pl.pallas_call(
+        fold_kernel,
+        grid=(n // 2, shards // deep),
+        in_specs=[pl.BlockSpec(block, stay)] * 2 + [pl.BlockSpec(block, go)] * 2 + [ANY_SPEC] * len(after),
+        out_specs=[pl.BlockSpec(block, lambda i, d: (i, d, 0, 0))] * 2
+        + [pl.BlockSpec((8, 128), lambda i, d: (0, 0))],
+        out_shape=[jax.ShapeDtypeStruct((n // 2, shards, r, c), BF)] * 2 + [MARK],
+        compiler_params=pltpu.CompilerParams(vmem_limit_bytes=32 * MIB),
+        cost_estimate=cost(3),
+    )(left, right, left, right, *after)
+
+
+def close_kernel(counts, *refs):
+    total, first, mark = refs[-3:]
+    mark[...] = jnp.zeros_like(mark)
+    row = n = 0
+    for count in counts:
+        value = refs[n][0, 0].astype(F32)
+        for m in range(1, count):
+            value += refs[n + m][0, 0].astype(F32)
+        value = rnd(value)
+        n += count
+        rows = pl.ds(row, value.shape[0])
+        total[0, rows, :] = value
+
+        @pl.when(pl.program_id(0) == min(1, pl.num_programs(0) - 1))
+        def _():
+            first[rows, :] = value
+
+        row += value.shape[0]
+
+
+def close(groups, after=()):
+    _, shards, _, c = groups[0][0].shape
+    height = sum(group[0].shape[2] for group in groups)
+    flat = [a for group in groups for a in group]
+    return pl.pallas_call(
+        functools.partial(close_kernel, [len(group) for group in groups]),
+        grid=(shards,),
+        in_specs=[pl.BlockSpec((1, 1) + a.shape[2:], lambda d: (0, d, 0, 0)) for a in flat]
+        + [ANY_SPEC] * len(after),
+        out_specs=[
+            pl.BlockSpec((1, height, c), lambda d: (d, 0, 0)),
+            pl.BlockSpec((height, c), lambda d: (0, 0)),
+            pl.BlockSpec((8, 128), lambda d: (0, 0)),
+        ],
+        out_shape=[
+            jax.ShapeDtypeStruct((shards, height, c), BF),
+            jax.ShapeDtypeStruct((height, c), BF),
+            MARK,
+        ],
+        compiler_params=pltpu.CompilerParams(vmem_limit_bytes=32 * MIB),
+        cost_estimate=cost(3),
+    )(*flat, *after)
+
+
+def close_parts_kernel(count, *refs):
+    value = refs[0][...].astype(F32)
+    for m in range(1, count):
+        value += refs[m][...].astype(F32)
+    refs[-2][...] = rnd(value)
+    refs[-1][...] = jnp.zeros_like(refs[-1])
+
+
+def close_parts(parts, after=()):
+    return pl.pallas_call(
+        functools.partial(close_parts_kernel, len(parts)),
+        in_specs=[VMEM_SPEC] * len(parts) + [ANY_SPEC] * len(after),
+        out_specs=[VMEM_SPEC] * 2,
+        out_shape=[jax.ShapeDtypeStruct(parts[0].shape, BF), MARK],
+        compiler_params=pltpu.CompilerParams(vmem_limit_bytes=32 * MIB),
+        cost_estimate=cost(1),
+    )(*parts, *after)
+
+
+def join_kernel(travel, part, *refs):
+    total, mark = refs[-2:]
+    total[...] = add_low(travel[...], part[0])
+    mark[...] = jnp.zeros_like(mark)
+
+
+def join(travel, parts, d, after=()):
+    r, c = travel.shape
+    return pl.pallas_call(
+        join_kernel,
+        grid=(1,),
+        in_specs=[
+            pl.BlockSpec((r, c), lambda i: (0, 0)),
+            pl.BlockSpec((1, r, c), lambda i: (d, 0, 0)),
+        ]
+        + [ANY_SPEC] * len(after),
+        out_specs=[pl.BlockSpec((r, c), lambda i: (0, 0)), pl.BlockSpec((8, 128), lambda i: (0, 0))],
+        out_shape=[jax.ShapeDtypeStruct((r, c), BF), MARK],
+        compiler_params=pltpu.CompilerParams(vmem_limit_bytes=32 * MIB),
+        cost_estimate=cost(1),
+    )(travel, parts, *after)
+
+
+def direct(parts, replicas):
+    return [part if m == 0 else swap(part, 2 * m, replicas) for m, part in enumerate(parts)]
+
+
+def spread_kernel(left, right, *refs):
+    count = left.shape[0]
+    for m in range(count):
+        refs[-1 - count + m][...] = add_low(left[m], right[m])
+    refs[-1][...] = jnp.zeros_like(refs[-1])
+
+
+def spread(left, right, after=()):
+    n, shards, r, c = left.shape
+    block = pl.BlockSpec((n, 1, r, c), lambda d: (0, d, 0, 0))
+    part = pl.BlockSpec((1, r, c), lambda d: (d, 0, 0))
+    return pl.pallas_call(
+        spread_kernel,
+        grid=(shards,),
+        in_specs=[block] * 2 + [ANY_SPEC] * len(after),
+        out_specs=[part] * n + [pl.BlockSpec((8, 128), lambda d: (0, 0))],
+        out_shape=[jax.ShapeDtypeStruct((shards, r, c), BF)] * n + [MARK],
+        compiler_params=pltpu.CompilerParams(vmem_limit_bytes=32 * MIB),
+        cost_estimate=cost(3),
+    )(left, right, *after)
+
+
+def gather_sum_kernel(count, place, *refs):
+    value = refs[0][...].astype(F32)
+    for m in range(1, count):
+        value += refs[m][...].astype(F32)
+    refs[-2][...] = rnd(value)
+    refs[-1][...] = jnp.zeros_like(refs[-1])
+
+
+def gather_sum(place, parts, after=()):
+    shards, r, c = parts[0].shape
+    return pl.pallas_call(
+        functools.partial(gather_sum_kernel, len(parts)),
+        grid_spec=pltpu.PrefetchScalarGridSpec(
+            num_scalar_prefetch=1,
+            grid=(shards,),
+            in_specs=[pl.BlockSpec((1, r, c), lambda d, s: (lax.rem(s[1] + d, shards), 0, 0))] * len(parts)
+            + [ANY_SPEC] * len(after),
+            out_specs=[
+                pl.BlockSpec((1, r, c), lambda d, s: (d, 0, 0)),
+                pl.BlockSpec((8, 128), lambda d, s: (0, 0)),
+            ],
+        ),
+        out_shape=[jax.ShapeDtypeStruct((shards, r, c), BF), MARK],
+        compiler_params=pltpu.CompilerParams(vmem_limit_bytes=32 * MIB),
+        cost_estimate=cost(2),
+    )(place, *parts, *after)
+
+
+class Scatter:
+    def __init__(self, keep, send, replicas, reverse, first=0):
+        self.replicas, self.reverse = replicas, reverse
+        self.bits = chip_bits(replicas, reverse)
+        bit = self.bits.pop(0) if first else 1
+        self.pair = (keep, swap(send, bit, replicas))
+
+    def step(self, mark):
+        keep, go, mark = fold(*self.pair, self.reverse, (mark,))
+        self.pair = (keep, swap(go, self.bits.pop(0), self.replicas))
+        return mark
 
 
 def flip_by(value, axis, me, replicas):
@@ -578,22 +1020,16 @@
     local = width // shards
     hidden = w_up.shape[2]
     w_qkv, w_out, w_up, w_down = w_qkv[0], w_out[0], w_up[0], w_down[0]
-    out_parts = 1
-    while w_out.shape[0] * out_parts // replicas < 16:
-        out_parts *= 2
-    cut_out = Cut(w_out.shape[0], width, out_parts, replicas, shards)
+    cut_out = Cut(w_out.shape[0], width, 1, replicas, shards)
     cut_up = Cut(w_up.shape[0], hidden, hidden // width, replicas, shards)
     cut_down = Cut(w_down.shape[0], width, 1, replicas, shards)
     cuts = (cut_out, cut_up, cut_down)
 
-    blocks = {0: tokens}
-    for d in range(1, shards // 2 + 1):
-        blocks[d] = turn(blocks[d - 1], shards)
-        if shards - d not in blocks:
-            blocks[shards - d] = turn(blocks[(shards - d + 1) % shards], shards, shards - 1)
-
     vectors = (ln1_gain, ln1_bias, q_bias, v_bias, out_bias, ln2_gain, ln2_bias, down_bias, up_bias)
     packed = jnp.concatenate(vectors, 1)
+    slim = w_qkv.shape[0] // replicas
+    mine = lax.dynamic_slice_in_dim(w_qkv, me * slim, slim, 0)
+    mine = mine.reshape(slim, 3, shards, local).transpose(2, 0, 1, 3).reshape(shards, slim, 3 * local)
     turned = [packed] + [turn(packed, shards, step) for step in range(shards - 1, 0, -1)]
     turned = jnp.concatenate(turned + turned, 0)
     packed_all = lax.dynamic_slice_in_dim(turned, lax.rem(shards - z, shards), shards)
@@ -610,29 +1046,40 @@
     bias_v = lax.dynamic_slice_in_dim(full[3], start_at, local, 1)
     bias_qkv = jnp.concatenate([bias_q, jnp.zeros_like(bias_q), bias_v], 1)
 
-    slim = w_qkv.shape[0] // replicas
-    mine = lax.dynamic_slice_in_dim(w_qkv, me * slim, slim, 0)
-    mine = mine.reshape(slim, 3, shards, local).transpose(2, 0, 1, 3).reshape(shards, slim, 3 * local)
-    mine = lax.all_to_all(mine, "fsdp", 0, 0, tiled=True)
+    piece = jnp.concatenate(
+        [cut.of(shard, me) for cut, shard in ((cut_out, w_out), (cut_up, w_up), (cut_down, w_down))], 0
+    )
+    piece = gate(piece, mine)
+    slots = around(piece, shards)
+    near = (slots[1], slots[shards - 1])
+    blocks = around(gate(tokens, packed, *near), shards)
+    mine = gate(lax.all_to_all(mine, "fsdp", 0, 0, tiled=True), *near)
     weight_qkv = flip_by(jnp.stack(share(mine, replicas)), 0, me, replicas)
     weight_qkv = weight_qkv.transpose(1, 0, 2, 3).reshape(width, 3 * local)
 
-    h_all = jnp.zeros((group_len, width), BF)
+    hiddens = [None] * shards
     combined = jnp.zeros((group_len, 3 * local), BF)
     for d in [0] + sorted(range(1, shards), key=lambda d: min(d, shards - d)):
-        h_all, combined = project(
-            place, blocks[d], gain_one, bias_one, weight_qkv, bias_qkv, h_all, combined, d, shards
+        if d == shards // 2:
+            early = mark
+        hiddens[d], combined, mark = project(
+            place, blocks[d], gain_one, bias_one, weight_qkv, bias_qkv, combined, d, shards
         )
 
-    lists = [
-        gather_weight(cut_out, place, w_out),
-        gather_weight(cut_up, place, w_up),
-        gather_weight(cut_down, place, w_down, True),
-    ]
+    edge = cut_out.r + cut_up.r
+    slots = [gate(slots[d], early) for d in range(1, shards)]
+    upper = jnp.stack([slot[:edge] for slot in slots])
+    lower = jnp.stack([slot[edge:] for slot in slots])
 
     low = window_low(cont_lengths[0], group_len)
     mixed, lse = attend(combined, low, head_dim)
-    attended = lax.all_to_all(mixed, "fsdp", 0, 1, tiled=True)
+    attended = [
+        lax.dynamic_slice_in_dim(mixed, lax.rem(z + d, shards) * rows, rows) for d in range(shards)
+    ]
+    attended = [turn(block, shards, d) if d else block for d, block in enumerate(attended)]
+    pause = lambda part: gate(part, mark)
+    lists = share(upper, replicas, False, pause) + share(lower, replicas, True, pause)
+    lists += [w_out, w_up, w_down]
     output, hidden_two, middle, acted, slope = feed_forward(
         place, attended, tokens, middle_vectors, bias_up, cuts, lists
     )
@@ -642,36 +1089,57 @@
         place, dm, slope, middle, middle_vectors, cuts, lists
     )
     grad_mixed = lax.all_to_all(do, "fsdp", 1, 0, tiled=True)
-    out_w_down = reduce_weight(cut_down, place, *weight_grad(cut_down, place, acted, dm))
-    out_w_up = reduce_weight(cut_up, place, *weight_grad(cut_up, place, hidden_two, du), True)
-    out_w_out = reduce_weight(cut_out, place, *weight_grad(cut_out, place, attended, da))
-
-    dq, dk, dv = attend_grad(combined, low, mixed, lse, grad_mixed, head_dim)
-    first_sums = jnp.zeros((8, width), F32)
+    terms = ((cut_down, acted, dm, False), (cut_up, hidden_two, du, True), (cut_out, attended, da, False))
+    mark = grad_bias_up
+    scatters = []
+    if all(cut.rows % 256 == 0 for cut in cuts):
+        gots = []
+        for cut, left, right, _ in terms:
+            send, mark = send_grad(cut, place, left, right, (mark,) if gots else ())
+            gots.append(swap(send, 1, replicas))
+        for (cut, left, right, reverse), got in zip(terms, gots):
+            stay, go, mark = keep_grad(cut, place, left, right, got, reverse, (mark,))
+            if cut is cut_out:
+                halves = (stay, go)
+                out = [halves[m % 2][m // 2 : m // 2 + 1] for m in range(replicas // 2)]
+            else:
+                scatters.append(Scatter(stay, go, replicas, reverse, True))
+    else:
+        turned = [attended[-d % shards] for d in range(shards)] * 2
+        joined = lax.dynamic_slice_in_dim(
+            jnp.concatenate(turned, 1), lax.rem(shards - z, shards) * local, width, 1
+        )
+        for cut, left, right, reverse in terms:
+            left = joined if left is attended else left
+            keep, send, mark = weight_grad(cut, place, left, right, (mark,))
+            if cut is cut_out:
+                *out, mark = spread(keep, swap(send, 1, replicas), (mark,))
+                out = [part[None] for part in out]
+            else:
+                scatters.append(Scatter(keep, send, replicas, reverse))
+        for scatter in scatters:
+            mark = scatter.step(mark)
+    down, up = scatters
+    out = direct(out, replicas)
+
+    dq, dk, dv, bias_sums = attend_grad(combined, low, mixed, lse, grad_mixed, head_dim, (mark,))
     parts = {}
-    for d in [*range(1, shards), 0]:
-        parts[d], part_sums = hidden_grad(place, blocks[d], dq, dk, dv, weight_qkv, d, shards)
-        first_sums += part_sums
-    travel = parts[1]
-    for d in range(2, shards):
-        travel = add_low(turn(travel, shards), parts[d])
-    input_grad = last(tokens, turn(travel, shards), parts[0], dx2, gain_one)
-
-    dc = jnp.concatenate([dq, dk, dv], 1)
-    grad_bias_qkv = jnp.sum(dc.astype(F32), 0)
-    grad_w_qkv = rnd(jnp.einsum("td,te->de", h_all, dc, preferred_element_type=F32))
-    rel = grad_w_qkv.reshape(shards, replicas, slim, 3 * local).transpose(1, 0, 2, 3)
-    rel = flip_by(rel, 0, me, replicas)
-    rel = rel.reshape(replicas // 2, 2, shards, slim, 3 * local)
-    piece = plane_scatter(rel[:, 0], rel[:, 1], replicas)
-    piece = lax.all_to_all(piece, "fsdp", 0, 0, tiled=True)
-    piece = piece.reshape(shards, slim, 3, local).transpose(1, 2, 0, 3).reshape(slim, 3 * width)
-    out_w_qkv = flip_by(jnp.stack(share(piece, replicas)), 0, me, replicas)
-    out_w_qkv = out_w_qkv.reshape(w_qkv.shape).astype(F32)
-
-    spread = jnp.zeros((width,), F32)
-    grad_bias_q = lax.dynamic_update_slice(spread, grad_bias_qkv[:local], (start_at,))
-    grad_bias_v = lax.dynamic_update_slice(spread, grad_bias_qkv[2 * local :], (start_at,))
+    parts[1 % shards], first_sums = hidden_grad(place, blocks[1 % shards], dq, dk, dv, weight_qkv, 1, shards)
+    travel = turn(parts[1 % shards], shards)
+    mark = first_sums
+    while down.bits:
+        mark = down.step(mark)
+        mark = up.step(mark)
+    out, mark = close_parts(out, (mark,))
+    for d in [*range(2, shards), 0]:
+        parts[d], mark = hidden_grad(
+            place, blocks[d], dq, dk, dv, weight_qkv, d, shards, (mark,)
+        )
+        first_sums += mark
+
+    blank = jnp.zeros((width,), F32)
+    grad_bias_q = lax.dynamic_update_slice(blank, bias_sums[:, 0].reshape(-1), (start_at,))
+    grad_bias_v = lax.dynamic_update_slice(blank, bias_sums[:, 1].reshape(-1), (start_at,))
     small = (
         first_sums[0],
         first_sums[1],
@@ -683,16 +1151,50 @@
         sums[0],
         grad_bias_up,
     )
-    total = jnp.concatenate([g.reshape(shards, -1) for g in small], 1)
-    bit = 1
-    while bit < replicas:
-        total = total + swap(total, bit, replicas)
-        bit *= 2
-    bit = 1
-    while bit < shards:
-        total = total + lax.ppermute(total, "fsdp", [(i, i ^ bit) for i in range(shards)])
-        bit *= 2
-    total = lax.dynamic_slice_in_dim(total, z, 1)
+    small = jnp.concatenate([g.reshape(shards, -1) for g in small], 1)
+    count = small.shape[1] // replicas
+    small = small.reshape(shards, replicas, count)
+    small = jnp.pad(small, ((0, 0), (0, 0), (0, 3 * local - count)))
+    others = list(range(2, shards))
+    if others:
+        step, mark = join(travel, parts[others[0]][None], 0, (mark,))
+        travel = turn(step, shards)
+    keep, send, mark = qkv_grad(place, hiddens, dq, dk, dv, small, slim, shards, (mark,))
+    got = swap(send, 1, replicas)
+
+    sums_all, first, mark = close(([out], up.pair, down.pair), (mark,))
+    ring = turn(first, shards)
+    *qkv, mark = spread(keep, got, (mark,))
+    qkv = direct(qkv, replicas)
+    come = None
+    for d in range(2, shards + 1):
+        total, mark = join(ring, sums_all, d % shards, (mark,))
+        if d < shards:
+            ring = turn(total, shards)
+        if come is None:
+            piece, mark = gather_sum(place, qkv, (mark,))
+            come = [piece[0]] + [turn(piece[e], shards, e) for e in range(1, shards)]
+    for d in others[1:]:
+        step, mark = join(travel, parts[d][None], 0, (mark,))
+        travel = turn(step, shards)
+    input_grad, last_mark = last(tokens, travel, parts[0], dx2, gain_one)
+    rows_qkv = jnp.concatenate(
+        [
+            jnp.concatenate([block[:slim, k * local : (k + 1) * local] for block in come], 1)
+            for k in range(3)
+        ],
+        0,
+    )
+    row_small = rnd(sum(block[slim, :count].astype(F32) for block in come))
+    row_small = jnp.pad(row_small[None], ((0, 15), (0, width - count)))
+    upper = jnp.concatenate([total[:edge], row_small], 0)
+    lower = jnp.concatenate([total[edge:], rows_qkv], 0)
+    own_a = gate(jnp.stack(share_chips(upper, replicas, False)), last_mark)
+    own_b = gate(jnp.stack(share_chips(lower, replicas, True)), last_mark)
+    out_w_out, out_w_up, out_w_down, out_w_qkv, total = widen(
+        cuts, slim, place, own_a, swap(own_a, 1, replicas), own_b, swap(own_b, 1, replicas)
+    )
+    total = total.reshape(replicas, 8, width)[:, 0, :count].reshape(1, -1)
     outs = []
     offset = 0
     for vector in vectors:

time: 622 us -> 535 us (0.86)
  waiting for transfers between devices: 291 us -> 214 us
  Pallas kernels: 152 us -> 185 us
  starting transfers between devices: 87.9 us -> 59.7 us
  other arithmetic: 34.6 us -> 10.8 us
  local copies, waits for them, and re-layouts: 37.7 us -> 54.4 us
  matrix products: 6.68 us -> 0 us
    ppermute x71 -> x43, waiting for transfers between devices: 151 us -> 75.6 us  [swap(): return lax.ppermute(value, 'dp', [(i, i ^ bit) for i in range(replicas)])]
    pallas_call x7 -> x30, Pallas kernels: 36.1 us -> 72.5 us  [the longest x4 25.3 us: wide_grad(): pl.pallas_call(functools.partial(wide_kernel, cut, other, reverse, len(le...]
    convert_element_type x23 -> x1, other arithmetic: 22 us -> 0.01 us  [rnd(): return v.astype(BF)]
    ppermute x71 -> x43, starting transfers between devices: 40.7 us -> 27.1 us  [swap(): return lax.ppermute(value, 'dp', [(i, i ^ bit) for i in range(replicas)])]
    unnamed x115 -> x188, local copies, waits for them, and re-layouts: 24 us -> 32.2 us
    another operation x8 -> x12, local copies, waits for them, and re-layouts: 0.2 us -> 8.18 us  [the longest x3 4.52 us: body(): upper = jnp.stack([slot[:edge] for slot in slots])]
    all_to_all x3 -> x1, starting transfers between devices: 11.4 us -> 4.08 us  [body(): mine = gate(lax.all_to_all(mine, 'fsdp', 0, 0, tiled=True), *near)]
    dot_general x1 -> x0, matrix products: 6.68 us -> none  [body(): jnp.einsum('td,te->de', h_all, dc, preferred_element_type=F32)]
  transfers between devices with their start and end apart: 104 -> 66, of which waited for: 44 -> 28; matrix products, arithmetic and copies ran while one was open for 9% -> 5% of each run, Pallas kernels for 16% -> 28%
where the time goes in v3:
time: 535 us; the launch traced here: 526 us
  waiting for transfers between devices  214 us (40%)
  Pallas kernels  185 us (35%)
  starting transfers between devices  59.7 us (11%)
  local copies, waits for them, and re-layouts  54.4 us (10%)
  other arithmetic  10.8 us (2%)
    ppermute x21, waiting for transfers between devices, turn(): lax.ppermute(value, 'fsdp', [(i, (i + step) % shards) for i in range(shar...  136 us
    ppermute x43, waiting for transfers between devices, swap(): return lax.ppermute(value, 'dp', [(i, i ^ bit) for i in range(replicas)])  75.6 us
    unnamed x188, local copies, waits for them, and re-layouts  32.2 us
    pallas_call x1, Pallas kernels, attend_grad(): pl.pallas_call(functools.partial(attend_grad_kernel, group_len, head_dim)...  28.7 us
    ppermute x43, starting transfers between devices, swap(): return lax.ppermute(value, 'dp', [(i, i ^ bit) for i in range(replicas)])  27.1 us
    pallas_call x4, Pallas kernels, wide_grad(): pl.pallas_call(functools.partial(wide_kernel, cut, other, reverse, len(le...  25.3 us
    pallas_call x1, Pallas kernels, feed_forward(): pl.pallas_call(functools.partial(forward_kernel, cuts, min(1024, hidden))...  24.3 us
    pallas_call x1, Pallas kernels, feed_backward(): pl.pallas_call(functools.partial(backward_kernel, cuts, min(1024, hidden)...  23.7 us
  transfers between devices with their start and end apart: 66, of which 28 were waited for; matrix products, arithmetic and copies ran while one was open for 5% of the time, Pallas kernels for 28%

profile of v3, /device:TPU:0, one launch (start us, length us, event | category | flops | bytes accessed | tf_op | source)
XLA Modules:
  0.0 526.2 jit_solution(13790760913054518140)
XLA Ops:
  6.1 3.0 collective-permute-start.3
  9.2 2.0 collective-permute-start.4
  11.4 2.1 collective-permute-start
  14.5 4.1 all-to-all-start
  19.6 18.4 %collective-permute-done = bf16[1,3072]{1,0:T(2,128)(2,1)S(1)} collective-permute-done((bf16[1,3072]{1,0:T(2,128)(2,1)S(1)}, bf16[1,3072]{1,0:T(2,128)(2,1)S(1)}, u32[]{:S(2)}, u32[]{:S(2)}) %collective-permute-start) | collective-permute-done | bytes 6176 | tf_op jit(solution)/shard_map/ppermute | solution.py:757
  39.4 3.2 all-to-all-done.refs_0_
  46.4 3.8 collective-permute-start.14
  52.8 5.4 %collective-permute-done.12 = bf16[4,32,768]{2,1,0:T(8,128)(2,1)S(1)} collective-permute-done((bf16[4,32,768]{2,1,0:T(8,128)(2,1)S(1)}, bf16[4,32,768]{2,1,0:T(8,128)(2,1)S(1)}, u32[]{:S(2)}, u32[]{:S(2)}) %collective-permute-start.12) | collective-permute-done | bytes 196640 | tf_op jit(solution)/shard_map/ppermute | solution.py:744
  61.2 1.6 copy-done.12
  62.7 2.6 shard_map.274
  66.4 8.1 %collective-permute-done.5.block = bf16[512,1024]{1,0:T(8,128)(2,1)S(1)} collective-permute-done((bf16[512,1024]{1,0:T(8,128)(2,1)}, bf16[512,1024]{1,0:T(8,128)(2,1)S(1)}, u32[]{:S(2)}, u32[]{:S(2)}) %collective-permute-start.5) | collective-permute-done | bytes 1048608 | tf_op jit(solution)/shard_map/ppermute | solution.py:757
  74.5 2.6 shard_map.275
  77.0 17.0 %collective-permute-done.14.block = bf16[512,1024]{1,0:T(8,128)(2,1)S(1)} collective-permute-done((bf16[512,1024]{1,0:T(8,128)(2,1)}, bf16[512,1024]{1,0:T(8,128)(2,1)S(1)}, u32[]{:S(2)}, u32[]{:S(2)}) %collective-permute-start.14) | collective-permute-done | bytes 1048608 | tf_op jit(solution)/shard_map/ppermute | solution.py:757
  94.0 2.1 shard_map.276
  97.7 1.7 slice_bitcast_fusion.3
  99.4 1.7 slice_bitcast_fusion
  101.1 7.5 %collective-permute-done.18.refs_0_ = bf16[288,1024]{1,0:T(8,128)(2,1)} collective-permute-done((bf16[288,1024]{1,0:T(8,128)(2,1)}, bf16[288,1024]{1,0:T(8,128)(2,1)}, u32[]{:S(2)}, u32[]{:S(2)}) %collective-permute-start.18) | collective-permute-done | bytes 589856 | tf_op jit(solution)/shard_map/ppermute | solution.py:757
  108.6 1.7 slice_bitcast_fusion.1
  111.4 2.2 pad_maximum_fusion.2.refs_4_.refs_0_
  119.3 19.2 %collective-permute-done.20.refs_0_ = bf16[3,160,1024]{2,1,0:T(8,128)(2,1)S(1)} collective-permute-done((bf16[3,160,1024]{2,1,0:T(8,128)(2,1)}, bf16[3,160,1024]{2,1,0:T(8,128)(2,1)S(1)}, u32[]{:S(2)}, u32[]{:S(2)}) %collective-permute-start.20) | collective-permute-done | bytes 983072 | tf_op jit(solution)/shard_map/ppermute | solution.py:744
  144.3 2.1 shard_map.277
  148.0 5.5 %collective-permute-done.27.refs_14_.refs_10_ = bf16[3,128,1024]{2,1,0:T(8,128)(2,1)} collective-permute-done((bf16[3,128,1024]{2,1,0:T(8,128)(2,1)}, bf16[3,128,1024]{2,1,0:T(8,128)(2,1)}, u32[]{:S(2)}, u32[]{:S(2)}) %collective-permute-start.27) | collective-permute-done | bytes 786464 | tf_op jit(solution)/shard_map/ppermute | solution.py:744
  154.6 17.7 %shard_map.278 = (bf16[2048,256]{1,0:T(8,128)(2,1)}, f32[2,2,2048]{2,1,0:T(2,128)}) custom-call(bf16[2048,768]{1,0:T(8,128)(2,1)} %copy-done.2, bf16[2048,768]{1,0:T(8,128)(2,1)} %copy-done.2, bf16[2048,768]{1,0:T(8,128)(2,1)} %copy-done.2, s32[1,2048]{1,0:T(1,128)} %bitcast.159), custom_call_target="tpu_custom_call" | custom-call | flops 1800000000 | bytes 1 | tf_op jit(solution)/shard_map/pallas_call | solution.py:129
  173.0 2.0 constant_dynamic-slice_fusion.1
  175.2 10.7 %collective-permute-done.15.refs_1_ = bf16[512,256]{1,0:T(8,128)(2,1)S(1)} collective-permute-done((bf16[512,256]{1,0:T(8,128)(2,1)S(1)}, bf16[512,256]{1,0:T(8,128)(2,1)S(1)}, u32[]{:S(2)}, u32[]{:S(2)}) %collective-permute-start.15) | collective-permute-done | bytes 262176 | tf_op jit(solution)/shard_map/ppermute | solution.py:757
  186.4 10.1 %collective-permute-done.16.refs_2_ = bf16[512,256]{1,0:T(8,128)(2,1)} collective-permute-done((bf16[512,256]{1,0:T(8,128)(2,1)S(1)}, bf16[512,256]{1,0:T(8,128)(2,1)}, u32[]{:S(2)}, u32[]{:S(2)}) %collective-permute-start.16) | collective-permute-done | bytes 262176 | tf_op jit(solution)/shard_map/ppermute | solution.py:757
  200.5 3.0 collective-permute-done.30.refs_17_.refs_13_
  204.8 24.3 %shard_map.284 = (bf16[512,1024]{1,0:T(8,128)(2,1)}, bf16[512,1024]{1,0:T(8,128)(2,1)}, f32[512,1024]{1,0:T(8,128)}, bf16[512,4096]{1,0:T(8,128)(2,1)}, bf16[512,4096]{1,0:T(8,128)(2,1)}) custom-call(s32[2]{0:T(128)} %copy-done.48, bf16[512,1024]{1,0:T(8,128)(2,1)} %tokens.3, f32[8,1024]{1,0:T(8,128)} %concatenate.41.vectors, f32[1,4096]{1,0:T(1,128)} %bitcast.161, ...), custom_call_target="tpu_custom_call" | custom-call | flops 2400000000 | bytes 1 | tf_op jit(solution)/shard_map/pallas_call | solution.py:328
  229.1 7.1 %shard_map.286 = (bf16[4,4,128,1024]{3,2,1,0:T(8,128)(2,1)}, f32[8,128]{1,0:T(8,128)}) custom-call(s32[2]{0:T(128)} %copy-done.48, bf16[512,4096]{1,0:T(8,128)(2,1)} %get-tuple-element.117.left, bf16[512,1024]{1,0:T(8,128)(2,1)} %right.3), custom_call_target="tpu_custom_call" | custom-call | flops 750000000 | bytes 1 | tf_op jit(solution)/shard_map/pallas_call | solution.py:573
  236.4 23.7 %shard_map.285 = (bf16[512,4096]{1,0:T(8,128)(2,1)}, f32[512,1024]{1,0:T(8,128)}, bf16[512,1024]{1,0:T(8,128)(2,1)}, bf16[512,1024]{1,0:T(8,128)(2,1)}, f32[1,4096]{1,0:T(1,128)}, /*index=5*/f32[8,1024]{1,0:T(8,128)}) custom-call(s32[2]{0:T(128)} %copy-done.48, bf16[512,1024]{1,0:T(8,128)(2,1)} %right.3, bf16[512,4096]{1,0:T(8,128)(2,1)} %get-tuple-element.111.slope, ...), custom_call_target="tpu_custom_call" | custom-call | flops 2400000000 | bytes 1 | tf_op jit(solution)/shard_map/pallas_call | solution.py:384
  260.1 7.5 %shard_map.287 = (bf16[4,4,128,1024]{3,2,1,0:T(8,128)(2,1)}, f32[8,128]{1,0:T(8,128)}) custom-call(s32[2]{0:T(128)} %copy-done.48, bf16[512,4096]{1,0:T(8,128)(2,1)} %get-tuple-element.115.right, bf16[512,1024]{1,0:T(8,128)(2,1)} %get-tuple-element.116.refs_0_, f32[8,128]{1,0:T(8,128)} %get-tuple-element.118.refs_1_), custom_call_target="tpu_custom_call" | custom-call | flops 600000000 | bytes 1 | tf_op jit(solution)/shard_map/pallas_call | solution.py:509
  269.1 5.2 all-to-all-start.1
  274.2 4.1 shard_map.288
  278.3 8.4 %shard_map.289 = (bf16[2,4,128,1024]{3,2,1,0:T(8,128)(2,1)}, bf16[2,4,128,1024]{3,2,1,0:T(8,128)(2,1)}, f32[8,128]{1,0:T(8,128)}) custom-call(s32[2]{0:T(128)} %copy-done.48, bf16[512,4096]{1,0:T(8,128)(2,1)} %get-tuple-element.117.left, bf16[512,1024]{1,0:T(8,128)(2,1)} %right.3, bf16[4,4,128,1024]{3,2,1,0:T(8,128)(2,1)} %collective-permute-done.35.got, ...), custom_call_target="tpu_custom_call" | custom-call | flops 750000000 | bytes 1 | tf_op jit(solution)/shard_map/pallas_call | solution.py:573
  288.2 9.2 %shard_map.290 = (bf16[2,4,128,1024]{3,2,1,0:T(8,128)(2,1)}, bf16[2,4,128,1024]{3,2,1,0:T(8,128)(2,1)}, f32[8,128]{1,0:T(8,128)}) custom-call(s32[2]{0:T(128)} %copy-done.48, bf16[512,4096]{1,0:T(8,128)(2,1)} %get-tuple-element.115.right, bf16[512,1024]{1,0:T(8,128)(2,1)} %get-tuple-element.116.refs_0_, ...), custom_call_target="tpu_custom_call" | custom-call | flops 600000000 | bytes 1 | tf_op jit(solution)/shard_map/pallas_call | solution.py:509
  301.3 4.4 shard_map.291
  305.8 1.9 fusion.8
  308.2 1.8 fusion.9
  310.5 2.4 collective-permute-start.39
  313.9 28.7 %shard_map.292 = (bf16[2048,256]{1,0:T(8,128)(2,1)}, bf16[2048,256]{1,0:T(8,128)(2,1)}, bf16[2048,256]{1,0:T(8,128)(2,1)}, f32[2,2,128]{2,1,0:T(2,128)}) custom-call(bf16[2048,768]{1,0:T(8,128)(2,1)} %copy-done.2, bf16[2048,768]{1,0:T(8,128)(2,1)} %copy-done.2, bf16[2048,768]{1,0:T(8,128)(2,1)} %copy-done.2, s32[1,2048]{1,0:T(1,128)} %bitcast.160, ...), custom_call_target="tpu_custom_call" | custom-call | flops 2800000000 | bytes 1 | tf_op jit(solution)/shard_map/pallas_call | solution.py:148
  347.5 2.9 shard_map.293
  350.4 2.4 collective-permute-start.36
  352.7 3.8 shard_map.294
  357.5 3.6 shard_map.295
  364.0 1.9 shard_map.297
  366.9 1.9 shard_map.298
  369.8 1.9 shard_map.299
  374.0 2.9 collective-permute-done.36.travel
  382.1 7.1 %shard_map.301 = (bf16[4,4,48,768]{3,2,1,0:T(8,128)(2,1)}, bf16[4,4,48,768]{3,2,1,0:T(8,128)(2,1)}, f32[8,128]{1,0:T(8,128)S(1)}) custom-call(s32[2]{0:T(128)S(1)} %copy-done.49, bf16[2048,256]{1,0:T(8,128)(2,1)S(1)} %copy-done.7, bf16[2048,256]{1,0:T(8,128)(2,1)S(1)} %copy-done.9, bf16[2048,256]{1,0:T(8,128)(2,1)S(1)} %copy-done.11, ...), custom_call_target="tpu_custom_call" | custom-call | flops 650000000 | bytes 1 | tf_op jit(solution)/shard_map/pallas_call | solution.py:634
  389.1 7.7 %collective-permute-done.43.refs_2_ = bf16[1,4,128,1024]{3,2,1,0:T(8,128)(2,1)} collective-permute-done((bf16[1,4,128,1024]{3,2,1,0:T(8,128)(2,1)}, bf16[1,4,128,1024]{3,2,1,0:T(8,128)(2,1)}, u32[]{:S(2)}, u32[]{:S(2)}) %collective-permute-start.43) | collective-permute-done | bytes 1048608 | tf_op jit(solution)/shard_map/ppermute | solution.py:744
  397.1 2.7 shard_map.302
  405.1 9.2 %collective-permute-done.45.travel = bf16[288,1024]{1,0:T(8,128)(2,1)S(1)} collective-permute-done((bf16[288,1024]{1,0:T(8,128)(2,1)S(1)}, bf16[288,1024]{1,0:T(8,128)(2,1)S(1)}, u32[]{:S(2)}, u32[]{:S(2)}) %collective-permute-start.45) | collective-permute-done | bytes 589856 | tf_op jit(solution)/shard_map/ppermute | solution.py:757
  416.8 2.5 collective-permute-start.55
  419.9 1.9 collective-permute-start.53
  421.8 10.9 %collective-permute-done.47.travel = bf16[288,1024]{1,0:T(8,128)(2,1)S(1)} collective-permute-done((bf16[288,1024]{1,0:T(8,128)(2,1)S(1)}, bf16[288,1024]{1,0:T(8,128)(2,1)S(1)}, u32[]{:S(2)}, u32[]{:S(2)}) %collective-permute-start.47) | collective-permute-done | bytes 589856 | tf_op jit(solution)/shard_map/ppermute | solution.py:757
  432.9 19.5 %collective-permute-done.55 = bf16[48,768]{1,0:T(8,128)(2,1)S(1)} collective-permute-done((bf16[48,768]{1,0:T(8,128)(2,1)S(1)}, bf16[48,768]{1,0:T(8,128)(2,1)S(1)}, u32[]{:S(2)}, u32[]{:S(2)}) %collective-permute-start.55) | collective-permute-done | bytes 73760 | tf_op jit(solution)/shard_map/ppermute | solution.py:757
  452.4 17.3 %collective-permute-done.54 = bf16[48,768]{1,0:T(8,128)(2,1)S(1)} collective-permute-done((bf16[48,768]{1,0:T(8,128)(2,1)S(1)}, bf16[48,768]{1,0:T(8,128)(2,1)S(1)}, u32[]{:S(2)}, u32[]{:S(2)}) %collective-permute-start.54) | collective-permute-done | bytes 73760 | tf_op jit(solution)/shard_map/ppermute | solution.py:757
  473.3 9.2 %collective-permute-done.61 = bf16[224,1024]{1,0:T(8,128)(2,1)S(1)} collective-permute-done((bf16[224,1024]{1,0:T(8,128)(2,1)S(1)}, bf16[224,1024]{1,0:T(8,128)(2,1)S(1)}, u32[]{:S(2)}, u32[]{:S(2)}) %collective-permute-start.61) | collective-permute-done | bytes 458784 | tf_op jit(solution)/shard_map/ppermute | solution.py:744
  485.1 16.7 %collective-permute-done.56 = bf16[176,1024]{1,0:T(8,128)(2,1)S(1)} collective-permute-done((bf16[176,1024]{1,0:T(8,128)(2,1)S(1)}, bf16[176,1024]{1,0:T(8,128)(2,1)S(1)}, u32[]{:S(2)}, u32[]{:S(2)}) %collective-permute-start.56) | collective-permute-done | bytes 360480 | tf_op jit(solution)/shard_map/ppermute | solution.py:744
  505.3 2.6 shard_map.309
  508.5 2.2 collective-permute-done.58
  510.6 2.3 pad_maximum_fusion.1.refs_0_
  512.9 3.4 collective-permute-done.59.other_a
  517.7 7.1 %shard_map.312 = (f32[256,1024]{1,0:T(8,128)}, f32[256,4096]{1,0:T(8,128)}, f32[1024,1024]{1,0:T(8,128)}, f32[256,3072]{1,0:T(8,128)}, f32[64,1024]{1,0:T(8,128)S(1)}) custom-call(s32[2]{0:T(128)S(1)} %copy-done.49, bf16[4,176,1024]{2,1,0:T(8,128)(2,1)S(1)} %copy-done.15, bf16[4,176,1024]{2,1,0:T(8,128)(2,1)S(1)} %collective-permute-done.59.other_a, ...), custom_call_target="tpu_custom_call" | custom-call | flops 700000000 | bytes 1 | tf_op jit(solution)/shard_map/pallas_call | solution.py:680
  (375 shorter events, 91.0 us)
Async XLA Ops:
  6.1 36.5 %collective-permute-start.3 = (bf16[288,1024]{1,0:T(8,128)(2,1)}, bf16[288,1024]{1,0:T(8,128)(2,1)}, u32[]{:S(2)}, u32[]{:S(2)}) collective-permute-start(bf16[288,1024]{1,0:T(8,128)(2,1)} %shard_map.271), channel_id=1, source_target_pairs={{0,1},{1,2},{2,3},{3,0},{4,5},{5,6},{6,7},{7,4},{8,9},{9,10},{10,1... | collective-permute-start | bytes 1769480 | tf_op jit(solution)/shard_map/ppermute | solution.py:757
  9.2 33.5 %collective-permute-start.4 = (bf16[288,1024]{1,0:T(8,128)(2,1)}, bf16[288,1024]{1,0:T(8,128)(2,1)}, u32[]{:S(2)}, u32[]{:S(2)}) collective-permute-start(bf16[288,1024]{1,0:T(8,128)(2,1)} %shard_map.271), channel_id=1, source_target_pairs={{0,3},{1,0},{2,1},{3,2},{4,7},{5,4},{6,5},{7,6},{8,11},{9,8},{10,9... | collective-permute-start | bytes 1769480 | tf_op jit(solution)/shard_map/ppermute | solution.py:757
  11.4 26.7 %collective-permute-start = (bf16[1,3072]{1,0:T(2,128)(2,1)S(1)}, bf16[1,3072]{1,0:T(2,128)(2,1)S(1)}, u32[]{:S(2)}, u32[]{:S(2)}) collective-permute-start(bf16[1,3072]{1,0:T(2,128)(2,1)S(1)} %constant_dynamic-update-slice_fusion.refs_1_), channel_id=1, source_target_pairs={{0,3},{1,0},{2,1},{3,2},{4,7},{5,4},{6,5},{7,6},{8,11},{9,8},{10,9... | collective-permute-start | bytes 18440 | tf_op jit(solution)/shard_map/ppermute | solution.py:757
  13.5 25.6 %collective-permute-start.1 = (bf16[1,3072]{1,0:T(2,128)(2,1)S(1)}, bf16[1,3072]{1,0:T(2,128)(2,1)S(1)}, u32[]{:S(2)}, u32[]{:S(2)}) collective-permute-start(bf16[1,3072]{1,0:T(2,128)(2,1)S(1)} %constant_dynamic-update-slice_fusion.refs_1_), channel_id=1, source_target_pairs={{0,2},{1,3},{2,0},{3,1},{4,6},{5,7},{6,4},{7,5},{8,10},{9,11},{10,... | collective-permute-start | bytes 18440 | tf_op jit(solution)/shard_map/ppermute | solution.py:757
  13.5 25.6 %collective-permute-start.2 = (bf16[1,3072]{1,0:T(2,128)(2,1)S(1)}, bf16[1,3072]{1,0:T(2,128)(2,1)S(1)}, u32[]{:S(2)}, u32[]{:S(2)}) collective-permute-start(bf16[1,3072]{1,0:T(2,128)(2,1)S(1)} %constant_dynamic-update-slice_fusion.refs_1_), channel_id=1, source_target_pairs={{0,1},{1,2},{2,3},{3,0},{4,5},{5,6},{6,7},{7,4},{8,9},{9,10},{10,1... | collective-permute-start | bytes 18440 | tf_op jit(solution)/shard_map/ppermute | solution.py:757
  14.5 28.1 %all-to-all-start = ((bf16[4,32,768]{2,1,0:T(8,128)(2,1)}), bf16[4,32,768]{2,1,0:T(8,128)(2,1)S(1)}, u32[]{:S(2)}, u32[]{:S(2)}) async-start(bf16[4,32,768]{2,1,0:T(8,128)(2,1)} %reshape.206.refs_1_), calls=%async_computation | async-start | bytes 393216 | tf_op jit(solution)/shard_map/all_to_all | solution.py:1056
  43.3 7.5 %collective-permute-start.7 = (bf16[4,32,768]{2,1,0:T(8,128)(2,1)}, bf16[4,32,768]{2,1,0:T(8,128)(2,1)S(1)}, u32[]{:S(2)}, u32[]{:S(2)}) collective-permute-start(bf16[4,32,768]{2,1,0:T(8,128)(2,1)} %shard_map.273), channel_id=1, source_target_pairs={{0,4},{4,0},{8,12},{12,8},{16,20},{20,16},{24,28},{28,24},{1,5},{5... | collective-permute-start | bytes 589832 | tf_op jit(solution)/shard_map/ppermute | solution.py:744
  43.3 7.5 %collective-permute-start.8 = (bf16[4,32,768]{2,1,0:T(8,128)(2,1)}, bf16[4,32,768]{2,1,0:T(8,128)(2,1)S(1)}, u32[]{:S(2)}, u32[]{:S(2)}) collective-permute-start(bf16[4,32,768]{2,1,0:T(8,128)(2,1)} %shard_map.273), channel_id=1, source_target_pairs={{0,8},{4,12},{8,0},{12,4},{16,24},{20,28},{24,16},{28,20},{1,9},{5... | collective-permute-start | bytes 589832 | tf_op jit(solution)/shard_map/ppermute | solution.py:744
  44.9 7.5 %collective-permute-start.10 = (bf16[4,32,768]{2,1,0:T(8,128)(2,1)}, bf16[4,32,768]{2,1,0:T(8,128)(2,1)S(1)}, u32[]{:S(2)}, u32[]{:S(2)}) collective-permute-start(bf16[4,32,768]{2,1,0:T(8,128)(2,1)} %shard_map.273), channel_id=1, source_target_pairs={{0,16},{4,20},{8,24},{12,28},{16,0},{20,4},{24,8},{28,12},{1,17},{... | collective-permute-start | bytes 589832 | tf_op jit(solution)/shard_map/ppermute | solution.py:744
  46.4 28.1 %collective-permute-start.5 = (bf16[512,1024]{1,0:T(8,128)(2,1)}, bf16[512,1024]{1,0:T(8,128)(2,1)S(1)}, u32[]{:S(2)}, u32[]{:S(2)}) collective-permute-start(bf16[512,1024]{1,0:T(8,128)(2,1)} %shard_map.272.block), channel_id=1, source_target_pairs={{0,1},{1,2},{2,3},{3,0},{4,5},{5,6},{6,7},{7,4},{8,9},{9,10},{10,1... | collective-permute-start | bytes 3145736 | tf_op jit(solution)/shard_map/ppermute | solution.py:757
  46.4 47.6 %collective-permute-start.14 = (bf16[512,1024]{1,0:T(8,128)(2,1)}, bf16[512,1024]{1,0:T(8,128)(2,1)S(1)}, u32[]{:S(2)}, u32[]{:S(2)}) collective-permute-start(bf16[512,1024]{1,0:T(8,128)(2,1)} %shard_map.272.block), channel_id=1, source_target_pairs={{0,3},{1,0},{2,1},{3,2},{4,7},{5,4},{6,5},{7,6},{8,11},{9,8},{10,9... | collective-permute-start | bytes 3145736 | tf_op jit(solution)/shard_map/ppermute | solution.py:757
  50.9 7.3 %collective-permute-start.12 = (bf16[4,32,768]{2,1,0:T(8,128)(2,1)S(1)}, bf16[4,32,768]{2,1,0:T(8,128)(2,1)S(1)}, u32[]{:S(2)}, u32[]{:S(2)}) collective-permute-start(bf16[4,32,768]{2,1,0:T(8,128)(2,1)S(1)} %collective-permute-done.8), channel_id=1, source_target_pairs={{0,16},{4,20},{8,24},{12,28},{16,0},{20,4},{24,8},{28,12},{1,17},{... | collective-permute-start | bytes 589832 | tf_op jit(solution)/shard_map/ppermute | solution.py:744
  52.4 56.2 %collective-permute-start.18 = (bf16[288,1024]{1,0:T(8,128)(2,1)}, bf16[288,1024]{1,0:T(8,128)(2,1)}, u32[]{:S(2)}, u32[]{:S(2)}) collective-permute-start(bf16[288,1024]{1,0:T(8,128)(2,1)} %collective-permute-done.3.refs_2_.refs_1_.refs_0_), channel_id=1, source_target_pairs={{0,1},{1,2},{2,3},{3,0},{4,5},{5,6},{6,7},{7,4},{8,9},{9,10},{10,1... | collective-permute-start | bytes 1769480 | tf_op jit(solution)/shard_map/ppermute | solution.py:757
  52.5 5.7 %collective-permute-start.11 = (bf16[4,32,768]{2,1,0:T(8,128)(2,1)S(1)}, bf16[4,32,768]{2,1,0:T(8,128)(2,1)S(1)}, u32[]{:S(2)}, u32[]{:S(2)}) collective-permute-start(bf16[4,32,768]{2,1,0:T(8,128)(2,1)S(1)} %collective-permute-done.10), channel_id=1, source_target_pairs={{0,4},{4,0},{8,12},{12,8},{16,20},{20,16},{24,28},{28,24},{1,5},{5... | collective-permute-start | bytes 589832 | tf_op jit(solution)/shard_map/ppermute | solution.py:744
  113.6 24.9 %collective-permute-start.20 = (bf16[3,160,1024]{2,1,0:T(8,128)(2,1)}, bf16[3,160,1024]{2,1,0:T(8,128)(2,1)S(1)}, u32[]{:S(2)}, u32[]{:S(2)}) collective-permute-start(bf16[3,160,1024]{2,1,0:T(8,128)(2,1)} %pad_maximum_fusion.2.refs_4_.refs_0_), channel_id=1, source_target_pairs={{0,8},{4,12},{8,0},{12,4},{16,24},{20,28},{24,16},{28,20},{1,9},{5... | collective-permute-start | bytes 2949128 | tf_op jit(solution)/shard_map/ppermute | solution.py:744
  114.2 25.8 %collective-permute-start.6 = (bf16[512,1024]{1,0:T(8,128)(2,1)S(1)}, bf16[512,1024]{1,0:T(8,128)(2,1)S(1)}, u32[]{:S(2)}, u32[]{:S(2)}) collective-permute-start(bf16[512,1024]{1,0:T(8,128)(2,1)S(1)} %copy-done.23), channel_id=1, source_target_pairs={{0,1},{1,2},{2,3},{3,0},{4,5},{5,6},{6,7},{7,4},{8,9},{9,10},{10,1... | collective-permute-start | bytes 3145736 | tf_op jit(solution)/shard_map/ppermute | solution.py:757
  117.3 36.2 %collective-permute-start.27 = (bf16[3,128,1024]{2,1,0:T(8,128)(2,1)}, bf16[3,128,1024]{2,1,0:T(8,128)(2,1)}, u32[]{:S(2)}, u32[]{:S(2)}) collective-permute-start(bf16[3,128,1024]{2,1,0:T(8,128)(2,1)} %pad_maximum_fusion.3.refs_12_.refs_8_), channel_id=1, source_target_pairs={{0,8},{4,12},{8,0},{12,4},{16,24},{20,28},{24,16},{28,20},{1,9},{5... | collective-permute-start | bytes 2359304 | tf_op jit(solution)/shard_map/ppermute | solution.py:744
  118.8 35.8 %collective-permute-start.29 = (bf16[3,128,1024]{2,1,0:T(8,128)(2,1)}, bf16[3,128,1024]{2,1,0:T(8,128)(2,1)}, u32[]{:S(2)}, u32[]{:S(2)}) collective-permute-start(bf16[3,128,1024]{2,1,0:T(8,128)(2,1)} %pad_maximum_fusion.3.refs_12_.refs_8_), channel_id=1, source_target_pairs={{0,16},{4,20},{8,24},{12,28},{16,0},{20,4},{24,8},{28,12},{1,17},{... | collective-permute-start | bytes 2359304 | tf_op jit(solution)/shard_map/ppermute | solution.py:744
  119.3 55.6 %collective-permute-start.19 = (bf16[3,160,1024]{2,1,0:T(8,128)(2,1)}, bf16[3,160,1024]{2,1,0:T(8,128)(2,1)}, u32[]{:S(2)}, u32[]{:S(2)}) collective-permute-start(bf16[3,160,1024]{2,1,0:T(8,128)(2,1)} %pad_maximum_fusion.2.refs_4_.refs_0_), channel_id=1, source_target_pairs={{0,4},{4,0},{8,12},{12,8},{16,20},{20,16},{24,28},{28,24},{1,5},{5... | collective-permute-start | bytes 2949128 | tf_op jit(solution)/shard_map/ppermute | solution.py:744
  138.5 33.8 %collective-permute-start.26 = (bf16[3,128,1024]{2,1,0:T(8,128)(2,1)}, bf16[3,128,1024]{2,1,0:T(8,128)(2,1)}, u32[]{:S(2)}, u32[]{:S(2)}) collective-permute-start(bf16[3,128,1024]{2,1,0:T(8,128)(2,1)} %pad_maximum_fusion.3.refs_12_.refs_8_), channel_id=1, source_target_pairs={{0,4},{4,0},{8,12},{12,8},{16,20},{20,16},{24,28},{28,24},{1,5},{5... | collective-permute-start | bytes 2359304 | tf_op jit(solution)/shard_map/ppermute | solution.py:744
  140.9 34.0 %collective-permute-start.22 = (bf16[3,160,1024]{2,1,0:T(8,128)(2,1)}, bf16[3,160,1024]{2,1,0:T(8,128)(2,1)}, u32[]{:S(2)}, u32[]{:S(2)}) collective-permute-start(bf16[3,160,1024]{2,1,0:T(8,128)(2,1)} %pad_maximum_fusion.2.refs_4_.refs_0_), channel_id=1, source_target_pairs={{0,16},{4,20},{8,24},{12,28},{16,0},{20,4},{24,8},{28,12},{1,17},{... | collective-permute-start | bytes 2949128 | tf_op jit(solution)/shard_map/ppermute | solution.py:744
  153.5 44.5 %collective-permute-start.24 = (bf16[3,160,1024]{2,1,0:T(8,128)(2,1)}, bf16[3,160,1024]{2,1,0:T(8,128)(2,1)}, u32[]{:S(2)}, u32[]{:S(2)}) collective-permute-start(bf16[3,160,1024]{2,1,0:T(8,128)(2,1)} %shard_map.282.refs_6_.refs_2_), channel_id=1, source_target_pairs={{0,16},{4,20},{8,24},{12,28},{16,0},{20,4},{24,8},{28,12},{1,17},{... | collective-permute-start | bytes 2949128 | tf_op jit(solution)/shard_map/ppermute | solution.py:744
  154.6 43.9 %collective-permute-start.28 = (bf16[3,128,1024]{2,1,0:T(8,128)(2,1)}, bf16[3,128,1024]{2,1,0:T(8,128)(2,1)}, u32[]{:S(2)}, u32[]{:S(2)}) collective-permute-start(bf16[3,128,1024]{2,1,0:T(8,128)(2,1)} %collective-permute-done.27.refs_14_.refs_10_), channel_id=1, source_target_pairs={{0,4},{4,0},{8,12},{12,8},{16,20},{20,16},{24,28},{28,24},{1,5},{5... | collective-permute-start | bytes 2359304 | tf_op jit(solution)/shard_map/ppermute | solution.py:744
  172.4 26.2 %collective-permute-start.31 = (bf16[3,128,1024]{2,1,0:T(8,128)(2,1)}, bf16[3,128,1024]{2,1,0:T(8,128)(2,1)}, u32[]{:S(2)}, u32[]{:S(2)}) collective-permute-start(bf16[3,128,1024]{2,1,0:T(8,128)(2,1)} %shard_map.283.refs_16_.refs_12_), channel_id=1, source_target_pairs={{0,8},{4,12},{8,0},{12,4},{16,24},{20,28},{24,16},{28,20},{1,9},{5... | collective-permute-start | bytes 2359304 | tf_op jit(solution)/shard_map/ppermute | solution.py:744
  174.9 11.0 %collective-permute-start.15 = (bf16[512,256]{1,0:T(8,128)(2,1)S(1)}, bf16[512,256]{1,0:T(8,128)(2,1)S(1)}, u32[]{:S(2)}, u32[]{:S(2)}) collective-permute-start(bf16[512,256]{1,0:T(8,128)(2,1)S(1)} %get-tuple-element.197), channel_id=1, source_target_pairs={{0,1},{1,2},{2,3},{3,0},{4,5},{5,6},{6,7},{7,4},{8,9},{9,10},{10,1... | collective-permute-start | bytes 786440 | tf_op jit(solution)/shard_map/ppermute | solution.py:757
  174.9 21.5 %collective-permute-start.16 = (bf16[512,256]{1,0:T(8,128)(2,1)S(1)}, bf16[512,256]{1,0:T(8,128)(2,1)}, u32[]{:S(2)}, u32[]{:S(2)}) collective-permute-start(bf16[512,256]{1,0:T(8,128)(2,1)S(1)} %get-tuple-element.196), channel_id=1, source_target_pairs={{0,2},{1,3},{2,0},{3,1},{4,6},{5,7},{6,4},{7,5},{8,10},{9,11},{10,... | collective-permute-start | bytes 786440 | tf_op jit(solution)/shard_map/ppermute | solution.py:757
  186.0 12.0 %collective-permute-start.17 = (bf16[512,256]{1,0:T(8,128)(2,1)S(1)}, bf16[512,256]{1,0:T(8,128)(2,1)}, u32[]{:S(2)}, u32[]{:S(2)}) collective-permute-start(bf16[512,256]{1,0:T(8,128)(2,1)S(1)} %get-tuple-element.195), channel_id=1, source_target_pairs={{0,3},{1,0},{2,1},{3,2},{4,7},{5,4},{6,5},{7,6},{8,11},{9,8},{10,9... | collective-permute-start | bytes 786440 | tf_op jit(solution)/shard_map/ppermute | solution.py:757
  196.4 7.0 %collective-permute-start.23 = (bf16[3,160,1024]{2,1,0:T(8,128)(2,1)}, bf16[3,160,1024]{2,1,0:T(8,128)(2,1)S(1)}, u32[]{:S(2)}, u32[]{:S(2)}) collective-permute-start(bf16[3,160,1024]{2,1,0:T(8,128)(2,1)} %collective-permute-done.22.refs_8_.refs_4_), channel_id=1, source_target_pairs={{0,4},{4,0},{8,12},{12,8},{16,20},{20,16},{24,28},{28,24},{1,5},{5... | collective-permute-start | bytes 2949128 | tf_op jit(solution)/shard_map/ppermute | solution.py:744
  198.0 5.4 %collective-permute-start.21 = (bf16[3,160,1024]{2,1,0:T(8,128)(2,1)S(1)}, bf16[3,160,1024]{2,1,0:T(8,128)(2,1)S(1)}, u32[]{:S(2)}, u32[]{:S(2)}) collective-permute-start(bf16[3,160,1024]{2,1,0:T(8,128)(2,1)S(1)} %copy-done.54), channel_id=1, source_target_pairs={{0,4},{4,0},{8,12},{12,8},{16,20},{20,16},{24,28},{28,24},{1,5},{5... | collective-permute-start | bytes 2949128 | tf_op jit(solution)/shard_map/ppermute | solution.py:744
  198.0 6.6 %collective-permute-start.25 = (bf16[3,160,1024]{2,1,0:T(8,128)(2,1)}, bf16[3,160,1024]{2,1,0:T(8,128)(2,1)}, u32[]{:S(2)}, u32[]{:S(2)}) collective-permute-start(bf16[3,160,1024]{2,1,0:T(8,128)(2,1)} %collective-permute-done.24.refs_10_.refs_6_), channel_id=1, source_target_pairs={{0,4},{4,0},{8,12},{12,8},{16,20},{20,16},{24,28},{28,24},{1,5},{5... | collective-permute-start | bytes 2949128 | tf_op jit(solution)/shard_map/ppermute | solution.py:744
  198.5 4.9 collective-permute-start.30
  198.6 6.0 %collective-permute-start.32 = (bf16[3,128,1024]{2,1,0:T(8,128)(2,1)}, bf16[3,128,1024]{2,1,0:T(8,128)(2,1)}, u32[]{:S(2)}, u32[]{:S(2)}) collective-permute-start(bf16[3,128,1024]{2,1,0:T(8,128)(2,1)} %collective-permute-done.31.refs_18_.refs_14_), channel_id=1, source_target_pairs={{0,4},{4,0},{8,12},{12,8},{16,20},{20,16},{24,28},{28,24},{1,5},{5... | collective-permute-start | bytes 2359304 | tf_op jit(solution)/shard_map/ppermute | solution.py:744
  236.3 42.0 %collective-permute-start.35 = (bf16[4,4,128,1024]{3,2,1,0:T(8,128)(2,1)}, bf16[4,4,128,1024]{3,2,1,0:T(8,128)(2,1)}, u32[]{:S(2)}, u32[]{:S(2)}) collective-permute-start(bf16[4,4,128,1024]{3,2,1,0:T(8,128)(2,1)} %get-tuple-element.122), channel_id=1, source_target_pairs={{0,4},{4,0},{8,12},{12,8},{16,20},{20,16},{24,28},{28,24},{1,5},{5... | collective-permute-start | bytes 12582920 | tf_op jit(solution)/shard_map/ppermute | solution.py:744
  267.6 20.6 %collective-permute-start.34 = (bf16[4,4,128,1024]{3,2,1,0:T(8,128)(2,1)}, bf16[4,4,128,1024]{3,2,1,0:T(8,128)(2,1)}, u32[]{:S(2)}, u32[]{:S(2)}) collective-permute-start(bf16[4,4,128,1024]{3,2,1,0:T(8,128)(2,1)} %get-tuple-element.121), channel_id=1, source_target_pairs={{0,4},{4,0},{8,12},{12,8},{16,20},{20,16},{24,28},{28,24},{1,5},{5... | collective-permute-start | bytes 12582920 | tf_op jit(solution)/shard_map/ppermute | solution.py:744
  269.1 43.8 %all-to-all-start.1 = ((bf16[512,4,256]{2,0,1:T(8,128)(2,1)}), bf16[512,4,256]{2,0,1:T(8,128)(2,1)S(1)}, u32[]{:S(2)}, u32[]{:S(2)}) async-start(bf16[512,4,256]{2,0,1:T(8,128)(2,1)} %bitcast.121), calls=%async_computation.1 | async-start | bytes 2097152 | tf_op jit(solution)/shard_map/all_to_all | solution.py:1091
  278.3 22.0 %collective-permute-start.33 = (bf16[4,4,32,1024]{3,2,1,0:T(8,128)(2,1)}, bf16[4,4,32,1024]{3,2,1,0:T(8,128)(2,1)S(1)}, u32[]{:S(2)}, u32[]{:S(2)}) collective-permute-start(bf16[4,4,32,1024]{3,2,1,0:T(8,128)(2,1)} %get-tuple-element.120), channel_id=1, source_target_pairs={{0,4},{4,0},{8,12},{12,8},{16,20},{20,16},{24,28},{28,24},{1,5},{5... | collective-permute-start | bytes 3145736 | tf_op jit(solution)/shard_map/ppermute | solution.py:744
  286.7 63.6 %collective-permute-start.41 = (bf16[2,4,128,1024]{3,2,1,0:T(8,128)(2,1)}, bf16[2,4,128,1024]{3,2,1,0:T(8,128)(2,1)}, u32[]{:S(2)}, u32[]{:S(2)}) collective-permute-start(bf16[2,4,128,1024]{3,2,1,0:T(8,128)(2,1)} %get-tuple-element.136), channel_id=1, source_target_pairs={{0,8},{4,12},{8,0},{12,4},{16,24},{20,28},{24,16},{28,20},{1,9},{5... | collective-permute-start | bytes 6291464 | tf_op jit(solution)/shard_map/ppermute | solution.py:744
  297.5 60.1 %collective-permute-start.40 = (bf16[2,4,128,1024]{3,2,1,0:T(8,128)(2,1)}, bf16[2,4,128,1024]{3,2,1,0:T(8,128)(2,1)}, u32[]{:S(2)}, u32[]{:S(2)}) collective-permute-start(bf16[2,4,128,1024]{3,2,1,0:T(8,128)(2,1)} %get-tuple-element.134), channel_id=1, source_target_pairs={{0,16},{4,20},{8,24},{12,28},{16,0},{20,4},{24,8},{28,12},{1,17},{... | collective-permute-start | bytes 6291464 | tf_op jit(solution)/shard_map/ppermute | solution.py:744
  307.6 53.5 %collective-permute-start.37 = (bf16[1,4,32,1024]{3,2,1,0:T(8,128)(2,1)}, bf16[1,4,32,1024]{3,2,1,0:T(8,128)(2,1)S(1)}, u32[]{:S(2)}, u32[]{:S(2)}) collective-permute-start(bf16[1,4,32,1024]{3,2,1,0:T(8,128)(2,1)} %get-tuple-element.200), channel_id=1, source_target_pairs={{0,8},{4,12},{8,0},{12,4},{16,24},{20,28},{24,16},{28,20},{1,9},{5... | collective-permute-start | bytes 786440 | tf_op jit(solution)/shard_map/ppermute | solution.py:744
  309.9 51.3 %collective-permute-start.38 = (bf16[1,4,32,1024]{3,2,1,0:T(8,128)(2,1)}, bf16[1,4,32,1024]{3,2,1,0:T(8,128)(2,1)S(1)}, u32[]{:S(2)}, u32[]{:S(2)}) collective-permute-start(bf16[1,4,32,1024]{3,2,1,0:T(8,128)(2,1)} %get-tuple-element.201), channel_id=1, source_target_pairs={{0,16},{4,20},{8,24},{12,28},{16,0},{20,4},{24,8},{28,12},{1,17},{... | collective-permute-start | bytes 786440 | tf_op jit(solution)/shard_map/ppermute | solution.py:744
  310.5 51.4 %collective-permute-start.39 = (bf16[1,4,32,1024]{3,2,1,0:T(8,128)(2,1)}, bf16[1,4,32,1024]{3,2,1,0:T(8,128)(2,1)}, u32[]{:S(2)}, u32[]{:S(2)}) collective-permute-start(bf16[1,4,32,1024]{3,2,1,0:T(8,128)(2,1)} %get-tuple-element.199), channel_id=1, source_target_pairs={{0,24},{4,28},{8,16},{12,20},{16,8},{20,12},{24,0},{28,4},{1,25},{... | collective-permute-start | bytes 786440 | tf_op jit(solution)/shard_map/ppermute | solution.py:744
  350.4 26.5 %collective-permute-start.36 = (bf16[512,1024]{1,0:T(8,128)(2,1)}, bf16[512,1024]{1,0:T(8,128)(2,1)}, u32[]{:S(2)}, u32[]{:S(2)}) collective-permute-start(bf16[512,1024]{1,0:T(8,128)(2,1)} %get-tuple-element.130), channel_id=1, source_target_pairs={{0,1},{1,2},{2,3},{3,0},{4,5},{5,6},{6,7},{7,4},{8,9},{9,10},{10,1... | collective-permute-start | bytes 3145736 | tf_op jit(solution)/shard_map/ppermute | solution.py:757
  372.7 24.1 %collective-permute-start.43 = (bf16[1,4,128,1024]{3,2,1,0:T(8,128)(2,1)}, bf16[1,4,128,1024]{3,2,1,0:T(8,128)(2,1)}, u32[]{:S(2)}, u32[]{:S(2)}) collective-permute-start(bf16[1,4,128,1024]{3,2,1,0:T(8,128)(2,1)} %get-tuple-element.149), channel_id=1, source_target_pairs={{0,8},{4,12},{8,0},{12,4},{16,24},{20,28},{24,16},{28,20},{1,9},{5... | collective-permute-start | bytes 3145736 | tf_op jit(solution)/shard_map/ppermute | solution.py:744
  373.3 23.8 %collective-permute-start.44 = (bf16[1,4,128,1024]{3,2,1,0:T(8,128)(2,1)}, bf16[1,4,128,1024]{3,2,1,0:T(8,128)(2,1)}, u32[]{:S(2)}, u32[]{:S(2)}) collective-permute-start(bf16[1,4,128,1024]{3,2,1,0:T(8,128)(2,1)} %get-tuple-element.151), channel_id=1, source_target_pairs={{0,16},{4,20},{8,24},{12,28},{16,0},{20,4},{24,8},{28,12},{1,17},{... | collective-permute-start | bytes 3145736 | tf_op jit(solution)/shard_map/ppermute | solution.py:744
  389.1 11.9 %collective-permute-start.46 = (bf16[4,4,48,768]{3,2,1,0:T(8,128)(2,1)}, bf16[4,4,48,768]{3,2,1,0:T(8,128)(2,1)S(1)}, u32[]{:S(2)}, u32[]{:S(2)}) collective-permute-start(bf16[4,4,48,768]{3,2,1,0:T(8,128)(2,1)} %get-tuple-element.164), channel_id=1, source_target_pairs={{0,4},{4,0},{8,12},{12,8},{16,20},{20,16},{24,28},{28,24},{1,5},{5... | collective-permute-start | bytes 3538952 | tf_op jit(solution)/shard_map/ppermute | solution.py:744
  399.7 14.6 %collective-permute-start.45 = (bf16[288,1024]{1,0:T(8,128)(2,1)S(1)}, bf16[288,1024]{1,0:T(8,128)(2,1)S(1)}, u32[]{:S(2)}, u32[]{:S(2)}) collective-permute-start(bf16[288,1024]{1,0:T(8,128)(2,1)S(1)} %get-tuple-element.161), channel_id=1, source_target_pairs={{0,1},{1,2},{2,3},{3,0},{4,5},{5,6},{6,7},{7,4},{8,9},{9,10},{10,1... | collective-permute-start | bytes 1769480 | tf_op jit(solution)/shard_map/ppermute | solution.py:757
  401.6 14.4 %collective-permute-start.48 = (bf16[4,48,768]{2,1,0:T(8,128)(2,1)S(1)}, bf16[4,48,768]{2,1,0:T(8,128)(2,1)S(1)}, u32[]{:S(2)}, u32[]{:S(2)}) collective-permute-start(bf16[4,48,768]{2,1,0:T(8,128)(2,1)S(1)} %get-tuple-element.169), channel_id=1, source_target_pairs={{0,8},{4,12},{8,0},{12,4},{16,24},{20,28},{24,16},{28,20},{1,9},{5... | collective-permute-start | bytes 884744 | tf_op jit(solution)/shard_map/ppermute | solution.py:744
  403.1 12.9 %collective-permute-start.49 = (bf16[4,48,768]{2,1,0:T(8,128)(2,1)S(1)}, bf16[4,48,768]{2,1,0:T(8,128)(2,1)S(1)}, u32[]{:S(2)}, u32[]{:S(2)}) collective-permute-start(bf16[4,48,768]{2,1,0:T(8,128)(2,1)S(1)} %get-tuple-element.170), channel_id=1, source_target_pairs={{0,16},{4,20},{8,24},{12,28},{16,0},{20,4},{24,8},{28,12},{1,17},{... | collective-permute-start | bytes 884744 | tf_op jit(solution)/shard_map/ppermute | solution.py:744
  403.6 12.3 %collective-permute-start.50 = (bf16[4,48,768]{2,1,0:T(8,128)(2,1)S(1)}, bf16[4,48,768]{2,1,0:T(8,128)(2,1)S(1)}, u32[]{:S(2)}, u32[]{:S(2)}) collective-permute-start(bf16[4,48,768]{2,1,0:T(8,128)(2,1)S(1)} %get-tuple-element.171), channel_id=1, source_target_pairs={{0,24},{4,28},{8,16},{12,20},{16,8},{20,12},{24,0},{28,4},{1,25},{... | collective-permute-start | bytes 884744 | tf_op jit(solution)/shard_map/ppermute | solution.py:744
  414.5 18.2 %collective-permute-start.47 = (bf16[288,1024]{1,0:T(8,128)(2,1)S(1)}, bf16[288,1024]{1,0:T(8,128)(2,1)S(1)}, u32[]{:S(2)}, u32[]{:S(2)}) collective-permute-start(bf16[288,1024]{1,0:T(8,128)(2,1)S(1)} %get-tuple-element.167), channel_id=1, source_target_pairs={{0,1},{1,2},{2,3},{3,0},{4,5},{5,6},{6,7},{7,4},{8,9},{9,10},{10,1... | collective-permute-start | bytes 1769480 | tf_op jit(solution)/shard_map/ppermute | solution.py:757
  414.5 55.9 %collective-permute-start.42 = (bf16[512,1024]{1,0:T(8,128)(2,1)S(1)}, bf16[512,1024]{1,0:T(8,128)(2,1)S(1)}, u32[]{:S(2)}, u32[]{:S(2)}) collective-permute-start(bf16[512,1024]{1,0:T(8,128)(2,1)S(1)} %get-tuple-element.145), channel_id=1, source_target_pairs={{0,1},{1,2},{2,3},{3,0},{4,5},{5,6},{6,7},{7,4},{8,9},{9,10},{10,1... | collective-permute-start | bytes 3145736 | tf_op jit(solution)/shard_map/ppermute | solution.py:757
  416.8 35.6 %collective-permute-start.55 = (bf16[48,768]{1,0:T(8,128)(2,1)S(1)}, bf16[48,768]{1,0:T(8,128)(2,1)S(1)}, u32[]{:S(2)}, u32[]{:S(2)}) collective-permute-start(bf16[48,768]{1,0:T(8,128)(2,1)S(1)} %get-tuple-element.206), channel_id=1, source_target_pairs={{0,3},{1,0},{2,1},{3,2},{4,7},{5,4},{6,5},{7,6},{8,11},{9,8},{10,9... | collective-permute-start | bytes 221192 | tf_op jit(solution)/shard_map/ppermute | solution.py:757
  419.3 50.3 %collective-permute-start.54 = (bf16[48,768]{1,0:T(8,128)(2,1)S(1)}, bf16[48,768]{1,0:T(8,128)(2,1)S(1)}, u32[]{:S(2)}, u32[]{:S(2)}) collective-permute-start(bf16[48,768]{1,0:T(8,128)(2,1)S(1)} %get-tuple-element.207), channel_id=1, source_target_pairs={{0,2},{1,3},{2,0},{3,1},{4,6},{5,7},{6,4},{7,5},{8,10},{9,11},{10,... | collective-permute-start | bytes 221192 | tf_op jit(solution)/shard_map/ppermute | solution.py:757
  419.9 49.8 %collective-permute-start.53 = (bf16[48,768]{1,0:T(8,128)(2,1)S(1)}, bf16[48,768]{1,0:T(8,128)(2,1)S(1)}, u32[]{:S(2)}, u32[]{:S(2)}) collective-permute-start(bf16[48,768]{1,0:T(8,128)(2,1)S(1)} %get-tuple-element.208), channel_id=1, source_target_pairs={{0,1},{1,2},{2,3},{3,0},{4,5},{5,6},{6,7},{7,4},{8,9},{9,10},{10,1... | collective-permute-start | bytes 221192 | tf_op jit(solution)/shard_map/ppermute | solution.py:757
  432.8 36.8 %collective-permute-start.51 = (bf16[288,1024]{1,0:T(8,128)(2,1)S(1)}, bf16[288,1024]{1,0:T(8,128)(2,1)S(1)}, u32[]{:S(2)}, u32[]{:S(2)}) collective-permute-start(bf16[288,1024]{1,0:T(8,128)(2,1)S(1)} %get-tuple-element.174), channel_id=1, source_target_pairs={{0,1},{1,2},{2,3},{3,0},{4,5},{5,6},{6,7},{7,4},{8,9},{9,10},{10,1... | collective-permute-start | bytes 1769480 | tf_op jit(solution)/shard_map/ppermute | solution.py:757
  469.9 12.5 %collective-permute-start.61 = (bf16[224,1024]{1,0:T(8,128)(2,1)S(1)}, bf16[224,1024]{1,0:T(8,128)(2,1)S(1)}, u32[]{:S(2)}, u32[]{:S(2)}) collective-permute-start(bf16[224,1024]{1,0:T(8,128)(2,1)S(1)} %maximum_maximum_fusion), channel_id=1, source_target_pairs={{0,16},{4,20},{8,24},{12,28},{16,0},{20,4},{24,8},{28,12},{1,17},{... | collective-permute-start | bytes 1376264 | tf_op jit(solution)/shard_map/ppermute | solution.py:744
  471.5 32.6 %collective-permute-start.52 = (bf16[512,1024]{1,0:T(8,128)(2,1)S(1)}, bf16[512,1024]{1,0:T(8,128)(2,1)S(1)}, u32[]{:S(2)}, u32[]{:S(2)}) collective-permute-start(bf16[512,1024]{1,0:T(8,128)(2,1)S(1)} %get-tuple-element.177), channel_id=1, source_target_pairs={{0,1},{1,2},{2,3},{3,0},{4,5},{5,6},{6,7},{7,4},{8,9},{9,10},{10,1... | collective-permute-start | bytes 3145736 | tf_op jit(solution)/shard_map/ppermute | solution.py:757
  471.8 30.9 %collective-permute-start.60 = (bf16[224,1024]{1,0:T(8,128)(2,1)S(1)}, bf16[224,1024]{1,0:T(8,128)(2,1)S(1)}, u32[]{:S(2)}, u32[]{:S(2)}) collective-permute-start(bf16[224,1024]{1,0:T(8,128)(2,1)S(1)} %maximum_maximum_fusion), channel_id=1, source_target_pairs={{0,8},{4,12},{8,0},{12,4},{16,24},{20,28},{24,16},{28,20},{1,9},{5... | collective-permute-start | bytes 1376264 | tf_op jit(solution)/shard_map/ppermute | solution.py:744
  482.4 20.3 %collective-permute-start.62 = (bf16[224,1024]{1,0:T(8,128)(2,1)S(1)}, bf16[224,1024]{1,0:T(8,128)(2,1)S(1)}, u32[]{:S(2)}, u32[]{:S(2)}) collective-permute-start(bf16[224,1024]{1,0:T(8,128)(2,1)S(1)} %collective-permute-done.61), channel_id=1, source_target_pairs={{0,8},{4,12},{8,0},{12,4},{16,24},{20,28},{24,16},{28,20},{1,9},{5... | collective-permute-start | bytes 1376264 | tf_op jit(solution)/shard_map/ppermute | solution.py:744
  483.9 18.0 %collective-permute-start.56 = (bf16[176,1024]{1,0:T(8,128)(2,1)S(1)}, bf16[176,1024]{1,0:T(8,128)(2,1)S(1)}, u32[]{:S(2)}, u32[]{:S(2)}) collective-permute-start(bf16[176,1024]{1,0:T(8,128)(2,1)S(1)} %get-tuple-element.204), channel_id=1, source_target_pairs={{0,8},{4,12},{8,0},{12,4},{16,24},{20,28},{24,16},{28,20},{1,9},{5... | collective-permute-start | bytes 1081352 | tf_op jit(solution)/shard_map/ppermute | solution.py:744
  484.6 23.9 %collective-permute-start.57 = (bf16[176,1024]{1,0:T(8,128)(2,1)S(1)}, bf16[176,1024]{1,0:T(8,128)(2,1)S(1)}, u32[]{:S(2)}, u32[]{:S(2)}) collective-permute-start(bf16[176,1024]{1,0:T(8,128)(2,1)S(1)} %get-tuple-element.204), channel_id=1, source_target_pairs={{0,16},{4,20},{8,24},{12,28},{16,0},{20,4},{24,8},{28,12},{1,17},{... | collective-permute-start | bytes 1081352 | tf_op jit(solution)/shard_map/ppermute | solution.py:744
  501.8 8.8 %collective-permute-start.58 = (bf16[176,1024]{1,0:T(8,128)(2,1)S(1)}, bf16[176,1024]{1,0:T(8,128)(2,1)}, u32[]{:S(2)}, u32[]{:S(2)}) collective-permute-start(bf16[176,1024]{1,0:T(8,128)(2,1)S(1)} %collective-permute-done.56), channel_id=1, source_target_pairs={{0,16},{4,20},{8,24},{12,28},{16,0},{20,4},{24,8},{28,12},{1,17},{... | collective-permute-start | bytes 1081352 | tf_op jit(solution)/shard_map/ppermute | solution.py:744
  508.5 7.9 %collective-permute-start.63 = (bf16[4,224,1024]{2,1,0:T(8,128)(2,1)}, bf16[4,224,1024]{2,1,0:T(8,128)(2,1)}, u32[]{:S(2)}, u32[]{:S(2)}) collective-permute-start(bf16[4,224,1024]{2,1,0:T(8,128)(2,1)} %shard_map.311.own_b), channel_id=1, source_target_pairs={{0,4},{4,0},{8,12},{12,8},{16,20},{20,16},{24,28},{28,24},{1,5},{5... | collective-permute-start | bytes 5505032 | tf_op jit(solution)/shard_map/ppermute | solution.py:744
  512.9 3.4 collective-permute-start.59
  (79 other events, 654.5 us)

commit v4 on v3

--- a/solution.py
+++ b/solution.py
@@ -661,16 +661,16 @@
         row += cut_up.r
         spot = pl.ds(pl.multiple_of(piece * 8, 8), 8)
         small[spot, :] = left[m, row : row + 8].astype(F32)
-        row = cut_down.r
-        w_down[cut_down.spot(piece)] = right[m, 0:row].astype(F32)
+        above, below = row + 16, cut_down.r
+        w_down[cut_down.spot(piece)] = right[m, 0:below].astype(F32)
         spot = pl.ds(pl.multiple_of(piece * qkv_rows, 8), qkv_rows)
         shards, local = cut_out.shards, width // cut_out.shards
         for k in range(3):
             for d in range(shards):
                 column = k * width + lax.rem(place[1] + shards - d, shards) * local
-                part = right[m, row : row + qkv_rows, d * local : (d + 1) * local].astype(F32)
+                source, row = (right, below + (k - 1) * qkv_rows) if k else (left, above)
+                part = source[m, row : row + qkv_rows, d * local : (d + 1) * local].astype(F32)
                 w_qkv[spot, pl.ds(pl.multiple_of(column, 128), local)] = part
-            row += qkv_rows
 
 
 def widen(cuts, qkv_rows, place, own_a, other_a, own_b, other_b):
@@ -768,6 +768,20 @@
         more = {m | bit: swap(part, bit, replicas) for m, part in parts.items()}
         parts |= {m: part if n else pause(part) for m, part in more.items()}
     return [parts[2 * m] for m in range(replicas // 2)]
+
+
+def share_both(upper, lower, replicas):
+    first, second = {0: upper}, {0: lower}
+    for one, two in zip(chip_bits(replicas, False), chip_bits(replicas, True)):
+        more = {m | one: swap(part, one, replicas) for m, part in first.items()}
+        even = {m | two: swap(part, two, replicas) for m, part in second.items()}
+        if len(first) == 1 and replicas > 4:
+            more = {m: gate(part, *even.values()) for m, part in more.items()}
+            even = {m: gate(part, *more.values()) for m, part in even.items()}
+        first |= more
+        second |= even
+    slots = [2 * m for m in range(replicas // 2)]
+    return jnp.stack([first[m] for m in slots]), jnp.stack([second[m] for m in slots])
 
 
 def share(piece, replicas, reverse=False, pause=lambda part: part):
@@ -1131,11 +1145,15 @@
         mark = down.step(mark)
         mark = up.step(mark)
     out, mark = close_parts(out, (mark,))
-    for d in [*range(2, shards), 0]:
+    others = list(range(2, shards))
+    for d in [*others, 0]:
         parts[d], mark = hidden_grad(
             place, blocks[d], dq, dk, dv, weight_qkv, d, shards, (mark,)
         )
         first_sums += mark
+        if d == 2:
+            step, mark = join(travel, parts[d][None], 0, (mark,))
+            travel = turn(step, shards)
 
     blank = jnp.zeros((width,), F32)
     grad_bias_q = lax.dynamic_update_slice(blank, bias_sums[:, 0].reshape(-1), (start_at,))
@@ -1155,13 +1173,12 @@
     count = small.shape[1] // replicas
     small = small.reshape(shards, replicas, count)
     small = jnp.pad(small, ((0, 0), (0, 0), (0, 3 * local - count)))
-    others = list(range(2, shards))
-    if others:
-        step, mark = join(travel, parts[others[0]][None], 0, (mark,))
-        travel = turn(step, shards)
     keep, send, mark = qkv_grad(place, hiddens, dq, dk, dv, small, slim, shards, (mark,))
     got = swap(send, 1, replicas)
 
+    late = None
+    if others[1:]:
+        late, mark = join(travel, parts[others[1]][None], 0, (mark,))
     sums_all, first, mark = close(([out], up.pair, down.pair), (mark,))
     ring = turn(first, shards)
     *qkv, mark = spread(keep, got, (mark,))
@@ -1174,7 +1191,9 @@
         if come is None:
             piece, mark = gather_sum(place, qkv, (mark,))
             come = [piece[0]] + [turn(piece[e], shards, e) for e in range(1, shards)]
-    for d in others[1:]:
+    if late is not None:
+        travel = turn(gate(late, mark), shards)
+    for d in others[2:]:
         step, mark = join(travel, parts[d][None], 0, (mark,))
         travel = turn(step, shards)
     input_grad, last_mark = last(tokens, travel, parts[0], dx2, gain_one)
@@ -1187,10 +1206,10 @@
     )
     row_small = rnd(sum(block[slim, :count].astype(F32) for block in come))
     row_small = jnp.pad(row_small[None], ((0, 15), (0, width - count)))
-    upper = jnp.concatenate([total[:edge], row_small], 0)
-    lower = jnp.concatenate([total[edge:], rows_qkv], 0)
-    own_a = gate(jnp.stack(share_chips(upper, replicas, False)), last_mark)
-    own_b = gate(jnp.stack(share_chips(lower, replicas, True)), last_mark)
+    upper = jnp.concatenate([total[:edge], row_small, rows_qkv[:slim]], 0)
+    lower = jnp.concatenate([total[edge:], rows_qkv[slim:]], 0)
+    own_a, own_b = share_both(upper, lower, replicas)
+    own_a, own_b = gate(own_a, last_mark), gate(own_b, last_mark)
     out_w_out, out_w_up, out_w_down, out_w_qkv, total = widen(
         cuts, slim, place, own_a, swap(own_a, 1, replicas), own_b, swap(own_b, 1, replicas)
     )

time: 535 us -> 516 us (0.964)
  waiting for transfers between devices: 214 us -> 176 us
  starting transfers between devices: 59.7 us -> 77.2 us
    ppermute x43, waiting for transfers between devices: 75.6 us -> 53.1 us  [swap(): return lax.ppermute(value, 'dp', [(i, i ^ bit) for i in range(replicas)])]
    ppermute x43, starting transfers between devices: 27.1 us -> 44.1 us  [swap(): return lax.ppermute(value, 'dp', [(i, i ^ bit) for i in range(replicas)])]
    ppermute x21, waiting for transfers between devices: 136 us -> 119 us  [turn(): lax.ppermute(value, 'fsdp', [(i, (i + step) % shards) for i in range(shar...]
    unnamed x188 -> x214, local copies, waits for them, and re-layouts: 32.2 us -> 39.2 us
  transfers between devices with their start and end apart: 66 -> 66, of which waited for: 28 -> 29; matrix products, arithmetic and copies ran while one was open for 5% -> 5% of each run, Pallas kernels for 28% -> 28%
where the time goes in v4:
time: 516 us; the launch traced here: 508 us
  Pallas kernels  182 us (35%)
  waiting for transfers between devices  176 us (34%)
  starting transfers between devices  77.2 us (15%)
  local copies, waits for them, and re-layouts  58.7 us (11%)
  other arithmetic  12.2 us (2%)
    ppermute x21, waiting for transfers between devices, turn(): lax.ppermute(value, 'fsdp', [(i, (i + step) % shards) for i in range(shar...  119 us
    ppermute x43, waiting for transfers between devices, swap(): return lax.ppermute(value, 'dp', [(i, i ^ bit) for i in range(replicas)])  53.1 us
    ppermute x43, starting transfers between devices, swap(): return lax.ppermute(value, 'dp', [(i, i ^ bit) for i in range(replicas)])  44.1 us
    unnamed x214, local copies, waits for them, and re-layouts  39.2 us
    pallas_call x1, Pallas kernels, attend_grad(): pl.pallas_call(functools.partial(attend_grad_kernel, group_len, head_dim)...  28.7 us
    pallas_call x4, Pallas kernels, wide_grad(): pl.pallas_call(functools.partial(wide_kernel, cut, other, reverse, len(le...  25.2 us
    pallas_call x1, Pallas kernels, feed_forward(): pl.pallas_call(functools.partial(forward_kernel, cuts, min(1024, hidden))...  24.3 us
    ppermute x21, starting transfers between devices, turn(): lax.ppermute(value, 'fsdp', [(i, (i + step) % shards) for i in range(shar...  23.9 us
  transfers between devices with their start and end apart: 66, of which 29 were waited for; matrix products, arithmetic and copies ran while one was open for 5% of the time, Pallas kernels for 28%

profile of v4, /device:TPU:0, one launch (start us, length us, event | category | flops | bytes accessed | tf_op | source)
XLA Modules:
  0.0 508.0 jit_solution(16181396600647248401)
XLA Ops:
  6.1 3.0 collective-permute-start.3
  9.2 2.0 collective-permute-start.4
  11.4 2.1 collective-permute-start
  14.5 4.1 all-to-all-start
  19.6 18.4 %collective-permute-done = bf16[1,3072]{1,0:T(2,128)(2,1)S(1)} collective-permute-done((bf16[1,3072]{1,0:T(2,128)(2,1)S(1)}, bf16[1,3072]{1,0:T(2,128)(2,1)S(1)}, u32[]{:S(2)}, u32[]{:S(2)}) %collective-permute-start) | collective-permute-done | bytes 6176 | tf_op jit(solution)/shard_map/ppermute | solution.py:757
  39.4 3.2 all-to-all-done.refs_0_
  47.2 3.8 collective-permute-start.14
  53.6 5.4 %collective-permute-done.12 = bf16[4,32,768]{2,1,0:T(8,128)(2,1)S(1)} collective-permute-done((bf16[4,32,768]{2,1,0:T(8,128)(2,1)S(1)}, bf16[4,32,768]{2,1,0:T(8,128)(2,1)S(1)}, u32[]{:S(2)}, u32[]{:S(2)}) %collective-permute-start.12) | collective-permute-done | bytes 196640 | tf_op jit(solution)/shard_map/ppermute | solution.py:744
  63.6 2.6 shard_map.274
  67.1 8.2 %collective-permute-done.5.block = bf16[512,1024]{1,0:T(8,128)(2,1)S(1)} collective-permute-done((bf16[512,1024]{1,0:T(8,128)(2,1)}, bf16[512,1024]{1,0:T(8,128)(2,1)S(1)}, u32[]{:S(2)}, u32[]{:S(2)}) %collective-permute-start.5) | collective-permute-done | bytes 1048608 | tf_op jit(solution)/shard_map/ppermute | solution.py:757
  75.3 2.6 shard_map.275
  77.9 17.0 %collective-permute-done.14.block = bf16[512,1024]{1,0:T(8,128)(2,1)S(1)} collective-permute-done((bf16[512,1024]{1,0:T(8,128)(2,1)}, bf16[512,1024]{1,0:T(8,128)(2,1)S(1)}, u32[]{:S(2)}, u32[]{:S(2)}) %collective-permute-start.14) | collective-permute-done | bytes 1048608 | tf_op jit(solution)/shard_map/ppermute | solution.py:757
  94.9 2.1 shard_map.276
  100.2 1.7 slice_bitcast_fusion
  101.9 7.5 %collective-permute-done.18.refs_0_ = bf16[288,1024]{1,0:T(8,128)(2,1)} collective-permute-done((bf16[288,1024]{1,0:T(8,128)(2,1)}, bf16[288,1024]{1,0:T(8,128)(2,1)}, u32[]{:S(2)}, u32[]{:S(2)}) %collective-permute-start.18) | collective-permute-done | bytes 589856 | tf_op jit(solution)/shard_map/ppermute | solution.py:757
  109.4 1.7 slice_bitcast_fusion.1
  112.3 2.2 pad_maximum_fusion.2.refs_4_.refs_0_
  120.1 19.2 %collective-permute-done.20.refs_0_ = bf16[3,160,1024]{2,1,0:T(8,128)(2,1)S(1)} collective-permute-done((bf16[3,160,1024]{2,1,0:T(8,128)(2,1)}, bf16[3,160,1024]{2,1,0:T(8,128)(2,1)S(1)}, u32[]{:S(2)}, u32[]{:S(2)}) %collective-permute-start.20) | collective-permute-done | bytes 983072 | tf_op jit(solution)/shard_map/ppermute | solution.py:744
  145.1 2.1 shard_map.277
  148.8 5.5 %collective-permute-done.27.refs_14_.refs_10_ = bf16[3,128,1024]{2,1,0:T(8,128)(2,1)} collective-permute-done((bf16[3,128,1024]{2,1,0:T(8,128)(2,1)}, bf16[3,128,1024]{2,1,0:T(8,128)(2,1)}, u32[]{:S(2)}, u32[]{:S(2)}) %collective-permute-start.27) | collective-permute-done | bytes 786464 | tf_op jit(solution)/shard_map/ppermute | solution.py:744
  155.4 17.7 %shard_map.278 = (bf16[2048,256]{1,0:T(8,128)(2,1)}, f32[2,2,2048]{2,1,0:T(2,128)}) custom-call(bf16[2048,768]{1,0:T(8,128)(2,1)} %copy-done.2, bf16[2048,768]{1,0:T(8,128)(2,1)} %copy-done.2, bf16[2048,768]{1,0:T(8,128)(2,1)} %copy-done.2, s32[1,2048]{1,0:T(1,128)} %bitcast.156), custom_call_target="tpu_custom_call" | custom-call | flops 1800000000 | bytes 1 | tf_op jit(solution)/shard_map/pallas_call | solution.py:129
  173.8 1.9 constant_dynamic-slice_fusion.1
  176.0 10.7 %collective-permute-done.15.refs_1_ = bf16[512,256]{1,0:T(8,128)(2,1)S(1)} collective-permute-done((bf16[512,256]{1,0:T(8,128)(2,1)S(1)}, bf16[512,256]{1,0:T(8,128)(2,1)S(1)}, u32[]{:S(2)}, u32[]{:S(2)}) %collective-permute-start.15) | collective-permute-done | bytes 262176 | tf_op jit(solution)/shard_map/ppermute | solution.py:757
  187.2 10.1 %collective-permute-done.16.refs_2_ = bf16[512,256]{1,0:T(8,128)(2,1)} collective-permute-done((bf16[512,256]{1,0:T(8,128)(2,1)S(1)}, bf16[512,256]{1,0:T(8,128)(2,1)}, u32[]{:S(2)}, u32[]{:S(2)}) %collective-permute-start.16) | collective-permute-done | bytes 262176 | tf_op jit(solution)/shard_map/ppermute | solution.py:757
  201.3 3.0 collective-permute-done.30.refs_17_.refs_13_
  205.5 24.3 %shard_map.284 = (bf16[512,1024]{1,0:T(8,128)(2,1)}, bf16[512,1024]{1,0:T(8,128)(2,1)}, f32[512,1024]{1,0:T(8,128)}, bf16[512,4096]{1,0:T(8,128)(2,1)}, bf16[512,4096]{1,0:T(8,128)(2,1)}) custom-call(s32[2]{0:T(128)} %copy-done.49, bf16[512,1024]{1,0:T(8,128)(2,1)} %tokens.3, f32[8,1024]{1,0:T(8,128)} %concatenate.41.vectors, f32[1,4096]{1,0:T(1,128)} %bitcast.158, ...), custom_call_target="tpu_custom_call" | custom-call | flops 2400000000 | bytes 1 | tf_op jit(solution)/shard_map/pallas_call | solution.py:328
  229.9 7.1 %shard_map.286 = (bf16[4,4,128,1024]{3,2,1,0:T(8,128)(2,1)}, f32[8,128]{1,0:T(8,128)}) custom-call(s32[2]{0:T(128)} %copy-done.49, bf16[512,4096]{1,0:T(8,128)(2,1)} %get-tuple-element.118.left, bf16[512,1024]{1,0:T(8,128)(2,1)} %right.3), custom_call_target="tpu_custom_call" | custom-call | flops 750000000 | bytes 1 | tf_op jit(solution)/shard_map/pallas_call | solution.py:573
  237.1 23.4 %shard_map.285 = (bf16[512,4096]{1,0:T(8,128)(2,1)}, f32[512,1024]{1,0:T(8,128)}, bf16[512,1024]{1,0:T(8,128)(2,1)}, bf16[512,1024]{1,0:T(8,128)(2,1)}, f32[1,4096]{1,0:T(1,128)}, /*index=5*/f32[8,1024]{1,0:T(8,128)}) custom-call(s32[2]{0:T(128)} %copy-done.49, bf16[512,1024]{1,0:T(8,128)(2,1)} %right.3, bf16[512,4096]{1,0:T(8,128)(2,1)} %get-tuple-element.112.slope, ...), custom_call_target="tpu_custom_call" | custom-call | flops 2400000000 | bytes 1 | tf_op jit(solution)/shard_map/pallas_call | solution.py:384
  260.5 7.5 %shard_map.287 = (bf16[4,4,128,1024]{3,2,1,0:T(8,128)(2,1)}, f32[8,128]{1,0:T(8,128)}) custom-call(s32[2]{0:T(128)} %copy-done.49, bf16[512,4096]{1,0:T(8,128)(2,1)} %get-tuple-element.116.right, bf16[512,1024]{1,0:T(8,128)(2,1)} %get-tuple-element.117.refs_0_, f32[8,128]{1,0:T(8,128)} %get-tuple-element.119.refs_1_), custom_call_target="tpu_custom_call" | custom-call | flops 600000000 | bytes 1 | tf_op jit(solution)/shard_map/pallas_call | solution.py:509
  269.4 5.2 %all-to-all-start.1 = ((bf16[512,4,256]{2,0,1:T(8,128)(2,1)}), bf16[512,4,256]{2,0,1:T(8,128)(2,1)S(1)}, u32[]{:S(2)}, u32[]{:S(2)}) async-start(bf16[512,4,256]{2,0,1:T(8,128)(2,1)} %bitcast.121), calls=%async_computation.1 | async-start | bytes 2097152 | tf_op jit(solution)/shard_map/all_to_all | solution.py:1105
  274.6 4.0 shard_map.288
  278.7 8.4 %shard_map.289 = (bf16[2,4,128,1024]{3,2,1,0:T(8,128)(2,1)}, bf16[2,4,128,1024]{3,2,1,0:T(8,128)(2,1)}, f32[8,128]{1,0:T(8,128)}) custom-call(s32[2]{0:T(128)} %copy-done.49, bf16[512,4096]{1,0:T(8,128)(2,1)} %get-tuple-element.118.left, bf16[512,1024]{1,0:T(8,128)(2,1)} %right.3, bf16[4,4,128,1024]{3,2,1,0:T(8,128)(2,1)} %collective-permute-done.35.got, ...), custom_call_target="tpu_custom_call" | custom-call | flops 750000000 | bytes 1 | tf_op jit(solution)/shard_map/pallas_call | solution.py:573
  288.5 9.1 %shard_map.290 = (bf16[2,4,128,1024]{3,2,1,0:T(8,128)(2,1)}, bf16[2,4,128,1024]{3,2,1,0:T(8,128)(2,1)}, f32[8,128]{1,0:T(8,128)}) custom-call(s32[2]{0:T(128)} %copy-done.49, bf16[512,4096]{1,0:T(8,128)(2,1)} %get-tuple-element.116.right, bf16[512,1024]{1,0:T(8,128)(2,1)} %get-tuple-element.117.refs_0_, ...), custom_call_target="tpu_custom_call" | custom-call | flops 600000000 | bytes 1 | tf_op jit(solution)/shard_map/pallas_call | solution.py:509
  300.3 4.5 shard_map.291
  305.8 28.7 %shard_map.292 = (bf16[2048,256]{1,0:T(8,128)(2,1)}, bf16[2048,256]{1,0:T(8,128)(2,1)}, bf16[2048,256]{1,0:T(8,128)(2,1)}, f32[2,2,128]{2,1,0:T(2,128)}) custom-call(bf16[2048,768]{1,0:T(8,128)(2,1)} %copy-done.2, bf16[2048,768]{1,0:T(8,128)(2,1)} %copy-done.2, bf16[2048,768]{1,0:T(8,128)(2,1)} %copy-done.2, s32[1,2048]{1,0:T(1,128)} %bitcast.157, ...), custom_call_target="tpu_custom_call" | custom-call | flops 2800000000 | bytes 1 | tf_op jit(solution)/shard_map/pallas_call | solution.py:148
  338.2 2.9 shard_map.293
  341.1 2.4 collective-permute-start.36
  347.5 2.4 collective-permute-start.39
  352.1 2.7 shard_map.294
  356.8 2.7 shard_map.295
  364.2 1.9 shard_map.297
  366.2 2.4 collective-permute-done.36.travel
  368.5 2.4 shard_map.298
  371.1 1.9 shard_map.299
  374.0 1.9 shard_map.300
  383.1 7.1 %shard_map.301 = (bf16[4,4,48,768]{3,2,1,0:T(8,128)(2,1)}, bf16[4,4,48,768]{3,2,1,0:T(8,128)(2,1)}, f32[8,128]{1,0:T(8,128)S(1)}) custom-call(s32[2]{0:T(128)S(1)} %copy-done.50, bf16[2048,256]{1,0:T(8,128)(2,1)S(1)} %copy-done.7, bf16[2048,256]{1,0:T(8,128)(2,1)S(1)} %copy-done.10, bf16[2048,256]{1,0:T(8,128)(2,1)S(1)} %copy-done.13, ...), custom_call_target="tpu_custom_call" | custom-call | flops 650000000 | bytes 1 | tf_op jit(solution)/shard_map/pallas_call | solution.py:634
  390.3 7.2 %collective-permute-done.42.travel = bf16[512,1024]{1,0:T(8,128)(2,1)} collective-permute-done((bf16[512,1024]{1,0:T(8,128)(2,1)}, bf16[512,1024]{1,0:T(8,128)(2,1)}, u32[]{:S(2)}, u32[]{:S(2)}) %collective-permute-start.42) | collective-permute-done | bytes 1048608 | tf_op jit(solution)/shard_map/ppermute | solution.py:757
  399.0 2.6 collective-permute-done.43.refs_2_
  407.4 10.2 %collective-permute-done.45.travel = bf16[288,1024]{1,0:T(8,128)(2,1)S(1)} collective-permute-done((bf16[288,1024]{1,0:T(8,128)(2,1)S(1)}, bf16[288,1024]{1,0:T(8,128)(2,1)S(1)}, u32[]{:S(2)}, u32[]{:S(2)}) %collective-permute-start.45) | collective-permute-done | bytes 589856 | tf_op jit(solution)/shard_map/ppermute | solution.py:757
  419.0 3.5 collective-permute-start.55
  422.5 1.7 collective-permute-start.53
  424.2 9.0 %collective-permute-done.55 = bf16[48,768]{1,0:T(8,128)(2,1)S(1)} collective-permute-done((bf16[48,768]{1,0:T(8,128)(2,1)S(1)}, bf16[48,768]{1,0:T(8,128)(2,1)S(1)}, u32[]{:S(2)}, u32[]{:S(2)}) %collective-permute-start.55) | collective-permute-done | bytes 73760 | tf_op jit(solution)/shard_map/ppermute | solution.py:757
  433.2 2.8 collective-permute-done.47.travel
  436.1 2.1 collective-permute-start.51
  438.2 12.0 %collective-permute-done.54 = bf16[48,768]{1,0:T(8,128)(2,1)S(1)} collective-permute-done((bf16[48,768]{1,0:T(8,128)(2,1)S(1)}, bf16[48,768]{1,0:T(8,128)(2,1)S(1)}, u32[]{:S(2)}, u32[]{:S(2)}) %collective-permute-start.54) | collective-permute-done | bytes 73760 | tf_op jit(solution)/shard_map/ppermute | solution.py:757
  452.8 15.6 %collective-permute-start.57 = (bf16[192,1024]{1,0:T(8,128)(2,1)S(1)}, bf16[192,1024]{1,0:T(8,128)(2,1)S(1)}, u32[]{:S(2)}, u32[]{:S(2)}) collective-permute-start(bf16[192,1024]{1,0:T(8,128)(2,1)S(1)} %maximum_maximum_fusion), channel_id=1, source_target_pairs={{0,16},{4,20},{8,24},{12,28},{16,0},{20,4},{24,8},{28,12},{1,17},{... | collective-permute-start | bytes 1179656 | tf_op jit(solution)/shard_map/ppermute | solution.py:744
  468.5 5.7 %collective-permute-done.57.refs_1_.refs_0_ = bf16[192,1024]{1,0:T(8,128)(2,1)S(1)} collective-permute-done((bf16[192,1024]{1,0:T(8,128)(2,1)S(1)}, bf16[192,1024]{1,0:T(8,128)(2,1)S(1)}, u32[]{:S(2)}, u32[]{:S(2)}) %collective-permute-start.57) | collective-permute-done | bytes 393248 | tf_op jit(solution)/shard_map/ppermute | solution.py:744
  475.7 3.0 collective-permute-start.59
  480.8 4.4 collective-permute-done.59
  485.2 2.7 pad_maximum_fusion.refs_0_
  487.9 2.6 shard_map.310
  492.1 2.5 pad_maximum_fusion.1.refs_0_
  494.5 3.6 collective-permute-done.63.other_b
  499.6 7.0 %shard_map.315 = (f32[256,1024]{1,0:T(8,128)}, f32[256,4096]{1,0:T(8,128)}, f32[1024,1024]{1,0:T(8,128)}, f32[256,3072]{1,0:T(8,128)}, f32[64,1024]{1,0:T(8,128)S(1)}) custom-call(s32[2]{0:T(128)S(1)} %copy-done.50, bf16[4,208,1024]{2,1,0:T(8,128)(2,1)S(1)} %copy-done.16, bf16[4,208,1024]{2,1,0:T(8,128)(2,1)} %collective-permute-done.60.other_a, ...), custom_call_target="tpu_custom_call" | custom-call | flops 700000000 | bytes 1 | tf_op jit(solution)/shard_map/pallas_call | solution.py:680
  (405 shorter events, 97.0 us)
Async XLA Ops:
  6.1 36.5 %collective-permute-start.3 = (bf16[288,1024]{1,0:T(8,128)(2,1)}, bf16[288,1024]{1,0:T(8,128)(2,1)}, u32[]{:S(2)}, u32[]{:S(2)}) collective-permute-start(bf16[288,1024]{1,0:T(8,128)(2,1)} %shard_map.271), channel_id=1, source_target_pairs={{0,1},{1,2},{2,3},{3,0},{4,5},{5,6},{6,7},{7,4},{8,9},{9,10},{10,1... | collective-permute-start | bytes 1769480 | tf_op jit(solution)/shard_map/ppermute | solution.py:757
  9.2 33.5 %collective-permute-start.4 = (bf16[288,1024]{1,0:T(8,128)(2,1)}, bf16[288,1024]{1,0:T(8,128)(2,1)S(1)}, u32[]{:S(2)}, u32[]{:S(2)}) collective-permute-start(bf16[288,1024]{1,0:T(8,128)(2,1)} %shard_map.271), channel_id=1, source_target_pairs={{0,3},{1,0},{2,1},{3,2},{4,7},{5,4},{6,5},{7,6},{8,11},{9,8},{10,9... | collective-permute-start | bytes 1769480 | tf_op jit(solution)/shard_map/ppermute | solution.py:757
  11.4 26.7 %collective-permute-start = (bf16[1,3072]{1,0:T(2,128)(2,1)S(1)}, bf16[1,3072]{1,0:T(2,128)(2,1)S(1)}, u32[]{:S(2)}, u32[]{:S(2)}) collective-permute-start(bf16[1,3072]{1,0:T(2,128)(2,1)S(1)} %constant_dynamic-update-slice_fusion.refs_1_), channel_id=1, source_target_pairs={{0,3},{1,0},{2,1},{3,2},{4,7},{5,4},{6,5},{7,6},{8,11},{9,8},{10,9... | collective-permute-start | bytes 18440 | tf_op jit(solution)/shard_map/ppermute | solution.py:757
  13.5 25.6 %collective-permute-start.1 = (bf16[1,3072]{1,0:T(2,128)(2,1)S(1)}, bf16[1,3072]{1,0:T(2,128)(2,1)S(1)}, u32[]{:S(2)}, u32[]{:S(2)}) collective-permute-start(bf16[1,3072]{1,0:T(2,128)(2,1)S(1)} %constant_dynamic-update-slice_fusion.refs_1_), channel_id=1, source_target_pairs={{0,2},{1,3},{2,0},{3,1},{4,6},{5,7},{6,4},{7,5},{8,10},{9,11},{10,... | collective-permute-start | bytes 18440 | tf_op jit(solution)/shard_map/ppermute | solution.py:757
  13.5 25.6 %collective-permute-start.2 = (bf16[1,3072]{1,0:T(2,128)(2,1)S(1)}, bf16[1,3072]{1,0:T(2,128)(2,1)S(1)}, u32[]{:S(2)}, u32[]{:S(2)}) collective-permute-start(bf16[1,3072]{1,0:T(2,128)(2,1)S(1)} %constant_dynamic-update-slice_fusion.refs_1_), channel_id=1, source_target_pairs={{0,1},{1,2},{2,3},{3,0},{4,5},{5,6},{6,7},{7,4},{8,9},{9,10},{10,1... | collective-permute-start | bytes 18440 | tf_op jit(solution)/shard_map/ppermute | solution.py:757
  14.5 28.1 %all-to-all-start = ((bf16[4,32,768]{2,1,0:T(8,128)(2,1)}), bf16[4,32,768]{2,1,0:T(8,128)(2,1)S(1)}, u32[]{:S(2)}, u32[]{:S(2)}) async-start(bf16[4,32,768]{2,1,0:T(8,128)(2,1)} %reshape.206.refs_1_), calls=%async_computation | async-start | bytes 393216 | tf_op jit(solution)/shard_map/all_to_all | solution.py:1070
  44.1 7.5 %collective-permute-start.7 = (bf16[4,32,768]{2,1,0:T(8,128)(2,1)}, bf16[4,32,768]{2,1,0:T(8,128)(2,1)S(1)}, u32[]{:S(2)}, u32[]{:S(2)}) collective-permute-start(bf16[4,32,768]{2,1,0:T(8,128)(2,1)} %shard_map.273), channel_id=1, source_target_pairs={{0,4},{4,0},{8,12},{12,8},{16,20},{20,16},{24,28},{28,24},{1,5},{5... | collective-permute-start | bytes 589832 | tf_op jit(solution)/shard_map/ppermute | solution.py:744
  44.2 7.5 %collective-permute-start.8 = (bf16[4,32,768]{2,1,0:T(8,128)(2,1)}, bf16[4,32,768]{2,1,0:T(8,128)(2,1)S(1)}, u32[]{:S(2)}, u32[]{:S(2)}) collective-permute-start(bf16[4,32,768]{2,1,0:T(8,128)(2,1)} %shard_map.273), channel_id=1, source_target_pairs={{0,8},{4,12},{8,0},{12,4},{16,24},{20,28},{24,16},{28,20},{1,9},{5... | collective-permute-start | bytes 589832 | tf_op jit(solution)/shard_map/ppermute | solution.py:744
  45.7 7.5 %collective-permute-start.10 = (bf16[4,32,768]{2,1,0:T(8,128)(2,1)}, bf16[4,32,768]{2,1,0:T(8,128)(2,1)S(1)}, u32[]{:S(2)}, u32[]{:S(2)}) collective-permute-start(bf16[4,32,768]{2,1,0:T(8,128)(2,1)} %shard_map.273), channel_id=1, source_target_pairs={{0,16},{4,20},{8,24},{12,28},{16,0},{20,4},{24,8},{28,12},{1,17},{... | collective-permute-start | bytes 589832 | tf_op jit(solution)/shard_map/ppermute | solution.py:744
  47.2 28.1 %collective-permute-start.5 = (bf16[512,1024]{1,0:T(8,128)(2,1)}, bf16[512,1024]{1,0:T(8,128)(2,1)S(1)}, u32[]{:S(2)}, u32[]{:S(2)}) collective-permute-start(bf16[512,1024]{1,0:T(8,128)(2,1)} %shard_map.272.block), channel_id=1, source_target_pairs={{0,1},{1,2},{2,3},{3,0},{4,5},{5,6},{6,7},{7,4},{8,9},{9,10},{10,1... | collective-permute-start | bytes 3145736 | tf_op jit(solution)/shard_map/ppermute | solution.py:757
  47.2 47.6 %collective-permute-start.14 = (bf16[512,1024]{1,0:T(8,128)(2,1)}, bf16[512,1024]{1,0:T(8,128)(2,1)S(1)}, u32[]{:S(2)}, u32[]{:S(2)}) collective-permute-start(bf16[512,1024]{1,0:T(8,128)(2,1)} %shard_map.272.block), channel_id=1, source_target_pairs={{0,3},{1,0},{2,1},{3,2},{4,7},{5,4},{6,5},{7,6},{8,11},{9,8},{10,9... | collective-permute-start | bytes 3145736 | tf_op jit(solution)/shard_map/ppermute | solution.py:757
  51.7 7.3 %collective-permute-start.12 = (bf16[4,32,768]{2,1,0:T(8,128)(2,1)S(1)}, bf16[4,32,768]{2,1,0:T(8,128)(2,1)S(1)}, u32[]{:S(2)}, u32[]{:S(2)}) collective-permute-start(bf16[4,32,768]{2,1,0:T(8,128)(2,1)S(1)} %collective-permute-done.8), channel_id=1, source_target_pairs={{0,16},{4,20},{8,24},{12,28},{16,0},{20,4},{24,8},{28,12},{1,17},{... | collective-permute-start | bytes 589832 | tf_op jit(solution)/shard_map/ppermute | solution.py:744
  53.2 56.2 %collective-permute-start.18 = (bf16[288,1024]{1,0:T(8,128)(2,1)}, bf16[288,1024]{1,0:T(8,128)(2,1)}, u32[]{:S(2)}, u32[]{:S(2)}) collective-permute-start(bf16[288,1024]{1,0:T(8,128)(2,1)} %collective-permute-done.3.refs_2_.refs_1_.refs_0_), channel_id=1, source_target_pairs={{0,1},{1,2},{2,3},{3,0},{4,5},{5,6},{6,7},{7,4},{8,9},{9,10},{10,1... | collective-permute-start | bytes 1769480 | tf_op jit(solution)/shard_map/ppermute | solution.py:757
  53.3 5.7 %collective-permute-start.11 = (bf16[4,32,768]{2,1,0:T(8,128)(2,1)S(1)}, bf16[4,32,768]{2,1,0:T(8,128)(2,1)S(1)}, u32[]{:S(2)}, u32[]{:S(2)}) collective-permute-start(bf16[4,32,768]{2,1,0:T(8,128)(2,1)S(1)} %collective-permute-done.10), channel_id=1, source_target_pairs={{0,4},{4,0},{8,12},{12,8},{16,20},{20,16},{24,28},{28,24},{1,5},{5... | collective-permute-start | bytes 589832 | tf_op jit(solution)/shard_map/ppermute | solution.py:744
  114.4 24.9 %collective-permute-start.20 = (bf16[3,160,1024]{2,1,0:T(8,128)(2,1)}, bf16[3,160,1024]{2,1,0:T(8,128)(2,1)S(1)}, u32[]{:S(2)}, u32[]{:S(2)}) collective-permute-start(bf16[3,160,1024]{2,1,0:T(8,128)(2,1)} %pad_maximum_fusion.2.refs_4_.refs_0_), channel_id=1, source_target_pairs={{0,8},{4,12},{8,0},{12,4},{16,24},{20,28},{24,16},{28,20},{1,9},{5... | collective-permute-start | bytes 2949128 | tf_op jit(solution)/shard_map/ppermute | solution.py:744
  115.0 25.8 %collective-permute-start.6 = (bf16[512,1024]{1,0:T(8,128)(2,1)S(1)}, bf16[512,1024]{1,0:T(8,128)(2,1)S(1)}, u32[]{:S(2)}, u32[]{:S(2)}) collective-permute-start(bf16[512,1024]{1,0:T(8,128)(2,1)S(1)} %copy-done.25), channel_id=1, source_target_pairs={{0,1},{1,2},{2,3},{3,0},{4,5},{5,6},{6,7},{7,4},{8,9},{9,10},{10,1... | collective-permute-start | bytes 3145736 | tf_op jit(solution)/shard_map/ppermute | solution.py:757
  118.1 36.2 %collective-permute-start.27 = (bf16[3,128,1024]{2,1,0:T(8,128)(2,1)}, bf16[3,128,1024]{2,1,0:T(8,128)(2,1)}, u32[]{:S(2)}, u32[]{:S(2)}) collective-permute-start(bf16[3,128,1024]{2,1,0:T(8,128)(2,1)} %pad_maximum_fusion.3.refs_12_.refs_8_), channel_id=1, source_target_pairs={{0,8},{4,12},{8,0},{12,4},{16,24},{20,28},{24,16},{28,20},{1,9},{5... | collective-permute-start | bytes 2359304 | tf_op jit(solution)/shard_map/ppermute | solution.py:744
  119.6 35.8 %collective-permute-start.29 = (bf16[3,128,1024]{2,1,0:T(8,128)(2,1)}, bf16[3,128,1024]{2,1,0:T(8,128)(2,1)}, u32[]{:S(2)}, u32[]{:S(2)}) collective-permute-start(bf16[3,128,1024]{2,1,0:T(8,128)(2,1)} %pad_maximum_fusion.3.refs_12_.refs_8_), channel_id=1, source_target_pairs={{0,16},{4,20},{8,24},{12,28},{16,0},{20,4},{24,8},{28,12},{1,17},{... | collective-permute-start | bytes 2359304 | tf_op jit(solution)/shard_map/ppermute | solution.py:744
  120.1 55.6 %collective-permute-start.19 = (bf16[3,160,1024]{2,1,0:T(8,128)(2,1)}, bf16[3,160,1024]{2,1,0:T(8,128)(2,1)}, u32[]{:S(2)}, u32[]{:S(2)}) collective-permute-start(bf16[3,160,1024]{2,1,0:T(8,128)(2,1)} %pad_maximum_fusion.2.refs_4_.refs_0_), channel_id=1, source_target_pairs={{0,4},{4,0},{8,12},{12,8},{16,20},{20,16},{24,28},{28,24},{1,5},{5... | collective-permute-start | bytes 2949128 | tf_op jit(solution)/shard_map/ppermute | solution.py:744
  139.3 33.8 %collective-permute-start.26 = (bf16[3,128,1024]{2,1,0:T(8,128)(2,1)}, bf16[3,128,1024]{2,1,0:T(8,128)(2,1)}, u32[]{:S(2)}, u32[]{:S(2)}) collective-permute-start(bf16[3,128,1024]{2,1,0:T(8,128)(2,1)} %pad_maximum_fusion.3.refs_12_.refs_8_), channel_id=1, source_target_pairs={{0,4},{4,0},{8,12},{12,8},{16,20},{20,16},{24,28},{28,24},{1,5},{5... | collective-permute-start | bytes 2359304 | tf_op jit(solution)/shard_map/ppermute | solution.py:744
  141.8 33.9 %collective-permute-start.22 = (bf16[3,160,1024]{2,1,0:T(8,128)(2,1)}, bf16[3,160,1024]{2,1,0:T(8,128)(2,1)}, u32[]{:S(2)}, u32[]{:S(2)}) collective-permute-start(bf16[3,160,1024]{2,1,0:T(8,128)(2,1)} %pad_maximum_fusion.2.refs_4_.refs_0_), channel_id=1, source_target_pairs={{0,16},{4,20},{8,24},{12,28},{16,0},{20,4},{24,8},{28,12},{1,17},{... | collective-permute-start | bytes 2949128 | tf_op jit(solution)/shard_map/ppermute | solution.py:744
  154.3 44.5 %collective-permute-start.24 = (bf16[3,160,1024]{2,1,0:T(8,128)(2,1)}, bf16[3,160,1024]{2,1,0:T(8,128)(2,1)}, u32[]{:S(2)}, u32[]{:S(2)}) collective-permute-start(bf16[3,160,1024]{2,1,0:T(8,128)(2,1)} %shard_map.282.refs_6_.refs_2_), channel_id=1, source_target_pairs={{0,16},{4,20},{8,24},{12,28},{16,0},{20,4},{24,8},{28,12},{1,17},{... | collective-permute-start | bytes 2949128 | tf_op jit(solution)/shard_map/ppermute | solution.py:744
  155.4 43.9 %collective-permute-start.28 = (bf16[3,128,1024]{2,1,0:T(8,128)(2,1)}, bf16[3,128,1024]{2,1,0:T(8,128)(2,1)}, u32[]{:S(2)}, u32[]{:S(2)}) collective-permute-start(bf16[3,128,1024]{2,1,0:T(8,128)(2,1)} %collective-permute-done.27.refs_14_.refs_10_), channel_id=1, source_target_pairs={{0,4},{4,0},{8,12},{12,8},{16,20},{20,16},{24,28},{28,24},{1,5},{5... | collective-permute-start | bytes 2359304 | tf_op jit(solution)/shard_map/ppermute | solution.py:744
  173.2 26.2 %collective-permute-start.31 = (bf16[3,128,1024]{2,1,0:T(8,128)(2,1)}, bf16[3,128,1024]{2,1,0:T(8,128)(2,1)}, u32[]{:S(2)}, u32[]{:S(2)}) collective-permute-start(bf16[3,128,1024]{2,1,0:T(8,128)(2,1)} %shard_map.283.refs_16_.refs_12_), channel_id=1, source_target_pairs={{0,8},{4,12},{8,0},{12,4},{16,24},{20,28},{24,16},{28,20},{1,9},{5... | collective-permute-start | bytes 2359304 | tf_op jit(solution)/shard_map/ppermute | solution.py:744
  175.7 11.0 %collective-permute-start.15 = (bf16[512,256]{1,0:T(8,128)(2,1)S(1)}, bf16[512,256]{1,0:T(8,128)(2,1)S(1)}, u32[]{:S(2)}, u32[]{:S(2)}) collective-permute-start(bf16[512,256]{1,0:T(8,128)(2,1)S(1)} %get-tuple-element.199), channel_id=1, source_target_pairs={{0,1},{1,2},{2,3},{3,0},{4,5},{5,6},{6,7},{7,4},{8,9},{9,10},{10,1... | collective-permute-start | bytes 786440 | tf_op jit(solution)/shard_map/ppermute | solution.py:757
  175.7 21.5 %collective-permute-start.16 = (bf16[512,256]{1,0:T(8,128)(2,1)S(1)}, bf16[512,256]{1,0:T(8,128)(2,1)}, u32[]{:S(2)}, u32[]{:S(2)}) collective-permute-start(bf16[512,256]{1,0:T(8,128)(2,1)S(1)} %get-tuple-element.198), channel_id=1, source_target_pairs={{0,2},{1,3},{2,0},{3,1},{4,6},{5,7},{6,4},{7,5},{8,10},{9,11},{10,... | collective-permute-start | bytes 786440 | tf_op jit(solution)/shard_map/ppermute | solution.py:757
  186.8 12.0 %collective-permute-start.17 = (bf16[512,256]{1,0:T(8,128)(2,1)S(1)}, bf16[512,256]{1,0:T(8,128)(2,1)}, u32[]{:S(2)}, u32[]{:S(2)}) collective-permute-start(bf16[512,256]{1,0:T(8,128)(2,1)S(1)} %get-tuple-element.197), channel_id=1, source_target_pairs={{0,3},{1,0},{2,1},{3,2},{4,7},{5,4},{6,5},{7,6},{8,11},{9,8},{10,9... | collective-permute-start | bytes 786440 | tf_op jit(solution)/shard_map/ppermute | solution.py:757
  197.2 7.0 %collective-permute-start.23 = (bf16[3,160,1024]{2,1,0:T(8,128)(2,1)}, bf16[3,160,1024]{2,1,0:T(8,128)(2,1)S(1)}, u32[]{:S(2)}, u32[]{:S(2)}) collective-permute-start(bf16[3,160,1024]{2,1,0:T(8,128)(2,1)} %collective-permute-done.22.refs_8_.refs_4_), channel_id=1, source_target_pairs={{0,4},{4,0},{8,12},{12,8},{16,20},{20,16},{24,28},{28,24},{1,5},{5... | collective-permute-start | bytes 2949128 | tf_op jit(solution)/shard_map/ppermute | solution.py:744
  198.8 5.4 %collective-permute-start.21 = (bf16[3,160,1024]{2,1,0:T(8,128)(2,1)S(1)}, bf16[3,160,1024]{2,1,0:T(8,128)(2,1)S(1)}, u32[]{:S(2)}, u32[]{:S(2)}) collective-permute-start(bf16[3,160,1024]{2,1,0:T(8,128)(2,1)S(1)} %copy-done.59), channel_id=1, source_target_pairs={{0,4},{4,0},{8,12},{12,8},{16,20},{20,16},{24,28},{28,24},{1,5},{5... | collective-permute-start | bytes 2949128 | tf_op jit(solution)/shard_map/ppermute | solution.py:744
  198.8 6.6 %collective-permute-start.25 = (bf16[3,160,1024]{2,1,0:T(8,128)(2,1)}, bf16[3,160,1024]{2,1,0:T(8,128)(2,1)}, u32[]{:S(2)}, u32[]{:S(2)}) collective-permute-start(bf16[3,160,1024]{2,1,0:T(8,128)(2,1)} %collective-permute-done.24.refs_10_.refs_6_), channel_id=1, source_target_pairs={{0,4},{4,0},{8,12},{12,8},{16,20},{20,16},{24,28},{28,24},{1,5},{5... | collective-permute-start | bytes 2949128 | tf_op jit(solution)/shard_map/ppermute | solution.py:744
  199.3 4.9 collective-permute-start.30
  199.4 6.0 %collective-permute-start.32 = (bf16[3,128,1024]{2,1,0:T(8,128)(2,1)}, bf16[3,128,1024]{2,1,0:T(8,128)(2,1)}, u32[]{:S(2)}, u32[]{:S(2)}) collective-permute-start(bf16[3,128,1024]{2,1,0:T(8,128)(2,1)} %collective-permute-done.31.refs_18_.refs_14_), channel_id=1, source_target_pairs={{0,4},{4,0},{8,12},{12,8},{16,20},{20,16},{24,28},{28,24},{1,5},{5... | collective-permute-start | bytes 2359304 | tf_op jit(solution)/shard_map/ppermute | solution.py:744
  237.0 41.7 %collective-permute-start.35 = (bf16[4,4,128,1024]{3,2,1,0:T(8,128)(2,1)}, bf16[4,4,128,1024]{3,2,1,0:T(8,128)(2,1)}, u32[]{:S(2)}, u32[]{:S(2)}) collective-permute-start(bf16[4,4,128,1024]{3,2,1,0:T(8,128)(2,1)} %get-tuple-element.123), channel_id=1, source_target_pairs={{0,4},{4,0},{8,12},{12,8},{16,20},{20,16},{24,28},{28,24},{1,5},{5... | collective-permute-start | bytes 12582920 | tf_op jit(solution)/shard_map/ppermute | solution.py:744
  268.0 20.5 %collective-permute-start.34 = (bf16[4,4,128,1024]{3,2,1,0:T(8,128)(2,1)}, bf16[4,4,128,1024]{3,2,1,0:T(8,128)(2,1)}, u32[]{:S(2)}, u32[]{:S(2)}) collective-permute-start(bf16[4,4,128,1024]{3,2,1,0:T(8,128)(2,1)} %get-tuple-element.122), channel_id=1, source_target_pairs={{0,4},{4,0},{8,12},{12,8},{16,20},{20,16},{24,28},{28,24},{1,5},{5... | collective-permute-start | bytes 12582920 | tf_op jit(solution)/shard_map/ppermute | solution.py:744
  269.4 35.4 %all-to-all-start.1 = ((bf16[512,4,256]{2,0,1:T(8,128)(2,1)}), bf16[512,4,256]{2,0,1:T(8,128)(2,1)S(1)}, u32[]{:S(2)}, u32[]{:S(2)}) async-start(bf16[512,4,256]{2,0,1:T(8,128)(2,1)} %bitcast.121), calls=%async_computation.1 | async-start | bytes 2097152 | tf_op jit(solution)/shard_map/all_to_all | solution.py:1105
  278.7 20.5 %collective-permute-start.33 = (bf16[4,4,32,1024]{3,2,1,0:T(8,128)(2,1)}, bf16[4,4,32,1024]{3,2,1,0:T(8,128)(2,1)S(1)}, u32[]{:S(2)}, u32[]{:S(2)}) collective-permute-start(bf16[4,4,32,1024]{3,2,1,0:T(8,128)(2,1)} %get-tuple-element.121), channel_id=1, source_target_pairs={{0,4},{4,0},{8,12},{12,8},{16,20},{20,16},{24,28},{28,24},{1,5},{5... | collective-permute-start | bytes 3145736 | tf_op jit(solution)/shard_map/ppermute | solution.py:744
  287.0 60.5 %collective-permute-start.41 = (bf16[2,4,128,1024]{3,2,1,0:T(8,128)(2,1)}, bf16[2,4,128,1024]{3,2,1,0:T(8,128)(2,1)}, u32[]{:S(2)}, u32[]{:S(2)}) collective-permute-start(bf16[2,4,128,1024]{3,2,1,0:T(8,128)(2,1)} %get-tuple-element.137), channel_id=1, source_target_pairs={{0,8},{4,12},{8,0},{12,4},{16,24},{20,28},{24,16},{28,20},{1,9},{5... | collective-permute-start | bytes 6291464 | tf_op jit(solution)/shard_map/ppermute | solution.py:744
  297.6 59.1 %collective-permute-start.40 = (bf16[2,4,128,1024]{3,2,1,0:T(8,128)(2,1)}, bf16[2,4,128,1024]{3,2,1,0:T(8,128)(2,1)}, u32[]{:S(2)}, u32[]{:S(2)}) collective-permute-start(bf16[2,4,128,1024]{3,2,1,0:T(8,128)(2,1)} %get-tuple-element.135), channel_id=1, source_target_pairs={{0,16},{4,20},{8,24},{12,28},{16,0},{20,4},{24,8},{28,12},{1,17},{... | collective-permute-start | bytes 6291464 | tf_op jit(solution)/shard_map/ppermute | solution.py:744
  341.1 27.4 %collective-permute-start.36 = (bf16[512,1024]{1,0:T(8,128)(2,1)}, bf16[512,1024]{1,0:T(8,128)(2,1)}, u32[]{:S(2)}, u32[]{:S(2)}) collective-permute-start(bf16[512,1024]{1,0:T(8,128)(2,1)} %get-tuple-element.131), channel_id=1, source_target_pairs={{0,1},{1,2},{2,3},{3,0},{4,5},{5,6},{6,7},{7,4},{8,9},{9,10},{10,1... | collective-permute-start | bytes 3145736 | tf_op jit(solution)/shard_map/ppermute | solution.py:757
  345.7 15.7 %collective-permute-start.37 = (bf16[1,4,32,1024]{3,2,1,0:T(8,128)(2,1)}, bf16[1,4,32,1024]{3,2,1,0:T(8,128)(2,1)S(1)}, u32[]{:S(2)}, u32[]{:S(2)}) collective-permute-start(bf16[1,4,32,1024]{3,2,1,0:T(8,128)(2,1)} %get-tuple-element.202), channel_id=1, source_target_pairs={{0,8},{4,12},{8,0},{12,4},{16,24},{20,28},{24,16},{28,20},{1,9},{5... | collective-permute-start | bytes 786440 | tf_op jit(solution)/shard_map/ppermute | solution.py:744
  347.0 14.4 %collective-permute-start.38 = (bf16[1,4,32,1024]{3,2,1,0:T(8,128)(2,1)}, bf16[1,4,32,1024]{3,2,1,0:T(8,128)(2,1)S(1)}, u32[]{:S(2)}, u32[]{:S(2)}) collective-permute-start(bf16[1,4,32,1024]{3,2,1,0:T(8,128)(2,1)} %get-tuple-element.203), channel_id=1, source_target_pairs={{0,16},{4,20},{8,24},{12,28},{16,0},{20,4},{24,8},{28,12},{1,17},{... | collective-permute-start | bytes 786440 | tf_op jit(solution)/shard_map/ppermute | solution.py:744
  347.5 14.6 %collective-permute-start.39 = (bf16[1,4,32,1024]{3,2,1,0:T(8,128)(2,1)}, bf16[1,4,32,1024]{3,2,1,0:T(8,128)(2,1)}, u32[]{:S(2)}, u32[]{:S(2)}) collective-permute-start(bf16[1,4,32,1024]{3,2,1,0:T(8,128)(2,1)} %get-tuple-element.201), channel_id=1, source_target_pairs={{0,24},{4,28},{8,16},{12,20},{16,8},{20,12},{24,0},{28,4},{1,25},{... | collective-permute-start | bytes 786440 | tf_op jit(solution)/shard_map/ppermute | solution.py:744
  371.0 26.6 %collective-permute-start.42 = (bf16[512,1024]{1,0:T(8,128)(2,1)}, bf16[512,1024]{1,0:T(8,128)(2,1)}, u32[]{:S(2)}, u32[]{:S(2)}) collective-permute-start(bf16[512,1024]{1,0:T(8,128)(2,1)} %get-tuple-element.144), channel_id=1, source_target_pairs={{0,1},{1,2},{2,3},{3,0},{4,5},{5,6},{6,7},{7,4},{8,9},{9,10},{10,1... | collective-permute-start | bytes 3145736 | tf_op jit(solution)/shard_map/ppermute | solution.py:757
  377.0 24.6 %collective-permute-start.43 = (bf16[1,4,128,1024]{3,2,1,0:T(8,128)(2,1)}, bf16[1,4,128,1024]{3,2,1,0:T(8,128)(2,1)S(1)}, u32[]{:S(2)}, u32[]{:S(2)}) collective-permute-start(bf16[1,4,128,1024]{3,2,1,0:T(8,128)(2,1)} %copy-done.56), channel_id=1, source_target_pairs={{0,8},{4,12},{8,0},{12,4},{16,24},{20,28},{24,16},{28,20},{1,9},{5... | collective-permute-start | bytes 3145736 | tf_op jit(solution)/shard_map/ppermute | solution.py:744
  377.6 24.2 %collective-permute-start.44 = (bf16[1,4,128,1024]{3,2,1,0:T(8,128)(2,1)}, bf16[1,4,128,1024]{3,2,1,0:T(8,128)(2,1)S(1)}, u32[]{:S(2)}, u32[]{:S(2)}) collective-permute-start(bf16[1,4,128,1024]{3,2,1,0:T(8,128)(2,1)} %copy-done.55), channel_id=1, source_target_pairs={{0,16},{4,20},{8,24},{12,28},{16,0},{20,4},{24,8},{28,12},{1,17},{... | collective-permute-start | bytes 3145736 | tf_op jit(solution)/shard_map/ppermute | solution.py:744
  390.2 13.1 %collective-permute-start.46 = (bf16[4,4,48,768]{3,2,1,0:T(8,128)(2,1)}, bf16[4,4,48,768]{3,2,1,0:T(8,128)(2,1)S(1)}, u32[]{:S(2)}, u32[]{:S(2)}) collective-permute-start(bf16[4,4,48,768]{3,2,1,0:T(8,128)(2,1)} %get-tuple-element.167), channel_id=1, source_target_pairs={{0,4},{4,0},{8,12},{12,8},{16,20},{20,16},{24,28},{28,24},{1,5},{5... | collective-permute-start | bytes 3538952 | tf_op jit(solution)/shard_map/ppermute | solution.py:744
  402.5 15.2 %collective-permute-start.45 = (bf16[288,1024]{1,0:T(8,128)(2,1)S(1)}, bf16[288,1024]{1,0:T(8,128)(2,1)S(1)}, u32[]{:S(2)}, u32[]{:S(2)}) collective-permute-start(bf16[288,1024]{1,0:T(8,128)(2,1)S(1)} %get-tuple-element.164), channel_id=1, source_target_pairs={{0,1},{1,2},{2,3},{3,0},{4,5},{5,6},{6,7},{7,4},{8,9},{9,10},{10,1... | collective-permute-start | bytes 1769480 | tf_op jit(solution)/shard_map/ppermute | solution.py:757
  403.9 14.0 %collective-permute-start.48 = (bf16[4,48,768]{2,1,0:T(8,128)(2,1)S(1)}, bf16[4,48,768]{2,1,0:T(8,128)(2,1)S(1)}, u32[]{:S(2)}, u32[]{:S(2)}) collective-permute-start(bf16[4,48,768]{2,1,0:T(8,128)(2,1)S(1)} %get-tuple-element.172), channel_id=1, source_target_pairs={{0,8},{4,12},{8,0},{12,4},{16,24},{20,28},{24,16},{28,20},{1,9},{5... | collective-permute-start | bytes 884744 | tf_op jit(solution)/shard_map/ppermute | solution.py:744
  405.4 12.8 %collective-permute-start.49 = (bf16[4,48,768]{2,1,0:T(8,128)(2,1)S(1)}, bf16[4,48,768]{2,1,0:T(8,128)(2,1)S(1)}, u32[]{:S(2)}, u32[]{:S(2)}) collective-permute-start(bf16[4,48,768]{2,1,0:T(8,128)(2,1)S(1)} %get-tuple-element.173), channel_id=1, source_target_pairs={{0,16},{4,20},{8,24},{12,28},{16,0},{20,4},{24,8},{28,12},{1,17},{... | collective-permute-start | bytes 884744 | tf_op jit(solution)/shard_map/ppermute | solution.py:744
  405.9 12.3 %collective-permute-start.50 = (bf16[4,48,768]{2,1,0:T(8,128)(2,1)S(1)}, bf16[4,48,768]{2,1,0:T(8,128)(2,1)S(1)}, u32[]{:S(2)}, u32[]{:S(2)}) collective-permute-start(bf16[4,48,768]{2,1,0:T(8,128)(2,1)S(1)} %get-tuple-element.174), channel_id=1, source_target_pairs={{0,24},{4,28},{8,16},{12,20},{16,8},{20,12},{24,0},{28,4},{1,25},{... | collective-permute-start | bytes 884744 | tf_op jit(solution)/shard_map/ppermute | solution.py:744
  417.8 18.2 %collective-permute-start.47 = (bf16[288,1024]{1,0:T(8,128)(2,1)S(1)}, bf16[288,1024]{1,0:T(8,128)(2,1)S(1)}, u32[]{:S(2)}, u32[]{:S(2)}) collective-permute-start(bf16[288,1024]{1,0:T(8,128)(2,1)S(1)} %get-tuple-element.170), channel_id=1, source_target_pairs={{0,1},{1,2},{2,3},{3,0},{4,5},{5,6},{6,7},{7,4},{8,9},{9,10},{10,1... | collective-permute-start | bytes 1769480 | tf_op jit(solution)/shard_map/ppermute | solution.py:757
  419.0 14.2 %collective-permute-start.55 = (bf16[48,768]{1,0:T(8,128)(2,1)S(1)}, bf16[48,768]{1,0:T(8,128)(2,1)S(1)}, u32[]{:S(2)}, u32[]{:S(2)}) collective-permute-start(bf16[48,768]{1,0:T(8,128)(2,1)S(1)} %get-tuple-element.206), channel_id=1, source_target_pairs={{0,3},{1,0},{2,1},{3,2},{4,7},{5,4},{6,5},{7,6},{8,11},{9,8},{10,9... | collective-permute-start | bytes 221192 | tf_op jit(solution)/shard_map/ppermute | solution.py:757
  422.5 27.7 %collective-permute-start.54 = (bf16[48,768]{1,0:T(8,128)(2,1)S(1)}, bf16[48,768]{1,0:T(8,128)(2,1)S(1)}, u32[]{:S(2)}, u32[]{:S(2)}) collective-permute-start(bf16[48,768]{1,0:T(8,128)(2,1)S(1)} %get-tuple-element.207), channel_id=1, source_target_pairs={{0,2},{1,3},{2,0},{3,1},{4,6},{5,7},{6,4},{7,5},{8,10},{9,11},{10,... | collective-permute-start | bytes 221192 | tf_op jit(solution)/shard_map/ppermute | solution.py:757
  422.5 27.7 %collective-permute-start.53 = (bf16[48,768]{1,0:T(8,128)(2,1)S(1)}, bf16[48,768]{1,0:T(8,128)(2,1)S(1)}, u32[]{:S(2)}, u32[]{:S(2)}) collective-permute-start(bf16[48,768]{1,0:T(8,128)(2,1)S(1)} %get-tuple-element.208), channel_id=1, source_target_pairs={{0,1},{1,2},{2,3},{3,0},{4,5},{5,6},{6,7},{7,4},{8,9},{9,10},{10,1... | collective-permute-start | bytes 221192 | tf_op jit(solution)/shard_map/ppermute | solution.py:757
  436.1 14.1 %collective-permute-start.51 = (bf16[288,1024]{1,0:T(8,128)(2,1)S(1)}, bf16[288,1024]{1,0:T(8,128)(2,1)S(1)}, u32[]{:S(2)}, u32[]{:S(2)}) collective-permute-start(bf16[288,1024]{1,0:T(8,128)(2,1)S(1)} %get-tuple-element.177), channel_id=1, source_target_pairs={{0,1},{1,2},{2,3},{3,0},{4,5},{5,6},{6,7},{7,4},{8,9},{9,10},{10,1... | collective-permute-start | bytes 1769480 | tf_op jit(solution)/shard_map/ppermute | solution.py:757
  451.0 36.9 %collective-permute-start.52 = (bf16[512,1024]{1,0:T(8,128)(2,1)}, bf16[512,1024]{1,0:T(8,128)(2,1)S(1)}, u32[]{:S(2)}, u32[]{:S(2)}) collective-permute-start(bf16[512,1024]{1,0:T(8,128)(2,1)} %shard_map.309), channel_id=1, source_target_pairs={{0,1},{1,2},{2,3},{3,0},{4,5},{5,6},{6,7},{7,4},{8,9},{9,10},{10,1... | collective-permute-start | bytes 3145736 | tf_op jit(solution)/shard_map/ppermute | solution.py:757
  451.2 22.9 %collective-permute-start.56 = (bf16[208,1024]{1,0:T(8,128)(2,1)S(1)}, bf16[208,1024]{1,0:T(8,128)(2,1)S(1)}, u32[]{:S(2)}, u32[]{:S(2)}) collective-permute-start(bf16[208,1024]{1,0:T(8,128)(2,1)S(1)} %fusion.3), channel_id=1, source_target_pairs={{0,8},{4,12},{8,0},{12,4},{16,24},{20,28},{24,16},{28,20},{1,9},{5... | collective-permute-start | bytes 1277960 | tf_op jit(solution)/shard_map/ppermute | solution.py:744
  452.8 21.4 %collective-permute-start.57 = (bf16[192,1024]{1,0:T(8,128)(2,1)S(1)}, bf16[192,1024]{1,0:T(8,128)(2,1)S(1)}, u32[]{:S(2)}, u32[]{:S(2)}) collective-permute-start(bf16[192,1024]{1,0:T(8,128)(2,1)S(1)} %maximum_maximum_fusion), channel_id=1, source_target_pairs={{0,16},{4,20},{8,24},{12,28},{16,0},{20,4},{24,8},{28,12},{1,17},{... | collective-permute-start | bytes 1179656 | tf_op jit(solution)/shard_map/ppermute | solution.py:744
  468.4 12.4 %collective-permute-start.58 = (bf16[208,1024]{1,0:T(8,128)(2,1)S(1)}, bf16[208,1024]{1,0:T(8,128)(2,1)}, u32[]{:S(2)}, u32[]{:S(2)}) collective-permute-start(bf16[208,1024]{1,0:T(8,128)(2,1)S(1)} %fusion.3), channel_id=1, source_target_pairs={{0,16},{4,20},{8,24},{12,28},{16,0},{20,4},{24,8},{28,12},{1,17},{... | collective-permute-start | bytes 1277960 | tf_op jit(solution)/shard_map/ppermute | solution.py:744
  475.7 9.5 %collective-permute-start.59 = (bf16[208,1024]{1,0:T(8,128)(2,1)}, bf16[208,1024]{1,0:T(8,128)(2,1)}, u32[]{:S(2)}, u32[]{:S(2)}) collective-permute-start(bf16[208,1024]{1,0:T(8,128)(2,1)} %shard_map.311.refs_1_), channel_id=1, source_target_pairs={{0,16},{4,20},{8,24},{12,28},{16,0},{20,4},{24,8},{28,12},{1,17},{... | collective-permute-start | bytes 1277960 | tf_op jit(solution)/shard_map/ppermute | solution.py:744
  478.7 12.4 %collective-permute-start.61 = (bf16[192,1024]{1,0:T(8,128)(2,1)}, bf16[192,1024]{1,0:T(8,128)(2,1)}, u32[]{:S(2)}, u32[]{:S(2)}) collective-permute-start(bf16[192,1024]{1,0:T(8,128)(2,1)} %copy-done.75), channel_id=1, source_target_pairs={{0,8},{4,12},{8,0},{12,4},{16,24},{20,28},{24,16},{28,20},{1,9},{5... | collective-permute-start | bytes 1179656 | tf_op jit(solution)/shard_map/ppermute | solution.py:744
  479.3 11.8 %collective-permute-start.62 = (bf16[192,1024]{1,0:T(8,128)(2,1)}, bf16[192,1024]{1,0:T(8,128)(2,1)}, u32[]{:S(2)}, u32[]{:S(2)}) collective-permute-start(bf16[192,1024]{1,0:T(8,128)(2,1)} %shard_map.313), channel_id=1, source_target_pairs={{0,8},{4,12},{8,0},{12,4},{16,24},{20,28},{24,16},{28,20},{1,9},{5... | collective-permute-start | bytes 1179656 | tf_op jit(solution)/shard_map/ppermute | solution.py:744
  491.1 7.1 %collective-permute-start.60 = (bf16[4,208,1024]{2,1,0:T(8,128)(2,1)}, bf16[4,208,1024]{2,1,0:T(8,128)(2,1)}, u32[]{:S(2)}, u32[]{:S(2)}) collective-permute-start(bf16[4,208,1024]{2,1,0:T(8,128)(2,1)} %shard_map.312.own_a), channel_id=1, source_target_pairs={{0,4},{4,0},{8,12},{12,8},{16,20},{20,16},{24,28},{28,24},{1,5},{5... | collective-permute-start | bytes 5111816 | tf_op jit(solution)/shard_map/ppermute | solution.py:744
  494.5 3.6 collective-permute-start.63
  (92 other events, 693.6 us)

commit v5 on v4

--- a/solution.py
+++ b/solution.py
@@ -284,18 +284,15 @@
 
 def gelu_both(u):
     square = u * u
-    t = jnp.tanh(GELU_A * u * (1.0 + GELU_B * square))
-    value = 0.5 * u * (1.0 + t)
-    slope = 0.5 * (1.0 + t) + 0.5 * u * (1.0 - t * t) * (GELU_A * (1.0 + 3.0 * GELU_B * square))
-    return value, slope
-
-
-def forward_kernel(cuts, step, place, tokens, vectors, bias_up, *refs):
-    shards = cuts[0].shards
-    mixed, refs = refs[:shards], refs[shards:]
-    count = 2 * cuts[0].replicas + 3
-    lists, refs = refs[:count], refs[count:]
-    out, hidden, middle, acted, slope, w_out, w_up, w_down, *sems = refs
+    s = 0.5 * jnp.tanh(u * (GELU_A + GELU_A * GELU_B * square)) + 0.5
+    value = u * s
+    return value, s + value * (1.0 - s) * (2.0 * GELU_A + 6.0 * GELU_A * GELU_B * square)
+
+
+def feed_kernel(cuts, step, place, tokens, dm, vectors, bias_up, *refs):
+    shards, count = cuts[0].shards, 2 * cuts[0].replicas + 3
+    mixed, lists, refs = refs[:shards], refs[shards : shards + count], refs[shards + count :]
+    out, hidden, acted, du, dx2, da, do, grad_up, sums, w_out, w_up, w_down, slope, *sems = refs
     loads = loads_of(cuts, place, lists, (w_out, w_up, w_down), sems)
     for copies in loads:
         start(copies)
@@ -305,71 +302,32 @@
     for d in range(shards):
         at = pl.multiple_of(lax.rem(place[1] + shards - d, shards) * local, 16)
         stream += dot_mm(mixed[d][...], w_out[pl.ds(at, local), :])
-    middle[...] = stream
-    normal, _ = moments(stream)
+    normal, scale = moments(stream)
     hidden[...] = rnd(normal * vectors[1:2, :] + vectors[2:3, :])
+    total = vectors[3:4, :] + stream
     finish(loads[1])
-    finish(loads[2])
-    total = vectors[3:4, :] + stream
     for block in range(0, w_up.shape[1], step):
         columns = slice(block, block + step)
-        u = dot_mm(hidden[...], w_up[:, columns]) + bias_up[:, columns]
-        value, grad = gelu_both(u)
+        value, grad = gelu_both(dot_mm(hidden[...], w_up[:, columns]) + bias_up[:, columns])
         value = rnd(value)
         acted[:, columns] = value
         slope[:, columns] = rnd(grad)
+        if block == 0:
+            finish(loads[2])
         total += dot_mm(value, w_down[columns, :])
     out[...] = rnd(total)
-
-
-def feed_forward(place, mixed, tokens, vectors, bias_up, cuts, lists):
-    rows, width = tokens.shape
-    hidden = bias_up.shape[1]
-    return pl.pallas_call(
-        functools.partial(forward_kernel, cuts, min(1024, hidden)),
-        in_specs=[SMEM_SPEC] + [VMEM_SPEC] * (3 + len(mixed)) + [ANY_SPEC] * len(lists),
-        out_specs=[VMEM_SPEC] * 5,
-        out_shape=[
-            jax.ShapeDtypeStruct((rows, width), BF),
-            jax.ShapeDtypeStruct((rows, width), BF),
-            jax.ShapeDtypeStruct((rows, width), F32),
-            jax.ShapeDtypeStruct((rows, hidden), BF),
-            jax.ShapeDtypeStruct((rows, hidden), BF),
-        ],
-        scratch_shapes=[
-            pltpu.VMEM((width, width), BF),
-            pltpu.VMEM((width, hidden), BF),
-            pltpu.VMEM((hidden, width), BF),
-        ]
-        + [pltpu.SemaphoreType.DMA((cut.copies,)) for cut in cuts],
-        compiler_params=pltpu.CompilerParams(vmem_limit_bytes=60 * MIB),
-        cost_estimate=cost(24),
-    )(place, tokens, vectors, bias_up, *mixed, *lists)
-
-
-def backward_kernel(cuts, step, place, dm, slope, middle, vectors, *refs):
-    count = 2 * cuts[0].replicas + 3
-    lists, refs = refs[:count], refs[count:]
-    du, dx2, da, do, grad_up, sums, w_out, w_up, w_down, *sems = refs
-    loads = loads_of(cuts, place, lists, (w_out, w_up, w_down), sems)[::-1]
-    for copies in loads:
-        start(copies)
-    finish(loads[0])
-    finish(loads[1])
-    dh2 = jnp.zeros(middle.shape, F32)
+    dh2 = jnp.zeros(stream.shape, F32)
     for block in range(0, w_up.shape[1], step):
         columns = slice(block, block + step)
         part = rnd(dot_last(dm[...], w_down[columns, :]) * slope[:, columns].astype(F32))
         du[:, columns] = part
         grad_up[:, columns] = jnp.sum(part.astype(F32), 0, keepdims=True)
         dh2 += dot_last(part, w_up[:, columns])
-    normal, scale = moments(middle[...])
     incoming = dm[...].astype(F32)
     stream = incoming + norm_grad(dh2, vectors[1:2, :], normal, scale)
     dx2[...] = stream
     low = rnd(stream)
     da[...] = low
-    finish(loads[2])
     do[...] = rnd(dot_last(low, w_out[...]))
     sums[0:1, :] = jnp.sum(incoming, 0, keepdims=True)
     sums[1:2, :] = jnp.sum(dh2 * normal, 0, keepdims=True)
@@ -378,30 +336,27 @@
     sums[4:8, :] = jnp.zeros((4, sums.shape[1]), F32)
 
 
-def feed_backward(place, dm, slope, middle, vectors, cuts, lists):
-    rows, width = dm.shape
-    hidden = slope.shape[1]
-    return pl.pallas_call(
-        functools.partial(backward_kernel, cuts, min(1024, hidden)),
-        in_specs=[SMEM_SPEC] + [VMEM_SPEC] * 4 + [ANY_SPEC] * len(lists),
-        out_specs=[VMEM_SPEC] * 6,
-        out_shape=[
-            jax.ShapeDtypeStruct((rows, hidden), BF),
-            jax.ShapeDtypeStruct((rows, width), F32),
-            jax.ShapeDtypeStruct((rows, width), BF),
-            jax.ShapeDtypeStruct((rows, width), BF),
-            jax.ShapeDtypeStruct((1, hidden), F32),
-            jax.ShapeDtypeStruct((8, width), F32),
-        ],
+def feed(place, mixed, tokens, dm, vectors, bias_up, cuts, lists):
+    rows, width = tokens.shape
+    hidden = bias_up.shape[1]
+    shapes = [((rows, width), BF), ((rows, width), BF), ((rows, hidden), BF), ((rows, hidden), BF)]
+    shapes += [((rows, width), F32), ((rows, width), BF), ((rows, width), BF)]
+    shapes += [((1, hidden), F32), ((8, width), F32)]
+    return pl.pallas_call(
+        functools.partial(feed_kernel, cuts, min(1024, hidden)),
+        in_specs=[SMEM_SPEC] + [VMEM_SPEC] * (4 + len(mixed)) + [ANY_SPEC] * len(lists),
+        out_specs=[VMEM_SPEC] * len(shapes),
+        out_shape=[jax.ShapeDtypeStruct(*shape) for shape in shapes],
         scratch_shapes=[
             pltpu.VMEM((width, width), BF),
             pltpu.VMEM((width, hidden), BF),
             pltpu.VMEM((hidden, width), BF),
+            pltpu.VMEM((rows, hidden), BF),
         ]
         + [pltpu.SemaphoreType.DMA((cut.copies,)) for cut in cuts],
         compiler_params=pltpu.CompilerParams(vmem_limit_bytes=60 * MIB),
-        cost_estimate=cost(24),
-    )(place, dm, slope, middle, vectors, *lists)
+        cost_estimate=cost(40),
+    )(place, tokens, dm, vectors, bias_up, *mixed, *lists)
 
 
 def weight_grad_kernel(cut, place, left, right, *refs):
@@ -1091,17 +1046,14 @@
         lax.dynamic_slice_in_dim(mixed, lax.rem(z + d, shards) * rows, rows) for d in range(shards)
     ]
     attended = [turn(block, shards, d) if d else block for d, block in enumerate(attended)]
-    pause = lambda part: gate(part, mark)
+    pause = lambda part: gate(part, lse)
     lists = share(upper, replicas, False, pause) + share(lower, replicas, True, pause)
     lists += [w_out, w_up, w_down]
-    output, hidden_two, middle, acted, slope = feed_forward(
-        place, attended, tokens, middle_vectors, bias_up, cuts, lists
+    dm = cotangent
+    output, hidden_two, acted, du, dx2, da, do, grad_bias_up, sums = feed(
+        place, attended, tokens, dm, middle_vectors, bias_up, cuts, lists
     )
 
-    dm = cotangent
-    du, dx2, da, do, grad_bias_up, sums = feed_backward(
-        place, dm, slope, middle, middle_vectors, cuts, lists
-    )
     grad_mixed = lax.all_to_all(do, "fsdp", 1, 0, tiled=True)
     terms = ((cut_down, acted, dm, False), (cut_up, hidden_two, du, True), (cut_out, attended, da, False))
     mark = grad_bias_up

time: 516 us -> 497 us (0.963)
  Pallas kernels: 182 us -> 166 us
  starting transfers between devices: 77.2 us -> 61.3 us
  waiting for transfers between devices: 176 us -> 189 us
    ppermute x43, starting transfers between devices: 44.1 us -> 28.9 us  [swap(): return lax.ppermute(value, 'dp', [(i, i ^ bit) for i in range(replicas)])]
    pallas_call x2 -> x1, Pallas kernels: 47.8 us -> 34 us  [feed(): pl.pallas_call(functools.partial(feed_kernel, cuts, min(1024, hidden)), i...]
    ppermute x21, waiting for transfers between devices: 119 us -> 133 us  [turn(): lax.ppermute(value, 'fsdp', [(i, (i + step) % shards) for i in range(shar...]
    unnamed x214 -> x216, local copies, waits for them, and re-layouts: 39.2 us -> 39.8 us
  transfers between devices with their start and end apart: 66 -> 66, of which waited for: 29 -> 25; matrix products, arithmetic and copies ran while one was open for 5% -> 4% of each run, Pallas kernels for 28% -> 23%
where the time goes in v5:
time: 497 us; the launch traced here: 489 us
  waiting for transfers between devices  189 us (38%)
  Pallas kernels  166 us (33%)
  starting transfers between devices  61.3 us (12%)
  local copies, waits for them, and re-layouts  57.4 us (12%)
  other arithmetic  12.1 us (2%)
    ppermute x21, waiting for transfers between devices, turn(): lax.ppermute(value, 'fsdp', [(i, (i + step) % shards) for i in range(shar...  133 us
    ppermute x43, waiting for transfers between devices, swap(): return lax.ppermute(value, 'dp', [(i, i ^ bit) for i in range(replicas)])  56.5 us
    unnamed x216, local copies, waits for them, and re-layouts  39.8 us
    pallas_call x1, Pallas kernels, feed(): pl.pallas_call(functools.partial(feed_kernel, cuts, min(1024, hidden)), i...  34 us
    ppermute x43, starting transfers between devices, swap(): return lax.ppermute(value, 'dp', [(i, i ^ bit) for i in range(replicas)])  28.9 us
    pallas_call x1, Pallas kernels, attend_grad(): pl.pallas_call(functools.partial(attend_grad_kernel, group_len, head_dim)...  28.7 us
    pallas_call x4, Pallas kernels, wide_grad(): pl.pallas_call(functools.partial(wide_kernel, cut, other, reverse, len(le...  25.1 us
    ppermute x21, starting transfers between devices, turn(): lax.ppermute(value, 'fsdp', [(i, (i + step) % shards) for i in range(shar...  23.9 us
  transfers between devices with their start and end apart: 66, of which 25 were waited for; matrix products, arithmetic and copies ran while one was open for 4% of the time, Pallas kernels for 23%

profile of v5, /device:TPU:0, one launch (start us, length us, event | category | flops | bytes accessed | tf_op | source)
XLA Modules:
  0.0 488.6 jit_solution(17428536650757413684)
XLA Ops:
  6.1 3.0 collective-permute-start.3
  9.1 2.0 collective-permute-start.4
  11.2 3.4 all-to-all-start
  14.8 3.8 collective-permute-start
  20.8 18.2 %collective-permute-done = bf16[1,3072]{1,0:T(2,128)(2,1)S(1)} collective-permute-done((bf16[1,3072]{1,0:T(2,128)(2,1)S(1)}, bf16[1,3072]{1,0:T(2,128)(2,1)S(1)}, u32[]{:S(2)}, u32[]{:S(2)}) %collective-permute-start) | collective-permute-done | bytes 6176 | tf_op jit(solution)/shard_map/ppermute | solution.py:712
  38.9 3.7 collective-permute-done.1
  44.5 1.5 collective-permute-start.8
  46.0 1.5 collective-permute-start.10
  47.9 3.4 collective-permute-start.14
  52.0 1.5 collective-permute-start.12
  54.0 5.3 %collective-permute-done.12 = bf16[4,32,768]{2,1,0:T(8,128)(2,1)S(1)} collective-permute-done((bf16[4,32,768]{2,1,0:T(8,128)(2,1)S(1)}, bf16[4,32,768]{2,1,0:T(8,128)(2,1)S(1)}, u32[]{:S(2)}, u32[]{:S(2)}) %collective-permute-start.12) | collective-permute-done | bytes 196640 | tf_op jit(solution)/shard_map/ppermute | solution.py:699
  62.3 1.6 copy-done.14
  63.9 2.6 shard_map.274
  67.5 8.1 %collective-permute-done.5.block = bf16[512,1024]{1,0:T(8,128)(2,1)S(1)} collective-permute-done((bf16[512,1024]{1,0:T(8,128)(2,1)}, bf16[512,1024]{1,0:T(8,128)(2,1)S(1)}, u32[]{:S(2)}, u32[]{:S(2)}) %collective-permute-start.5) | collective-permute-done | bytes 1048608 | tf_op jit(solution)/shard_map/ppermute | solution.py:712
  75.6 2.6 shard_map.275
  78.2 17.1 %collective-permute-done.14.block = bf16[512,1024]{1,0:T(8,128)(2,1)S(1)} collective-permute-done((bf16[512,1024]{1,0:T(8,128)(2,1)}, bf16[512,1024]{1,0:T(8,128)(2,1)S(1)}, u32[]{:S(2)}, u32[]{:S(2)}) %collective-permute-start.14) | collective-permute-done | bytes 1048608 | tf_op jit(solution)/shard_map/ppermute | solution.py:712
  95.3 2.1 shard_map.276
  98.9 10.7 %collective-permute-done.18.refs_0_ = bf16[288,1024]{1,0:T(8,128)(2,1)S(1)} collective-permute-done((bf16[288,1024]{1,0:T(8,128)(2,1)}, bf16[288,1024]{1,0:T(8,128)(2,1)S(1)}, u32[]{:S(2)}, u32[]{:S(2)}) %collective-permute-start.18) | collective-permute-done | bytes 589856 | tf_op jit(solution)/shard_map/ppermute | solution.py:712
  110.5 1.7 slice_bitcast_fusion.1
  112.2 1.7 slice_bitcast_fusion
  115.0 2.1 pad_maximum_fusion.2.refs_4_
  123.8 18.2 %collective-permute-done.20.refs_0_ = bf16[3,160,1024]{2,1,0:T(8,128)(2,1)S(1)} collective-permute-done((bf16[3,160,1024]{2,1,0:T(8,128)(2,1)}, bf16[3,160,1024]{2,1,0:T(8,128)(2,1)S(1)}, u32[]{:S(2)}, u32[]{:S(2)}) %collective-permute-start.20) | collective-permute-done | bytes 983072 | tf_op jit(solution)/shard_map/ppermute | solution.py:699
  144.1 2.6 shard_map.277
  146.7 1.7 copy-done.2
  149.4 17.6 %shard_map.278 = (bf16[2048,256]{1,0:T(8,128)(2,1)}, f32[2,2,2048]{2,1,0:T(2,128)}) custom-call(bf16[2048,768]{1,0:T(8,128)(2,1)} %copy-done.2, bf16[2048,768]{1,0:T(8,128)(2,1)} %copy-done.2, bf16[2048,768]{1,0:T(8,128)(2,1)} %copy-done.2, s32[1,2048]{1,0:T(1,128)} %bitcast.153), custom_call_target="tpu_custom_call" | custom-call | flops 1800000000 | bytes 1 | tf_op jit(solution)/shard_map/pallas_call | solution.py:129
  170.2 11.0 %collective-permute-done.15.refs_1_ = bf16[512,256]{1,0:T(8,128)(2,1)S(1)} collective-permute-done((bf16[512,256]{1,0:T(8,128)(2,1)S(1)}, bf16[512,256]{1,0:T(8,128)(2,1)S(1)}, u32[]{:S(2)}, u32[]{:S(2)}) %collective-permute-start.15) | collective-permute-done | bytes 262176 | tf_op jit(solution)/shard_map/ppermute | solution.py:712
  181.6 9.9 %collective-permute-done.16.refs_2_ = bf16[512,256]{1,0:T(8,128)(2,1)S(1)} collective-permute-done((bf16[512,256]{1,0:T(8,128)(2,1)S(1)}, bf16[512,256]{1,0:T(8,128)(2,1)S(1)}, u32[]{:S(2)}, u32[]{:S(2)}) %collective-permute-start.16) | collective-permute-done | bytes 262176 | tf_op jit(solution)/shard_map/ppermute | solution.py:712
  195.2 3.2 collective-permute-done.30.refs_17_
  199.5 34.0 %shard_map.284 = (bf16[512,1024]{1,0:T(8,128)(2,1)}, bf16[512,1024]{1,0:T(8,128)(2,1)}, bf16[512,4096]{1,0:T(8,128)(2,1)}, bf16[512,4096]{1,0:T(8,128)(2,1)}, f3...) custom-call(s32[2]{0:T(128)} %copy-done.48, ...), custom_call_target="tpu_custom_call" | custom-call | flops 4000000000 | bytes 1 | tf_op jit(solution)/shard_map/pallas_call | solution.py:345
  233.5 7.1 %shard_map.285 = (bf16[4,4,128,1024]{3,2,1,0:T(8,128)(2,1)}, f32[8,128]{1,0:T(8,128)}) custom-call(s32[2]{0:T(128)} %copy-done.48, bf16[512,4096]{1,0:T(8,128)(2,1)} %get-tuple-element.112.left, bf16[512,1024]{1,0:T(8,128)(2,1)} %right.3), custom_call_target="tpu_custom_call" | custom-call | flops 750000000 | bytes 1 | tf_op jit(solution)/shard_map/pallas_call | solution.py:528
  240.8 7.5 %shard_map.286 = (bf16[4,4,128,1024]{3,2,1,0:T(8,128)(2,1)}, f32[8,128]{1,0:T(8,128)}) custom-call(s32[2]{0:T(128)} %copy-done.48, bf16[512,4096]{1,0:T(8,128)(2,1)} %get-tuple-element.110.right, bf16[512,1024]{1,0:T(8,128)(2,1)} %get-tuple-element.111.refs_0_, f32[8,128]{1,0:T(8,128)} %get-tuple-element.113.refs_1_), custom_call_target="tpu_custom_call" | custom-call | flops 600000000 | bytes 1 | tf_op jit(solution)/shard_map/pallas_call | solution.py:464
  249.7 5.2 %all-to-all-start.1 = ((bf16[512,4,256]{2,0,1:T(8,128)(2,1)}), bf16[512,4,256]{2,0,1:T(8,128)(2,1)S(1)}, u32[]{:S(2)}, u32[]{:S(2)}) async-start(bf16[512,4,256]{2,0,1:T(8,128)(2,1)} %bitcast.121), calls=%async_computation.1 | async-start | bytes 2097152 | tf_op jit(solution)/shard_map/all_to_all | solution.py:1057
  254.8 4.1 shard_map.287
  258.9 8.3 %shard_map.288 = (bf16[2,4,128,1024]{3,2,1,0:T(8,128)(2,1)}, bf16[2,4,128,1024]{3,2,1,0:T(8,128)(2,1)}, f32[8,128]{1,0:T(8,128)}) custom-call(s32[2]{0:T(128)} %copy-done.48, bf16[512,4096]{1,0:T(8,128)(2,1)} %get-tuple-element.112.left, bf16[512,1024]{1,0:T(8,128)(2,1)} %right.3, bf16[4,4,128,1024]{3,2,1,0:T(8,128)(2,1)} %collective-permute-done.35.got, ...), custom_call_target="tpu_custom_call" | custom-call | flops 750000000 | bytes 1 | tf_op jit(solution)/shard_map/pallas_call | solution.py:528
  268.2 9.1 %shard_map.289 = (bf16[2,4,128,1024]{3,2,1,0:T(8,128)(2,1)}, bf16[2,4,128,1024]{3,2,1,0:T(8,128)(2,1)}, f32[8,128]{1,0:T(8,128)}) custom-call(s32[2]{0:T(128)} %copy-done.48, bf16[512,4096]{1,0:T(8,128)(2,1)} %get-tuple-element.110.right, bf16[512,1024]{1,0:T(8,128)(2,1)} %get-tuple-element.111.refs_0_, ...), custom_call_target="tpu_custom_call" | custom-call | flops 600000000 | bytes 1 | tf_op jit(solution)/shard_map/pallas_call | solution.py:464
  279.4 4.4 shard_map.290
  284.9 28.7 %shard_map.291 = (bf16[2048,256]{1,0:T(8,128)(2,1)}, bf16[2048,256]{1,0:T(8,128)(2,1)}, bf16[2048,256]{1,0:T(8,128)(2,1)}, f32[2,2,128]{2,1,0:T(2,128)}) custom-call(bf16[2048,768]{1,0:T(8,128)(2,1)} %copy-done.2, bf16[2048,768]{1,0:T(8,128)(2,1)} %copy-done.2, bf16[2048,768]{1,0:T(8,128)(2,1)} %copy-done.2, s32[1,2048]{1,0:T(1,128)} %bitcast.154, ...), custom_call_target="tpu_custom_call" | custom-call | flops 2800000000 | bytes 1 | tf_op jit(solution)/shard_map/pallas_call | solution.py:148
  317.3 2.9 shard_map.292
  320.2 2.3 collective-permute-start.36
  324.7 1.5 collective-permute-start.37
  329.5 1.6 copy-done.20
  331.1 2.7 shard_map.293
  335.8 2.7 shard_map.294
  343.3 1.9 shard_map.296
  345.2 2.4 collective-permute-done.36.travel
  350.0 1.9 shard_map.298
  352.9 1.9 shard_map.299
  363.2 7.1 %shard_map.300 = (bf16[4,4,48,768]{3,2,1,0:T(8,128)(2,1)}, bf16[4,4,48,768]{3,2,1,0:T(8,128)(2,1)}, f32[8,128]{1,0:T(8,128)S(1)}) custom-call(s32[2]{0:T(128)S(1)} %copy-done.49, bf16[2048,256]{1,0:T(8,128)(2,1)S(1)} %copy-done.7, bf16[2048,256]{1,0:T(8,128)(2,1)S(1)} %copy-done.10, bf16[2048,256]{1,0:T(8,128)(2,1)S(1)} %copy-done.13, ...), custom_call_target="tpu_custom_call" | custom-call | flops 650000000 | bytes 1 | tf_op jit(solution)/shard_map/pallas_call | solution.py:589
  370.3 12.1 %collective-permute-done.42.travel = bf16[512,1024]{1,0:T(8,128)(2,1)S(1)} collective-permute-done((bf16[512,1024]{1,0:T(8,128)(2,1)}, bf16[512,1024]{1,0:T(8,128)(2,1)S(1)}, u32[]{:S(2)}, u32[]{:S(2)}) %collective-permute-start.42) | collective-permute-done | bytes 1048608 | tf_op jit(solution)/shard_map/ppermute | solution.py:712
  385.5 1.6 collective-permute-start.48
  389.0 10.8 %collective-permute-done.45.travel = bf16[288,1024]{1,0:T(8,128)(2,1)S(1)} collective-permute-done((bf16[288,1024]{1,0:T(8,128)(2,1)S(1)}, bf16[288,1024]{1,0:T(8,128)(2,1)S(1)}, u32[]{:S(2)}, u32[]{:S(2)}) %collective-permute-start.45) | collective-permute-done | bytes 589856 | tf_op jit(solution)/shard_map/ppermute | solution.py:712
  401.4 3.9 collective-permute-start.54
  405.3 12.8 %collective-permute-done.53 = bf16[48,768]{1,0:T(8,128)(2,1)S(1)} collective-permute-done((bf16[48,768]{1,0:T(8,128)(2,1)S(1)}, bf16[48,768]{1,0:T(8,128)(2,1)S(1)}, u32[]{:S(2)}, u32[]{:S(2)}) %collective-permute-start.53) | collective-permute-done | bytes 73760 | tf_op jit(solution)/shard_map/ppermute | solution.py:712
  418.3 13.7 %collective-permute-done.54 = bf16[48,768]{1,0:T(8,128)(2,1)S(1)} collective-permute-done((bf16[48,768]{1,0:T(8,128)(2,1)S(1)}, bf16[48,768]{1,0:T(8,128)(2,1)S(1)}, u32[]{:S(2)}, u32[]{:S(2)}) %collective-permute-start.54) | collective-permute-done | bytes 73760 | tf_op jit(solution)/shard_map/ppermute | solution.py:712
  432.9 1.6 collective-permute-start.56
  434.5 2.2 collective-permute-start.52
  438.9 10.0 %collective-permute-done.57.refs_1_.refs_0_ = bf16[192,1024]{1,0:T(8,128)(2,1)S(1)} collective-permute-done((bf16[192,1024]{1,0:T(8,128)(2,1)S(1)}, bf16[192,1024]{1,0:T(8,128)(2,1)S(1)}, u32[]{:S(2)}, u32[]{:S(2)}) %collective-permute-start.57) | collective-permute-done | bytes 393248 | tf_op jit(solution)/shard_map/ppermute | solution.py:699
  453.1 5.1 %collective-permute-done.58 = bf16[208,1024]{1,0:T(8,128)(2,1)} collective-permute-done((bf16[208,1024]{1,0:T(8,128)(2,1)S(1)}, bf16[208,1024]{1,0:T(8,128)(2,1)}, u32[]{:S(2)}, u32[]{:S(2)}) %collective-permute-start.58) | collective-permute-done | bytes 426016 | tf_op jit(solution)/shard_map/ppermute | solution.py:699
  458.2 7.6 %collective-permute-done.59 = bf16[208,1024]{1,0:T(8,128)(2,1)} collective-permute-done((bf16[208,1024]{1,0:T(8,128)(2,1)}, bf16[208,1024]{1,0:T(8,128)(2,1)}, u32[]{:S(2)}, u32[]{:S(2)}) %collective-permute-start.59) | collective-permute-done | bytes 426016 | tf_op jit(solution)/shard_map/ppermute | solution.py:699
  465.7 2.7 pad_maximum_fusion.refs_0_
  468.4 2.6 shard_map.309
  472.6 2.5 pad_maximum_fusion.1.refs_0_
  475.0 3.6 collective-permute-done.63.other_b
  480.1 7.0 %shard_map.314 = (f32[256,1024]{1,0:T(8,128)}, f32[256,4096]{1,0:T(8,128)}, f32[1024,1024]{1,0:T(8,128)}, f32[256,3072]{1,0:T(8,128)}, f32[64,1024]{1,0:T(8,128)S(1)}) custom-call(s32[2]{0:T(128)S(1)} %copy-done.49, bf16[4,208,1024]{2,1,0:T(8,128)(2,1)S(1)} %copy-done.16, bf16[4,208,1024]{2,1,0:T(8,128)(2,1)} %collective-permute-done.60.other_a, ...), custom_call_target="tpu_custom_call" | custom-call | flops 700000000 | bytes 1 | tf_op jit(solution)/shard_map/pallas_call | solution.py:635
  (406 shorter events, 87.5 us)
Async XLA Ops:
  6.1 36.9 %collective-permute-start.3 = (bf16[288,1024]{1,0:T(8,128)(2,1)}, bf16[288,1024]{1,0:T(8,128)(2,1)}, u32[]{:S(2)}, u32[]{:S(2)}) collective-permute-start(bf16[288,1024]{1,0:T(8,128)(2,1)} %shard_map.271), channel_id=1, source_target_pairs={{0,1},{1,2},{2,3},{3,0},{4,5},{5,6},{6,7},{7,4},{8,9},{9,10},{10,1... | collective-permute-start | bytes 1769480 | tf_op jit(solution)/shard_map/ppermute | solution.py:712
  9.1 33.8 %collective-permute-start.4 = (bf16[288,1024]{1,0:T(8,128)(2,1)}, bf16[288,1024]{1,0:T(8,128)(2,1)S(1)}, u32[]{:S(2)}, u32[]{:S(2)}) collective-permute-start(bf16[288,1024]{1,0:T(8,128)(2,1)} %shard_map.271), channel_id=1, source_target_pairs={{0,3},{1,0},{2,1},{3,2},{4,7},{5,4},{6,5},{7,6},{8,11},{9,8},{10,9... | collective-permute-start | bytes 1769480 | tf_op jit(solution)/shard_map/ppermute | solution.py:712
  11.2 31.8 %all-to-all-start = ((bf16[4,32,768]{2,1,0:T(8,128)(2,1)}), bf16[4,32,768]{2,1,0:T(8,128)(2,1)S(1)}, u32[]{:S(2)}, u32[]{:S(2)}) async-start(bf16[4,32,768]{2,1,0:T(8,128)(2,1)} %reshape.206.refs_1_), calls=%async_computation | async-start | bytes 393216 | tf_op jit(solution)/shard_map/all_to_all | solution.py:1025
  14.8 24.2 %collective-permute-start = (bf16[1,3072]{1,0:T(2,128)(2,1)S(1)}, bf16[1,3072]{1,0:T(2,128)(2,1)S(1)}, u32[]{:S(2)}, u32[]{:S(2)}) collective-permute-start(bf16[1,3072]{1,0:T(2,128)(2,1)S(1)} %constant_dynamic-update-slice_fusion.refs_1_), channel_id=1, source_target_pairs={{0,3},{1,0},{2,1},{3,2},{4,7},{5,4},{6,5},{7,6},{8,11},{9,8},{10,9... | collective-permute-start | bytes 18440 | tf_op jit(solution)/shard_map/ppermute | solution.py:712
  18.6 24.0 %collective-permute-start.1 = (bf16[1,3072]{1,0:T(2,128)(2,1)S(1)}, bf16[1,3072]{1,0:T(2,128)(2,1)S(1)}, u32[]{:S(2)}, u32[]{:S(2)}) collective-permute-start(bf16[1,3072]{1,0:T(2,128)(2,1)S(1)} %constant_dynamic-update-slice_fusion.refs_1_), channel_id=1, source_target_pairs={{0,2},{1,3},{2,0},{3,1},{4,6},{5,7},{6,4},{7,5},{8,10},{9,11},{10,... | collective-permute-start | bytes 18440 | tf_op jit(solution)/shard_map/ppermute | solution.py:712
  18.6 24.0 %collective-permute-start.2 = (bf16[1,3072]{1,0:T(2,128)(2,1)S(1)}, bf16[1,3072]{1,0:T(2,128)(2,1)S(1)}, u32[]{:S(2)}, u32[]{:S(2)}) collective-permute-start(bf16[1,3072]{1,0:T(2,128)(2,1)S(1)} %constant_dynamic-update-slice_fusion.refs_1_), channel_id=1, source_target_pairs={{0,1},{1,2},{2,3},{3,0},{4,5},{5,6},{6,7},{7,4},{8,9},{9,10},{10,1... | collective-permute-start | bytes 18440 | tf_op jit(solution)/shard_map/ppermute | solution.py:712
  44.5 7.5 %collective-permute-start.7 = (bf16[4,32,768]{2,1,0:T(8,128)(2,1)}, bf16[4,32,768]{2,1,0:T(8,128)(2,1)S(1)}, u32[]{:S(2)}, u32[]{:S(2)}) collective-permute-start(bf16[4,32,768]{2,1,0:T(8,128)(2,1)} %shard_map.273), channel_id=1, source_target_pairs={{0,4},{4,0},{8,12},{12,8},{16,20},{20,16},{24,28},{28,24},{1,5},{5... | collective-permute-start | bytes 589832 | tf_op jit(solution)/shard_map/ppermute | solution.py:699
  44.5 7.5 %collective-permute-start.8 = (bf16[4,32,768]{2,1,0:T(8,128)(2,1)}, bf16[4,32,768]{2,1,0:T(8,128)(2,1)S(1)}, u32[]{:S(2)}, u32[]{:S(2)}) collective-permute-start(bf16[4,32,768]{2,1,0:T(8,128)(2,1)} %shard_map.273), channel_id=1, source_target_pairs={{0,8},{4,12},{8,0},{12,4},{16,24},{20,28},{24,16},{28,20},{1,9},{5... | collective-permute-start | bytes 589832 | tf_op jit(solution)/shard_map/ppermute | solution.py:699
  46.0 7.5 %collective-permute-start.10 = (bf16[4,32,768]{2,1,0:T(8,128)(2,1)}, bf16[4,32,768]{2,1,0:T(8,128)(2,1)S(1)}, u32[]{:S(2)}, u32[]{:S(2)}) collective-permute-start(bf16[4,32,768]{2,1,0:T(8,128)(2,1)} %shard_map.273), channel_id=1, source_target_pairs={{0,16},{4,20},{8,24},{12,28},{16,0},{20,4},{24,8},{28,12},{1,17},{... | collective-permute-start | bytes 589832 | tf_op jit(solution)/shard_map/ppermute | solution.py:699
  47.5 28.1 %collective-permute-start.5 = (bf16[512,1024]{1,0:T(8,128)(2,1)}, bf16[512,1024]{1,0:T(8,128)(2,1)S(1)}, u32[]{:S(2)}, u32[]{:S(2)}) collective-permute-start(bf16[512,1024]{1,0:T(8,128)(2,1)} %shard_map.272.block), channel_id=1, source_target_pairs={{0,1},{1,2},{2,3},{3,0},{4,5},{5,6},{6,7},{7,4},{8,9},{9,10},{10,1... | collective-permute-start | bytes 3145736 | tf_op jit(solution)/shard_map/ppermute | solution.py:712
  47.9 47.3 %collective-permute-start.14 = (bf16[512,1024]{1,0:T(8,128)(2,1)}, bf16[512,1024]{1,0:T(8,128)(2,1)S(1)}, u32[]{:S(2)}, u32[]{:S(2)}) collective-permute-start(bf16[512,1024]{1,0:T(8,128)(2,1)} %shard_map.272.block), channel_id=1, source_target_pairs={{0,3},{1,0},{2,1},{3,2},{4,7},{5,4},{6,5},{7,6},{8,11},{9,8},{10,9... | collective-permute-start | bytes 3145736 | tf_op jit(solution)/shard_map/ppermute | solution.py:712
  52.0 7.3 %collective-permute-start.12 = (bf16[4,32,768]{2,1,0:T(8,128)(2,1)S(1)}, bf16[4,32,768]{2,1,0:T(8,128)(2,1)S(1)}, u32[]{:S(2)}, u32[]{:S(2)}) collective-permute-start(bf16[4,32,768]{2,1,0:T(8,128)(2,1)S(1)} %collective-permute-done.8), channel_id=1, source_target_pairs={{0,16},{4,20},{8,24},{12,28},{16,0},{20,4},{24,8},{28,12},{1,17},{... | collective-permute-start | bytes 589832 | tf_op jit(solution)/shard_map/ppermute | solution.py:699
  53.6 56.1 %collective-permute-start.18 = (bf16[288,1024]{1,0:T(8,128)(2,1)}, bf16[288,1024]{1,0:T(8,128)(2,1)S(1)}, u32[]{:S(2)}, u32[]{:S(2)}) collective-permute-start(bf16[288,1024]{1,0:T(8,128)(2,1)} %collective-permute-done.3.refs_2_.refs_1_.refs_0_), channel_id=1, source_target_pairs={{0,1},{1,2},{2,3},{3,0},{4,5},{5,6},{6,7},{7,4},{8,9},{9,10},{10,1... | collective-permute-start | bytes 1769480 | tf_op jit(solution)/shard_map/ppermute | solution.py:712
  54.0 5.3 %collective-permute-start.11 = (bf16[4,32,768]{2,1,0:T(8,128)(2,1)S(1)}, bf16[4,32,768]{2,1,0:T(8,128)(2,1)S(1)}, u32[]{:S(2)}, u32[]{:S(2)}) collective-permute-start(bf16[4,32,768]{2,1,0:T(8,128)(2,1)S(1)} %collective-permute-done.10), channel_id=1, source_target_pairs={{0,4},{4,0},{8,12},{12,8},{16,20},{20,16},{24,28},{28,24},{1,5},{5... | collective-permute-start | bytes 589832 | tf_op jit(solution)/shard_map/ppermute | solution.py:699
  117.1 24.9 %collective-permute-start.20 = (bf16[3,160,1024]{2,1,0:T(8,128)(2,1)}, bf16[3,160,1024]{2,1,0:T(8,128)(2,1)S(1)}, u32[]{:S(2)}, u32[]{:S(2)}) collective-permute-start(bf16[3,160,1024]{2,1,0:T(8,128)(2,1)} %pad_maximum_fusion.2.refs_4_), channel_id=1, source_target_pairs={{0,8},{4,12},{8,0},{12,4},{16,24},{20,28},{24,16},{28,20},{1,9},{5... | collective-permute-start | bytes 2949128 | tf_op jit(solution)/shard_map/ppermute | solution.py:699
  117.7 25.8 %collective-permute-start.6 = (bf16[512,1024]{1,0:T(8,128)(2,1)S(1)}, bf16[512,1024]{1,0:T(8,128)(2,1)S(1)}, u32[]{:S(2)}, u32[]{:S(2)}) collective-permute-start(bf16[512,1024]{1,0:T(8,128)(2,1)S(1)} %copy-done.25), channel_id=1, source_target_pairs={{0,1},{1,2},{2,3},{3,0},{4,5},{5,6},{6,7},{7,4},{8,9},{9,10},{10,1... | collective-permute-start | bytes 3145736 | tf_op jit(solution)/shard_map/ppermute | solution.py:712
  121.7 45.3 %collective-permute-start.29 = (bf16[3,128,1024]{2,1,0:T(8,128)(2,1)}, bf16[3,128,1024]{2,1,0:T(8,128)(2,1)}, u32[]{:S(2)}, u32[]{:S(2)}) collective-permute-start(bf16[3,128,1024]{2,1,0:T(8,128)(2,1)} %pad_maximum_fusion.3.refs_12_), channel_id=1, source_target_pairs={{0,16},{4,20},{8,24},{12,28},{16,0},{20,4},{24,8},{28,12},{1,17},{... | collective-permute-start | bytes 2359304 | tf_op jit(solution)/shard_map/ppermute | solution.py:699
  122.3 45.7 %collective-permute-start.27 = (bf16[3,128,1024]{2,1,0:T(8,128)(2,1)}, bf16[3,128,1024]{2,1,0:T(8,128)(2,1)}, u32[]{:S(2)}, u32[]{:S(2)}) collective-permute-start(bf16[3,128,1024]{2,1,0:T(8,128)(2,1)} %pad_maximum_fusion.3.refs_12_), channel_id=1, source_target_pairs={{0,8},{4,12},{8,0},{12,4},{16,24},{20,28},{24,16},{28,20},{1,9},{5... | collective-permute-start | bytes 2359304 | tf_op jit(solution)/shard_map/ppermute | solution.py:699
  123.8 44.3 %collective-permute-start.26 = (bf16[3,128,1024]{2,1,0:T(8,128)(2,1)}, bf16[3,128,1024]{2,1,0:T(8,128)(2,1)}, u32[]{:S(2)}, u32[]{:S(2)}) collective-permute-start(bf16[3,128,1024]{2,1,0:T(8,128)(2,1)} %pad_maximum_fusion.3.refs_12_), channel_id=1, source_target_pairs={{0,4},{4,0},{8,12},{12,8},{16,20},{20,16},{24,28},{28,24},{1,5},{5... | collective-permute-start | bytes 2359304 | tf_op jit(solution)/shard_map/ppermute | solution.py:699
  142.0 28.1 %collective-permute-start.22 = (bf16[3,160,1024]{2,1,0:T(8,128)(2,1)}, bf16[3,160,1024]{2,1,0:T(8,128)(2,1)}, u32[]{:S(2)}, u32[]{:S(2)}) collective-permute-start(bf16[3,160,1024]{2,1,0:T(8,128)(2,1)} %pad_maximum_fusion.2.refs_4_), channel_id=1, source_target_pairs={{0,16},{4,20},{8,24},{12,28},{16,0},{20,4},{24,8},{28,12},{1,17},{... | collective-permute-start | bytes 2949128 | tf_op jit(solution)/shard_map/ppermute | solution.py:699
  143.5 26.6 %collective-permute-start.19 = (bf16[3,160,1024]{2,1,0:T(8,128)(2,1)}, bf16[3,160,1024]{2,1,0:T(8,128)(2,1)}, u32[]{:S(2)}, u32[]{:S(2)}) collective-permute-start(bf16[3,160,1024]{2,1,0:T(8,128)(2,1)} %pad_maximum_fusion.2.refs_4_), channel_id=1, source_target_pairs={{0,4},{4,0},{8,12},{12,8},{16,20},{20,16},{24,28},{28,24},{1,5},{5... | collective-permute-start | bytes 2949128 | tf_op jit(solution)/shard_map/ppermute | solution.py:699
  167.1 25.7 %collective-permute-start.24 = (bf16[3,160,1024]{2,1,0:T(8,128)(2,1)}, bf16[3,160,1024]{2,1,0:T(8,128)(2,1)}, u32[]{:S(2)}, u32[]{:S(2)}) collective-permute-start(bf16[3,160,1024]{2,1,0:T(8,128)(2,1)} %shard_map.282.refs_6_), channel_id=1, source_target_pairs={{0,16},{4,20},{8,24},{12,28},{16,0},{20,4},{24,8},{28,12},{1,17},{... | collective-permute-start | bytes 2949128 | tf_op jit(solution)/shard_map/ppermute | solution.py:699
  168.0 25.2 %collective-permute-start.28 = (bf16[3,128,1024]{2,1,0:T(8,128)(2,1)}, bf16[3,128,1024]{2,1,0:T(8,128)(2,1)}, u32[]{:S(2)}, u32[]{:S(2)}) collective-permute-start(bf16[3,128,1024]{2,1,0:T(8,128)(2,1)} %collective-permute-done.27.refs_14_), channel_id=1, source_target_pairs={{0,4},{4,0},{8,12},{12,8},{16,20},{20,16},{24,28},{28,24},{1,5},{5... | collective-permute-start | bytes 2359304 | tf_op jit(solution)/shard_map/ppermute | solution.py:699
  168.1 25.2 %collective-permute-start.31 = (bf16[3,128,1024]{2,1,0:T(8,128)(2,1)}, bf16[3,128,1024]{2,1,0:T(8,128)(2,1)}, u32[]{:S(2)}, u32[]{:S(2)}) collective-permute-start(bf16[3,128,1024]{2,1,0:T(8,128)(2,1)} %shard_map.283.refs_16_), channel_id=1, source_target_pairs={{0,8},{4,12},{8,0},{12,4},{16,24},{20,28},{24,16},{28,20},{1,9},{5... | collective-permute-start | bytes 2359304 | tf_op jit(solution)/shard_map/ppermute | solution.py:699
  170.1 11.1 %collective-permute-start.15 = (bf16[512,256]{1,0:T(8,128)(2,1)S(1)}, bf16[512,256]{1,0:T(8,128)(2,1)S(1)}, u32[]{:S(2)}, u32[]{:S(2)}) collective-permute-start(bf16[512,256]{1,0:T(8,128)(2,1)S(1)} %get-tuple-element.193), channel_id=1, source_target_pairs={{0,1},{1,2},{2,3},{3,0},{4,5},{5,6},{6,7},{7,4},{8,9},{9,10},{10,1... | collective-permute-start | bytes 786440 | tf_op jit(solution)/shard_map/ppermute | solution.py:712
  170.1 21.4 %collective-permute-start.16 = (bf16[512,256]{1,0:T(8,128)(2,1)S(1)}, bf16[512,256]{1,0:T(8,128)(2,1)S(1)}, u32[]{:S(2)}, u32[]{:S(2)}) collective-permute-start(bf16[512,256]{1,0:T(8,128)(2,1)S(1)} %get-tuple-element.192), channel_id=1, source_target_pairs={{0,2},{1,3},{2,0},{3,1},{4,6},{5,7},{6,4},{7,5},{8,10},{9,11},{10,... | collective-permute-start | bytes 786440 | tf_op jit(solution)/shard_map/ppermute | solution.py:712
  181.2 11.5 %collective-permute-start.17 = (bf16[512,256]{1,0:T(8,128)(2,1)S(1)}, bf16[512,256]{1,0:T(8,128)(2,1)S(1)}, u32[]{:S(2)}, u32[]{:S(2)}) collective-permute-start(bf16[512,256]{1,0:T(8,128)(2,1)S(1)} %get-tuple-element.191), channel_id=1, source_target_pairs={{0,3},{1,0},{2,1},{3,2},{4,7},{5,4},{6,5},{7,6},{8,11},{9,8},{10,9... | collective-permute-start | bytes 786440 | tf_op jit(solution)/shard_map/ppermute | solution.py:712
  191.5 6.8 %collective-permute-start.23 = (bf16[3,160,1024]{2,1,0:T(8,128)(2,1)}, bf16[3,160,1024]{2,1,0:T(8,128)(2,1)S(1)}, u32[]{:S(2)}, u32[]{:S(2)}) collective-permute-start(bf16[3,160,1024]{2,1,0:T(8,128)(2,1)} %collective-permute-done.22.refs_8_), channel_id=1, source_target_pairs={{0,4},{4,0},{8,12},{12,8},{16,20},{20,16},{24,28},{28,24},{1,5},{5... | collective-permute-start | bytes 2949128 | tf_op jit(solution)/shard_map/ppermute | solution.py:699
  192.7 5.7 %collective-permute-start.21 = (bf16[3,160,1024]{2,1,0:T(8,128)(2,1)S(1)}, bf16[3,160,1024]{2,1,0:T(8,128)(2,1)}, u32[]{:S(2)}, u32[]{:S(2)}) collective-permute-start(bf16[3,160,1024]{2,1,0:T(8,128)(2,1)S(1)} %copy-done.60), channel_id=1, source_target_pairs={{0,4},{4,0},{8,12},{12,8},{16,20},{20,16},{24,28},{28,24},{1,5},{5... | collective-permute-start | bytes 2949128 | tf_op jit(solution)/shard_map/ppermute | solution.py:699
  192.7 6.8 %collective-permute-start.25 = (bf16[3,160,1024]{2,1,0:T(8,128)(2,1)}, bf16[3,160,1024]{2,1,0:T(8,128)(2,1)}, u32[]{:S(2)}, u32[]{:S(2)}) collective-permute-start(bf16[3,160,1024]{2,1,0:T(8,128)(2,1)} %collective-permute-done.24.refs_10_), channel_id=1, source_target_pairs={{0,4},{4,0},{8,12},{12,8},{16,20},{20,16},{24,28},{28,24},{1,5},{5... | collective-permute-start | bytes 2949128 | tf_op jit(solution)/shard_map/ppermute | solution.py:699
  193.2 5.1 %collective-permute-start.30 = (bf16[3,128,1024]{2,1,0:T(8,128)(2,1)}, bf16[3,128,1024]{2,1,0:T(8,128)(2,1)}, u32[]{:S(2)}, u32[]{:S(2)}) collective-permute-start(bf16[3,128,1024]{2,1,0:T(8,128)(2,1)} %shard_map.283.refs_16_), channel_id=1, source_target_pairs={{0,4},{4,0},{8,12},{12,8},{16,20},{20,16},{24,28},{28,24},{1,5},{5... | collective-permute-start | bytes 2359304 | tf_op jit(solution)/shard_map/ppermute | solution.py:699
  193.3 6.2 %collective-permute-start.32 = (bf16[3,128,1024]{2,1,0:T(8,128)(2,1)}, bf16[3,128,1024]{2,1,0:T(8,128)(2,1)}, u32[]{:S(2)}, u32[]{:S(2)}) collective-permute-start(bf16[3,128,1024]{2,1,0:T(8,128)(2,1)} %collective-permute-done.31.refs_18_), channel_id=1, source_target_pairs={{0,4},{4,0},{8,12},{12,8},{16,20},{20,16},{24,28},{28,24},{1,5},{5... | collective-permute-start | bytes 2359304 | tf_op jit(solution)/shard_map/ppermute | solution.py:699
  240.6 18.3 %collective-permute-start.35 = (bf16[4,4,128,1024]{3,2,1,0:T(8,128)(2,1)}, bf16[4,4,128,1024]{3,2,1,0:T(8,128)(2,1)}, u32[]{:S(2)}, u32[]{:S(2)}) collective-permute-start(bf16[4,4,128,1024]{3,2,1,0:T(8,128)(2,1)} %get-tuple-element.117), channel_id=1, source_target_pairs={{0,4},{4,0},{8,12},{12,8},{16,20},{20,16},{24,28},{28,24},{1,5},{5... | collective-permute-start | bytes 12582920 | tf_op jit(solution)/shard_map/ppermute | solution.py:699
  248.3 19.9 %collective-permute-start.34 = (bf16[4,4,128,1024]{3,2,1,0:T(8,128)(2,1)}, bf16[4,4,128,1024]{3,2,1,0:T(8,128)(2,1)}, u32[]{:S(2)}, u32[]{:S(2)}) collective-permute-start(bf16[4,4,128,1024]{3,2,1,0:T(8,128)(2,1)} %get-tuple-element.116), channel_id=1, source_target_pairs={{0,4},{4,0},{8,12},{12,8},{16,20},{20,16},{24,28},{28,24},{1,5},{5... | collective-permute-start | bytes 12582920 | tf_op jit(solution)/shard_map/ppermute | solution.py:699
  249.7 34.2 %all-to-all-start.1 = ((bf16[512,4,256]{2,0,1:T(8,128)(2,1)}), bf16[512,4,256]{2,0,1:T(8,128)(2,1)S(1)}, u32[]{:S(2)}, u32[]{:S(2)}) async-start(bf16[512,4,256]{2,0,1:T(8,128)(2,1)} %bitcast.121), calls=%async_computation.1 | async-start | bytes 2097152 | tf_op jit(solution)/shard_map/all_to_all | solution.py:1057
  258.9 19.6 %collective-permute-start.33 = (bf16[4,4,32,1024]{3,2,1,0:T(8,128)(2,1)}, bf16[4,4,32,1024]{3,2,1,0:T(8,128)(2,1)S(1)}, u32[]{:S(2)}, u32[]{:S(2)}) collective-permute-start(bf16[4,4,32,1024]{3,2,1,0:T(8,128)(2,1)} %get-tuple-element.115), channel_id=1, source_target_pairs={{0,4},{4,0},{8,12},{12,8},{16,20},{20,16},{24,28},{28,24},{1,5},{5... | collective-permute-start | bytes 3145736 | tf_op jit(solution)/shard_map/ppermute | solution.py:699
  267.3 60.3 %collective-permute-start.41 = (bf16[2,4,128,1024]{3,2,1,0:T(8,128)(2,1)}, bf16[2,4,128,1024]{3,2,1,0:T(8,128)(2,1)}, u32[]{:S(2)}, u32[]{:S(2)}) collective-permute-start(bf16[2,4,128,1024]{3,2,1,0:T(8,128)(2,1)} %get-tuple-element.131), channel_id=1, source_target_pairs={{0,8},{4,12},{8,0},{12,4},{16,24},{20,28},{24,16},{28,20},{1,9},{5... | collective-permute-start | bytes 6291464 | tf_op jit(solution)/shard_map/ppermute | solution.py:699
  277.3 58.5 %collective-permute-start.40 = (bf16[2,4,128,1024]{3,2,1,0:T(8,128)(2,1)}, bf16[2,4,128,1024]{3,2,1,0:T(8,128)(2,1)}, u32[]{:S(2)}, u32[]{:S(2)}) collective-permute-start(bf16[2,4,128,1024]{3,2,1,0:T(8,128)(2,1)} %get-tuple-element.129), channel_id=1, source_target_pairs={{0,16},{4,20},{8,24},{12,28},{16,0},{20,4},{24,8},{28,12},{1,17},{... | collective-permute-start | bytes 6291464 | tf_op jit(solution)/shard_map/ppermute | solution.py:699
  320.2 27.4 %collective-permute-start.36 = (bf16[512,1024]{1,0:T(8,128)(2,1)}, bf16[512,1024]{1,0:T(8,128)(2,1)}, u32[]{:S(2)}, u32[]{:S(2)}) collective-permute-start(bf16[512,1024]{1,0:T(8,128)(2,1)} %get-tuple-element.125), channel_id=1, source_target_pairs={{0,1},{1,2},{2,3},{3,0},{4,5},{5,6},{6,7},{7,4},{8,9},{9,10},{10,1... | collective-permute-start | bytes 3145736 | tf_op jit(solution)/shard_map/ppermute | solution.py:712
  324.7 15.7 %collective-permute-start.37 = (bf16[1,4,32,1024]{3,2,1,0:T(8,128)(2,1)}, bf16[1,4,32,1024]{3,2,1,0:T(8,128)(2,1)S(1)}, u32[]{:S(2)}, u32[]{:S(2)}) collective-permute-start(bf16[1,4,32,1024]{3,2,1,0:T(8,128)(2,1)} %get-tuple-element.196), channel_id=1, source_target_pairs={{0,8},{4,12},{8,0},{12,4},{16,24},{20,28},{24,16},{28,20},{1,9},{5... | collective-permute-start | bytes 786440 | tf_op jit(solution)/shard_map/ppermute | solution.py:699
  327.0 13.5 %collective-permute-start.38 = (bf16[1,4,32,1024]{3,2,1,0:T(8,128)(2,1)}, bf16[1,4,32,1024]{3,2,1,0:T(8,128)(2,1)S(1)}, u32[]{:S(2)}, u32[]{:S(2)}) collective-permute-start(bf16[1,4,32,1024]{3,2,1,0:T(8,128)(2,1)} %get-tuple-element.197), channel_id=1, source_target_pairs={{0,16},{4,20},{8,24},{12,28},{16,0},{20,4},{24,8},{28,12},{1,17},{... | collective-permute-start | bytes 786440 | tf_op jit(solution)/shard_map/ppermute | solution.py:699
  327.5 13.7 %collective-permute-start.39 = (bf16[1,4,32,1024]{3,2,1,0:T(8,128)(2,1)}, bf16[1,4,32,1024]{3,2,1,0:T(8,128)(2,1)}, u32[]{:S(2)}, u32[]{:S(2)}) collective-permute-start(bf16[1,4,32,1024]{3,2,1,0:T(8,128)(2,1)} %get-tuple-element.195), channel_id=1, source_target_pairs={{0,24},{4,28},{8,16},{12,20},{16,8},{20,12},{24,0},{28,4},{1,25},{... | collective-permute-start | bytes 786440 | tf_op jit(solution)/shard_map/ppermute | solution.py:699
  355.9 26.5 %collective-permute-start.42 = (bf16[512,1024]{1,0:T(8,128)(2,1)}, bf16[512,1024]{1,0:T(8,128)(2,1)S(1)}, u32[]{:S(2)}, u32[]{:S(2)}) collective-permute-start(bf16[512,1024]{1,0:T(8,128)(2,1)} %copy-done.55), channel_id=1, source_target_pairs={{0,1},{1,2},{2,3},{3,0},{4,5},{5,6},{6,7},{7,4},{8,9},{9,10},{10,1... | collective-permute-start | bytes 3145736 | tf_op jit(solution)/shard_map/ppermute | solution.py:712
  356.2 26.5 %collective-permute-start.43 = (bf16[1,4,128,1024]{3,2,1,0:T(8,128)(2,1)}, bf16[1,4,128,1024]{3,2,1,0:T(8,128)(2,1)S(1)}, u32[]{:S(2)}, u32[]{:S(2)}) collective-permute-start(bf16[1,4,128,1024]{3,2,1,0:T(8,128)(2,1)} %copy-done.54), channel_id=1, source_target_pairs={{0,8},{4,12},{8,0},{12,4},{16,24},{20,28},{24,16},{28,20},{1,9},{5... | collective-permute-start | bytes 3145736 | tf_op jit(solution)/shard_map/ppermute | solution.py:699
  357.7 25.0 %collective-permute-start.44 = (bf16[1,4,128,1024]{3,2,1,0:T(8,128)(2,1)}, bf16[1,4,128,1024]{3,2,1,0:T(8,128)(2,1)S(1)}, u32[]{:S(2)}, u32[]{:S(2)}) collective-permute-start(bf16[1,4,128,1024]{3,2,1,0:T(8,128)(2,1)} %copy-done.53), channel_id=1, source_target_pairs={{0,16},{4,20},{8,24},{12,28},{16,0},{20,4},{24,8},{28,12},{1,17},{... | collective-permute-start | bytes 3145736 | tf_op jit(solution)/shard_map/ppermute | solution.py:699
  370.2 14.1 %collective-permute-start.46 = (bf16[4,4,48,768]{3,2,1,0:T(8,128)(2,1)}, bf16[4,4,48,768]{3,2,1,0:T(8,128)(2,1)S(1)}, u32[]{:S(2)}, u32[]{:S(2)}) collective-permute-start(bf16[4,4,48,768]{3,2,1,0:T(8,128)(2,1)} %get-tuple-element.161), channel_id=1, source_target_pairs={{0,4},{4,0},{8,12},{12,8},{16,20},{20,16},{24,28},{28,24},{1,5},{5... | collective-permute-start | bytes 3538952 | tf_op jit(solution)/shard_map/ppermute | solution.py:699
  384.3 15.5 %collective-permute-start.45 = (bf16[288,1024]{1,0:T(8,128)(2,1)S(1)}, bf16[288,1024]{1,0:T(8,128)(2,1)S(1)}, u32[]{:S(2)}, u32[]{:S(2)}) collective-permute-start(bf16[288,1024]{1,0:T(8,128)(2,1)S(1)} %get-tuple-element.158), channel_id=1, source_target_pairs={{0,1},{1,2},{2,3},{3,0},{4,5},{5,6},{6,7},{7,4},{8,9},{9,10},{10,1... | collective-permute-start | bytes 1769480 | tf_op jit(solution)/shard_map/ppermute | solution.py:712
  385.5 14.5 %collective-permute-start.48 = (bf16[4,48,768]{2,1,0:T(8,128)(2,1)S(1)}, bf16[4,48,768]{2,1,0:T(8,128)(2,1)S(1)}, u32[]{:S(2)}, u32[]{:S(2)}) collective-permute-start(bf16[4,48,768]{2,1,0:T(8,128)(2,1)S(1)} %get-tuple-element.166), channel_id=1, source_target_pairs={{0,8},{4,12},{8,0},{12,4},{16,24},{20,28},{24,16},{28,20},{1,9},{5... | collective-permute-start | bytes 884744 | tf_op jit(solution)/shard_map/ppermute | solution.py:699
  387.0 13.4 %collective-permute-start.49 = (bf16[4,48,768]{2,1,0:T(8,128)(2,1)S(1)}, bf16[4,48,768]{2,1,0:T(8,128)(2,1)S(1)}, u32[]{:S(2)}, u32[]{:S(2)}) collective-permute-start(bf16[4,48,768]{2,1,0:T(8,128)(2,1)S(1)} %get-tuple-element.167), channel_id=1, source_target_pairs={{0,16},{4,20},{8,24},{12,28},{16,0},{20,4},{24,8},{28,12},{1,17},{... | collective-permute-start | bytes 884744 | tf_op jit(solution)/shard_map/ppermute | solution.py:699
  387.6 12.9 %collective-permute-start.50 = (bf16[4,48,768]{2,1,0:T(8,128)(2,1)S(1)}, bf16[4,48,768]{2,1,0:T(8,128)(2,1)S(1)}, u32[]{:S(2)}, u32[]{:S(2)}) collective-permute-start(bf16[4,48,768]{2,1,0:T(8,128)(2,1)S(1)} %get-tuple-element.168), channel_id=1, source_target_pairs={{0,24},{4,28},{8,16},{12,20},{16,8},{20,12},{24,0},{28,4},{1,25},{... | collective-permute-start | bytes 884744 | tf_op jit(solution)/shard_map/ppermute | solution.py:699
  399.9 18.2 %collective-permute-start.47 = (bf16[288,1024]{1,0:T(8,128)(2,1)S(1)}, bf16[288,1024]{1,0:T(8,128)(2,1)S(1)}, u32[]{:S(2)}, u32[]{:S(2)}) collective-permute-start(bf16[288,1024]{1,0:T(8,128)(2,1)S(1)} %get-tuple-element.164), channel_id=1, source_target_pairs={{0,1},{1,2},{2,3},{3,0},{4,5},{5,6},{6,7},{7,4},{8,9},{9,10},{10,1... | collective-permute-start | bytes 1769480 | tf_op jit(solution)/shard_map/ppermute | solution.py:712
  401.3 16.8 %collective-permute-start.53 = (bf16[48,768]{1,0:T(8,128)(2,1)S(1)}, bf16[48,768]{1,0:T(8,128)(2,1)S(1)}, u32[]{:S(2)}, u32[]{:S(2)}) collective-permute-start(bf16[48,768]{1,0:T(8,128)(2,1)S(1)} %get-tuple-element.202), channel_id=1, source_target_pairs={{0,1},{1,2},{2,3},{3,0},{4,5},{5,6},{6,7},{7,4},{8,9},{9,10},{10,1... | collective-permute-start | bytes 221192 | tf_op jit(solution)/shard_map/ppermute | solution.py:712
  401.4 30.7 %collective-permute-start.54 = (bf16[48,768]{1,0:T(8,128)(2,1)S(1)}, bf16[48,768]{1,0:T(8,128)(2,1)S(1)}, u32[]{:S(2)}, u32[]{:S(2)}) collective-permute-start(bf16[48,768]{1,0:T(8,128)(2,1)S(1)} %get-tuple-element.201), channel_id=1, source_target_pairs={{0,2},{1,3},{2,0},{3,1},{4,6},{5,7},{6,4},{7,5},{8,10},{9,11},{10,... | collective-permute-start | bytes 221192 | tf_op jit(solution)/shard_map/ppermute | solution.py:712
  405.3 26.8 %collective-permute-start.55 = (bf16[48,768]{1,0:T(8,128)(2,1)S(1)}, bf16[48,768]{1,0:T(8,128)(2,1)S(1)}, u32[]{:S(2)}, u32[]{:S(2)}) collective-permute-start(bf16[48,768]{1,0:T(8,128)(2,1)S(1)} %get-tuple-element.200), channel_id=1, source_target_pairs={{0,3},{1,0},{2,1},{3,2},{4,7},{5,4},{6,5},{7,6},{8,11},{9,8},{10,9... | collective-permute-start | bytes 221192 | tf_op jit(solution)/shard_map/ppermute | solution.py:712
  418.3 13.9 %collective-permute-start.51 = (bf16[288,1024]{1,0:T(8,128)(2,1)S(1)}, bf16[288,1024]{1,0:T(8,128)(2,1)S(1)}, u32[]{:S(2)}, u32[]{:S(2)}) collective-permute-start(bf16[288,1024]{1,0:T(8,128)(2,1)S(1)} %get-tuple-element.171), channel_id=1, source_target_pairs={{0,1},{1,2},{2,3},{3,0},{4,5},{5,6},{6,7},{7,4},{8,9},{9,10},{10,1... | collective-permute-start | bytes 1769480 | tf_op jit(solution)/shard_map/ppermute | solution.py:712
  432.9 16.0 %collective-permute-start.56 = (bf16[208,1024]{1,0:T(8,128)(2,1)S(1)}, bf16[208,1024]{1,0:T(8,128)(2,1)S(1)}, u32[]{:S(2)}, u32[]{:S(2)}) collective-permute-start(bf16[208,1024]{1,0:T(8,128)(2,1)S(1)} %fusion.3), channel_id=1, source_target_pairs={{0,8},{4,12},{8,0},{12,4},{16,24},{20,28},{24,16},{28,20},{1,9},{5... | collective-permute-start | bytes 1277960 | tf_op jit(solution)/shard_map/ppermute | solution.py:699
  434.5 33.9 %collective-permute-start.52 = (bf16[512,1024]{1,0:T(8,128)(2,1)}, bf16[512,1024]{1,0:T(8,128)(2,1)S(1)}, u32[]{:S(2)}, u32[]{:S(2)}) collective-permute-start(bf16[512,1024]{1,0:T(8,128)(2,1)} %shard_map.308), channel_id=1, source_target_pairs={{0,1},{1,2},{2,3},{3,0},{4,5},{5,6},{6,7},{7,4},{8,9},{9,10},{10,1... | collective-permute-start | bytes 3145736 | tf_op jit(solution)/shard_map/ppermute | solution.py:712
  436.8 12.1 %collective-permute-start.57 = (bf16[192,1024]{1,0:T(8,128)(2,1)S(1)}, bf16[192,1024]{1,0:T(8,128)(2,1)S(1)}, u32[]{:S(2)}, u32[]{:S(2)}) collective-permute-start(bf16[192,1024]{1,0:T(8,128)(2,1)S(1)} %maximum_maximum_fusion), channel_id=1, source_target_pairs={{0,16},{4,20},{8,24},{12,28},{16,0},{20,4},{24,8},{28,12},{1,17},{... | collective-permute-start | bytes 1179656 | tf_op jit(solution)/shard_map/ppermute | solution.py:699
  437.4 20.7 %collective-permute-start.58 = (bf16[208,1024]{1,0:T(8,128)(2,1)S(1)}, bf16[208,1024]{1,0:T(8,128)(2,1)}, u32[]{:S(2)}, u32[]{:S(2)}) collective-permute-start(bf16[208,1024]{1,0:T(8,128)(2,1)S(1)} %fusion.3), channel_id=1, source_target_pairs={{0,16},{4,20},{8,24},{12,28},{16,0},{20,4},{24,8},{28,12},{1,17},{... | collective-permute-start | bytes 1277960 | tf_op jit(solution)/shard_map/ppermute | solution.py:699
  450.4 15.3 %collective-permute-start.59 = (bf16[208,1024]{1,0:T(8,128)(2,1)}, bf16[208,1024]{1,0:T(8,128)(2,1)}, u32[]{:S(2)}, u32[]{:S(2)}) collective-permute-start(bf16[208,1024]{1,0:T(8,128)(2,1)} %shard_map.310.refs_1_), channel_id=1, source_target_pairs={{0,16},{4,20},{8,24},{12,28},{16,0},{20,4},{24,8},{28,12},{1,17},{... | collective-permute-start | bytes 1277960 | tf_op jit(solution)/shard_map/ppermute | solution.py:699
  451.0 20.6 %collective-permute-start.61 = (bf16[192,1024]{1,0:T(8,128)(2,1)}, bf16[192,1024]{1,0:T(8,128)(2,1)}, u32[]{:S(2)}, u32[]{:S(2)}) collective-permute-start(bf16[192,1024]{1,0:T(8,128)(2,1)} %copy-done.76), channel_id=1, source_target_pairs={{0,8},{4,12},{8,0},{12,4},{16,24},{20,28},{24,16},{28,20},{1,9},{5... | collective-permute-start | bytes 1179656 | tf_op jit(solution)/shard_map/ppermute | solution.py:699
  451.8 19.8 %collective-permute-start.62 = (bf16[192,1024]{1,0:T(8,128)(2,1)}, bf16[192,1024]{1,0:T(8,128)(2,1)}, u32[]{:S(2)}, u32[]{:S(2)}) collective-permute-start(bf16[192,1024]{1,0:T(8,128)(2,1)} %shard_map.312), channel_id=1, source_target_pairs={{0,8},{4,12},{8,0},{12,4},{16,24},{20,28},{24,16},{28,20},{1,9},{5... | collective-permute-start | bytes 1179656 | tf_op jit(solution)/shard_map/ppermute | solution.py:699
  471.6 7.1 %collective-permute-start.60 = (bf16[4,208,1024]{2,1,0:T(8,128)(2,1)}, bf16[4,208,1024]{2,1,0:T(8,128)(2,1)}, u32[]{:S(2)}, u32[]{:S(2)}) collective-permute-start(bf16[4,208,1024]{2,1,0:T(8,128)(2,1)} %shard_map.311.own_a), channel_id=1, source_target_pairs={{0,4},{4,0},{8,12},{12,8},{16,20},{20,16},{24,28},{28,24},{1,5},{5... | collective-permute-start | bytes 5111816 | tf_op jit(solution)/shard_map/ppermute | solution.py:699
  475.0 3.6 collective-permute-start.63
  (93 other events, 735.6 us)

commit v6 on v5

--- a/solution.py
+++ b/solution.py
@@ -13,7 +13,7 @@
 F32 = jnp.float32
 BF = jnp.bfloat16
 MIB = 2**20
-COST_UNIT = 10**8
+COST_UNIT = 6 * 10**7
 
 
 def rnd(v):

time: 497 us -> 498 us (level)
    unnamed x216 -> x218, local copies, waits for them, and re-layouts: 39.8 us -> 39.8 us
where the time goes in v6:
time: 498 us; the launch traced here: 490 us
  waiting for transfers between devices  191 us (38%)
  Pallas kernels  167 us (34%)
  starting transfers between devices  61.1 us (12%)
  local copies, waits for them, and re-layouts  57.4 us (12%)
  other arithmetic  12.1 us (2%)
    ppermute x21, waiting for transfers between devices, turn(): lax.ppermute(value, 'fsdp', [(i, (i + step) % shards) for i in range(shar...  134 us
    ppermute x43, waiting for transfers between devices, swap(): return lax.ppermute(value, 'dp', [(i, i ^ bit) for i in range(replicas)])  56.8 us
    unnamed x218, local copies, waits for them, and re-layouts  39.8 us
    pallas_call x1, Pallas kernels, feed(): pl.pallas_call(functools.partial(feed_kernel, cuts, min(1024, hidden)), i...  34 us
    ppermute x43, starting transfers between devices, swap(): return lax.ppermute(value, 'dp', [(i, i ^ bit) for i in range(replicas)])  28.8 us
    pallas_call x1, Pallas kernels, attend_grad(): pl.pallas_call(functools.partial(attend_grad_kernel, group_len, head_dim)...  28.7 us
    pallas_call x4, Pallas kernels, wide_grad(): pl.pallas_call(functools.partial(wide_kernel, cut, other, reverse, len(le...  25.1 us
    ppermute x21, starting transfers between devices, turn(): lax.ppermute(value, 'fsdp', [(i, (i + step) % shards) for i in range(shar...  23.8 us
  transfers between devices with their start and end apart: 66, of which 25 were waited for; matrix products, arithmetic and copies ran while one was open for 4% of the time, Pallas kernels for 23%

profile of v6, /device:TPU:0, one launch (start us, length us, event | category | flops | bytes accessed | tf_op | source)
XLA Modules:
  0.0 490.0 jit_solution(6541546176534854651)
XLA Ops:
  6.1 3.0 collective-permute-start.3
  9.1 2.0 collective-permute-start.4
  11.2 3.4 all-to-all-start
  14.8 3.8 collective-permute-start
  20.8 18.2 %collective-permute-done = bf16[1,3072]{1,0:T(2,128)(2,1)S(1)} collective-permute-done((bf16[1,3072]{1,0:T(2,128)(2,1)S(1)}, bf16[1,3072]{1,0:T(2,128)(2,1)S(1)}, u32[]{:S(2)}, u32[]{:S(2)}) %collective-permute-start) | collective-permute-done | bytes 6176 | tf_op jit(solution)/shard_map/ppermute | solution.py:712
  38.9 3.7 collective-permute-done.1
  44.5 1.5 collective-permute-start.8
  46.0 1.5 collective-permute-start.10
  47.9 3.4 collective-permute-start.14
  52.0 1.5 collective-permute-start.12
  54.0 5.3 %collective-permute-done.12 = bf16[4,32,768]{2,1,0:T(8,128)(2,1)S(1)} collective-permute-done((bf16[4,32,768]{2,1,0:T(8,128)(2,1)S(1)}, bf16[4,32,768]{2,1,0:T(8,128)(2,1)S(1)}, u32[]{:S(2)}, u32[]{:S(2)}) %collective-permute-start.12) | collective-permute-done | bytes 196640 | tf_op jit(solution)/shard_map/ppermute | solution.py:699
  62.3 1.6 copy-done.14
  63.9 2.6 shard_map.274
  67.5 8.1 %collective-permute-done.5.block = bf16[512,1024]{1,0:T(8,128)(2,1)S(1)} collective-permute-done((bf16[512,1024]{1,0:T(8,128)(2,1)}, bf16[512,1024]{1,0:T(8,128)(2,1)S(1)}, u32[]{:S(2)}, u32[]{:S(2)}) %collective-permute-start.5) | collective-permute-done | bytes 1048608 | tf_op jit(solution)/shard_map/ppermute | solution.py:712
  75.6 2.6 shard_map.275
  78.2 17.1 %collective-permute-done.14.block = bf16[512,1024]{1,0:T(8,128)(2,1)S(1)} collective-permute-done((bf16[512,1024]{1,0:T(8,128)(2,1)}, bf16[512,1024]{1,0:T(8,128)(2,1)S(1)}, u32[]{:S(2)}, u32[]{:S(2)}) %collective-permute-start.14) | collective-permute-done | bytes 1048608 | tf_op jit(solution)/shard_map/ppermute | solution.py:712
  95.3 2.1 shard_map.276
  98.9 10.7 %collective-permute-done.18.refs_0_ = bf16[288,1024]{1,0:T(8,128)(2,1)S(1)} collective-permute-done((bf16[288,1024]{1,0:T(8,128)(2,1)}, bf16[288,1024]{1,0:T(8,128)(2,1)S(1)}, u32[]{:S(2)}, u32[]{:S(2)}) %collective-permute-start.18) | collective-permute-done | bytes 589856 | tf_op jit(solution)/shard_map/ppermute | solution.py:712
  110.5 1.7 slice_bitcast_fusion.1
  112.2 1.7 slice_bitcast_fusion
  115.0 2.1 pad_maximum_fusion.2.refs_4_
  123.7 18.3 %collective-permute-done.20.refs_0_ = bf16[3,160,1024]{2,1,0:T(8,128)(2,1)S(1)} collective-permute-done((bf16[3,160,1024]{2,1,0:T(8,128)(2,1)}, bf16[3,160,1024]{2,1,0:T(8,128)(2,1)S(1)}, u32[]{:S(2)}, u32[]{:S(2)}) %collective-permute-start.20) | collective-permute-done | bytes 983072 | tf_op jit(solution)/shard_map/ppermute | solution.py:699
  144.1 2.6 shard_map.277
  146.7 1.7 copy-done.2
  149.4 17.6 %shard_map.278 = (bf16[2048,256]{1,0:T(8,128)(2,1)}, f32[2,2,2048]{2,1,0:T(2,128)}) custom-call(bf16[2048,768]{1,0:T(8,128)(2,1)} %copy-done.2, bf16[2048,768]{1,0:T(8,128)(2,1)} %copy-done.2, bf16[2048,768]{1,0:T(8,128)(2,1)} %copy-done.2, s32[1,2048]{1,0:T(1,128)} %bitcast.153), custom_call_target="tpu_custom_call" | custom-call | flops 1080000000 | bytes 1 | tf_op jit(solution)/shard_map/pallas_call | solution.py:129
  170.2 11.0 %collective-permute-done.15.refs_1_ = bf16[512,256]{1,0:T(8,128)(2,1)S(1)} collective-permute-done((bf16[512,256]{1,0:T(8,128)(2,1)S(1)}, bf16[512,256]{1,0:T(8,128)(2,1)S(1)}, u32[]{:S(2)}, u32[]{:S(2)}) %collective-permute-start.15) | collective-permute-done | bytes 262176 | tf_op jit(solution)/shard_map/ppermute | solution.py:712
  181.6 9.9 %collective-permute-done.16.refs_2_ = bf16[512,256]{1,0:T(8,128)(2,1)S(1)} collective-permute-done((bf16[512,256]{1,0:T(8,128)(2,1)S(1)}, bf16[512,256]{1,0:T(8,128)(2,1)S(1)}, u32[]{:S(2)}, u32[]{:S(2)}) %collective-permute-start.16) | collective-permute-done | bytes 262176 | tf_op jit(solution)/shard_map/ppermute | solution.py:712
  195.1 3.2 collective-permute-done.30.refs_17_
  199.5 34.0 %shard_map.284 = (bf16[512,1024]{1,0:T(8,128)(2,1)}, bf16[512,1024]{1,0:T(8,128)(2,1)}, bf16[512,4096]{1,0:T(8,128)(2,1)}, bf16[512,4096]{1,0:T(8,128)(2,1)}, f3...) custom-call(s32[2]{0:T(128)} %copy-done.48, ...), custom_call_target="tpu_custom_call" | custom-call | flops 2400000000 | bytes 1 | tf_op jit(solution)/shard_map/pallas_call | solution.py:345
  233.5 7.1 %shard_map.285 = (bf16[4,4,128,1024]{3,2,1,0:T(8,128)(2,1)}, f32[8,128]{1,0:T(8,128)}) custom-call(s32[2]{0:T(128)} %copy-done.48, bf16[512,4096]{1,0:T(8,128)(2,1)} %get-tuple-element.112.left, bf16[512,1024]{1,0:T(8,128)(2,1)} %right.3), custom_call_target="tpu_custom_call" | custom-call | flops 450000000 | bytes 1 | tf_op jit(solution)/shard_map/pallas_call | solution.py:528
  240.7 7.5 %shard_map.286 = (bf16[4,4,128,1024]{3,2,1,0:T(8,128)(2,1)}, f32[8,128]{1,0:T(8,128)}) custom-call(s32[2]{0:T(128)} %copy-done.48, bf16[512,4096]{1,0:T(8,128)(2,1)} %get-tuple-element.110.right, bf16[512,1024]{1,0:T(8,128)(2,1)} %get-tuple-element.111.refs_0_, f32[8,128]{1,0:T(8,128)} %get-tuple-element.113.refs_1_), custom_call_target="tpu_custom_call" | custom-call | flops 360000000 | bytes 1 | tf_op jit(solution)/shard_map/pallas_call | solution.py:464
  249.7 5.1 %all-to-all-start.1 = ((bf16[512,4,256]{2,0,1:T(8,128)(2,1)}), bf16[512,4,256]{2,0,1:T(8,128)(2,1)S(1)}, u32[]{:S(2)}, u32[]{:S(2)}) async-start(bf16[512,4,256]{2,0,1:T(8,128)(2,1)} %bitcast.121), calls=%async_computation.1 | async-start | bytes 2097152 | tf_op jit(solution)/shard_map/all_to_all | solution.py:1057
  254.8 4.1 shard_map.287
  258.9 8.5 %shard_map.288 = (bf16[2,4,128,1024]{3,2,1,0:T(8,128)(2,1)}, bf16[2,4,128,1024]{3,2,1,0:T(8,128)(2,1)}, f32[8,128]{1,0:T(8,128)}) custom-call(s32[2]{0:T(128)} %copy-done.48, bf16[512,4096]{1,0:T(8,128)(2,1)} %get-tuple-element.112.left, bf16[512,1024]{1,0:T(8,128)(2,1)} %right.3, bf16[4,4,128,1024]{3,2,1,0:T(8,128)(2,1)} %collective-permute-done.35.got, ...), custom_call_target="tpu_custom_call" | custom-call | flops 450000000 | bytes 1 | tf_op jit(solution)/shard_map/pallas_call | solution.py:528
  268.4 9.1 %shard_map.289 = (bf16[2,4,128,1024]{3,2,1,0:T(8,128)(2,1)}, bf16[2,4,128,1024]{3,2,1,0:T(8,128)(2,1)}, f32[8,128]{1,0:T(8,128)}) custom-call(s32[2]{0:T(128)} %copy-done.48, bf16[512,4096]{1,0:T(8,128)(2,1)} %get-tuple-element.110.right, bf16[512,1024]{1,0:T(8,128)(2,1)} %get-tuple-element.111.refs_0_, ...), custom_call_target="tpu_custom_call" | custom-call | flops 360000000 | bytes 1 | tf_op jit(solution)/shard_map/pallas_call | solution.py:464
  279.5 4.4 shard_map.290
  285.0 28.7 %shard_map.291 = (bf16[2048,256]{1,0:T(8,128)(2,1)}, bf16[2048,256]{1,0:T(8,128)(2,1)}, bf16[2048,256]{1,0:T(8,128)(2,1)}, f32[2,2,128]{2,1,0:T(2,128)}) custom-call(bf16[2048,768]{1,0:T(8,128)(2,1)} %copy-done.2, bf16[2048,768]{1,0:T(8,128)(2,1)} %copy-done.2, bf16[2048,768]{1,0:T(8,128)(2,1)} %copy-done.2, s32[1,2048]{1,0:T(1,128)} %bitcast.154, ...), custom_call_target="tpu_custom_call" | custom-call | flops 1680000000 | bytes 1 | tf_op jit(solution)/shard_map/pallas_call | solution.py:148
  317.4 2.9 shard_map.292
  320.3 2.3 collective-permute-start.36
  329.5 1.6 copy-done.20
  331.1 2.7 shard_map.293
  335.8 2.7 shard_map.294
  343.3 1.9 shard_map.296
  345.2 2.7 collective-permute-done.36.travel
  350.4 1.9 shard_map.298
  353.3 1.9 shard_map.299
  363.5 7.1 %shard_map.300 = (bf16[4,4,48,768]{3,2,1,0:T(8,128)(2,1)}, bf16[4,4,48,768]{3,2,1,0:T(8,128)(2,1)}, f32[8,128]{1,0:T(8,128)S(1)}) custom-call(s32[2]{0:T(128)S(1)} %copy-done.49, bf16[2048,256]{1,0:T(8,128)(2,1)S(1)} %copy-done.7, bf16[2048,256]{1,0:T(8,128)(2,1)S(1)} %copy-done.10, bf16[2048,256]{1,0:T(8,128)(2,1)S(1)} %copy-done.13, ...), custom_call_target="tpu_custom_call" | custom-call | flops 390000000 | bytes 1 | tf_op jit(solution)/shard_map/pallas_call | solution.py:589
  370.7 12.4 %collective-permute-done.42.travel = bf16[512,1024]{1,0:T(8,128)(2,1)S(1)} collective-permute-done((bf16[512,1024]{1,0:T(8,128)(2,1)}, bf16[512,1024]{1,0:T(8,128)(2,1)S(1)}, u32[]{:S(2)}, u32[]{:S(2)}) %collective-permute-start.42) | collective-permute-done | bytes 1048608 | tf_op jit(solution)/shard_map/ppermute | solution.py:712
  386.2 1.6 collective-permute-start.48
  389.7 11.1 %collective-permute-done.45.travel = bf16[288,1024]{1,0:T(8,128)(2,1)S(1)} collective-permute-done((bf16[288,1024]{1,0:T(8,128)(2,1)S(1)}, bf16[288,1024]{1,0:T(8,128)(2,1)S(1)}, u32[]{:S(2)}, u32[]{:S(2)}) %collective-permute-start.45) | collective-permute-done | bytes 589856 | tf_op jit(solution)/shard_map/ppermute | solution.py:712
  402.4 3.9 collective-permute-start.54
  406.3 12.9 %collective-permute-done.53 = bf16[48,768]{1,0:T(8,128)(2,1)S(1)} collective-permute-done((bf16[48,768]{1,0:T(8,128)(2,1)S(1)}, bf16[48,768]{1,0:T(8,128)(2,1)S(1)}, u32[]{:S(2)}, u32[]{:S(2)}) %collective-permute-start.53) | collective-permute-done | bytes 73760 | tf_op jit(solution)/shard_map/ppermute | solution.py:712
  419.5 14.0 %collective-permute-done.54 = bf16[48,768]{1,0:T(8,128)(2,1)S(1)} collective-permute-done((bf16[48,768]{1,0:T(8,128)(2,1)S(1)}, bf16[48,768]{1,0:T(8,128)(2,1)S(1)}, u32[]{:S(2)}, u32[]{:S(2)}) %collective-permute-start.54) | collective-permute-done | bytes 73760 | tf_op jit(solution)/shard_map/ppermute | solution.py:712
  434.3 1.6 collective-permute-start.56
  435.9 2.2 collective-permute-start.52
  438.7 1.6 collective-permute-start.58
  440.3 10.0 %collective-permute-done.57.refs_1_.refs_0_ = bf16[192,1024]{1,0:T(8,128)(2,1)S(1)} collective-permute-done((bf16[192,1024]{1,0:T(8,128)(2,1)S(1)}, bf16[192,1024]{1,0:T(8,128)(2,1)S(1)}, u32[]{:S(2)}, u32[]{:S(2)}) %collective-permute-start.57) | collective-permute-done | bytes 393248 | tf_op jit(solution)/shard_map/ppermute | solution.py:699
  454.4 5.2 %collective-permute-done.58 = bf16[208,1024]{1,0:T(8,128)(2,1)} collective-permute-done((bf16[208,1024]{1,0:T(8,128)(2,1)S(1)}, bf16[208,1024]{1,0:T(8,128)(2,1)}, u32[]{:S(2)}, u32[]{:S(2)}) %collective-permute-start.58) | collective-permute-done | bytes 426016 | tf_op jit(solution)/shard_map/ppermute | solution.py:699
  459.6 7.6 %collective-permute-done.59 = bf16[208,1024]{1,0:T(8,128)(2,1)} collective-permute-done((bf16[208,1024]{1,0:T(8,128)(2,1)}, bf16[208,1024]{1,0:T(8,128)(2,1)}, u32[]{:S(2)}, u32[]{:S(2)}) %collective-permute-start.59) | collective-permute-done | bytes 426016 | tf_op jit(solution)/shard_map/ppermute | solution.py:699
  467.1 2.7 pad_maximum_fusion.refs_0_
  469.8 2.6 shard_map.309
  474.0 2.5 pad_maximum_fusion.1.refs_0_
  476.5 3.6 collective-permute-done.63.other_b
  481.5 7.0 %shard_map.314 = (f32[256,1024]{1,0:T(8,128)}, f32[256,4096]{1,0:T(8,128)}, f32[1024,1024]{1,0:T(8,128)}, f32[256,3072]{1,0:T(8,128)}, f32[64,1024]{1,0:T(8,128)S(1)}) custom-call(s32[2]{0:T(128)S(1)} %copy-done.49, bf16[4,208,1024]{2,1,0:T(8,128)(2,1)S(1)} %copy-done.16, bf16[4,208,1024]{2,1,0:T(8,128)(2,1)} %collective-permute-done.60.other_a, ...), custom_call_target="tpu_custom_call" | custom-call | flops 420000000 | bytes 1 | tf_op jit(solution)/shard_map/pallas_call | solution.py:635
  (408 shorter events, 87.1 us)
Async XLA Ops:
  6.1 36.9 %collective-permute-start.3 = (bf16[288,1024]{1,0:T(8,128)(2,1)}, bf16[288,1024]{1,0:T(8,128)(2,1)}, u32[]{:S(2)}, u32[]{:S(2)}) collective-permute-start(bf16[288,1024]{1,0:T(8,128)(2,1)} %shard_map.271), channel_id=1, source_target_pairs={{0,1},{1,2},{2,3},{3,0},{4,5},{5,6},{6,7},{7,4},{8,9},{9,10},{10,1... | collective-permute-start | bytes 1769480 | tf_op jit(solution)/shard_map/ppermute | solution.py:712
  9.1 33.8 %collective-permute-start.4 = (bf16[288,1024]{1,0:T(8,128)(2,1)}, bf16[288,1024]{1,0:T(8,128)(2,1)S(1)}, u32[]{:S(2)}, u32[]{:S(2)}) collective-permute-start(bf16[288,1024]{1,0:T(8,128)(2,1)} %shard_map.271), channel_id=1, source_target_pairs={{0,3},{1,0},{2,1},{3,2},{4,7},{5,4},{6,5},{7,6},{8,11},{9,8},{10,9... | collective-permute-start | bytes 1769480 | tf_op jit(solution)/shard_map/ppermute | solution.py:712
  11.2 31.8 %all-to-all-start = ((bf16[4,32,768]{2,1,0:T(8,128)(2,1)}), bf16[4,32,768]{2,1,0:T(8,128)(2,1)S(1)}, u32[]{:S(2)}, u32[]{:S(2)}) async-start(bf16[4,32,768]{2,1,0:T(8,128)(2,1)} %reshape.206.refs_1_), calls=%async_computation | async-start | bytes 393216 | tf_op jit(solution)/shard_map/all_to_all | solution.py:1025
  14.8 24.2 %collective-permute-start = (bf16[1,3072]{1,0:T(2,128)(2,1)S(1)}, bf16[1,3072]{1,0:T(2,128)(2,1)S(1)}, u32[]{:S(2)}, u32[]{:S(2)}) collective-permute-start(bf16[1,3072]{1,0:T(2,128)(2,1)S(1)} %constant_dynamic-update-slice_fusion.refs_1_), channel_id=1, source_target_pairs={{0,3},{1,0},{2,1},{3,2},{4,7},{5,4},{6,5},{7,6},{8,11},{9,8},{10,9... | collective-permute-start | bytes 18440 | tf_op jit(solution)/shard_map/ppermute | solution.py:712
  18.6 24.0 %collective-permute-start.1 = (bf16[1,3072]{1,0:T(2,128)(2,1)S(1)}, bf16[1,3072]{1,0:T(2,128)(2,1)S(1)}, u32[]{:S(2)}, u32[]{:S(2)}) collective-permute-start(bf16[1,3072]{1,0:T(2,128)(2,1)S(1)} %constant_dynamic-update-slice_fusion.refs_1_), channel_id=1, source_target_pairs={{0,2},{1,3},{2,0},{3,1},{4,6},{5,7},{6,4},{7,5},{8,10},{9,11},{10,... | collective-permute-start | bytes 18440 | tf_op jit(solution)/shard_map/ppermute | solution.py:712
  18.6 24.0 %collective-permute-start.2 = (bf16[1,3072]{1,0:T(2,128)(2,1)S(1)}, bf16[1,3072]{1,0:T(2,128)(2,1)S(1)}, u32[]{:S(2)}, u32[]{:S(2)}) collective-permute-start(bf16[1,3072]{1,0:T(2,128)(2,1)S(1)} %constant_dynamic-update-slice_fusion.refs_1_), channel_id=1, source_target_pairs={{0,1},{1,2},{2,3},{3,0},{4,5},{5,6},{6,7},{7,4},{8,9},{9,10},{10,1... | collective-permute-start | bytes 18440 | tf_op jit(solution)/shard_map/ppermute | solution.py:712
  44.5 7.5 %collective-permute-start.7 = (bf16[4,32,768]{2,1,0:T(8,128)(2,1)}, bf16[4,32,768]{2,1,0:T(8,128)(2,1)S(1)}, u32[]{:S(2)}, u32[]{:S(2)}) collective-permute-start(bf16[4,32,768]{2,1,0:T(8,128)(2,1)} %shard_map.273), channel_id=1, source_target_pairs={{0,4},{4,0},{8,12},{12,8},{16,20},{20,16},{24,28},{28,24},{1,5},{5... | collective-permute-start | bytes 589832 | tf_op jit(solution)/shard_map/ppermute | solution.py:699
  44.5 7.5 %collective-permute-start.8 = (bf16[4,32,768]{2,1,0:T(8,128)(2,1)}, bf16[4,32,768]{2,1,0:T(8,128)(2,1)S(1)}, u32[]{:S(2)}, u32[]{:S(2)}) collective-permute-start(bf16[4,32,768]{2,1,0:T(8,128)(2,1)} %shard_map.273), channel_id=1, source_target_pairs={{0,8},{4,12},{8,0},{12,4},{16,24},{20,28},{24,16},{28,20},{1,9},{5... | collective-permute-start | bytes 589832 | tf_op jit(solution)/shard_map/ppermute | solution.py:699
  46.0 7.5 %collective-permute-start.10 = (bf16[4,32,768]{2,1,0:T(8,128)(2,1)}, bf16[4,32,768]{2,1,0:T(8,128)(2,1)S(1)}, u32[]{:S(2)}, u32[]{:S(2)}) collective-permute-start(bf16[4,32,768]{2,1,0:T(8,128)(2,1)} %shard_map.273), channel_id=1, source_target_pairs={{0,16},{4,20},{8,24},{12,28},{16,0},{20,4},{24,8},{28,12},{1,17},{... | collective-permute-start | bytes 589832 | tf_op jit(solution)/shard_map/ppermute | solution.py:699
  47.5 28.1 %collective-permute-start.5 = (bf16[512,1024]{1,0:T(8,128)(2,1)}, bf16[512,1024]{1,0:T(8,128)(2,1)S(1)}, u32[]{:S(2)}, u32[]{:S(2)}) collective-permute-start(bf16[512,1024]{1,0:T(8,128)(2,1)} %shard_map.272.block), channel_id=1, source_target_pairs={{0,1},{1,2},{2,3},{3,0},{4,5},{5,6},{6,7},{7,4},{8,9},{9,10},{10,1... | collective-permute-start | bytes 3145736 | tf_op jit(solution)/shard_map/ppermute | solution.py:712
  47.9 47.3 %collective-permute-start.14 = (bf16[512,1024]{1,0:T(8,128)(2,1)}, bf16[512,1024]{1,0:T(8,128)(2,1)S(1)}, u32[]{:S(2)}, u32[]{:S(2)}) collective-permute-start(bf16[512,1024]{1,0:T(8,128)(2,1)} %shard_map.272.block), channel_id=1, source_target_pairs={{0,3},{1,0},{2,1},{3,2},{4,7},{5,4},{6,5},{7,6},{8,11},{9,8},{10,9... | collective-permute-start | bytes 3145736 | tf_op jit(solution)/shard_map/ppermute | solution.py:712
  52.0 7.3 %collective-permute-start.12 = (bf16[4,32,768]{2,1,0:T(8,128)(2,1)S(1)}, bf16[4,32,768]{2,1,0:T(8,128)(2,1)S(1)}, u32[]{:S(2)}, u32[]{:S(2)}) collective-permute-start(bf16[4,32,768]{2,1,0:T(8,128)(2,1)S(1)} %collective-permute-done.8), channel_id=1, source_target_pairs={{0,16},{4,20},{8,24},{12,28},{16,0},{20,4},{24,8},{28,12},{1,17},{... | collective-permute-start | bytes 589832 | tf_op jit(solution)/shard_map/ppermute | solution.py:699
  53.6 56.1 %collective-permute-start.18 = (bf16[288,1024]{1,0:T(8,128)(2,1)}, bf16[288,1024]{1,0:T(8,128)(2,1)S(1)}, u32[]{:S(2)}, u32[]{:S(2)}) collective-permute-start(bf16[288,1024]{1,0:T(8,128)(2,1)} %collective-permute-done.3.refs_2_.refs_1_.refs_0_), channel_id=1, source_target_pairs={{0,1},{1,2},{2,3},{3,0},{4,5},{5,6},{6,7},{7,4},{8,9},{9,10},{10,1... | collective-permute-start | bytes 1769480 | tf_op jit(solution)/shard_map/ppermute | solution.py:712
  54.0 5.3 %collective-permute-start.11 = (bf16[4,32,768]{2,1,0:T(8,128)(2,1)S(1)}, bf16[4,32,768]{2,1,0:T(8,128)(2,1)S(1)}, u32[]{:S(2)}, u32[]{:S(2)}) collective-permute-start(bf16[4,32,768]{2,1,0:T(8,128)(2,1)S(1)} %collective-permute-done.10), channel_id=1, source_target_pairs={{0,4},{4,0},{8,12},{12,8},{16,20},{20,16},{24,28},{28,24},{1,5},{5... | collective-permute-start | bytes 589832 | tf_op jit(solution)/shard_map/ppermute | solution.py:699
  117.1 24.9 %collective-permute-start.20 = (bf16[3,160,1024]{2,1,0:T(8,128)(2,1)}, bf16[3,160,1024]{2,1,0:T(8,128)(2,1)S(1)}, u32[]{:S(2)}, u32[]{:S(2)}) collective-permute-start(bf16[3,160,1024]{2,1,0:T(8,128)(2,1)} %pad_maximum_fusion.2.refs_4_), channel_id=1, source_target_pairs={{0,8},{4,12},{8,0},{12,4},{16,24},{20,28},{24,16},{28,20},{1,9},{5... | collective-permute-start | bytes 2949128 | tf_op jit(solution)/shard_map/ppermute | solution.py:699
  117.7 25.8 %collective-permute-start.6 = (bf16[512,1024]{1,0:T(8,128)(2,1)S(1)}, bf16[512,1024]{1,0:T(8,128)(2,1)S(1)}, u32[]{:S(2)}, u32[]{:S(2)}) collective-permute-start(bf16[512,1024]{1,0:T(8,128)(2,1)S(1)} %copy-done.25), channel_id=1, source_target_pairs={{0,1},{1,2},{2,3},{3,0},{4,5},{5,6},{6,7},{7,4},{8,9},{9,10},{10,1... | collective-permute-start | bytes 3145736 | tf_op jit(solution)/shard_map/ppermute | solution.py:712
  121.7 45.3 %collective-permute-start.29 = (bf16[3,128,1024]{2,1,0:T(8,128)(2,1)}, bf16[3,128,1024]{2,1,0:T(8,128)(2,1)}, u32[]{:S(2)}, u32[]{:S(2)}) collective-permute-start(bf16[3,128,1024]{2,1,0:T(8,128)(2,1)} %pad_maximum_fusion.3.refs_12_), channel_id=1, source_target_pairs={{0,16},{4,20},{8,24},{12,28},{16,0},{20,4},{24,8},{28,12},{1,17},{... | collective-permute-start | bytes 2359304 | tf_op jit(solution)/shard_map/ppermute | solution.py:699
  122.2 45.9 %collective-permute-start.27 = (bf16[3,128,1024]{2,1,0:T(8,128)(2,1)}, bf16[3,128,1024]{2,1,0:T(8,128)(2,1)}, u32[]{:S(2)}, u32[]{:S(2)}) collective-permute-start(bf16[3,128,1024]{2,1,0:T(8,128)(2,1)} %pad_maximum_fusion.3.refs_12_), channel_id=1, source_target_pairs={{0,8},{4,12},{8,0},{12,4},{16,24},{20,28},{24,16},{28,20},{1,9},{5... | collective-permute-start | bytes 2359304 | tf_op jit(solution)/shard_map/ppermute | solution.py:699
  123.7 44.5 %collective-permute-start.26 = (bf16[3,128,1024]{2,1,0:T(8,128)(2,1)}, bf16[3,128,1024]{2,1,0:T(8,128)(2,1)}, u32[]{:S(2)}, u32[]{:S(2)}) collective-permute-start(bf16[3,128,1024]{2,1,0:T(8,128)(2,1)} %pad_maximum_fusion.3.refs_12_), channel_id=1, source_target_pairs={{0,4},{4,0},{8,12},{12,8},{16,20},{20,16},{24,28},{28,24},{1,5},{5... | collective-permute-start | bytes 2359304 | tf_op jit(solution)/shard_map/ppermute | solution.py:699
  142.0 28.1 %collective-permute-start.22 = (bf16[3,160,1024]{2,1,0:T(8,128)(2,1)}, bf16[3,160,1024]{2,1,0:T(8,128)(2,1)}, u32[]{:S(2)}, u32[]{:S(2)}) collective-permute-start(bf16[3,160,1024]{2,1,0:T(8,128)(2,1)} %pad_maximum_fusion.2.refs_4_), channel_id=1, source_target_pairs={{0,16},{4,20},{8,24},{12,28},{16,0},{20,4},{24,8},{28,12},{1,17},{... | collective-permute-start | bytes 2949128 | tf_op jit(solution)/shard_map/ppermute | solution.py:699
  143.5 26.6 %collective-permute-start.19 = (bf16[3,160,1024]{2,1,0:T(8,128)(2,1)}, bf16[3,160,1024]{2,1,0:T(8,128)(2,1)}, u32[]{:S(2)}, u32[]{:S(2)}) collective-permute-start(bf16[3,160,1024]{2,1,0:T(8,128)(2,1)} %pad_maximum_fusion.2.refs_4_), channel_id=1, source_target_pairs={{0,4},{4,0},{8,12},{12,8},{16,20},{20,16},{24,28},{28,24},{1,5},{5... | collective-permute-start | bytes 2949128 | tf_op jit(solution)/shard_map/ppermute | solution.py:699
  167.1 25.6 %collective-permute-start.24 = (bf16[3,160,1024]{2,1,0:T(8,128)(2,1)}, bf16[3,160,1024]{2,1,0:T(8,128)(2,1)}, u32[]{:S(2)}, u32[]{:S(2)}) collective-permute-start(bf16[3,160,1024]{2,1,0:T(8,128)(2,1)} %shard_map.282.refs_6_), channel_id=1, source_target_pairs={{0,16},{4,20},{8,24},{12,28},{16,0},{20,4},{24,8},{28,12},{1,17},{... | collective-permute-start | bytes 2949128 | tf_op jit(solution)/shard_map/ppermute | solution.py:699
  168.1 25.1 %collective-permute-start.28 = (bf16[3,128,1024]{2,1,0:T(8,128)(2,1)}, bf16[3,128,1024]{2,1,0:T(8,128)(2,1)}, u32[]{:S(2)}, u32[]{:S(2)}) collective-permute-start(bf16[3,128,1024]{2,1,0:T(8,128)(2,1)} %collective-permute-done.27.refs_14_), channel_id=1, source_target_pairs={{0,4},{4,0},{8,12},{12,8},{16,20},{20,16},{24,28},{28,24},{1,5},{5... | collective-permute-start | bytes 2359304 | tf_op jit(solution)/shard_map/ppermute | solution.py:699
  168.2 25.1 %collective-permute-start.31 = (bf16[3,128,1024]{2,1,0:T(8,128)(2,1)}, bf16[3,128,1024]{2,1,0:T(8,128)(2,1)}, u32[]{:S(2)}, u32[]{:S(2)}) collective-permute-start(bf16[3,128,1024]{2,1,0:T(8,128)(2,1)} %shard_map.283.refs_16_), channel_id=1, source_target_pairs={{0,8},{4,12},{8,0},{12,4},{16,24},{20,28},{24,16},{28,20},{1,9},{5... | collective-permute-start | bytes 2359304 | tf_op jit(solution)/shard_map/ppermute | solution.py:699
  170.1 11.1 %collective-permute-start.15 = (bf16[512,256]{1,0:T(8,128)(2,1)S(1)}, bf16[512,256]{1,0:T(8,128)(2,1)S(1)}, u32[]{:S(2)}, u32[]{:S(2)}) collective-permute-start(bf16[512,256]{1,0:T(8,128)(2,1)S(1)} %get-tuple-element.193), channel_id=1, source_target_pairs={{0,1},{1,2},{2,3},{3,0},{4,5},{5,6},{6,7},{7,4},{8,9},{9,10},{10,1... | collective-permute-start | bytes 786440 | tf_op jit(solution)/shard_map/ppermute | solution.py:712
  170.1 21.4 %collective-permute-start.16 = (bf16[512,256]{1,0:T(8,128)(2,1)S(1)}, bf16[512,256]{1,0:T(8,128)(2,1)S(1)}, u32[]{:S(2)}, u32[]{:S(2)}) collective-permute-start(bf16[512,256]{1,0:T(8,128)(2,1)S(1)} %get-tuple-element.192), channel_id=1, source_target_pairs={{0,2},{1,3},{2,0},{3,1},{4,6},{5,7},{6,4},{7,5},{8,10},{9,11},{10,... | collective-permute-start | bytes 786440 | tf_op jit(solution)/shard_map/ppermute | solution.py:712
  181.2 11.5 %collective-permute-start.17 = (bf16[512,256]{1,0:T(8,128)(2,1)S(1)}, bf16[512,256]{1,0:T(8,128)(2,1)S(1)}, u32[]{:S(2)}, u32[]{:S(2)}) collective-permute-start(bf16[512,256]{1,0:T(8,128)(2,1)S(1)} %get-tuple-element.191), channel_id=1, source_target_pairs={{0,3},{1,0},{2,1},{3,2},{4,7},{5,4},{6,5},{7,6},{8,11},{9,8},{10,9... | collective-permute-start | bytes 786440 | tf_op jit(solution)/shard_map/ppermute | solution.py:712
  191.5 6.8 %collective-permute-start.23 = (bf16[3,160,1024]{2,1,0:T(8,128)(2,1)}, bf16[3,160,1024]{2,1,0:T(8,128)(2,1)S(1)}, u32[]{:S(2)}, u32[]{:S(2)}) collective-permute-start(bf16[3,160,1024]{2,1,0:T(8,128)(2,1)} %collective-permute-done.22.refs_8_), channel_id=1, source_target_pairs={{0,4},{4,0},{8,12},{12,8},{16,20},{20,16},{24,28},{28,24},{1,5},{5... | collective-permute-start | bytes 2949128 | tf_op jit(solution)/shard_map/ppermute | solution.py:699
  192.7 5.7 %collective-permute-start.21 = (bf16[3,160,1024]{2,1,0:T(8,128)(2,1)S(1)}, bf16[3,160,1024]{2,1,0:T(8,128)(2,1)}, u32[]{:S(2)}, u32[]{:S(2)}) collective-permute-start(bf16[3,160,1024]{2,1,0:T(8,128)(2,1)S(1)} %copy-done.60), channel_id=1, source_target_pairs={{0,4},{4,0},{8,12},{12,8},{16,20},{20,16},{24,28},{28,24},{1,5},{5... | collective-permute-start | bytes 2949128 | tf_op jit(solution)/shard_map/ppermute | solution.py:699
  192.7 6.8 %collective-permute-start.25 = (bf16[3,160,1024]{2,1,0:T(8,128)(2,1)}, bf16[3,160,1024]{2,1,0:T(8,128)(2,1)}, u32[]{:S(2)}, u32[]{:S(2)}) collective-permute-start(bf16[3,160,1024]{2,1,0:T(8,128)(2,1)} %collective-permute-done.24.refs_10_), channel_id=1, source_target_pairs={{0,4},{4,0},{8,12},{12,8},{16,20},{20,16},{24,28},{28,24},{1,5},{5... | collective-permute-start | bytes 2949128 | tf_op jit(solution)/shard_map/ppermute | solution.py:699
  193.2 5.2 %collective-permute-start.30 = (bf16[3,128,1024]{2,1,0:T(8,128)(2,1)}, bf16[3,128,1024]{2,1,0:T(8,128)(2,1)}, u32[]{:S(2)}, u32[]{:S(2)}) collective-permute-start(bf16[3,128,1024]{2,1,0:T(8,128)(2,1)} %shard_map.283.refs_16_), channel_id=1, source_target_pairs={{0,4},{4,0},{8,12},{12,8},{16,20},{20,16},{24,28},{28,24},{1,5},{5... | collective-permute-start | bytes 2359304 | tf_op jit(solution)/shard_map/ppermute | solution.py:699
  193.3 6.2 %collective-permute-start.32 = (bf16[3,128,1024]{2,1,0:T(8,128)(2,1)}, bf16[3,128,1024]{2,1,0:T(8,128)(2,1)}, u32[]{:S(2)}, u32[]{:S(2)}) collective-permute-start(bf16[3,128,1024]{2,1,0:T(8,128)(2,1)} %collective-permute-done.31.refs_18_), channel_id=1, source_target_pairs={{0,4},{4,0},{8,12},{12,8},{16,20},{20,16},{24,28},{28,24},{1,5},{5... | collective-permute-start | bytes 2359304 | tf_op jit(solution)/shard_map/ppermute | solution.py:699
  240.6 18.3 %collective-permute-start.35 = (bf16[4,4,128,1024]{3,2,1,0:T(8,128)(2,1)}, bf16[4,4,128,1024]{3,2,1,0:T(8,128)(2,1)}, u32[]{:S(2)}, u32[]{:S(2)}) collective-permute-start(bf16[4,4,128,1024]{3,2,1,0:T(8,128)(2,1)} %get-tuple-element.117), channel_id=1, source_target_pairs={{0,4},{4,0},{8,12},{12,8},{16,20},{20,16},{24,28},{28,24},{1,5},{5... | collective-permute-start | bytes 12582920 | tf_op jit(solution)/shard_map/ppermute | solution.py:699
  248.2 20.1 %collective-permute-start.34 = (bf16[4,4,128,1024]{3,2,1,0:T(8,128)(2,1)}, bf16[4,4,128,1024]{3,2,1,0:T(8,128)(2,1)}, u32[]{:S(2)}, u32[]{:S(2)}) collective-permute-start(bf16[4,4,128,1024]{3,2,1,0:T(8,128)(2,1)} %get-tuple-element.116), channel_id=1, source_target_pairs={{0,4},{4,0},{8,12},{12,8},{16,20},{20,16},{24,28},{28,24},{1,5},{5... | collective-permute-start | bytes 12582920 | tf_op jit(solution)/shard_map/ppermute | solution.py:699
  249.7 34.3 %all-to-all-start.1 = ((bf16[512,4,256]{2,0,1:T(8,128)(2,1)}), bf16[512,4,256]{2,0,1:T(8,128)(2,1)S(1)}, u32[]{:S(2)}, u32[]{:S(2)}) async-start(bf16[512,4,256]{2,0,1:T(8,128)(2,1)} %bitcast.121), calls=%async_computation.1 | async-start | bytes 2097152 | tf_op jit(solution)/shard_map/all_to_all | solution.py:1057
  267.4 58.8 %collective-permute-start.41 = (bf16[2,4,128,1024]{3,2,1,0:T(8,128)(2,1)}, bf16[2,4,128,1024]{3,2,1,0:T(8,128)(2,1)}, u32[]{:S(2)}, u32[]{:S(2)}) collective-permute-start(bf16[2,4,128,1024]{3,2,1,0:T(8,128)(2,1)} %get-tuple-element.131), channel_id=1, source_target_pairs={{0,8},{4,12},{8,0},{12,4},{16,24},{20,28},{24,16},{28,20},{1,9},{5... | collective-permute-start | bytes 6291464 | tf_op jit(solution)/shard_map/ppermute | solution.py:699
  268.4 10.2 %collective-permute-start.33 = (bf16[4,4,32,1024]{3,2,1,0:T(8,128)(2,1)S(1)}, bf16[4,4,32,1024]{3,2,1,0:T(8,128)(2,1)S(1)}, u32[]{:S(2)}, u32[]{:S(2)}) collective-permute-start(bf16[4,4,32,1024]{3,2,1,0:T(8,128)(2,1)S(1)} %copy-done.90), channel_id=1, source_target_pairs={{0,4},{4,0},{8,12},{12,8},{16,20},{20,16},{24,28},{28,24},{1,5},{5... | collective-permute-start | bytes 3145736 | tf_op jit(solution)/shard_map/ppermute | solution.py:699
  277.5 58.3 %collective-permute-start.40 = (bf16[2,4,128,1024]{3,2,1,0:T(8,128)(2,1)}, bf16[2,4,128,1024]{3,2,1,0:T(8,128)(2,1)}, u32[]{:S(2)}, u32[]{:S(2)}) collective-permute-start(bf16[2,4,128,1024]{3,2,1,0:T(8,128)(2,1)} %get-tuple-element.129), channel_id=1, source_target_pairs={{0,16},{4,20},{8,24},{12,28},{16,0},{20,4},{24,8},{28,12},{1,17},{... | collective-permute-start | bytes 6291464 | tf_op jit(solution)/shard_map/ppermute | solution.py:699
  320.3 27.7 %collective-permute-start.36 = (bf16[512,1024]{1,0:T(8,128)(2,1)}, bf16[512,1024]{1,0:T(8,128)(2,1)}, u32[]{:S(2)}, u32[]{:S(2)}) collective-permute-start(bf16[512,1024]{1,0:T(8,128)(2,1)} %get-tuple-element.125), channel_id=1, source_target_pairs={{0,1},{1,2},{2,3},{3,0},{4,5},{5,6},{6,7},{7,4},{8,9},{9,10},{10,1... | collective-permute-start | bytes 3145736 | tf_op jit(solution)/shard_map/ppermute | solution.py:712
  323.4 17.1 %collective-permute-start.37 = (bf16[1,4,32,1024]{3,2,1,0:T(8,128)(2,1)}, bf16[1,4,32,1024]{3,2,1,0:T(8,128)(2,1)S(1)}, u32[]{:S(2)}, u32[]{:S(2)}) collective-permute-start(bf16[1,4,32,1024]{3,2,1,0:T(8,128)(2,1)} %get-tuple-element.196), channel_id=1, source_target_pairs={{0,8},{4,12},{8,0},{12,4},{16,24},{20,28},{24,16},{28,20},{1,9},{5... | collective-permute-start | bytes 786440 | tf_op jit(solution)/shard_map/ppermute | solution.py:699
  325.7 14.8 %collective-permute-start.38 = (bf16[1,4,32,1024]{3,2,1,0:T(8,128)(2,1)}, bf16[1,4,32,1024]{3,2,1,0:T(8,128)(2,1)S(1)}, u32[]{:S(2)}, u32[]{:S(2)}) collective-permute-start(bf16[1,4,32,1024]{3,2,1,0:T(8,128)(2,1)} %get-tuple-element.197), channel_id=1, source_target_pairs={{0,16},{4,20},{8,24},{12,28},{16,0},{20,4},{24,8},{28,12},{1,17},{... | collective-permute-start | bytes 786440 | tf_op jit(solution)/shard_map/ppermute | solution.py:699
  326.2 15.0 %collective-permute-start.39 = (bf16[1,4,32,1024]{3,2,1,0:T(8,128)(2,1)}, bf16[1,4,32,1024]{3,2,1,0:T(8,128)(2,1)}, u32[]{:S(2)}, u32[]{:S(2)}) collective-permute-start(bf16[1,4,32,1024]{3,2,1,0:T(8,128)(2,1)} %get-tuple-element.195), channel_id=1, source_target_pairs={{0,24},{4,28},{8,16},{12,20},{16,8},{20,12},{24,0},{28,4},{1,25},{... | collective-permute-start | bytes 786440 | tf_op jit(solution)/shard_map/ppermute | solution.py:699
  356.3 26.8 %collective-permute-start.42 = (bf16[512,1024]{1,0:T(8,128)(2,1)}, bf16[512,1024]{1,0:T(8,128)(2,1)S(1)}, u32[]{:S(2)}, u32[]{:S(2)}) collective-permute-start(bf16[512,1024]{1,0:T(8,128)(2,1)} %copy-done.55), channel_id=1, source_target_pairs={{0,1},{1,2},{2,3},{3,0},{4,5},{5,6},{6,7},{7,4},{8,9},{9,10},{10,1... | collective-permute-start | bytes 3145736 | tf_op jit(solution)/shard_map/ppermute | solution.py:712
  356.5 26.9 %collective-permute-start.43 = (bf16[1,4,128,1024]{3,2,1,0:T(8,128)(2,1)}, bf16[1,4,128,1024]{3,2,1,0:T(8,128)(2,1)S(1)}, u32[]{:S(2)}, u32[]{:S(2)}) collective-permute-start(bf16[1,4,128,1024]{3,2,1,0:T(8,128)(2,1)} %copy-done.54), channel_id=1, source_target_pairs={{0,8},{4,12},{8,0},{12,4},{16,24},{20,28},{24,16},{28,20},{1,9},{5... | collective-permute-start | bytes 3145736 | tf_op jit(solution)/shard_map/ppermute | solution.py:699
  358.0 25.4 %collective-permute-start.44 = (bf16[1,4,128,1024]{3,2,1,0:T(8,128)(2,1)}, bf16[1,4,128,1024]{3,2,1,0:T(8,128)(2,1)S(1)}, u32[]{:S(2)}, u32[]{:S(2)}) collective-permute-start(bf16[1,4,128,1024]{3,2,1,0:T(8,128)(2,1)} %copy-done.53), channel_id=1, source_target_pairs={{0,16},{4,20},{8,24},{12,28},{16,0},{20,4},{24,8},{28,12},{1,17},{... | collective-permute-start | bytes 3145736 | tf_op jit(solution)/shard_map/ppermute | solution.py:699
  370.6 14.4 %collective-permute-start.46 = (bf16[4,4,48,768]{3,2,1,0:T(8,128)(2,1)}, bf16[4,4,48,768]{3,2,1,0:T(8,128)(2,1)S(1)}, u32[]{:S(2)}, u32[]{:S(2)}) collective-permute-start(bf16[4,4,48,768]{3,2,1,0:T(8,128)(2,1)} %get-tuple-element.161), channel_id=1, source_target_pairs={{0,4},{4,0},{8,12},{12,8},{16,20},{20,16},{24,28},{28,24},{1,5},{5... | collective-permute-start | bytes 3538952 | tf_op jit(solution)/shard_map/ppermute | solution.py:699
  385.0 15.9 %collective-permute-start.45 = (bf16[288,1024]{1,0:T(8,128)(2,1)S(1)}, bf16[288,1024]{1,0:T(8,128)(2,1)S(1)}, u32[]{:S(2)}, u32[]{:S(2)}) collective-permute-start(bf16[288,1024]{1,0:T(8,128)(2,1)S(1)} %get-tuple-element.158), channel_id=1, source_target_pairs={{0,1},{1,2},{2,3},{3,0},{4,5},{5,6},{6,7},{7,4},{8,9},{9,10},{10,1... | collective-permute-start | bytes 1769480 | tf_op jit(solution)/shard_map/ppermute | solution.py:712
  386.2 14.9 %collective-permute-start.48 = (bf16[4,48,768]{2,1,0:T(8,128)(2,1)S(1)}, bf16[4,48,768]{2,1,0:T(8,128)(2,1)S(1)}, u32[]{:S(2)}, u32[]{:S(2)}) collective-permute-start(bf16[4,48,768]{2,1,0:T(8,128)(2,1)S(1)} %get-tuple-element.166), channel_id=1, source_target_pairs={{0,8},{4,12},{8,0},{12,4},{16,24},{20,28},{24,16},{28,20},{1,9},{5... | collective-permute-start | bytes 884744 | tf_op jit(solution)/shard_map/ppermute | solution.py:699
  387.7 13.8 %collective-permute-start.49 = (bf16[4,48,768]{2,1,0:T(8,128)(2,1)S(1)}, bf16[4,48,768]{2,1,0:T(8,128)(2,1)S(1)}, u32[]{:S(2)}, u32[]{:S(2)}) collective-permute-start(bf16[4,48,768]{2,1,0:T(8,128)(2,1)S(1)} %get-tuple-element.167), channel_id=1, source_target_pairs={{0,16},{4,20},{8,24},{12,28},{16,0},{20,4},{24,8},{28,12},{1,17},{... | collective-permute-start | bytes 884744 | tf_op jit(solution)/shard_map/ppermute | solution.py:699
  388.2 13.3 %collective-permute-start.50 = (bf16[4,48,768]{2,1,0:T(8,128)(2,1)S(1)}, bf16[4,48,768]{2,1,0:T(8,128)(2,1)S(1)}, u32[]{:S(2)}, u32[]{:S(2)}) collective-permute-start(bf16[4,48,768]{2,1,0:T(8,128)(2,1)S(1)} %get-tuple-element.168), channel_id=1, source_target_pairs={{0,24},{4,28},{8,16},{12,20},{16,8},{20,12},{24,0},{28,4},{1,25},{... | collective-permute-start | bytes 884744 | tf_op jit(solution)/shard_map/ppermute | solution.py:699
  401.0 18.3 %collective-permute-start.47 = (bf16[288,1024]{1,0:T(8,128)(2,1)S(1)}, bf16[288,1024]{1,0:T(8,128)(2,1)S(1)}, u32[]{:S(2)}, u32[]{:S(2)}) collective-permute-start(bf16[288,1024]{1,0:T(8,128)(2,1)S(1)} %get-tuple-element.164), channel_id=1, source_target_pairs={{0,1},{1,2},{2,3},{3,0},{4,5},{5,6},{6,7},{7,4},{8,9},{9,10},{10,1... | collective-permute-start | bytes 1769480 | tf_op jit(solution)/shard_map/ppermute | solution.py:712
  402.3 16.9 %collective-permute-start.53 = (bf16[48,768]{1,0:T(8,128)(2,1)S(1)}, bf16[48,768]{1,0:T(8,128)(2,1)S(1)}, u32[]{:S(2)}, u32[]{:S(2)}) collective-permute-start(bf16[48,768]{1,0:T(8,128)(2,1)S(1)} %get-tuple-element.202), channel_id=1, source_target_pairs={{0,1},{1,2},{2,3},{3,0},{4,5},{5,6},{6,7},{7,4},{8,9},{9,10},{10,1... | collective-permute-start | bytes 221192 | tf_op jit(solution)/shard_map/ppermute | solution.py:712
  402.4 31.1 %collective-permute-start.54 = (bf16[48,768]{1,0:T(8,128)(2,1)S(1)}, bf16[48,768]{1,0:T(8,128)(2,1)S(1)}, u32[]{:S(2)}, u32[]{:S(2)}) collective-permute-start(bf16[48,768]{1,0:T(8,128)(2,1)S(1)} %get-tuple-element.201), channel_id=1, source_target_pairs={{0,2},{1,3},{2,0},{3,1},{4,6},{5,7},{6,4},{7,5},{8,10},{9,11},{10,... | collective-permute-start | bytes 221192 | tf_op jit(solution)/shard_map/ppermute | solution.py:712
  406.3 27.2 %collective-permute-start.55 = (bf16[48,768]{1,0:T(8,128)(2,1)S(1)}, bf16[48,768]{1,0:T(8,128)(2,1)S(1)}, u32[]{:S(2)}, u32[]{:S(2)}) collective-permute-start(bf16[48,768]{1,0:T(8,128)(2,1)S(1)} %get-tuple-element.200), channel_id=1, source_target_pairs={{0,3},{1,0},{2,1},{3,2},{4,7},{5,4},{6,5},{7,6},{8,11},{9,8},{10,9... | collective-permute-start | bytes 221192 | tf_op jit(solution)/shard_map/ppermute | solution.py:712
  419.4 14.1 %collective-permute-start.51 = (bf16[288,1024]{1,0:T(8,128)(2,1)S(1)}, bf16[288,1024]{1,0:T(8,128)(2,1)S(1)}, u32[]{:S(2)}, u32[]{:S(2)}) collective-permute-start(bf16[288,1024]{1,0:T(8,128)(2,1)S(1)} %get-tuple-element.171), channel_id=1, source_target_pairs={{0,1},{1,2},{2,3},{3,0},{4,5},{5,6},{6,7},{7,4},{8,9},{9,10},{10,1... | collective-permute-start | bytes 1769480 | tf_op jit(solution)/shard_map/ppermute | solution.py:712
  434.3 16.0 %collective-permute-start.56 = (bf16[208,1024]{1,0:T(8,128)(2,1)S(1)}, bf16[208,1024]{1,0:T(8,128)(2,1)S(1)}, u32[]{:S(2)}, u32[]{:S(2)}) collective-permute-start(bf16[208,1024]{1,0:T(8,128)(2,1)S(1)} %fusion.3), channel_id=1, source_target_pairs={{0,8},{4,12},{8,0},{12,4},{16,24},{20,28},{24,16},{28,20},{1,9},{5... | collective-permute-start | bytes 1277960 | tf_op jit(solution)/shard_map/ppermute | solution.py:699
  435.9 33.9 %collective-permute-start.52 = (bf16[512,1024]{1,0:T(8,128)(2,1)}, bf16[512,1024]{1,0:T(8,128)(2,1)S(1)}, u32[]{:S(2)}, u32[]{:S(2)}) collective-permute-start(bf16[512,1024]{1,0:T(8,128)(2,1)} %shard_map.308), channel_id=1, source_target_pairs={{0,1},{1,2},{2,3},{3,0},{4,5},{5,6},{6,7},{7,4},{8,9},{9,10},{10,1... | collective-permute-start | bytes 3145736 | tf_op jit(solution)/shard_map/ppermute | solution.py:712
  438.2 12.1 %collective-permute-start.57 = (bf16[192,1024]{1,0:T(8,128)(2,1)S(1)}, bf16[192,1024]{1,0:T(8,128)(2,1)S(1)}, u32[]{:S(2)}, u32[]{:S(2)}) collective-permute-start(bf16[192,1024]{1,0:T(8,128)(2,1)S(1)} %maximum_maximum_fusion), channel_id=1, source_target_pairs={{0,16},{4,20},{8,24},{12,28},{16,0},{20,4},{24,8},{28,12},{1,17},{... | collective-permute-start | bytes 1179656 | tf_op jit(solution)/shard_map/ppermute | solution.py:699
  438.7 20.8 %collective-permute-start.58 = (bf16[208,1024]{1,0:T(8,128)(2,1)S(1)}, bf16[208,1024]{1,0:T(8,128)(2,1)}, u32[]{:S(2)}, u32[]{:S(2)}) collective-permute-start(bf16[208,1024]{1,0:T(8,128)(2,1)S(1)} %fusion.3), channel_id=1, source_target_pairs={{0,16},{4,20},{8,24},{12,28},{16,0},{20,4},{24,8},{28,12},{1,17},{... | collective-permute-start | bytes 1277960 | tf_op jit(solution)/shard_map/ppermute | solution.py:699
  451.8 15.3 %collective-permute-start.59 = (bf16[208,1024]{1,0:T(8,128)(2,1)}, bf16[208,1024]{1,0:T(8,128)(2,1)}, u32[]{:S(2)}, u32[]{:S(2)}) collective-permute-start(bf16[208,1024]{1,0:T(8,128)(2,1)} %shard_map.310.refs_1_), channel_id=1, source_target_pairs={{0,16},{4,20},{8,24},{12,28},{16,0},{20,4},{24,8},{28,12},{1,17},{... | collective-permute-start | bytes 1277960 | tf_op jit(solution)/shard_map/ppermute | solution.py:699
  452.3 20.7 %collective-permute-start.61 = (bf16[192,1024]{1,0:T(8,128)(2,1)}, bf16[192,1024]{1,0:T(8,128)(2,1)}, u32[]{:S(2)}, u32[]{:S(2)}) collective-permute-start(bf16[192,1024]{1,0:T(8,128)(2,1)} %copy-done.76), channel_id=1, source_target_pairs={{0,8},{4,12},{8,0},{12,4},{16,24},{20,28},{24,16},{28,20},{1,9},{5... | collective-permute-start | bytes 1179656 | tf_op jit(solution)/shard_map/ppermute | solution.py:699
  453.3 19.7 %collective-permute-start.62 = (bf16[192,1024]{1,0:T(8,128)(2,1)}, bf16[192,1024]{1,0:T(8,128)(2,1)}, u32[]{:S(2)}, u32[]{:S(2)}) collective-permute-start(bf16[192,1024]{1,0:T(8,128)(2,1)} %shard_map.312), channel_id=1, source_target_pairs={{0,8},{4,12},{8,0},{12,4},{16,24},{20,28},{24,16},{28,20},{1,9},{5... | collective-permute-start | bytes 1179656 | tf_op jit(solution)/shard_map/ppermute | solution.py:699
  473.0 7.1 %collective-permute-start.60 = (bf16[4,208,1024]{2,1,0:T(8,128)(2,1)}, bf16[4,208,1024]{2,1,0:T(8,128)(2,1)}, u32[]{:S(2)}, u32[]{:S(2)}) collective-permute-start(bf16[4,208,1024]{2,1,0:T(8,128)(2,1)} %shard_map.311.own_a), channel_id=1, source_target_pairs={{0,4},{4,0},{8,12},{12,8},{16,20},{20,16},{24,28},{28,24},{1,5},{5... | collective-permute-start | bytes 5111816 | tf_op jit(solution)/shard_map/ppermute | solution.py:699
  476.5 3.6 collective-permute-start.63
  (94 other events, 768.1 us)
